TPU v7x, 32 devices: a whole 2x2x4 slice. The times are simulated.
32 devices in a mesh: dp: 2 (over x), rows: 4 (over z), cols: 4 (over y, core).
Axes of the slice: x: 2, y: 2, z: 4, core: 2. Of those that a mesh axis runs over, the one named last changes fastest.
Arguments:
- block_input: bfloat16 [768, 32768], P('cols', ('dp', 'rows')), may hold values from -6 to 6
- norm_gain_one: float32 [768], P('cols'), may hold values from 0.1 to 1.9
- w_query: bfloat16 [768, 768], P('cols', 'rows'), may hold values from -0.21875 to 0.21875
- w_key: bfloat16 [768, 768], P('cols', 'rows'), may hold values from -0.21875 to 0.21875
- w_value: bfloat16 [768, 768], P('cols', 'rows'), may hold values from -0.21875 to 0.21875
- w_out: bfloat16 [768, 768], P('rows', 'cols'), may hold values from -4 to 4
- norm_gain_two: float32 [768], P('cols'), may hold values from 0.1 to 1.9
- w_up: bfloat16 [768, 3072], P('cols', 'rows'), may hold values from -0.21875 to 0.21875
- w_down: bfloat16 [768, 3072], P('cols', 'rows'), may hold values from -0.15625 to 0.15625
- piece_start: int32 [8, 8], P(('dp', 'cols')), may hold values from 0 to 4032, as said below
- piece_len: int32 [8, 8], P(('dp', 'cols')), may hold values from 64 to 256, as said below
- grad_y: bfloat16 [768, 32768], P('cols', ('dp', 'rows')), may hold values from -6 to 6
Outputs:
- block_output: bfloat16 [768, 32768], P('cols', ('dp', 'rows'))
- grad_x: float32 [768, 32768], P('cols', ('dp', 'rows'))
- grad_gain_one: float32 [768], P('cols')
- grad_query: float32 [768, 768], P('cols', 'rows')
- grad_key: float32 [768, 768], P('cols', 'rows')
- grad_value: float32 [768, 768], P('cols', 'rows')
- grad_out: float32 [768, 768], P('rows', 'cols')
- grad_gain_two: float32 [768], P('cols')
- grad_up: float32 [768, 3072], P('cols', 'rows')
- grad_down: float32 [768, 3072], P('cols', 'rows')
Inputs may be any that keep to these rules, and one draw needn't show every extreme that they name: `piece_start`: piece k of a sequence lies inside positions k * 512 to (k + 1) * 512 - 1, so pieces are in order and never meet. `piece_len`: every sequence has a piece of exactly 256 positions.
All inputs are finite; a program needn't handle non-finite values.
Results may differ from a plain program's by a relative error of at most 0.019.
Values may be sent and summed in bfloat16 or wider, within the bound.
No kernel may reach another device: no remote copies, remote signals or barrier semaphores. Data moves between devices by JAX's collectives and lax.ppermute only.
A program may use at most 320 MiB of HBM per device.

v0:
```python
import jax
import jax.numpy as jnp
from jax import lax
from jax.sharding import PartitionSpec as P

D = 768
HEADS = 12
HD = 64
WIN = 1536
PIECE = 256
NPIECE = 8
LEN = 4096
QBLK = 512


EPSILON = 1e-06
MASKED = -1e30


def token_sums(per_token):
    return lax.psum(per_token, "cols")


def rows_gather(block_rows):
    return lax.all_gather(block_rows, "rows", axis=0, tiled=True)


def cols_gather(block_rows):
    return lax.all_gather(block_rows, "cols", axis=0, tiled=True)


def rows_project(left, right):
    return lax.psum_scatter(
        jnp.dot(left, right, preferred_element_type=jnp.float32).astype(jnp.bfloat16),
        "rows",
        scatter_dimension=0,
        tiled=True,
    ).astype(jnp.float32)


def cols_project(left, right):
    return lax.psum_scatter(
        jnp.dot(left, right, preferred_element_type=jnp.float32),
        "cols",
        scatter_dimension=0,
        tiled=True,
    )


def transposed_product(left, right):
    return lax.dot_general(
        left, right, (((0,), (0,)), ((), ())), preferred_element_type=jnp.float32
    )


def smooth_gate(value):
    return jax.nn.gelu(value, approximate=True)


def norm_forward(value, gain):
    row_total = token_sums(jnp.sum(value * value, axis=1))
    norm_scale = lax.rsqrt(row_total / D + EPSILON)
    return (norm_scale, (value * norm_scale[:, None] * gain[None, :]).astype(jnp.bfloat16))


def norm_backward(value, norm_scale, gain, grad_normed):
    weighted = grad_normed * gain[None, :]
    inner_sum = token_sums(jnp.sum(value * weighted, axis=1))
    cubed = norm_scale * norm_scale * norm_scale
    grad_value = norm_scale[:, None] * weighted - value * (cubed * inner_sum / D)[:, None]
    grad_gain = jnp.sum(grad_normed * value * norm_scale[:, None], axis=0)
    return (grad_value, grad_gain)


def piece_labels(starts, lengths):
    places = jnp.arange(LEN, dtype=jnp.int32)[:, None]
    inside = (places >= starts[None, :]) & (places < (starts + lengths)[None, :])
    numbers = jnp.arange(1, NPIECE + 1, dtype=jnp.int32)[None, :]
    return jnp.sum(jnp.where(inside, numbers, 0), axis=1) - 1


def block_scores(queries, key_rows, labels, block_start, query_first, head_count):
    span = min(WIN + QBLK + PIECE, LEN)
    key_first = jnp.clip(block_start - WIN, 0, LEN - span)
    query_block = lax.dynamic_slice_in_dim(queries, block_start - query_first, QBLK, 0).reshape(
        QBLK, head_count, HD
    )
    key_block = lax.dynamic_slice_in_dim(key_rows, key_first, span, 0).reshape(span, head_count, HD)
    raw_scores = jnp.einsum(
        "qhd,khd->hqk", query_block, key_block, preferred_element_type=jnp.float32
    ) * HD ** (-0.5)
    query_pos = block_start + jnp.arange(QBLK, dtype=jnp.int32)
    key_pos = key_first + jnp.arange(span, dtype=jnp.int32)
    query_lab = lax.dynamic_slice_in_dim(labels, block_start, QBLK, 0)
    key_lab = lax.dynamic_slice_in_dim(labels, key_first, span, 0)
    near = (key_pos[None, :] <= query_pos[:, None]) & (query_pos[:, None] - key_pos[None, :] < WIN)
    same = (query_lab[:, None] == key_lab[None, :]) & (query_lab[:, None] >= 0)
    logits = jnp.where((near | same)[None], raw_scores, MASKED)
    return (logits, key_first, query_block, key_block)


def attend_forward(queries, key_rows, value_rows, labels, head_count, query_first):
    span = min(WIN + QBLK + PIECE, LEN)

    def one_block(block_start):
        logits, key_first, query_block, key_block = block_scores(
            queries, key_rows, labels, block_start, query_first, head_count
        )
        value_block = lax.dynamic_slice_in_dim(value_rows, key_first, span, 0).reshape(
            span, head_count, HD
        )
        row_peak = jnp.max(logits, axis=2, keepdims=True)
        expo_part = jnp.exp(logits - row_peak)
        row_total = jnp.sum(expo_part, axis=2, keepdims=True)
        prob_low = (expo_part / row_total).astype(jnp.bfloat16)
        block_out = jnp.einsum(
            "hqk,khd->qhd", prob_low, value_block, preferred_element_type=jnp.float32
        )
        return (block_out.reshape(QBLK, head_count * HD), (row_peak + jnp.log(row_total))[:, :, 0])

    block_starts = query_first + jnp.arange(queries.shape[0] // QBLK, dtype=jnp.int32) * QBLK
    block_outs, log_totals = lax.map(one_block, block_starts)
    return (block_outs.reshape(queries.shape[0], head_count * HD), log_totals)


def attend_backward(
    queries, key_rows, value_rows, labels, log_totals, grad_attended, head_count, query_first
):
    span = min(WIN + QBLK + PIECE, LEN)
    head_width = head_count * HD
    factor = HD ** (-0.5)

    def one_block(carry, block_items):
        grad_keys, grad_values = carry
        block_start, block_log = block_items
        logits, key_first, query_block, key_block = block_scores(
            queries, key_rows, labels, block_start, query_first, head_count
        )
        value_block = lax.dynamic_slice_in_dim(value_rows, key_first, span, 0).reshape(
            span, head_count, HD
        )
        grad_block = lax.dynamic_slice_in_dim(grad_attended, block_start - query_first, QBLK, 0)
        grad_block = grad_block.reshape(QBLK, head_count, HD)
        prob_full = jnp.exp(logits - block_log[:, :, None])
        prob_low = prob_full.astype(jnp.bfloat16)
        grad_probs = jnp.einsum(
            "qhd,khd->hqk", grad_block, value_block, preferred_element_type=jnp.float32
        )
        inner_sum = jnp.sum(prob_full * grad_probs, axis=2, keepdims=True)
        grad_scores = (prob_full * (grad_probs - inner_sum)).astype(jnp.bfloat16)
        grad_q = (
            jnp.einsum("hqk,khd->qhd", grad_scores, key_block, preferred_element_type=jnp.float32)
            * factor
        )
        grad_k = (
            jnp.einsum("hqk,qhd->khd", grad_scores, query_block, preferred_element_type=jnp.float32)
            * factor
        )
        grad_v = jnp.einsum(
            "hqk,qhd->khd", prob_low, grad_block, preferred_element_type=jnp.float32
        )
        old_keys = lax.dynamic_slice_in_dim(grad_keys, key_first, span, 0)
        grad_keys = lax.dynamic_update_slice_in_dim(
            grad_keys, old_keys + grad_k.reshape(span, head_width), key_first, 0
        )
        old_values = lax.dynamic_slice_in_dim(grad_values, key_first, span, 0)
        grad_values = lax.dynamic_update_slice_in_dim(
            grad_values, old_values + grad_v.reshape(span, head_width), key_first, 0
        )
        return ((grad_keys, grad_values), grad_q.reshape(QBLK, head_width))

    block_starts = query_first + jnp.arange(queries.shape[0] // QBLK, dtype=jnp.int32) * QBLK
    empty = jnp.zeros((key_rows.shape[0], head_width), jnp.float32)
    (grad_keys, grad_values), grad_queries = lax.scan(
        one_block, (empty, empty), (block_starts, log_totals)
    )
    return (grad_queries.reshape(queries.shape[0], head_width), grad_keys, grad_values)


def per_device(
    block_input,
    norm_gain_one,
    w_query,
    w_key,
    w_value,
    w_out,
    norm_gain_two,
    w_up,
    w_down,
    piece_start,
    piece_len,
    grad_y,
):
    row_count = lax.axis_size("rows")
    head_count = HEADS // row_count
    head_width = w_query.shape[1]
    residual = block_input.T.astype(jnp.float32)
    grad_rows = grad_y.T
    scale_one, normed_one = norm_forward(residual, norm_gain_one)
    joined = jnp.concatenate([w_query, w_key, w_value], axis=1)
    labels = jax.vmap(piece_labels)(piece_start, piece_len)
    seq_count = piece_start.shape[0]
    normed_one_all = rows_gather(normed_one)
    projected = cols_project(normed_one_all, joined).astype(jnp.bfloat16)
    queries = projected[:, :head_width].reshape(seq_count, LEN, head_width)
    key_rows = projected[:, head_width : 2 * head_width].reshape(seq_count, LEN, head_width)
    value_rows = projected[:, 2 * head_width :].reshape(seq_count, LEN, head_width)

    def forward_sequence(items):
        return attend_forward(items[0], items[1], items[2], items[3], head_count, 0)

    attn_mixed, log_totals = lax.map(forward_sequence, (queries, key_rows, value_rows, labels))
    attended = attn_mixed.reshape(seq_count * LEN, head_width).astype(jnp.bfloat16)
    attended_all = cols_gather(attended)
    middle = residual + rows_project(attended_all, w_out)
    scale_two, normed_two = norm_forward(middle, norm_gain_two)
    normed_two_all = rows_gather(normed_two)
    up_value = cols_project(normed_two_all, w_up)
    gate_act, gelu_pull = jax.vjp(smooth_gate, up_value)
    gate_all = cols_gather(gate_act.astype(jnp.bfloat16))
    mlp_out = rows_project(gate_all, w_down.T)
    grad_all = rows_gather(grad_rows)
    grad_down = transposed_product(grad_all, gate_all)
    grad_act = cols_project(grad_all, w_down)
    grad_upval = gelu_pull(grad_act)[0].astype(jnp.bfloat16)
    grad_up_all = cols_gather(grad_upval)
    grad_upw = transposed_product(normed_two_all, grad_up_all)
    grad_normed_two = rows_project(grad_up_all, w_up.T)
    output = (middle + mlp_out).astype(jnp.bfloat16)
    grad_mid_norm, grad_gain_two = norm_backward(middle, scale_two, norm_gain_two, grad_normed_two)
    grad_middle = grad_rows.astype(jnp.float32) + grad_mid_norm
    seq_count = piece_start.shape[0]
    grad_mid_all = rows_gather(grad_middle.astype(jnp.bfloat16))
    grad_outw = transposed_product(attended_all, grad_mid_all)
    grad_attended = cols_project(grad_mid_all, w_out.T).astype(jnp.bfloat16)
    grad_attended = grad_attended.reshape(seq_count, LEN, head_width)

    def backward_sequence(items):
        return attend_backward(
            items[0], items[1], items[2], items[3], items[4], items[5], head_count, 0
        )

    grad_q, grad_k, grad_v = lax.map(
        backward_sequence, (queries, key_rows, value_rows, labels, log_totals, grad_attended)
    )
    grad_projected = jnp.concatenate([grad_q, grad_k, grad_v], axis=-1)
    grad_projected = grad_projected.reshape(seq_count * LEN, 3 * head_width).astype(jnp.bfloat16)
    grad_proj_all = cols_gather(grad_projected)
    grad_joined = transposed_product(normed_one_all, grad_proj_all)
    grad_normed_one = rows_project(grad_proj_all, joined.T)
    grad_res_norm, grad_gain_one = norm_backward(
        residual, scale_one, norm_gain_one, grad_normed_one
    )
    grad_x = grad_middle + grad_res_norm
    grad_down, grad_upw, grad_outw, grad_joined = (
        lax.psum(grad_down.astype(jnp.bfloat16), "dp").astype(jnp.float32),
        lax.psum(grad_upw.astype(jnp.bfloat16), "dp").astype(jnp.float32),
        lax.psum(grad_outw.astype(jnp.bfloat16), "dp").astype(jnp.float32),
        lax.psum(grad_joined.astype(jnp.bfloat16), "dp").astype(jnp.float32),
    )
    gain_one_sum, gain_two_sum = lax.psum((grad_gain_one, grad_gain_two), ("dp", "rows"))
    grad_query = grad_joined[:, :head_width]
    grad_key = grad_joined[:, head_width : 2 * head_width]
    grad_value = grad_joined[:, 2 * head_width :]
    return (
        output.T,
        grad_x.T,
        gain_one_sum,
        grad_query,
        grad_key,
        grad_value,
        grad_outw,
        gain_two_sum,
        grad_upw,
        grad_down,
    )


def solution(mesh):
    return jax.shard_map(
        per_device,
        mesh=mesh,
        in_specs=(
            P("cols", ("dp", "rows")),
            P("cols"),
            P("cols", "rows"),
            P("cols", "rows"),
            P("cols", "rows"),
            P("rows", "cols"),
            P("cols"),
            P("cols", "rows"),
            P("cols", "rows"),
            P(("dp", "cols"), None),
            P(("dp", "cols"), None),
            P("cols", ("dp", "rows")),
        ),
        out_specs=(
            P("cols", ("dp", "rows")),
            P("cols", ("dp", "rows")),
            P("cols"),
            P("cols", "rows"),
            P("cols", "rows"),
            P("cols", "rows"),
            P("rows", "cols"),
            P("cols"),
            P("cols", "rows"),
            P("cols", "rows"),
        ),
        check_vma=False,
    )
```

profile of v0, /device:TPU:24, one launch (start us, length us, event | category | flops | bytes accessed | tf_op | source)
XLA Modules:
  0.0 3189.8 jit_solution(15321091390087707084)
XLA Ops:
  9.1 11.2 psum.70
  24.1 112.4 %all-gather.10.cloned.1.call-done = bf16[16384,192]{0,1:T(8,128)(2,1)} async-done(((bf16[4096,192]{0,1:T(8,128)(2,1)}), bf16[16384,192]{0,1:T(8,128)(2,1)}) %all-gather.10.cloned.1.call-update) | async-done | bytes 6291472 | tf_op jit(solution)/shard_map/all_gather | solution.py:25
  136.5 16.9 fusion.46
  154.7 261.6 %reduce-scatter.9.cloned.1.call-done = f32[4096,576]{0,1:T(8,128)} async-done(((f32[16384,576]{0,1:T(8,128)}), f32[4096,576]{0,1:T(8,128)}) %reduce-scatter.9.cloned.1.call-update) | async-done | bytes 9437200 | tf_op jit(solution)/shard_map/reduce_scatter | solution.py:42
  423.5 172.0 %while.50 = (s32[]{:T(128)}, bf16[8,512,192]{1,2,0:T(8,128)(2,1)}, f32[8,3,512]{2,1,0:T(4,128)}, s32[8]{0:T(128)}, bf16[4096,192]{0,1:T(8,128)(2,1)S(1)}, /*inde...) while((s32[]{:T(128)}, bf16[8,512,192]{1,2,0:T(8,128)(2,1)}, ...), condition=%wide.region_7.8_spmd, body=%wide.region_4.7_spmd.sunk | while | flops 956696320 | bytes 53783784 | solution.py:122
  598.9 46.5 %all-gather.12.cloned.1.call-done = bf16[16384,192]{0,1:T(8,128)(2,1)} async-done(((bf16[4096,192]{0,1:T(8,128)(2,1)}), bf16[16384,192]{0,1:T(8,128)(2,1)}) %all-gather.12.cloned.1.call-update) | async-done | bytes 6291472 | tf_op jit(solution)/shard_map/all_gather | solution.py:29
  653.3 109.5 %reduce-scatter.11.cloned.1.call-done = bf16[4096,192]{0,1:T(8,128)(2,1)} async-done(((bf16[16384,192]{0,1:T(8,128)(2,1)}), bf16[4096,192]{0,1:T(8,128)(2,1)}) %reduce-scatter.11.cloned.1.call-update) | async-done | bytes 1572880 | tf_op jit(solution)/shard_map/reduce_scatter | solution.py:33
  765.4 12.8 psum.71
  782.8 95.1 %all-gather.18.cloned.1.call-done = bf16[16384,192]{0,1:T(8,128)(2,1)} async-done(((bf16[4096,192]{0,1:T(8,128)(2,1)}), bf16[16384,192]{0,1:T(8,128)(2,1)}) %all-gather.18.cloned.1.call-update) | async-done | bytes 6291472 | tf_op jit(solution)/shard_map/all_gather | solution.py:25
  877.9 22.9 fusion.57
  900.9 92.7 %all-gather.14.cloned.1.call-done = bf16[16384,192]{0,1:T(8,128)(2,1)} async-done(((bf16[4096,192]{0,1:T(8,128)(2,1)}), bf16[16384,192]{0,1:T(8,128)(2,1)}) %all-gather.14.cloned.1.call-update) | async-done | bytes 6291472 | tf_op jit(solution)/shard_map/all_gather | solution.py:25
  993.6 30.7 fusion.56
  1024.3 316.5 %reduce-scatter.17.cloned.1.call-done = f32[4096,768]{1,0:T(8,128)} async-done(((f32[16384,768]{1,0:T(8,128)}), f32[4096,768]{1,0:T(8,128)}) %reduce-scatter.17.cloned.1.call-update) | async-done | bytes 12582928 | tf_op jit(solution)/shard_map/reduce_scatter | solution.py:42
  1340.8 345.8 %reduce-scatter.13.cloned.1.call-done = f32[4096,768]{1,0:T(8,128)} async-done(((f32[16384,768]{1,0:T(8,128)}), f32[4096,768]{1,0:T(8,128)}) %reduce-scatter.13.cloned.1.call-update) | async-done | bytes 12582928 | tf_op jit(solution)/shard_map/reduce_scatter | solution.py:42
  1686.6 18.2 fusion.20
  1705.1 154.7 %all-gather.20.cloned.1.call-done = bf16[16384,768]{1,0:T(8,128)(2,1)} async-done(((bf16[4096,768]{1,0:T(8,128)(2,1)}), bf16[16384,768]{1,0:T(8,128)(2,1)}) %all-gather.20.cloned.1.call-update) | async-done | bytes 25165840 | tf_op jit(solution)/shard_map/all_gather | solution.py:29
  1859.8 25.1 convolution_convert_fusion.1
  1885.0 110.1 %reduce-scatter.19.cloned.1.call-done = bf16[4096,192]{0,1:T(8,128)(2,1)} async-done(((bf16[16384,192]{0,1:T(8,128)(2,1)}), bf16[4096,192]{0,1:T(8,128)(2,1)}) %reduce-scatter.19.cloned.1.call-update) | async-done | bytes 1572880 | tf_op jit(solution)/shard_map/reduce_scatter | solution.py:33
  1999.0 11.4 psum.72
  2015.2 112.5 %all-gather.22.cloned.1.call-done = bf16[16384,192]{0,1:T(8,128)(2,1)} async-done(((bf16[4096,192]{0,1:T(8,128)(2,1)}), bf16[16384,192]{0,1:T(8,128)(2,1)}) %all-gather.22.cloned.1.call-update) | async-done | bytes 6291472 | tf_op jit(solution)/shard_map/all_gather | solution.py:25
  2127.7 9.0 fusion.58
  2137.6 99.7 %reduce-scatter.21.cloned.1.call-done = f32[4096,192]{0,1:T(8,128)} async-done(((f32[16384,192]{0,1:T(8,128)}), f32[4096,192]{0,1:T(8,128)}) %reduce-scatter.21.cloned.1.call-update) | async-done | bytes 3145744 | tf_op jit(solution)/shard_map/reduce_scatter | solution.py:42
  2245.9 519.1 %while.51 = (s32[]{:T(128)}, f32[4096,192]{0,1:T(8,128)}, f32[4096,192]{0,1:T(8,128)}, bf16[8,512,192]{1,2,0:T(8,128)(2,1)}, s32[8]{0:T(128)}, /*index=5*/bf16[4...) while((s32[]{:T(128)}, f32[4096,192]{0,1:T(8,128)}, ...), condition=%wide.region_20.21_spmd, body=%wide.region_18.20_spmd.sunk | while | flops 2306557696 | bytes 204266416 | solution.py:174
  2254.5 9.0 fusion.128
  2266.9 8.2 multiply_reduce_fusion.3
  2290.5 8.6 dynamic_update_slice.56
  2332.0 8.3 multiply_reduce_fusion.3
  2355.9 8.6 dynamic_update_slice.56
  2397.2 8.2 multiply_reduce_fusion.3
  2420.8 8.6 dynamic_update_slice.56
  2462.0 8.2 multiply_reduce_fusion.3
  2485.7 8.6 dynamic_update_slice.56
  2526.8 8.2 multiply_reduce_fusion.3
  2550.5 8.5 dynamic_update_slice.56
  2591.5 8.2 multiply_reduce_fusion.3
  2615.2 8.4 dynamic_update_slice.56
  2656.0 8.2 multiply_reduce_fusion.3
  2720.0 8.3 multiply_reduce_fusion.3
  2777.5 17.4 convolution_convert_fusion.5
  2795.0 16.9 fusion.43
  2818.9 79.6 %all-gather.24.cloned.1.call-done = bf16[1,16384,576]{1,2,0:T(8,128)(2,1)} async-done(((bf16[1,4096,576]{1,2,0:T(8,128)(2,1)}), bf16[1,16384,576]{1,2,0:T(8,128)(2,1)}) %all-gather.24.cloned.1.call-update) | async-done | bytes 18874384 | tf_op jit(solution)/shard_map/all_gather | solution.py:29
  2898.5 12.7 fusion.40
  2911.3 15.7 convolution_convert_fusion.3
  2928.0 25.2 convolution_convert_fusion.2
  2960.7 100.9 %reduce-scatter.23.cloned.1.call-done = bf16[4096,192]{0,1:T(8,128)(2,1)} async-done(((bf16[16384,192]{0,1:T(8,128)(2,1)}), bf16[4096,192]{0,1:T(8,128)(2,1)}) %reduce-scatter.23.cloned.1.call-update) | async-done | bytes 1572880 | tf_op jit(solution)/shard_map/reduce_scatter | solution.py:33
  3064.5 19.1 all-reduce
  3083.7 11.2 psum.73
  3094.9 80.8 %reduce-scatter.15.cloned.1.call-done = bf16[4096,192]{0,1:T(8,128)(2,1)} async-done(((bf16[16384,192]{0,1:T(8,128)(2,1)}), bf16[4096,192]{0,1:T(8,128)(2,1)}) %reduce-scatter.15.cloned.1.call-update) | async-done | bytes 1572880 | tf_op jit(solution)/shard_map/reduce_scatter | solution.py:33
  (473 shorter events, 610.9 us)
Async XLA Ops:
  7.2 986.4 %copy-start = (bf16[192,768]{1,0:T(8,128)(2,1)S(1)}, bf16[192,768]{1,0:T(8,128)(2,1)}, u32[]{:S(2)}) copy-start(bf16[192,768]{1,0:T(8,128)(2,1)} %param.23) | copy-start | bytes 884740
  7.2 129.3 %copy-start.21 = (bf16[192,192]{1,0:T(8,128)(2,1)S(1)}, bf16[192,192]{1,0:T(8,128)(2,1)}, u32[]{:S(2)}) copy-start(bf16[192,192]{1,0:T(8,128)(2,1)} %param.18) | copy-start | bytes 221188
  7.2 129.3 %copy-start.19 = (bf16[192,192]{1,0:T(8,128)(2,1)S(1)}, bf16[192,192]{1,0:T(8,128)(2,1)}, u32[]{:S(2)}) copy-start(bf16[192,192]{1,0:T(8,128)(2,1)} %param.19) | copy-start | bytes 221188
  7.2 129.3 %copy-start.17 = (bf16[192,192]{1,0:T(8,128)(2,1)S(1)}, bf16[192,192]{1,0:T(8,128)(2,1)}, u32[]{:S(2)}) copy-start(bf16[192,192]{1,0:T(8,128)(2,1)} %param.20) | copy-start | bytes 221188
  7.2 129.3 %all-gather.10.cloned.1.call-start = ((), (), s32[]{:S(2)}) async-start(), calls=%async_computation.8 | async-start | bytes 7864320 | tf_op jit(solution)/shard_map/all_gather | solution.py:25
  20.4 133.1 %copy-start.26 = (f32[4096]{0:T(1024)}, f32[4096]{0:T(1024)S(1)}, u32[]{:S(2)}) copy-start(f32[4096]{0:T(1024)S(1)} %psum.70) | copy-start | bytes 49156
  24.0 392.3 %reduce-scatter.9.cloned.1.call-start = ((), (), s32[]{:S(2)}) async-start(), calls=%async_computation.9 | async-start | bytes 47185920 | tf_op jit(solution)/shard_map/reduce_scatter | solution.py:42
  153.4 491.9 %all-gather.12.cloned.1.call-start = ((), (), s32[]{:S(2)}) async-start(), calls=%async_computation.10 | async-start | bytes 7864320 | tf_op jit(solution)/shard_map/all_gather | solution.py:29
  595.5 57.2 %copy-start.8 = (bf16[4096,192]{0,1:T(8,128)(2,1)}, bf16[4096,192]{0,1:T(8,128)(2,1)S(1)}, u32[]{:S(2)}) copy-start(bf16[4096,192]{0,1:T(8,128)(2,1)S(1)} %get-tuple-element.638) | copy-start | bytes 4718596
  595.5 49.9 %copy-start.13 = (bf16[192,192]{1,0:T(8,128)(2,1)S(1)}, bf16[192,192]{1,0:T(8,128)(2,1)}, u32[]{:S(2)}) copy-start(bf16[192,192]{1,0:T(8,128)(2,1)} %param.21) | copy-start | bytes 221188
  598.8 164.0 %reduce-scatter.11.cloned.1.call-start = ((), (), s32[]{:S(2)}) async-start(), calls=%async_computation.11 | async-start | bytes 7864320 | tf_op jit(solution)/shard_map/reduce_scatter | solution.py:33
  652.6 110.2 %copy-start.3 = (bf16[192,4096]{1,0:T(8,128)(2,1)S(1)}, bf16[192,4096]{1,0:T(8,128)(2,1)}, u32[]{:S(2)}) copy-start(bf16[192,4096]{1,0:T(8,128)(2,1)} %param.16) | copy-start | bytes 4718596
  652.7 225.3 %all-gather.18.cloned.1.call-start = ((), (), s32[]{:S(2)}) async-start(), calls=%async_computation.16 | async-start | bytes 7864320 | tf_op jit(solution)/shard_map/all_gather | solution.py:25
  653.2 340.3 %all-gather.14.cloned.1.call-start = ((), (), s32[]{:S(2)}) async-start(), calls=%async_computation.12 | async-start | bytes 7864320 | tf_op jit(solution)/shard_map/all_gather | solution.py:25
  782.7 558.1 %reduce-scatter.17.cloned.1.call-start = ((), (), s32[]{:S(2)}) async-start(), calls=%async_computation.17 | async-start | bytes 62914560 | tf_op jit(solution)/shard_map/reduce_scatter | solution.py:42
  900.8 785.8 %reduce-scatter.13.cloned.1.call-start = ((), (), s32[]{:S(2)}) async-start(), calls=%async_computation.13 | async-start | bytes 62914560 | tf_op jit(solution)/shard_map/reduce_scatter | solution.py:42
  1024.3 835.5 %all-gather.20.cloned.1.call-start = ((), (), s32[]{:S(2)}) async-start(), calls=%async_computation.18 | async-start | bytes 31457280 | tf_op jit(solution)/shard_map/all_gather | solution.py:29
  1704.9 290.2 %reduce-scatter.19.cloned.1.call-start = ((), (), s32[]{:S(2)}) async-start(), calls=%async_computation.19 | async-start | bytes 7864320 | tf_op jit(solution)/shard_map/reduce_scatter | solution.py:33
  1884.9 110.2 %copy-start.15 = (f32[4096]{0:T(1024)S(1)}, f32[4096]{0:T(1024)}, u32[]{:S(2)}) copy-start(f32[4096]{0:T(1024)} %copy-done.14) | copy-start | bytes 49156
  1884.9 110.2 %copy-start.31 = (f32[192]{0:T(256)S(1)}, f32[192]{0:T(256)}, u32[]{:S(2)}) copy-start(f32[192]{0:T(256)} %param.22) | copy-start | bytes 2308
  1884.9 125.4 %copy-start.28 = (f32[4096]{0:T(1024)S(1)}, f32[4096]{0:T(1024)}, u32[]{:S(2)}) copy-start(f32[4096]{0:T(1024)} %psum.71) | copy-start | bytes 49156
  1884.9 242.8 %all-gather.22.cloned.1.call-start = ((), (), s32[]{:S(2)}) async-start(), calls=%async_computation.20 | async-start | bytes 7864320 | tf_op jit(solution)/shard_map/all_gather | solution.py:25
  2015.2 222.1 %reduce-scatter.21.cloned.1.call-start = ((), (), s32[]{:S(2)}) async-start(), calls=%async_computation.21 | async-start | bytes 15728640 | tf_op jit(solution)/shard_map/reduce_scatter | solution.py:42
  2136.8 658.2 %all-gather.16.cloned.1.call-start = ((), (), s32[]{:S(2)}) async-start(), calls=%async_computation.14 | async-start | bytes 31457280 | tf_op jit(solution)/shard_map/all_gather | solution.py:29
  2137.6 761.0 %all-gather.24.cloned.1.call-start = ((), (), s32[]{:S(2)}) async-start(), calls=%async_computation.23 | async-start | bytes 23592960 | tf_op jit(solution)/shard_map/all_gather | solution.py:29
  2246.3 17.3 copy-start.9
  2313.5 15.2 copy-start.9
  2378.7 15.2 copy-start.9
  2443.5 15.2 copy-start.9
  2508.4 15.2 copy-start.9
  2573.0 15.2 copy-start.9
  2637.5 15.2 copy-start.9
  2701.6 15.1 copy-start.9
  2777.5 175.9 %all-reduce.4.cloned.1.call-start = ((), (), s32[]{:S(2)}) async-start(), calls=%async_computation.24 | async-start | bytes 1867776 | tf_op jit(solution)/shard_map/psum | solution.py:259
  2818.9 92.4 %copy-start.18 = (bf16[192,192]{1,0:T(8,128)(2,1)S(1)}, bf16[192,192]{1,0:T(8,128)(2,1)}, u32[]{:S(2)}) copy-start(bf16[192,192]{1,0:T(8,128)(2,1)} %param.20) | copy-start | bytes 221188
  2818.9 92.4 %copy-start.20 = (bf16[192,192]{1,0:T(8,128)(2,1)S(1)}, bf16[192,192]{1,0:T(8,128)(2,1)}, u32[]{:S(2)}) copy-start(bf16[192,192]{1,0:T(8,128)(2,1)} %param.19) | copy-start | bytes 221188
  2818.9 92.4 %copy-start.22 = (bf16[192,192]{1,0:T(8,128)(2,1)S(1)}, bf16[192,192]{1,0:T(8,128)(2,1)}, u32[]{:S(2)}) copy-start(bf16[192,192]{1,0:T(8,128)(2,1)} %param.18) | copy-start | bytes 221188
  2911.2 150.4 %reduce-scatter.23.cloned.1.call-start = ((), (), s32[]{:S(2)}) async-start(), calls=%async_computation.22 | async-start | bytes 7864320 | tf_op jit(solution)/shard_map/reduce_scatter | solution.py:33
  2927.1 248.5 %reduce-scatter.15.cloned.1.call-start = ((), (), s32[]{:S(2)}) async-start(), calls=%async_computation.15 | async-start | bytes 7864320 | tf_op jit(solution)/shard_map/reduce_scatter | solution.py:33
  2953.2 108.4 %copy-start.4 = (bf16[192,4096]{1,0:T(8,128)(2,1)S(1)}, bf16[192,4096]{1,0:T(8,128)(2,1)}, u32[]{:S(2)}) copy-start(bf16[192,4096]{1,0:T(8,128)(2,1)} %param.16) | copy-start | bytes 4718596
  2953.2 108.4 %copy-start.25 = (f32[4096]{0:T(1024)S(1)}, f32[4096]{0:T(1024)}, u32[]{:S(2)}) copy-start(f32[4096]{0:T(1024)} %copy-done.24) | copy-start | bytes 49156
  2953.2 108.4 %copy-start.33 = (f32[192]{0:T(256)S(1)}, f32[192]{0:T(256)}, u32[]{:S(2)}) copy-start(f32[192]{0:T(256)} %param.17) | copy-start | bytes 2308
  2953.3 111.3 %copy-start.34 = (f32[192]{0:T(256)S(1)}, f32[192]{0:T(256)}, u32[]{:S(2)}) copy-start(f32[192]{0:T(256)} %get-tuple-element.307) | copy-start | bytes 2308
  2953.3 141.6 %copy-start.27 = (f32[4096]{0:T(1024)S(1)}, f32[4096]{0:T(1024)}, u32[]{:S(2)}) copy-start(f32[4096]{0:T(1024)} %copy-done.26) | copy-start | bytes 49156
  2953.3 222.4 %copy-start.11 = (bf16[4096,192]{0,1:T(8,128)(2,1)S(1)}, bf16[4096,192]{0,1:T(8,128)(2,1)}, u32[]{:S(2)}) copy-start(bf16[4096,192]{0,1:T(8,128)(2,1)} %reduce-scatter.11.cloned.1.call-done) | copy-start | bytes 4718596
  2953.3 222.4 %copy-start.16 = (f32[4096]{0:T(1024)S(1)}, f32[4096]{0:T(1024)}, u32[]{:S(2)}) copy-start(f32[4096]{0:T(1024)} %copy-done.14) | copy-start | bytes 49156
  2953.3 222.3 %copy-start.30 = (f32[4096]{0:T(1024)S(1)}, f32[4096]{0:T(1024)}, u32[]{:S(2)}) copy-start(f32[4096]{0:T(1024)} %copy-done.29) | copy-start | bytes 49156
  2953.3 222.3 %copy-start.32 = (f32[192]{0:T(256)S(1)}, f32[192]{0:T(256)}, u32[]{:S(2)}) copy-start(f32[192]{0:T(256)} %param.22) | copy-start | bytes 2308
  (41 other events, 135.8 us)
Sparse Core Ops, SparseCore 0:
  24.2 112.3 all-gather.9
  153.6 262.7 reduce-scatter.8
  598.9 46.3 all-gather.11
  652.8 109.9 reduce-scatter.10
  764.3 113.5 all-gather.17
  880.0 113.5 all-gather.13
  996.3 344.3 reduce-scatter.16
  1343.4 343.1 reduce-scatter.12
  1705.0 154.7 all-gather.19
  1885.0 109.9 reduce-scatter.18
  2015.3 112.4 all-gather.21
  2136.9 100.2 reduce-scatter.20
  2238.9 154.7 all-gather.15
  2777.6 120.8 all-gather.23
  2911.4 38.0 all-reduce.3
  2951.6 110.0 reduce-scatter.22
  3063.8 111.7 reduce-scatter.14
where the time goes:
time: 3200 us; the launch traced here: 3190 us
  waiting for transfers between devices  2120 us (66%)
  matrix products  458 us (14%)
  local copies, waits for them, and re-layouts  272 us (8%)
  other arithmetic  214 us (7%)
  blocking collectives  65.7 us (2%)
  loops' own time  43.1 us (1%)
    reduce_scatter x4, waiting for transfers between devices, cols_project(): lax.psum_scatter(jnp.dot(left, right, preferred_element_type=jnp.float32)...  1020 us
    all_gather x4, waiting for transfers between devices, rows_gather(): return lax.all_gather(block_rows, 'rows', axis=0, tiled=True)  413 us
    reduce_scatter x4, waiting for transfers between devices, rows_project(): lax.psum_scatter(jnp.dot(left, right, preferred_element_type=jnp.float32)...  401 us
    all_gather x4, waiting for transfers between devices, cols_gather(): return lax.all_gather(block_rows, 'cols', axis=0, tiled=True)  281 us
    dot_general x16, matrix products, block_scores(): jnp.einsum('qhd,khd->hqk', query_block, key_block, preferred_element_type...  90.7 us
    dot_general x4, matrix products, cols_project(): jnp.dot(left, right, preferred_element_type=jnp.float32)  79.5 us
    dot_general x4, matrix products, rows_project(): jnp.dot(left, right, preferred_element_type=jnp.float32)  73.3 us
    dynamic_update_slice x8, local copies, waits for them, and re-layouts, one_block(): lax.dynamic_update_slice_in_dim(grad_values, old_values + grad_v.reshape(...  67.2 us
  transfers between devices with their start and end apart: 17, of which 15 were waited for; matrix products, arithmetic and copies ran while one was open for 20% of the time, Pallas kernels for 0%

commit v1 on v0

v1 whole, which is shorter than its diff:
```python
import functools
import math

import jax
import jax.numpy as jnp
from jax import lax
from jax.experimental import pallas as pl
from jax.experimental.pallas import tpu as pltpu
from jax.sharding import PartitionSpec as P


D = 768
HD = 64
LEN = 4096
HALF = 2048
B = 512
FB = 192
FF = 3072
PACK = 1792
EPSILON = 1e-06
MASKED = -1e30
SCALE = HD**-0.5
LOG2E = math.log2(math.e)
BF = jnp.bfloat16
F32 = jnp.float32
MIB = 1 << 20


def contract(left, right, dims):
    return lax.dot_general(left, right, (dims, ((), ())), preferred_element_type=F32)


def nn(left, right):
    return contract(left, right, ((1,), (0,)))


def nt(left, right):
    return contract(left, right, ((1,), (1,)))


def cols_swap(value, distance):
    return lax.ppermute(value, "cols", [(i, i ^ distance) for i in range(lax.axis_size("cols"))])


def rows_shift(value, step):
    count = lax.axis_size("rows")
    return lax.ppermute(value, "rows", [(i, (i + step) % count) for i in range(count)])


def dp_swap(value):
    return lax.ppermute(value, "dp", [(i, i ^ 1) for i in range(lax.axis_size("dp"))])


def qkv_kernel(tab, x0, x1, x23, gain, w, *refs):
    normed, scale, q_t, k, k_t, v, v_t = refs[-7:]
    i = pl.program_id(0)
    x = jnp.concatenate([x0[...], x1[...], x23[...]], axis=0).astype(F32)
    r1 = lax.rsqrt(jnp.sum(x * x, axis=0, keepdims=True) * (1.0 / D) + EPSILON)
    n_t = (x * r1 * gain[...]).astype(BF)
    normed[...] = n_t
    scale[...] = r1
    n = n_t.T
    k_val = nn(n, w[:, 384:768])
    k[...] = k_val.astype(BF)
    k_t[...] = k_val.T.astype(BF)
    v_val = nn(n, w[:, 768:1152])
    v[...] = v_val.astype(BF)
    v_t[...] = v_val.T.astype(BF)

    @pl.when(i < 2)
    def _():
        q_t[...] = (nn(n, w[:, 0:384]) * (SCALE * LOG2E)).T.astype(BF)


def project_half(order, x0, x1, x23, gain, w, half, old):
    base = half * (HALF // B)

    def cols_of(rows):
        return pl.BlockSpec((rows, B), lambda i, t: (0, t[i]))

    whole = lambda shape: pl.BlockSpec(shape, lambda i, t: (0, 0))
    major = pl.BlockSpec((B, 384), lambda i, t: (base + t[i], 0))
    minor = pl.BlockSpec((384, B), lambda i, t: (0, base + t[i]))
    kv = [jax.ShapeDtypeStruct(s, BF) for s in ((LEN, 384), (384, LEN)) * 2]
    return pl.pallas_call(
        qkv_kernel,
        grid_spec=pltpu.PrefetchScalarGridSpec(
            num_scalar_prefetch=1,
            grid=(HALF // B,),
            in_specs=[cols_of(FB), cols_of(FB), cols_of(2 * FB), whole((D, 1)), whole((D, 1152))]
            + [pl.BlockSpec(memory_space=pl.ANY)] * len(old),
            out_specs=[
                cols_of(D),
                cols_of(1),
                pl.BlockSpec((384, B), lambda i, t: (0, jnp.minimum(i, 1))),
                major,
                minor,
                major,
                minor,
            ],
        ),
        out_shape=[
            jax.ShapeDtypeStruct((D, HALF), BF),
            jax.ShapeDtypeStruct((1, HALF), F32),
            jax.ShapeDtypeStruct((384, HALF // 2), BF),
        ]
        + kv,
        input_output_aliases={6 + n: 3 + n for n in range(len(old))},
        compiler_params=pltpu.CompilerParams(vmem_limit_bytes=48 * MIB),
        cost_estimate=pl.CostEstimate(flops=6_000_000_000, bytes_accessed=20_000_000, transcendentals=0),
    )(order, x0, x1, x23, gain, w, *old)


def block_masks(first, last):
    key = lax.broadcasted_iota(jnp.int32, (B, B), 0)
    query = lax.broadcasted_iota(jnp.int32, (B, B), 1)
    piece = (key >= first) & (key < last) & (query >= first) & (query < last)
    return (key > query, (key <= query) | piece)


def masked(scores, masks, step, count):
    if step == count - 1:
        scores = jnp.where(masks[1], scores, MASKED)
    if count == 4 and step == 0:
        scores = jnp.where(masks[0], scores, MASKED)
    return scores


def head_rows(pair_t):
    row = lax.broadcasted_iota(jnp.int32, pair_t.shape, 0)
    zero = jnp.zeros((), pair_t.dtype)
    return [jnp.where((row // HD) == h, pair_t, zero) for h in range(2)]


def head_cols(pair):
    col = lax.broadcasted_iota(jnp.int32, pair.shape, 1)
    zero = jnp.zeros((), pair.dtype)
    return [jnp.where((col // HD) == h, pair, zero) for h in range(2)]


def for_counts(block, counts, body):
    if len(counts) == 1:
        body(counts[0])
        return
    visible = jnp.minimum(block, 3) + 1
    for count in counts:
        pl.when(visible == count)(functools.partial(body, count))


def attend_kernel(tab, q_t, k, v_t, o_t, log_total, *, counts):
    i = pl.program_id(1)
    block, first, last = tab[i], tab[2 + i], tab[4 + i]

    def body(count):
        masks = block_masks(first, last)
        starts = [pl.multiple_of((block - (count - 1) + t) * B, B) for t in range(count)]
        for h, q_head in enumerate(head_rows(q_t[...])):
            scores = [masked(nn(k[pl.ds(s, B), :], q_head), masks, t, count) for t, s in enumerate(starts)]
            peak = functools.reduce(jnp.maximum, [jnp.max(s, axis=0, keepdims=True) for s in scores])
            total, mixed = 0.0, 0.0
            for score, s in zip(scores, starts):
                part = jnp.exp2(score - peak)
                total = total + jnp.sum(part, axis=0, keepdims=True)
                mixed = mixed + nn(v_t[h * HD : (h + 1) * HD, pl.ds(s, B)], part.astype(BF))
            o_t[h * HD : (h + 1) * HD, :] = (mixed * (1.0 / total)).astype(BF)
            log_total[0, h : h + 1, :] = peak + jnp.log2(total)

    for_counts(block, counts, body)


def attend_specs(span):
    return (
        pl.BlockSpec((128, B), lambda p, i, t: (p, i)),
        pl.BlockSpec((1, 2, B), lambda p, i, t: (p, 0, i)),
        pl.BlockSpec((span, 128), lambda p, i, t: (0, p)),
        pl.BlockSpec((128, span), lambda p, i, t: (p, 0)),
    )


def attend_half(tab, q_t, k, v_t, half):
    query, stat, major, minor = attend_specs(LEN if half else HALF)
    units = 8 if half else 5
    return pl.pallas_call(
        functools.partial(attend_kernel, counts=(4,) if half else (1, 2, 3, 4)),
        grid_spec=pltpu.PrefetchScalarGridSpec(
            num_scalar_prefetch=1,
            grid=(3, 2),
            in_specs=[query, major, minor],
            out_specs=[query, stat],
        ),
        out_shape=[jax.ShapeDtypeStruct(q_t.shape, BF), jax.ShapeDtypeStruct((3, 2, 2 * B), F32)],
        compiler_params=pltpu.CompilerParams(vmem_limit_bytes=48 * MIB),
        cost_estimate=pl.CostEstimate(
            flops=units * 6 * 2 * 512 * B * B, bytes_accessed=10_000_000, transcendentals=units * 6 * B * B
        ),
    )(tab, q_t, k, v_t)


def attend_back_kernel(tab, q_t, do_t, o_t, log_total, k, v, k_t, *refs, counts, half):
    if half:
        dq_t, dk_high, dv_high, dk_low, dv_low, dk, dv = refs
    else:
        dk_start, dv_start, dq_t, dk_out, dv_out, dk, dv = refs
    i = pl.program_id(1)
    block, first, last = tab[i], tab[2 + i], tab[4 + i]

    @pl.when(i == 0)
    def _():
        dk[...] = jnp.zeros_like(dk) if half else dk_start[...]
        dv[...] = jnp.zeros_like(dv) if half else dv_start[...]

    def body(count):
        masks = block_masks(first, last)
        queries, grads = q_t[...], do_t[...]
        q_rows, g_rows = head_rows(queries), head_rows(grads)
        q_cols, g_cols = head_cols(queries.T), head_cols(grads.T)
        product = grads.astype(F32) * o_t[...].astype(F32)
        inner = [jnp.sum(product[h * HD : (h + 1) * HD], axis=0, keepdims=True) for h in range(2)]
        dq = [0.0, 0.0]
        for t in range(count):
            rows = pl.ds(pl.multiple_of((block - (count - 1) + t) * B, B), B)
            key_rows, value_rows = k[rows, :], v[rows, :]
            dk_part = dv_part = 0.0
            for h in range(2):
                score = masked(nn(key_rows, q_rows[h]), masks, t, count)
                probs = jnp.exp2(score - log_total[0, h : h + 1, :])
                grad_probs = nn(value_rows, g_rows[h])
                grad_scores = (probs * (grad_probs - inner[h])).astype(BF)
                dv_part = dv_part + nn(probs.astype(BF), g_cols[h])
                dk_part = dk_part + nn(grad_scores, q_cols[h])
                dq[h] = dq[h] + nn(k_t[h * HD : (h + 1) * HD, rows], grad_scores)
            dv[rows, :] += dv_part
            dk[rows, :] += dk_part
        for h in range(2):
            dq_t[h * HD : (h + 1) * HD, :] = (dq[h] * SCALE).astype(BF)

    for_counts(block, counts, body)

    @pl.when(i == 1)
    def _():
        unscale = 1.0 / LOG2E
        if half:
            dk_high[...] = (dk[HALF:, :] * unscale).astype(BF)
            dv_high[...] = dv[HALF:, :].astype(BF)
            dk_low[...] = dk[:HALF, :]
            dv_low[...] = dv[:HALF, :]
        else:
            dk_out[...] = (dk[...] * unscale).astype(BF)
            dv_out[...] = dv[...].astype(BF)


def attend_back_half(tab, q_t, do_t, o_t, log_total, k, v, k_t, half, start):
    span = LEN if half else HALF
    query, stat, major, minor = attend_specs(span)
    grad = pl.BlockSpec((HALF, 128), lambda p, i, t: (0, p))
    low = jax.ShapeDtypeStruct((HALF, 384), BF)
    wide = jax.ShapeDtypeStruct((HALF, 384), F32)
    units = 8 if half else 5
    return pl.pallas_call(
        functools.partial(attend_back_kernel, counts=(4,) if half else (1, 2, 3, 4), half=half),
        grid_spec=pltpu.PrefetchScalarGridSpec(
            num_scalar_prefetch=1,
            grid=(3, 2),
            in_specs=[query, query, query, stat, major, major, minor] + [grad] * len(start),
            out_specs=[query] + [grad] * (4 if half else 2),
            scratch_shapes=[pltpu.VMEM((span, 128), F32)] * 2,
        ),
        out_shape=[jax.ShapeDtypeStruct(q_t.shape, BF), low, low] + ([wide, wide] if half else []),
        compiler_params=pltpu.CompilerParams(vmem_limit_bytes=56 * MIB),
        cost_estimate=pl.CostEstimate(
            flops=units * 6 * 5 * 512 * B * B, bytes_accessed=20_000_000, transcendentals=units * 6 * B * B
        ),
    )(tab, q_t, do_t, o_t, log_total, k, v, k_t, *start)


def feed_kernel(sel, x_t, a_t, dy_t, wo_t, gain, *refs):
    pieces = refs[:16]
    out_t, gm_t, ga_t, gain_sum, g_near, g_far = refs[16:22]
    w_up, w_down, n_t, n, dy, mid, mlp, gn, stage, stage_out, in_sems, out_sems = refs[22:]
    parity, core = sel[0], sel[1]

    def loads(slot):
        copies = []
        for rel in range(4):
            place = rel if slot == 0 else (rel // 2) * 2 + lax.rem(parity + rel, 2)
            rows = pl.ds(place * FB, FB) if slot == 0 else pl.ds(pl.multiple_of(place * FB, FB), FB)
            for which, target in enumerate((w_up, w_down)):
                copies.append(
                    pltpu.make_async_copy(
                        pieces[slot * 4 + rel].at[:, which * D : (which + 1) * D],
                        target.at[slot, rows, :],
                        in_sems.at[slot, rel * 2 + which],
                    )
                )
        return copies

    for slot in range(4):
        for copy in loads(slot):
            copy.start()

    mid[...] = x_t[...].astype(F32) + nn(wo_t[...], a_t[...])
    r2 = lax.rsqrt(jnp.sum(mid[...] * mid[...], axis=0, keepdims=True) * (1.0 / D) + EPSILON)
    n_t[...] = (mid[...] * r2 * gain[...]).astype(BF)
    n[...] = n_t[...].T
    dy[...] = dy_t[...].T
    mlp[...] = mid[...]
    gn[...] = jnp.zeros_like(gn)
    for slot in range(4):
        for copy in loads(slot):
            copy.wait()

    def stores(slot, buffer):
        copies = []
        for side, target in enumerate((g_near, g_far)):
            for which in range(2):
                copies.append(
                    pltpu.make_async_copy(
                        stage.at[buffer, which, pl.ds(side * 384, 384), :],
                        target.at[slot, :, which * D : (which + 1) * D],
                        out_sems.at[buffer, side * 2 + which],
                    )
                )
        return copies

    root = math.sqrt(2.0 / math.pi)

    def chunk(slot, carry):
        buffer = lax.rem(slot, 2)

        @pl.when(slot >= 2)
        def _():
            for copy in stores(slot - 2, buffer):
                copy.wait()

        up = nn(n[...], w_up[slot])
        square = up * up
        half = 0.5 + 0.5 * jnp.tanh(up * (root + (root * 0.044715) * square))
        act = (up * half).astype(BF)
        slope = half + (2.0 * up) * (half - half * half) * (root + (3.0 * root * 0.044715) * square)
        stage[buffer, 1] = nn(dy_t[...], act).astype(BF)
        mlp[...] += nt(w_down[slot], act)
        grad_up = (nn(dy[...], w_down[slot]) * slope).astype(BF)
        stage[buffer, 0] = nn(n_t[...], grad_up).astype(BF)
        gn[...] += nt(w_up[slot], grad_up)
        for copy in stores(slot, buffer):
            copy.start()
        return carry

    lax.fori_loop(0, 4, chunk, 0)
    out_t[...] = mlp[...].astype(BF)
    weighted = gn[...] * gain[...]
    inner = jnp.sum(mid[...] * weighted, axis=0, keepdims=True)
    cubed = r2 * r2 * r2 * inner * (1.0 / D)
    gm_t[...] = (dy_t[...].astype(F32) + r2 * weighted - mid[...] * cubed).astype(BF)
    gain_sum[...] = jnp.sum(gn[...] * mid[...] * r2, axis=1, keepdims=True)
    ga_t[...] = contract(wo_t[...], gm_t[...], ((0,), (0,))).astype(BF)
    copies = []
    for slot in range(4):
        place = lax.rem(slot + 2 * core, 4)
        part = nt(gm_t[...], a_t[pl.ds(pl.multiple_of(place * FB, FB), FB), :])
        stage_out[slot] = jnp.concatenate([part, jnp.zeros((D, PACK - 2 * D - FB), F32)], axis=1).astype(BF)
        for side, target in enumerate((g_near, g_far)):
            copies.append(
                pltpu.make_async_copy(
                    stage_out.at[slot, pl.ds(side * 384, 384), :],
                    target.at[slot, :, 2 * D : PACK],
                    out_sems.at[2 + side, slot],
                )
            )
            copies[-1].start()
    for slot in (2, 3):
        for copy in stores(slot, slot % 2):
            copy.wait()
    for copy in copies:
        copy.wait()


def feed_forward(sel, x_t, a_t, dy_t, wo_t, gain, pieces):
    count = x_t.shape[1]
    vmem = pl.BlockSpec(memory_space=pltpu.VMEM)
    hbm = pl.BlockSpec(memory_space=pl.ANY)
    token = jax.ShapeDtypeStruct((D, count), BF)
    grads = jax.ShapeDtypeStruct((4, 384, PACK), BF)
    return pl.pallas_call(
        feed_kernel,
        in_specs=[pl.BlockSpec(memory_space=pltpu.SMEM)] + [vmem] * 5 + [hbm] * 16,
        out_specs=[vmem] * 4 + [hbm] * 2,
        out_shape=[token, token, token, jax.ShapeDtypeStruct((D, 1), F32), grads, grads],
        scratch_shapes=[
            pltpu.VMEM((4, D, D), BF),
            pltpu.VMEM((4, D, D), BF),
            pltpu.VMEM((D, count), BF),
            pltpu.VMEM((count, D), BF),
            pltpu.VMEM((count, D), BF),
            pltpu.VMEM((D, count), F32),
            pltpu.VMEM((D, count), F32),
            pltpu.VMEM((D, count), F32),
            pltpu.VMEM((2, 2, D, D), BF),
            pltpu.VMEM((4, D, PACK - 2 * D), BF),
            pltpu.SemaphoreType.DMA((4, 8)),
            pltpu.SemaphoreType.DMA((4, 4)),
        ],
        compiler_params=pltpu.CompilerParams(vmem_limit_bytes=62 * MIB),
        cost_estimate=pl.CostEstimate(
            flops=6 * count * (2 * D * FF + D * D), bytes_accessed=34_000_000, transcendentals=count * FF
        ),
    )(sel, x_t, a_t, dy_t, wo_t, gain, *pieces)


def qkv_back_kernel(tab, w, n_t, dq_t, dk, dv, *refs):
    start, (near, far, inner, gain_out, grad_w, acc, gain_acc) = refs[:-7], refs[-7:]
    i = pl.program_id(0)

    @pl.when(i == 0)
    def _():
        acc[...] = start[0][...] if start else jnp.zeros_like(acc)
        gain_acc[...] = start[1][...] if start else jnp.zeros_like(gain_acc)

    normed = n_t[...]
    acc[:, 384:768] += nn(normed, dk[...])
    acc[:, 768:1152] += nn(normed, dv[...])

    def finish(grad):
        near[...] = grad[:384].astype(BF)
        far[...] = grad[384:].astype(BF)
        product = grad * normed.astype(F32)
        inner[...] = jnp.sum(product, axis=0, keepdims=True)
        gain_acc[...] += jnp.sum(product, axis=1, keepdims=True)

    def key_part():
        return nt(w[:, 384:768], dk[...]) + nt(w[:, 768:1152], dv[...])

    @pl.when(i < 2)
    def _():
        acc[:, 0:384] += nt(normed, dq_t[...])
        finish(key_part() + nn(w[:, 0:384], dq_t[...]))

    @pl.when(i >= 2)
    def _():
        finish(key_part())

    @pl.when(i == pl.num_programs(0) - 1)
    def _():
        grad_w[...] = acc[...].astype(grad_w.dtype)
        gain_out[...] = gain_acc[...]


def project_back_half(order, w, n_t, dq_t, dk, dv, start):
    whole = lambda shape: pl.BlockSpec(shape, lambda i, t: (0, 0))

    def cols_of(rows):
        return pl.BlockSpec((rows, B), lambda i, t: (0, t[i]))

    major = pl.BlockSpec((B, 384), lambda i, t: (t[i], 0))
    low = jax.ShapeDtypeStruct((384, HALF), BF)
    return pl.pallas_call(
        qkv_back_kernel,
        grid_spec=pltpu.PrefetchScalarGridSpec(
            num_scalar_prefetch=1,
            grid=(HALF // B,),
            in_specs=[
                whole((D, 1152)),
                cols_of(D),
                pl.BlockSpec((384, B), lambda i, t: (0, jnp.minimum(i, 1))),
                major,
                major,
            ]
            + [whole((D, 1152)), whole((D, 1))][: len(start)],
            out_specs=[cols_of(384), cols_of(384), cols_of(1), whole((D, 1)), whole((D, 1152))],
            scratch_shapes=[pltpu.VMEM((D, 1152), F32), pltpu.VMEM((D, 1), F32)],
        ),
        out_shape=[
            low,
            low,
            jax.ShapeDtypeStruct((1, HALF), F32),
            jax.ShapeDtypeStruct((D, 1), F32),
            jax.ShapeDtypeStruct((D, 1152), BF if start else F32),
        ],
        compiler_params=pltpu.CompilerParams(vmem_limit_bytes=56 * MIB),
        cost_estimate=pl.CostEstimate(flops=12_000_000_000, bytes_accessed=20_000_000, transcendentals=0),
    )(order, w, n_t, dq_t, dk, dv, *start)


def per_device(
    block_input,
    norm_gain_one,
    w_query,
    w_key,
    w_value,
    w_out,
    norm_gain_two,
    w_up,
    w_down,
    piece_start,
    piece_len,
    grad_y,
):
    c = lax.axis_index("cols")
    r = lax.axis_index("rows")
    y, core = c // 2, c % 2
    parity = lax.axis_index("dp") % 2

    def by_pair(zero, one):
        return jnp.where(y == 0, jnp.array(zero, jnp.int32), jnp.array(one, jnp.int32))

    low_order = by_pair([0, 3, 1, 2], [1, 2, 0, 3])
    high_order = by_pair([0, 1, 2, 3], [2, 3, 0, 1])

    def take(array, block):
        return lax.dynamic_slice_in_dim(array, block * B, B, 1)

    small = jnp.concatenate(
        [norm_gain_one, norm_gain_two, piece_start[0].astype(F32), piece_len[0].astype(F32)]
    )
    small = jnp.stack([small, cols_swap(small, 2)])
    small = jnp.concatenate([small, cols_swap(small, 1)])
    gain_one = small[:, :FB].reshape(D, 1)
    gain_two = small[:, FB : 2 * FB].reshape(D, 1)
    apart = jnp.bitwise_xor(c, r)
    mine = jnp.where(apart == 0, 0, jnp.where(apart == 2, 1, jnp.where(apart == 1, 2, 3)))
    pieces = lax.dynamic_index_in_dim(small, mine, 0, keepdims=False)[2 * FB :].astype(jnp.int32)
    firsts = pieces[:8] - jnp.arange(8, dtype=jnp.int32) * B
    lasts = firsts + pieces[8:]

    def table(order, half):
        blocks = order[:2] + half * 4
        return jnp.concatenate([blocks, firsts[blocks], lasts[blocks]])

    tables = (table(low_order, 0), table(high_order, 1))
    orders = (low_order, high_order)

    def gather_half(half):
        own = block_input[:, half * HALF : (half + 1) * HALF]
        pair = cols_swap(own, 2)
        return own, pair, cols_swap(jnp.concatenate([own, pair]), 1)

    x_low = gather_half(0)

    ring = [jnp.concatenate([w_query, w_key, w_value], axis=1)]
    for _ in range(3):
        ring.append(rows_shift(ring[-1], 1))
    ring = jnp.stack(ring)
    ring = jnp.stack([ring, cols_swap(ring, 2)], axis=1)
    kept = lax.dynamic_slice_in_dim(ring, 2 * core, 2, 0)
    sent = lax.dynamic_slice_in_dim(ring, 2 - 2 * core, 2, 0)
    w_all = jnp.concatenate([kept, cols_swap(sent, 1)], axis=1)
    w_qkv = w_all.reshape(2, D, 3, FB).transpose(1, 2, 0, 3).reshape(D, 1152)

    x_high = gather_half(1)

    def blocks_of(which):
        low = jnp.where(which == 0, jnp.array([0, 3], jnp.int32), jnp.array([1, 2], jnp.int32))
        high = jnp.where(which == 0, jnp.array([4, 5], jnp.int32), jnp.array([6, 7], jnp.int32))
        return low, high

    def tokens_of(which, device):
        low, high = blocks_of(which)
        return jnp.concatenate([take(grad_y, low[device]), take(grad_y, high[device])], axis=1)

    own_core, other_core = tokens_of(y, core), tokens_of(y, 1 - core)
    away = jnp.stack([tokens_of(1 - y, core), tokens_of(1 - y, 1 - core)])
    arrived = cols_swap(away, 2)
    dy_far = cols_swap(jnp.concatenate([other_core, arrived[1]]), 1)
    dy_t = jnp.concatenate([own_core, arrived[0], dy_far])

    pad = jnp.zeros((FB, PACK - 2 * D - FB), BF)
    own_pack = jnp.concatenate([w_up, w_down, w_out.T, pad], axis=1)
    pair_pack = cols_swap(own_pack, 2)
    feed = [own_pack, pair_pack, cols_swap(own_pack, 1), cols_swap(pair_pack, 1)]
    moving = jnp.where(parity == 0, own_pack, pair_pack)
    for _ in range(3):
        moving = rows_shift(moving, 1)
        crossed = dp_swap(moving)
        feed += [moving, crossed, cols_swap(moving, 1), cols_swap(crossed, 1)]
    out_rows = []
    for slot in range(4):
        parts = [piece[:, 2 * D : 2 * D + FB] for piece in feed[slot * 4 : slot * 4 + 4]]
        if slot:
            even = parity == 0
            parts = [
                jnp.where(even, parts[0], parts[1]),
                jnp.where(even, parts[1], parts[0]),
                jnp.where(even, parts[2], parts[3]),
                jnp.where(even, parts[3], parts[2]),
            ]
        out_rows.append(jnp.concatenate(parts))
    wo_t = jnp.stack(out_rows)
    wo_t = jnp.concatenate([lax.dynamic_slice_in_dim(wo_t, 2 * core, 2, 0), lax.dynamic_slice_in_dim(wo_t, 2 - 2 * core, 2, 0)])
    wo_t = wo_t.transpose(1, 0, 2).reshape(D, D)

    normed_low, scale_low, q_low, *kv = project_half(low_order, *x_low, gain_one, w_qkv, 0, ())
    o_low, log_low = attend_half(tables[0], q_low, kv[0], kv[3], 0)
    *kv, o_low, log_low = lax.optimization_barrier((*kv, o_low, log_low))
    normed_high, scale_high, q_high, *kv = project_half(high_order, *x_high, gain_one, w_qkv, 1, tuple(kv))
    k, k_t, v, v_t = kv
    o_high, log_high = attend_half(tables[1], q_high, k, v_t, 1)

    def core_block(array, which):
        return lax.dynamic_slice_in_dim(array, which * B, B, 1)

    def both(low, high, which):
        return jnp.concatenate([core_block(low, which), core_block(high, which)], axis=1)

    a_t = jnp.concatenate([both(o_low, o_high, core), cols_swap(both(o_low, o_high, 1 - core), 1)])
    x_own = jnp.concatenate(
        [
            jnp.concatenate([take(piece, order[core]) for piece in halves])
            for order, halves in ((low_order, x_low), (high_order, x_high))
        ],
        axis=1,
    )
    sel = jnp.stack([parity, core])
    out_t, gm_t, ga_t, gain_two_sum, g_near, g_far = feed_forward(sel, x_own, a_t, dy_t, wo_t, gain_two, feed)

    ga_far = cols_swap(ga_t[384:], 1)
    ga_own = ga_t[:384]

    def tokens(half):
        own, other = core_block(ga_own, half), core_block(ga_far, half)
        first = jnp.where(core == 0, own, other)
        second = jnp.where(core == 0, other, own)
        return jnp.concatenate([first, second], axis=1)

    dq_high, dk_high, dv_high, dk_low, dv_low = attend_back_half(
        tables[1], q_high, tokens(1), o_high, log_high, k, v, k_t, 1, ()
    )
    near_high, far_high, inner_high, gain_part, w_part = project_back_half(
        high_order, w_qkv, normed_high, dq_high, dk_high, dv_high, ()
    )
    dq_low, dk_low, dv_low = attend_back_half(
        tables[0], q_low, tokens(0), o_low, log_low, k, v, k_t, 0, (dk_low, dv_low)
    )
    near_low, far_low, inner_low, gain_part, w_part = project_back_half(
        low_order, w_qkv, normed_low, dq_low, dk_low, dv_low, (w_part, gain_part)
    )

    both_t = jnp.stack([out_t, gm_t])
    rows_near, rows_far = both_t[:, :384], cols_swap(both_t[:, 384:], 1)
    here = [rows_near[:, :FB], rows_far[:, :FB]]
    there = cols_swap(jnp.concatenate([rows_near[:, FB:], rows_far[:, FB:]]), 2)
    there = [there[:2], there[2:]]

    def block_at(pair, device, half):
        parts = [part[:, :, half * B : (half + 1) * B] for part in here + there]
        same = device == core
        return jnp.where(
            pair == y, jnp.where(same, parts[0], parts[1]), jnp.where(same, parts[2], parts[3])
        )

    places = ((0, 0, 0), (1, 0, 0), (1, 1, 0), (0, 1, 0), (0, 0, 1), (0, 1, 1), (1, 0, 1), (1, 1, 1))
    joined = jnp.concatenate([block_at(*place) for place in places], axis=2)
    output, grad_middle = joined[0], joined[1]

    def grad_half(near, far, inner, scale, half):
        total = near.astype(F32) + cols_swap(far, 1).astype(F32)
        own = total[:FB] + cols_swap(total[FB:].astype(BF), 2).astype(F32)
        inner = inner + cols_swap(inner, 1)
        inner = inner + cols_swap(inner, 2)
        x = block_input[:, half * HALF : (half + 1) * HALF].astype(F32)
        gm = grad_middle[:, half * HALF : (half + 1) * HALF].astype(F32)
        return gm + scale * norm_gain_one[:, None] * own - x * (scale * scale * inner * (1.0 / D))

    grad_high = grad_half(near_high, far_high, inner_high, scale_high, 1)
    grad_low = grad_half(near_low, far_low, inner_low, scale_low, 0)
    grad_x = jnp.concatenate([grad_low, grad_high], axis=1)

    gains = jnp.stack([gain_part[:, 0] / gain_one[:, 0], gain_two_sum[:, 0]])
    gains = lax.psum(gains, ("dp", "rows")).reshape(2, 4, FB)
    gains = gains[:, :2] + cols_swap(gains[:, 2:], 1)
    gains = gains[:, 0] + cols_swap(gains[:, 1], 2)

    def dp_sum(part):
        if lax.axis_size("dp") == 2:
            return part.astype(F32) + dp_swap(part).astype(F32)
        return lax.psum(part.astype(F32), "dp")

    def ring_sum(parts):
        total = parts[3]
        for slot in (2, 1, 0):
            total = (rows_shift(total, -1).astype(F32) + parts[slot].astype(F32)).astype(BF)
        return total

    near = g_near.astype(F32) + cols_swap(g_far, 1).astype(F32)
    even = parity == 0
    keep = jnp.where(even, near[:, :FB], near[:, FB:])
    give = jnp.where(even, near[:, FB:], near[:, :FB]).astype(BF)
    keep = (keep + dp_swap(give).astype(F32)).astype(BF)
    total = ring_sum([keep[slot] for slot in range(4)])
    total = dp_sum(jnp.where(even, total, cols_swap(total, 2)))
    grad_up, grad_down, grad_out = total[:, :D], total[:, D : 2 * D], total[:, 2 * D : 2 * D + FB].T

    w_near, w_far = w_part[:384], cols_swap(w_part[384:], 1)
    first, second = jnp.where(core == 0, w_near, w_far), jnp.where(core == 0, w_far, w_near)
    stacked = jnp.stack([first, second]).reshape(2, 2, FB, 3, 2, FB).transpose(1, 0, 4, 2, 3, 5)
    stacked = stacked.reshape(2, 4, FB, 3 * FB)
    stacked = (stacked[0].astype(F32) + cols_swap(stacked[1], 2).astype(F32)).astype(BF)
    joined_grad = dp_sum(ring_sum([stacked[slot] for slot in range(4)]))
    return (
        output,
        grad_x,
        gains[0],
        joined_grad[:, :FB],
        joined_grad[:, FB : 2 * FB],
        joined_grad[:, 2 * FB :],
        grad_out,
        gains[1],
        grad_up,
        grad_down,
    )


def solution(mesh):
    return jax.shard_map(
        per_device,
        mesh=mesh,
        in_specs=(
            P("cols", ("dp", "rows")),
            P("cols"),
            P("cols", "rows"),
            P("cols", "rows"),
            P("cols", "rows"),
            P("rows", "cols"),
            P("cols"),
            P("cols", "rows"),
            P("cols", "rows"),
            P(("dp", "cols"), None),
            P(("dp", "cols"), None),
            P("cols", ("dp", "rows")),
        ),
        out_specs=(
            P("cols", ("dp", "rows")),
            P("cols", ("dp", "rows")),
            P("cols"),
            P("cols", "rows"),
            P("cols", "rows"),
            P("cols", "rows"),
            P("rows", "cols"),
            P("cols"),
            P("cols", "rows"),
            P("cols", "rows"),
        ),
        check_vma=False,
    )
```

time: 3200 us -> 615 us (0.19)
  waiting for transfers between devices: 2120 us -> 188 us
  matrix products: 458 us -> 0 us
  Pallas kernels: 0 us -> 206 us
  local copies, waits for them, and re-layouts: 272 us -> 81.7 us
  other arithmetic: 214 us -> 73.9 us
  blocking collectives: 65.7 us -> 17.3 us
  loops' own time: 43.1 us -> 0 us
    reduce_scatter x8 -> x0, waiting for transfers between devices: 1420 us -> none  [the longest x4 1020 us: cols_project(): lax.psum_scatter(jnp.dot(left, right, preferred_element_type=jnp.float32)...]
    all_gather x8 -> x0, waiting for transfers between devices: 694 us -> none  [the longest x4 413 us: rows_gather(): return lax.all_gather(block_rows, 'rows', axis=0, tiled=True)]
    dot_general x68 -> x0, matrix products: 458 us -> none  [the longest x16 90.7 us: block_scores(): jnp.einsum('qhd,khd->hqk', query_block, key_block, preferred_element_type...]
    pallas_call x0 -> x9, Pallas kernels: none -> 206 us  [the longest x2 68.4 us: attend_back_half(): pl.pallas_call(functools.partial(attend_back_kernel, counts=(4,) if half...]
    ppermute x0 -> x55, waiting for transfers between devices: none -> 188 us  [the longest x12 73 us: rows_shift(): lax.ppermute(value, 'rows', [(i, (i + step) % count) for i in range(count)])]
    dynamic_update_slice x32 -> x0, local copies, waits for them, and re-layouts: 142 us -> none  [the longest x8 67.2 us: one_block(): lax.dynamic_update_slice_in_dim(grad_values, old_values + grad_v.reshape(...]
    convert_element_type x17 -> x11, other arithmetic: 91.8 us -> 7.65 us  [the longest x1 4.3 us: per_device(): keep = (keep + dp_swap(give).astype(F32)).astype(BF)]
    dynamic_slice x80 -> x15, local copies, waits for them, and re-layouts: 68 us -> 11.2 us  [the longest x6 7.32 us: take(): return lax.dynamic_slice_in_dim(array, block * B, B, 1)]
  transfers between devices with their start and end apart: 17 -> 55, of which waited for: 15 -> 23; matrix products, arithmetic and copies ran while one was open for 20% -> 22% of each run, Pallas kernels for 0% -> 26%
where the time goes in v1:
time: 615 us; the launch traced here: 606 us
  Pallas kernels  206 us (33%)
  waiting for transfers between devices  188 us (31%)
  local copies, waits for them, and re-layouts  81.7 us (13%)
  other arithmetic  73.9 us (12%)
  starting transfers between devices  30.7 us (5%)
  blocking collectives  17.3 us (3%)
  between operations  8.78 us (1%)
    ppermute x12, waiting for transfers between devices, rows_shift(): lax.ppermute(value, 'rows', [(i, (i + step) % count) for i in range(count)])  73 us
    pallas_call x2, Pallas kernels, attend_back_half(): pl.pallas_call(functools.partial(attend_back_kernel, counts=(4,) if half...  68.4 us
    ppermute x37, waiting for transfers between devices, cols_swap(): lax.ppermute(value, 'cols', [(i, i ^ distance) for i in range(lax.axis_si...  61 us
    ppermute x6, waiting for transfers between devices, dp_swap(): lax.ppermute(value, 'dp', [(i, i ^ 1) for i in range(lax.axis_size('dp'))])  53.7 us
    pallas_call x1, Pallas kernels, feed_forward(): pl.pallas_call(feed_kernel, in_specs=[pl.BlockSpec(memory_space=pltpu.SME...  45.4 us
    pallas_call x2, Pallas kernels, attend_half(): pl.pallas_call(functools.partial(attend_kernel, counts=(4,) if half else...  38.6 us
    pallas_call x2, Pallas kernels, project_back_half(): pl.pallas_call(qkv_back_kernel, grid_spec=pltpu.PrefetchScalarGridSpec(nu...  32.7 us
    pallas_call x2, Pallas kernels, project_half(): pl.pallas_call(qkv_kernel, grid_spec=pltpu.PrefetchScalarGridSpec(num_sca...  21 us
  transfers between devices with their start and end apart: 55, of which 23 were waited for; matrix products, arithmetic and copies ran while one was open for 22% of the time, Pallas kernels for 26%

profile of v1, /device:TPU:24, one launch (start us, length us, event | category | flops | bytes accessed | tf_op | source)
XLA Modules:
  0.0 606.2 jit_solution(8867954668756264440)
XLA Ops:
  23.1 2.4 constant_dynamic-slice_fusion.9
  26.5 13.2 %collective-permute-done.4 = f32[400]{0:T(512)S(1)} collective-permute-done((f32[400]{0:T(512)S(1)}, f32[400]{0:T(512)S(1)}, u32[]{:S(2)}, u32[]{:S(2)}) %collective-permute-start.4) | collective-permute-done | bytes 1632 | tf_op jit(solution)/shard_map/ppermute | solution.py:42
  42.8 7.7 %collective-permute-done.7 = bf16[192,576]{1,0:T(8,128)(2,1)} collective-permute-done((bf16[192,576]{1,0:T(8,128)(2,1)}, bf16[192,576]{1,0:T(8,128)(2,1)}, u32[]{:S(2)}, u32[]{:S(2)}) %collective-permute-start.7) | collective-permute-done | bytes 221216 | tf_op jit(solution)/shard_map/ppermute | solution.py:47
  54.0 3.8 collective-permute-done.8
  57.8 2.8 pad_maximum_fusion.8
  61.2 10.2 %collective-permute-done.12 = bf16[2,192,1024]{2,1,0:T(8,128)(2,1)} collective-permute-done((bf16[2,192,1024]{2,1,0:T(8,128)(2,1)}, bf16[2,192,1024]{2,1,0:T(8,128)(2,1)}, u32[]{:S(2)}, u32[]{:S(2)}) %collective-permute-start.12) | collective-permute-done | bytes 786464 | tf_op jit(solution)/shard_map/ppermute | solution.py:42
  77.5 9.2 %collective-permute-done.17.refs_4_ = bf16[192,1792]{1,0:T(8,128)(2,1)} collective-permute-done((bf16[192,1792]{1,0:T(8,128)(2,1)S(1)}, bf16[192,1792]{1,0:T(8,128)(2,1)}, u32[]{:S(2)}, u32[]{:S(2)}) %collective-permute-start.17) | collective-permute-done | bytes 688160 | tf_op jit(solution)/shard_map/ppermute | solution.py:47
  88.1 3.2 collective-permute-done.9
  92.8 3.1 fusion.12
  102.4 2.7 pad_maximum_fusion.5.dy_t
  105.1 2.9 collective-permute-done.18.refs_5_
  109.6 7.6 %collective-permute-done.21.refs_8_ = bf16[192,1792]{1,0:T(8,128)(2,1)} collective-permute-done((bf16[192,1792]{1,0:T(8,128)(2,1)}, bf16[192,1792]{1,0:T(8,128)(2,1)}, u32[]{:S(2)}, u32[]{:S(2)}) %collective-permute-start.21) | collective-permute-done | bytes 688160 | tf_op jit(solution)/shard_map/ppermute | solution.py:47
  121.6 2.8 pad_maximum_fusion.1
  124.4 5.1 copy.70
  129.5 4.2 reshape.107
  135.0 2.7 copy.73.w
  140.5 10.4 %shard_map.375 = (bf16[768,2048]{1,0:T(8,128)(2,1)}, f32[1,2048]{1,0:T(1,128)S(1)}, bf16[384,1024]{1,0:T(8,128)(2,1)S(1)}, bf16[4096,384]{1,0:T(8,128)(2,1)}, bf...) custom-call(s32[4]{0:T(128)S(1)} %broadcast_select_fusion.33.tab, ...), custom_call_target="tpu_custom_call" | custom-call | flops 6000000000 | bytes 20000000 | tf_op jit(solution)/shard_map/pallas_call | solution.py:85
  150.9 2.2 copy-done.13
  153.1 16.3 %shard_map.376 = (bf16[384,1024]{1,0:T(8,128)(2,1)S(1)}, f32[3,2,1024]{2,1,0:T(2,128)S(1)}) custom-call(s32[6]{0:T(128)S(1)} %pad_add_fusion.1.tab, bf16[384,1024]{1,0:T(8,128)(2,1)S(1)} %get-tuple-element.62.q_t, bf16[4096,384]{1,0:T(8,128)(2,1)S(1)} %copy-done.13, bf16[384,4096]{1,0:T(8,128)(2,1)} %get-tuple-element.69.v_t.refs_3_), custom_call_target="tpu_custom_call" | custom-call | flops 8053063680 | bytes 10000000 | tf_op jit(solution)/shard_map/pallas_call | solution.py:183
  169.5 10.6 %shard_map.377 = (bf16[768,2048]{1,0:T(8,128)(2,1)}, f32[1,2048]{1,0:T(1,128)S(1)}, bf16[384,1024]{1,0:T(8,128)(2,1)S(1)}, bf16[4096,384]{1,0:T(8,128)(2,1)}, bf...) custom-call(s32[4]{0:T(128)S(1)} %broadcast_select_fusion.32.tab, ...), custom_call_target="tpu_custom_call", output_to_operand_aliasing={{3}: (6, {}), {4}: (7, {}), {5}: (8, {}), {6}: (9, {})} | custom-call | flops 6000000000 | bytes 20000000 | tf_op jit(solution)/shard_map/pallas_call | solution.py:85
  180.1 2.2 copy-done.14
  182.2 22.2 %shard_map.378 = (bf16[384,1024]{1,0:T(8,128)(2,1)S(1)}, f32[3,2,1024]{2,1,0:T(2,128)S(1)}) custom-call(s32[6]{0:T(128)S(1)} %pad_add_fusion.2.tab, bf16[384,1024]{1,0:T(8,128)(2,1)S(1)} %get-tuple-element.70.q_t, bf16[4096,384]{1,0:T(8,128)(2,1)S(1)} %copy-done.14, bf16[384,4096]{1,0:T(8,128)(2,1)} %get-tuple-element.72.v_t), custom_call_target="tpu_custom_call" | custom-call | flops 12884901888 | bytes 10000000 | tf_op jit(solution)/shard_map/pallas_call | solution.py:183
  212.3 11.3 %collective-permute-done.26.refs_13_ = bf16[192,1792]{1,0:T(8,128)(2,1)S(1)} collective-permute-done((bf16[192,1792]{1,0:T(8,128)(2,1)}, bf16[192,1792]{1,0:T(8,128)(2,1)S(1)}, u32[]{:S(2)}, u32[]{:S(2)}) %collective-permute-start.26) | collective-permute-done | bytes 688160 | tf_op jit(solution)/shard_map/ppermute | solution.py:51
  230.2 45.4 %shard_map.379 = (bf16[768,1024]{1,0:T(8,128)(2,1)}, bf16[768,1024]{1,0:T(8,128)(2,1)}, bf16[768,1024]{1,0:T(8,128)(2,1)}, f32[768,1]{1,0:T(8,128)}, bf16[4,384,...) custom-call(s32[2]{0:T(128)} %pad_add_fusion.sel, bf16[768,1024]{1,0:T(8,128)(2,1)} %maximum_maximum_fusion.x_t, ...), custom_call_target="tpu_custom_call" | custom-call | flops 32614907904 | bytes 34000000 | tf_op jit(solution)/shard_map/pallas_call | solution.py:384
  282.8 40.6 %shard_map.380 = (bf16[384,1024]{1,0:T(8,128)(2,1)}, bf16[2048,384]{1,0:T(8,128)(2,1)}, bf16[2048,384]{1,0:T(8,128)(2,1)}, f32[2048,384]{1,0:T(8,128)}, f32[2048,384]{1,0:T(8,128)}) custom-call(s32[6]{0:T(128)} %copy-done.11, bf16[384,1024]{1,0:T(8,128)(2,1)} %copy-done.15, bf16[384,1024]{1,0:T(8,128)(2,1)} %pad_maximum_fusion.13.do_t, ...), custom_call_target="tpu_custom_call" | custom-call | flops 32212254720 | bytes 20000000 | tf_op jit(solution)/shard_map/pallas_call | solution.py:259
  323.4 27.8 %shard_map.381 = (bf16[384,1024]{1,0:T(8,128)(2,1)}, bf16[2048,384]{1,0:T(8,128)(2,1)}, bf16[2048,384]{1,0:T(8,128)(2,1)}) custom-call(s32[6]{0:T(128)} %copy-done.12, bf16[384,1024]{1,0:T(8,128)(2,1)} %copy-done.16, bf16[384,1024]{1,0:T(8,128)(2,1)} %pad_maximum_fusion.12.do_t, bf16[384,1024]{1,0:T(8,128)(2,1)} %copy-done.5, f32[3,2,1024]{2,1,0:T(2,128)} %copy-done.17, ...), custom_call_target="tpu_custom_call" | custom-call | flops 20132659200 | bytes 20000000 | tf_op jit(solution)/shard_map/pallas_call | solution.py:259
  351.2 16.0 %shard_map.382 = (bf16[384,2048]{1,0:T(8,128)(2,1)}, bf16[384,2048]{1,0:T(8,128)(2,1)}, f32[1,2048]{1,0:T(1,128)}, f32[768,1]{1,0:T(8,128)}, f32[768,1152]{1,0:T(8,128)}) custom-call(s32[4]{0:T(128)} %copy-done.10, bf16[768,1152]{1,0:T(8,128)(2,1)} %copy-done, bf16[768,2048]{1,0:T(8,128)(2,1)} %get-tuple-element.88.n_t, ...), custom_call_target="tpu_custom_call" | custom-call | flops 12000000000 | bytes 20000000 | tf_op jit(solution)/shard_map/pallas_call | solution.py:456
  367.2 16.7 %shard_map.383 = (bf16[384,2048]{1,0:T(8,128)(2,1)}, bf16[384,2048]{1,0:T(8,128)(2,1)}, f32[1,2048]{1,0:T(1,128)}, f32[768,1]{1,0:T(8,128)}, bf16[768,1152]{1,0:T(8,128)(2,1)}) custom-call(s32[4]{0:T(128)} %copy-done.9, bf16[768,1152]{1,0:T(8,128)(2,1)} %copy-done, bf16[768,2048]{1,0:T(8,128)(2,1)} %get-tuple-element.77.n_t, ...), custom_call_target="tpu_custom_call" | custom-call | flops 12000000000 | bytes 20000000 | tf_op jit(solution)/shard_map/pallas_call | solution.py:456
  385.2 17.3 %psum.7 = f32[2,4,192]{2,1,0:T(4,128)S(1)} all-reduce(f32[2,4,192]{2,1,0:T(4,128)S(1)} %reshape.111), channel_id=1, replica_groups=mesh['dp'=2,'rows'=4,'cols'=4] {'dp','rows'}, use_global_device_ids=true, to_apply=%region_0.1 | all-reduce | flops 1536 | bytes 12288 | tf_op jit(solution)/shard_map/psum | solution.py:668
  415.2 3.6 stack.115
  418.7 2.7 copy.84
  421.4 3.4 stack.114
  424.8 2.7 copy.83
  436.8 20.4 %collective-permute-done.43 = bf16[4,192,576]{2,1,0:T(8,128)(2,1)} collective-permute-done((bf16[4,192,576]{2,1,0:T(8,128)(2,1)}, bf16[4,192,576]{2,1,0:T(8,128)(2,1)}, u32[]{:S(2)}, u32[]{:S(2)}) %collective-permute-start.43) | collective-permute-done | bytes 884768 | tf_op jit(solution)/shard_map/ppermute | solution.py:42
  457.2 2.3 copy.86
  459.6 5.4 convert_add_fusion
  472.1 4.7 collective-permute-done.44
  480.4 5.0 collective-permute-done.45
  486.4 4.4 collective-permute-done.30
  493.7 30.7 %collective-permute-done.49 = bf16[4,192,1792]{2,1,0:T(8,128)(2,1)} collective-permute-done((bf16[4,192,1792]{2,1,0:T(8,128)(2,1)S(1)}, bf16[4,192,1792]{2,1,0:T(8,128)(2,1)}, u32[]{:S(2)}, u32[]{:S(2)}) %collective-permute-start.49) | collective-permute-done | bytes 2752544 | tf_op jit(solution)/shard_map/ppermute | solution.py:51
  524.5 4.3 add_convert_fusion
  534.5 12.4 %collective-permute-done.50 = bf16[192,1792]{1,0:T(8,128)(2,1)S(1)} collective-permute-done((bf16[192,1792]{1,0:T(8,128)(2,1)S(1)}, bf16[192,1792]{1,0:T(8,128)(2,1)S(1)}, u32[]{:S(2)}, u32[]{:S(2)}) %collective-permute-start.50) | collective-permute-done | bytes 688160 | tf_op jit(solution)/shard_map/ppermute | solution.py:47
  550.3 12.2 %collective-permute-done.51 = bf16[192,1792]{1,0:T(8,128)(2,1)S(1)} collective-permute-done((bf16[192,1792]{1,0:T(8,128)(2,1)S(1)}, bf16[192,1792]{1,0:T(8,128)(2,1)S(1)}, u32[]{:S(2)}, u32[]{:S(2)}) %collective-permute-start.51) | collective-permute-done | bytes 688160 | tf_op jit(solution)/shard_map/ppermute | solution.py:47
  562.8 3.4 slice_bitcast_fusion
  566.2 10.5 %collective-permute-done.52 = bf16[192,1792]{1,0:T(8,128)(2,1)S(1)} collective-permute-done((bf16[192,1792]{1,0:T(8,128)(2,1)S(1)}, bf16[192,1792]{1,0:T(8,128)(2,1)S(1)}, u32[]{:S(2)}, u32[]{:S(2)}) %collective-permute-start.52) | collective-permute-done | bytes 688160 | tf_op jit(solution)/shard_map/ppermute | solution.py:47
  577.4 2.7 fusion.7
  581.8 6.4 %collective-permute-done.53 = bf16[192,1792]{1,0:T(8,128)(2,1)S(1)} collective-permute-done((bf16[192,1792]{1,0:T(8,128)(2,1)S(1)}, bf16[192,1792]{1,0:T(8,128)(2,1)S(1)}, u32[]{:S(2)}, u32[]{:S(2)}) %collective-permute-start.53) | collective-permute-done | bytes 688160 | tf_op jit(solution)/shard_map/ppermute | solution.py:42
  594.0 8.7 %collective-permute-done.54 = bf16[192,1792]{1,0:T(8,128)(2,1)S(1)} collective-permute-done((bf16[192,1792]{1,0:T(8,128)(2,1)}, bf16[192,1792]{1,0:T(8,128)(2,1)S(1)}, u32[]{:S(2)}, u32[]{:S(2)}) %collective-permute-start.54) | collective-permute-done | bytes 688160 | tf_op jit(solution)/shard_map/ppermute | solution.py:51
  (373 shorter events, 128.9 us)
Async XLA Ops:
  2.3 72.0 %collective-permute-start.2 = (bf16[192,2048]{1,0:T(8,128)(2,1)S(1)}, bf16[192,2048]{1,0:T(8,128)(2,1)S(1)}, u32[]{:S(2)}, u32[]{:S(2)}) collective-permute-start(bf16[192,2048]{1,0:T(8,128)(2,1)S(1)} %get-tuple-element.165.x0), channel_id=1, source_target_pairs={{0,2},{1,3},{2,0},{3,1},{4,6},{5,7},{6,4},{7,5},{8,10},{9,11},{10,... | collective-permute-start | bytes 2359304 | tf_op jit(solution)/shard_map/ppermute | solution.py:42
  3.9 72.1 %collective-permute-start = (bf16[192,2048]{1,0:T(8,128)(2,1)S(1)}, bf16[192,2048]{1,0:T(8,128)(2,1)S(1)}, u32[]{:S(2)}, u32[]{:S(2)}) collective-permute-start(bf16[192,2048]{1,0:T(8,128)(2,1)S(1)} %get-tuple-element.164.x0), channel_id=1, source_target_pairs={{0,2},{1,3},{2,0},{3,1},{4,6},{5,7},{6,4},{7,5},{8,10},{9,11},{10,... | collective-permute-start | bytes 2359304 | tf_op jit(solution)/shard_map/ppermute | solution.py:42
  4.5 35.2 %collective-permute-start.4 = (f32[400]{0:T(512)S(1)}, f32[400]{0:T(512)S(1)}, u32[]{:S(2)}, u32[]{:S(2)}) collective-permute-start(f32[400]{0:T(512)S(1)} %pad_maximum_fusion.20), channel_id=1, source_target_pairs={{0,2},{1,3},{2,0},{3,1},{4,6},{5,7},{6,4},{7,5},{8,10},{9,11},{10,... | collective-permute-start | bytes 4808 | tf_op jit(solution)/shard_map/ppermute | solution.py:42
  6.9 35.6 %collective-permute-start.6 = (bf16[192,576]{1,0:T(8,128)(2,1)}, bf16[192,576]{1,0:T(8,128)(2,1)}, u32[]{:S(2)}, u32[]{:S(2)}) collective-permute-start(bf16[192,576]{1,0:T(8,128)(2,1)} %pad_maximum_fusion.16), channel_id=1, source_target_pairs={{0,4},{4,8},{8,12},{12,0},{1,5},{5,9},{9,13},{13,1},{2,6},{6,10},{... | collective-permute-start | bytes 663560 | tf_op jit(solution)/shard_map/ppermute | solution.py:47
  10.1 50.5 %collective-permute-start.14 = (bf16[192,1792]{1,0:T(8,128)(2,1)}, bf16[192,1792]{1,0:T(8,128)(2,1)}, u32[]{:S(2)}, u32[]{:S(2)}) collective-permute-start(bf16[192,1792]{1,0:T(8,128)(2,1)} %concatenate.115.refs_0_), channel_id=1, source_target_pairs={{0,2},{1,3},{2,0},{3,1},{4,6},{5,7},{6,4},{7,5},{8,10},{9,11},{10,... | collective-permute-start | bytes 2064392 | tf_op jit(solution)/shard_map/ppermute | solution.py:42
  41.0 30.5 %collective-permute-start.12 = (bf16[2,192,1024]{2,1,0:T(8,128)(2,1)}, bf16[2,192,1024]{2,1,0:T(8,128)(2,1)}, u32[]{:S(2)}, u32[]{:S(2)}) collective-permute-start(bf16[2,192,1024]{2,1,0:T(8,128)(2,1)} %pad_maximum_fusion.10), channel_id=1, source_target_pairs={{0,2},{1,3},{2,0},{3,1},{4,6},{5,7},{6,4},{7,5},{8,10},{9,11},{10,... | collective-permute-start | bytes 2359304 | tf_op jit(solution)/shard_map/ppermute | solution.py:42
  42.5 8.1 %collective-permute-start.7 = (bf16[192,576]{1,0:T(8,128)(2,1)}, bf16[192,576]{1,0:T(8,128)(2,1)}, u32[]{:S(2)}, u32[]{:S(2)}) collective-permute-start(bf16[192,576]{1,0:T(8,128)(2,1)} %collective-permute-done.6), channel_id=1, source_target_pairs={{0,4},{4,8},{8,12},{12,0},{1,5},{5,9},{9,13},{13,1},{2,6},{6,10},{... | collective-permute-start | bytes 663560 | tf_op jit(solution)/shard_map/ppermute | solution.py:47
  50.6 7.2 %collective-permute-start.8 = (bf16[192,576]{1,0:T(8,128)(2,1)}, bf16[192,576]{1,0:T(8,128)(2,1)}, u32[]{:S(2)}, u32[]{:S(2)}) collective-permute-start(bf16[192,576]{1,0:T(8,128)(2,1)} %collective-permute-done.7), channel_id=1, source_target_pairs={{0,4},{4,8},{8,12},{12,0},{1,5},{5,9},{9,13},{13,1},{2,6},{6,10},{... | collective-permute-start | bytes 663560 | tf_op jit(solution)/shard_map/ppermute | solution.py:47
  57.8 17.9 %collective-permute-start.15 = (bf16[192,1792]{1,0:T(8,128)(2,1)}, bf16[192,1792]{1,0:T(8,128)(2,1)S(1)}, u32[]{:S(2)}, u32[]{:S(2)}) collective-permute-start(bf16[192,1792]{1,0:T(8,128)(2,1)} %concatenate.115.refs_0_), channel_id=1, source_target_pairs={{0,1},{1,0},{2,3},{3,2},{4,5},{5,4},{6,7},{7,6},{8,9},{9,8},{10,11... | collective-permute-start | bytes 2064392 | tf_op jit(solution)/shard_map/ppermute | solution.py:42
  60.6 30.8 %collective-permute-start.9 = (bf16[4,192,576]{2,1,0:T(8,128)(2,1)}, bf16[4,192,576]{2,1,0:T(8,128)(2,1)}, u32[]{:S(2)}, u32[]{:S(2)}) collective-permute-start(bf16[4,192,576]{2,1,0:T(8,128)(2,1)} %get-tuple-element.180), channel_id=1, source_target_pairs={{0,2},{1,3},{2,0},{3,1},{4,6},{5,7},{6,4},{7,5},{8,10},{9,11},{10,... | collective-permute-start | bytes 2654216 | tf_op jit(solution)/shard_map/ppermute | solution.py:42
  71.4 15.3 %collective-permute-start.17 = (bf16[192,1792]{1,0:T(8,128)(2,1)S(1)}, bf16[192,1792]{1,0:T(8,128)(2,1)}, u32[]{:S(2)}, u32[]{:S(2)}) collective-permute-start(bf16[192,1792]{1,0:T(8,128)(2,1)S(1)} %broadcast_select_fusion.3), channel_id=1, source_target_pairs={{0,4},{4,8},{8,12},{12,0},{1,5},{5,9},{9,13},{13,1},{2,6},{6,10},{... | collective-permute-start | bytes 2064392 | tf_op jit(solution)/shard_map/ppermute | solution.py:47
  74.3 21.6 %collective-permute-start.16 = (bf16[192,1792]{1,0:T(8,128)(2,1)}, bf16[192,1792]{1,0:T(8,128)(2,1)}, u32[]{:S(2)}, u32[]{:S(2)}) collective-permute-start(bf16[192,1792]{1,0:T(8,128)(2,1)} %collective-permute-done.14.refs_1_), channel_id=1, source_target_pairs={{0,1},{1,0},{2,3},{3,2},{4,5},{5,4},{6,7},{7,6},{8,9},{9,8},{10,11... | collective-permute-start | bytes 2064392 | tf_op jit(solution)/shard_map/ppermute | solution.py:42
  75.6 41.6 %collective-permute-start.3 = (bf16[384,2048]{1,0:T(8,128)(2,1)}, bf16[384,2048]{1,0:T(8,128)(2,1)}, u32[]{:S(2)}, u32[]{:S(2)}) collective-permute-start(bf16[384,2048]{1,0:T(8,128)(2,1)} %pad_maximum_fusion.3), channel_id=1, source_target_pairs={{0,1},{1,0},{2,3},{3,2},{4,5},{5,4},{6,7},{7,6},{8,9},{9,8},{10,11... | collective-permute-start | bytes 4718600 | tf_op jit(solution)/shard_map/ppermute | solution.py:42
  76.1 22.9 %collective-permute-start.13 = (bf16[384,1024]{1,0:T(8,128)(2,1)}, bf16[384,1024]{1,0:T(8,128)(2,1)}, u32[]{:S(2)}, u32[]{:S(2)}) collective-permute-start(bf16[384,1024]{1,0:T(8,128)(2,1)} %pad_maximum_fusion.11), channel_id=1, source_target_pairs={{0,1},{1,0},{2,3},{3,2},{4,5},{5,4},{6,7},{7,6},{8,9},{9,8},{10,11... | collective-permute-start | bytes 2359304 | tf_op jit(solution)/shard_map/ppermute | solution.py:42
  86.7 51.0 %collective-permute-start.1 = (bf16[384,2048]{1,0:T(8,128)(2,1)}, bf16[384,2048]{1,0:T(8,128)(2,1)}, u32[]{:S(2)}, u32[]{:S(2)}) collective-permute-start(bf16[384,2048]{1,0:T(8,128)(2,1)} %pad_maximum_fusion.2), channel_id=1, source_target_pairs={{0,1},{1,0},{2,3},{3,2},{4,5},{5,4},{6,7},{7,6},{8,9},{9,8},{10,11... | collective-permute-start | bytes 4718600 | tf_op jit(solution)/shard_map/ppermute | solution.py:42
  91.4 16.6 %collective-permute-start.18 = (bf16[192,1792]{1,0:T(8,128)(2,1)}, bf16[192,1792]{1,0:T(8,128)(2,1)}, u32[]{:S(2)}, u32[]{:S(2)}) collective-permute-start(bf16[192,1792]{1,0:T(8,128)(2,1)} %collective-permute-done.17.refs_4_), channel_id=1, source_target_pairs={{0,16},{16,0},{1,17},{17,1},{2,18},{18,2},{3,19},{19,3},{4,20},{20... | collective-permute-start | bytes 2064392 | tf_op jit(solution)/shard_map/ppermute | solution.py:51
  95.9 25.1 %collective-permute-start.10 = (bf16[2,2,192,576]{3,2,0,1:T(8,128)(2,1)}, bf16[2,2,192,576]{3,2,0,1:T(8,128)(2,1)}, u32[]{:S(2)}, u32[]{:S(2)}) collective-permute-start(bf16[2,2,192,576]{3,2,0,1:T(8,128)(2,1)} %get-tuple-element.153), channel_id=1, source_target_pairs={{0,1},{1,0},{2,3},{3,2},{4,5},{5,4},{6,7},{7,6},{8,9},{9,8},{10,11... | collective-permute-start | bytes 2654216 | tf_op jit(solution)/shard_map/ppermute | solution.py:42
  99.0 18.2 %collective-permute-start.21 = (bf16[192,1792]{1,0:T(8,128)(2,1)}, bf16[192,1792]{1,0:T(8,128)(2,1)}, u32[]{:S(2)}, u32[]{:S(2)}) collective-permute-start(bf16[192,1792]{1,0:T(8,128)(2,1)} %collective-permute-done.17.refs_4_), channel_id=1, source_target_pairs={{0,4},{4,8},{8,12},{12,0},{1,5},{5,9},{9,13},{13,1},{2,6},{6,10},{... | collective-permute-start | bytes 2064392 | tf_op jit(solution)/shard_map/ppermute | solution.py:47
  108.0 100.2 %collective-permute-start.19 = (bf16[192,1792]{1,0:T(8,128)(2,1)}, bf16[192,1792]{1,0:T(8,128)(2,1)}, u32[]{:S(2)}, u32[]{:S(2)}) collective-permute-start(bf16[192,1792]{1,0:T(8,128)(2,1)} %collective-permute-done.17.refs_4_), channel_id=1, source_target_pairs={{0,1},{1,0},{2,3},{3,2},{4,5},{5,4},{6,7},{7,6},{8,9},{9,8},{10,11... | collective-permute-start | bytes 2064392 | tf_op jit(solution)/shard_map/ppermute | solution.py:42
  117.2 93.9 %collective-permute-start.20 = (bf16[192,1792]{1,0:T(8,128)(2,1)}, bf16[192,1792]{1,0:T(8,128)(2,1)}, u32[]{:S(2)}, u32[]{:S(2)}) collective-permute-start(bf16[192,1792]{1,0:T(8,128)(2,1)} %collective-permute-done.18.refs_5_), channel_id=1, source_target_pairs={{0,1},{1,0},{2,3},{3,2},{4,5},{5,4},{6,7},{7,6},{8,9},{9,8},{10,11... | collective-permute-start | bytes 2064392 | tf_op jit(solution)/shard_map/ppermute | solution.py:42
  117.2 88.4 %collective-permute-start.25 = (bf16[192,1792]{1,0:T(8,128)(2,1)}, bf16[192,1792]{1,0:T(8,128)(2,1)}, u32[]{:S(2)}, u32[]{:S(2)}) collective-permute-start(bf16[192,1792]{1,0:T(8,128)(2,1)} %collective-permute-done.21.refs_8_), channel_id=1, source_target_pairs={{0,4},{4,8},{8,12},{12,0},{1,5},{5,9},{9,13},{13,1},{2,6},{6,10},{... | collective-permute-start | bytes 2064392 | tf_op jit(solution)/shard_map/ppermute | solution.py:47
  121.1 87.4 %collective-permute-start.22 = (bf16[192,1792]{1,0:T(8,128)(2,1)}, bf16[192,1792]{1,0:T(8,128)(2,1)}, u32[]{:S(2)}, u32[]{:S(2)}) collective-permute-start(bf16[192,1792]{1,0:T(8,128)(2,1)} %collective-permute-done.21.refs_8_), channel_id=1, source_target_pairs={{0,16},{16,0},{1,17},{17,1},{2,18},{18,2},{3,19},{19,3},{4,20},{20... | collective-permute-start | bytes 2064392 | tf_op jit(solution)/shard_map/ppermute | solution.py:51
  205.5 18.2 %collective-permute-start.11 = (bf16[384,1024]{1,0:T(8,128)(2,1)S(1)}, bf16[384,1024]{1,0:T(8,128)(2,1)S(1)}, u32[]{:S(2)}, u32[]{:S(2)}) collective-permute-start(bf16[384,1024]{1,0:T(8,128)(2,1)S(1)} %pad_maximum_fusion.9), channel_id=1, source_target_pairs={{0,1},{1,0},{2,3},{3,2},{4,5},{5,4},{6,7},{7,6},{8,9},{9,8},{10,11... | collective-permute-start | bytes 2359304 | tf_op jit(solution)/shard_map/ppermute | solution.py:42
  205.6 18.1 %collective-permute-start.26 = (bf16[192,1792]{1,0:T(8,128)(2,1)}, bf16[192,1792]{1,0:T(8,128)(2,1)S(1)}, u32[]{:S(2)}, u32[]{:S(2)}) collective-permute-start(bf16[192,1792]{1,0:T(8,128)(2,1)} %collective-permute-done.25.refs_12_), channel_id=1, source_target_pairs={{0,16},{16,0},{1,17},{17,1},{2,18},{18,2},{3,19},{19,3},{4,20},{20... | collective-permute-start | bytes 2064392 | tf_op jit(solution)/shard_map/ppermute | solution.py:51
  208.2 16.9 %collective-permute-start.23 = (bf16[192,1792]{1,0:T(8,128)(2,1)}, bf16[192,1792]{1,0:T(8,128)(2,1)S(1)}, u32[]{:S(2)}, u32[]{:S(2)}) collective-permute-start(bf16[192,1792]{1,0:T(8,128)(2,1)} %collective-permute-done.21.refs_8_), channel_id=1, source_target_pairs={{0,1},{1,0},{2,3},{3,2},{4,5},{5,4},{6,7},{7,6},{8,9},{9,8},{10,11... | collective-permute-start | bytes 2064392 | tf_op jit(solution)/shard_map/ppermute | solution.py:42
  208.4 16.7 %collective-permute-start.24 = (bf16[192,1792]{1,0:T(8,128)(2,1)}, bf16[192,1792]{1,0:T(8,128)(2,1)S(1)}, u32[]{:S(2)}, u32[]{:S(2)}) collective-permute-start(bf16[192,1792]{1,0:T(8,128)(2,1)} %collective-permute-done.22.refs_9_), channel_id=1, source_target_pairs={{0,1},{1,0},{2,3},{3,2},{4,5},{5,4},{6,7},{7,6},{8,9},{9,8},{10,11... | collective-permute-start | bytes 2064392 | tf_op jit(solution)/shard_map/ppermute | solution.py:42
  211.1 15.4 %collective-permute-start.27 = (bf16[192,1792]{1,0:T(8,128)(2,1)}, bf16[192,1792]{1,0:T(8,128)(2,1)S(1)}, u32[]{:S(2)}, u32[]{:S(2)}) collective-permute-start(bf16[192,1792]{1,0:T(8,128)(2,1)} %collective-permute-done.25.refs_12_), channel_id=1, source_target_pairs={{0,1},{1,0},{2,3},{3,2},{4,5},{5,4},{6,7},{7,6},{8,9},{9,8},{10,11... | collective-permute-start | bytes 2064392 | tf_op jit(solution)/shard_map/ppermute | solution.py:42
  278.7 180.8 %collective-permute-start.48 = (bf16[4,384,1792]{2,1,0:T(8,128)(2,1)}, bf16[4,384,1792]{2,1,0:T(8,128)(2,1)}, u32[]{:S(2)}, u32[]{:S(2)}) collective-permute-start(bf16[4,384,1792]{2,1,0:T(8,128)(2,1)} %get-tuple-element.105), channel_id=1, source_target_pairs={{0,1},{1,0},{2,3},{3,2},{4,5},{5,4},{6,7},{7,6},{8,9},{9,8},{10,11... | collective-permute-start | bytes 16515080 | tf_op jit(solution)/shard_map/ppermute | solution.py:42
  404.7 7.3 %collective-permute-start.42 = (bf16[384,1152]{1,0:T(8,128)(2,1)S(1)}, bf16[384,1152]{1,0:T(8,128)(2,1)S(1)}, u32[]{:S(2)}, u32[]{:S(2)}) collective-permute-start(bf16[384,1152]{1,0:T(8,128)(2,1)S(1)} %slice.327), channel_id=1, source_target_pairs={{0,1},{1,0},{2,3},{3,2},{4,5},{5,4},{6,7},{7,6},{8,9},{9,8},{10,11... | collective-permute-start | bytes 2654216 | tf_op jit(solution)/shard_map/ppermute | solution.py:42
  408.2 24.5 %collective-permute-start.29 = (bf16[2,384,1024]{2,1,0:T(8,128)(2,1)}, bf16[2,384,1024]{2,1,0:T(8,128)(2,1)S(1)}, u32[]{:S(2)}, u32[]{:S(2)}) collective-permute-start(bf16[2,384,1024]{2,1,0:T(8,128)(2,1)} %fusion.1), channel_id=1, source_target_pairs={{0,1},{1,0},{2,3},{3,2},{4,5},{5,4},{6,7},{7,6},{8,9},{9,8},{10,11... | collective-permute-start | bytes 4718600 | tf_op jit(solution)/shard_map/ppermute | solution.py:42
  411.2 57.1 %collective-permute-start.32 = (bf16[384,2048]{1,0:T(8,128)(2,1)}, bf16[384,2048]{1,0:T(8,128)(2,1)}, u32[]{:S(2)}, u32[]{:S(2)}) collective-permute-start(bf16[384,2048]{1,0:T(8,128)(2,1)} %get-tuple-element.95), channel_id=1, source_target_pairs={{0,1},{1,0},{2,3},{3,2},{4,5},{5,4},{6,7},{7,6},{8,9},{9,8},{10,11... | collective-permute-start | bytes 4718600 | tf_op jit(solution)/shard_map/ppermute | solution.py:42
  411.6 20.6 %collective-permute-start.35 = (f32[1,2048]{1,0:T(1,128)S(1)}, f32[1,2048]{1,0:T(1,128)S(1)}, u32[]{:S(2)}, u32[]{:S(2)}) collective-permute-start(f32[1,2048]{1,0:T(1,128)S(1)} %add.198), channel_id=1, source_target_pairs={{0,2},{1,3},{2,0},{3,1},{4,6},{5,7},{6,4},{7,5},{8,10},{9,11},{10,... | collective-permute-start | bytes 24584 | tf_op jit(solution)/shard_map/ppermute | solution.py:42
  412.0 20.6 %collective-permute-start.39 = (f32[1,2048]{1,0:T(1,128)S(1)}, f32[1,2048]{1,0:T(1,128)S(1)}, u32[]{:S(2)}, u32[]{:S(2)}) collective-permute-start(f32[1,2048]{1,0:T(1,128)S(1)} %add.203), channel_id=1, source_target_pairs={{0,2},{1,3},{2,0},{3,1},{4,6},{5,7},{6,4},{7,5},{8,10},{9,11},{10,... | collective-permute-start | bytes 24584 | tf_op jit(solution)/shard_map/ppermute | solution.py:42
  432.2 25.0 %collective-permute-start.43 = (bf16[4,192,576]{2,1,0:T(8,128)(2,1)}, bf16[4,192,576]{2,1,0:T(8,128)(2,1)}, u32[]{:S(2)}, u32[]{:S(2)}) collective-permute-start(bf16[4,192,576]{2,1,0:T(8,128)(2,1)} %copy.85), channel_id=1, source_target_pairs={{0,2},{1,3},{2,0},{3,1},{4,6},{5,7},{6,4},{7,5},{8,10},{9,11},{10,... | collective-permute-start | bytes 2654216 | tf_op jit(solution)/shard_map/ppermute | solution.py:42
  432.6 44.3 %collective-permute-start.36 = (bf16[384,2048]{1,0:T(8,128)(2,1)}, bf16[384,2048]{1,0:T(8,128)(2,1)}, u32[]{:S(2)}, u32[]{:S(2)}) collective-permute-start(bf16[384,2048]{1,0:T(8,128)(2,1)} %get-tuple-element.99), channel_id=1, source_target_pairs={{0,1},{1,0},{2,3},{3,2},{4,5},{5,4},{6,7},{7,6},{8,9},{9,8},{10,11... | collective-permute-start | bytes 4718600 | tf_op jit(solution)/shard_map/ppermute | solution.py:42
  435.1 55.7 %collective-permute-start.30 = (bf16[4,192,1024]{2,1,0:T(8,128)(2,1)}, bf16[4,192,1024]{2,1,0:T(8,128)(2,1)S(1)}, u32[]{:S(2)}, u32[]{:S(2)}) collective-permute-start(bf16[4,192,1024]{2,1,0:T(8,128)(2,1)} %pad_maximum_fusion.7), channel_id=1, source_target_pairs={{0,2},{1,3},{2,0},{3,1},{4,6},{5,7},{6,4},{7,5},{8,10},{9,11},{10,... | collective-permute-start | bytes 4718600 | tf_op jit(solution)/shard_map/ppermute | solution.py:42
  465.5 59.0 %collective-permute-start.49 = (bf16[4,192,1792]{2,1,0:T(8,128)(2,1)S(1)}, bf16[4,192,1792]{2,1,0:T(8,128)(2,1)}, u32[]{:S(2)}, u32[]{:S(2)}) collective-permute-start(bf16[4,192,1792]{2,1,0:T(8,128)(2,1)S(1)} %select_convert_fusion), channel_id=1, source_target_pairs={{0,16},{16,0},{1,17},{17,1},{2,18},{18,2},{3,19},{19,3},{4,20},{20... | collective-permute-start | bytes 8257544 | tf_op jit(solution)/shard_map/ppermute | solution.py:51
  467.4 9.3 %collective-permute-start.44 = (bf16[192,576]{0,1:T(8,128)(2,1)S(1)}, bf16[192,576]{0,1:T(8,128)(2,1)S(1)}, u32[]{:S(2)}, u32[]{:S(2)}) collective-permute-start(bf16[192,576]{0,1:T(8,128)(2,1)S(1)} %slice_bitcast_fusion.11), channel_id=1, source_target_pairs={{0,12},{4,0},{8,4},{12,8},{1,13},{5,1},{9,5},{13,9},{2,14},{6,2},{... | collective-permute-start | bytes 663560 | tf_op jit(solution)/shard_map/ppermute | solution.py:47
  471.8 105.6 %collective-permute-start.33 = (bf16[192,2048]{1,0:T(8,128)(2,1)}, bf16[192,2048]{1,0:T(8,128)(2,1)}, u32[]{:S(2)}, u32[]{:S(2)}) collective-permute-start(bf16[192,2048]{1,0:T(8,128)(2,1)} %slice.575), channel_id=1, source_target_pairs={{0,2},{1,3},{2,0},{3,1},{4,6},{5,7},{6,4},{7,5},{8,10},{9,11},{10,... | collective-permute-start | bytes 2359304 | tf_op jit(solution)/shard_map/ppermute | solution.py:42
  476.8 8.6 %collective-permute-start.45 = (bf16[192,576]{0,1:T(8,128)(2,1)S(1)}, bf16[192,576]{0,1:T(8,128)(2,1)S(1)}, u32[]{:S(2)}, u32[]{:S(2)}) collective-permute-start(bf16[192,576]{0,1:T(8,128)(2,1)S(1)} %fusion.16), channel_id=1, source_target_pairs={{0,12},{4,0},{8,4},{12,8},{1,13},{5,1},{9,5},{13,9},{2,14},{6,2},{... | collective-permute-start | bytes 663560 | tf_op jit(solution)/shard_map/ppermute | solution.py:47
  480.1 97.3 %collective-permute-start.37 = (bf16[192,2048]{1,0:T(8,128)(2,1)}, bf16[192,2048]{1,0:T(8,128)(2,1)}, u32[]{:S(2)}, u32[]{:S(2)}) collective-permute-start(bf16[192,2048]{1,0:T(8,128)(2,1)} %slice.574), channel_id=1, source_target_pairs={{0,2},{1,3},{2,0},{3,1},{4,6},{5,7},{6,4},{7,5},{8,10},{9,11},{10,... | collective-permute-start | bytes 2359304 | tf_op jit(solution)/shard_map/ppermute | solution.py:42
  486.2 93.9 %collective-permute-start.46 = (bf16[192,576]{0,1:T(8,128)(2,1)}, bf16[192,576]{0,1:T(8,128)(2,1)}, u32[]{:S(2)}, u32[]{:S(2)}) collective-permute-start(bf16[192,576]{0,1:T(8,128)(2,1)} %fusion.15), channel_id=1, source_target_pairs={{0,12},{4,0},{8,4},{12,8},{1,13},{5,1},{9,5},{13,9},{2,14},{6,2},{... | collective-permute-start | bytes 663560 | tf_op jit(solution)/shard_map/ppermute | solution.py:47
  530.0 17.0 %collective-permute-start.50 = (bf16[192,1792]{1,0:T(8,128)(2,1)S(1)}, bf16[192,1792]{1,0:T(8,128)(2,1)S(1)}, u32[]{:S(2)}, u32[]{:S(2)}) collective-permute-start(bf16[192,1792]{1,0:T(8,128)(2,1)S(1)} %slice_bitcast_fusion.5), channel_id=1, source_target_pairs={{0,12},{4,0},{8,4},{12,8},{1,13},{5,1},{9,5},{13,9},{2,14},{6,2},{... | collective-permute-start | bytes 2064392 | tf_op jit(solution)/shard_map/ppermute | solution.py:47
  547.1 15.4 %collective-permute-start.51 = (bf16[192,1792]{1,0:T(8,128)(2,1)S(1)}, bf16[192,1792]{1,0:T(8,128)(2,1)S(1)}, u32[]{:S(2)}, u32[]{:S(2)}) collective-permute-start(bf16[192,1792]{1,0:T(8,128)(2,1)S(1)} %fusion.10), channel_id=1, source_target_pairs={{0,12},{4,0},{8,4},{12,8},{1,13},{5,1},{9,5},{13,9},{2,14},{6,2},{... | collective-permute-start | bytes 2064392 | tf_op jit(solution)/shard_map/ppermute | solution.py:47
  562.7 14.0 %collective-permute-start.52 = (bf16[192,1792]{1,0:T(8,128)(2,1)S(1)}, bf16[192,1792]{1,0:T(8,128)(2,1)S(1)}, u32[]{:S(2)}, u32[]{:S(2)}) collective-permute-start(bf16[192,1792]{1,0:T(8,128)(2,1)S(1)} %fusion.9), channel_id=1, source_target_pairs={{0,12},{4,0},{8,4},{12,8},{1,13},{5,1},{9,5},{13,9},{2,14},{6,2},{... | collective-permute-start | bytes 2064392 | tf_op jit(solution)/shard_map/ppermute | solution.py:47
  576.9 11.3 %collective-permute-start.53 = (bf16[192,1792]{1,0:T(8,128)(2,1)S(1)}, bf16[192,1792]{1,0:T(8,128)(2,1)S(1)}, u32[]{:S(2)}, u32[]{:S(2)}) collective-permute-start(bf16[192,1792]{1,0:T(8,128)(2,1)S(1)} %fusion.8), channel_id=1, source_target_pairs={{0,2},{1,3},{2,0},{3,1},{4,6},{5,7},{6,4},{7,5},{8,10},{9,11},{10,... | collective-permute-start | bytes 2064392 | tf_op jit(solution)/shard_map/ppermute | solution.py:42
  581.2 10.3 %collective-permute-start.47 = (bf16[192,576]{0,1:T(8,128)(2,1)S(1)}, bf16[192,576]{0,1:T(8,128)(2,1)S(1)}, u32[]{:S(2)}, u32[]{:S(2)}) collective-permute-start(bf16[192,576]{0,1:T(8,128)(2,1)S(1)} %fusion.14), channel_id=1, source_target_pairs={{0,16},{16,0},{1,17},{17,1},{2,18},{18,2},{3,19},{19,3},{4,20},{20... | collective-permute-start | bytes 663560 | tf_op jit(solution)/shard_map/ppermute | solution.py:51
  589.1 13.6 %collective-permute-start.54 = (bf16[192,1792]{1,0:T(8,128)(2,1)}, bf16[192,1792]{1,0:T(8,128)(2,1)S(1)}, u32[]{:S(2)}, u32[]{:S(2)}) collective-permute-start(bf16[192,1792]{1,0:T(8,128)(2,1)} %broadcast_select_fusion.2), channel_id=1, source_target_pairs={{0,16},{16,0},{1,17},{17,1},{2,18},{18,2},{3,19},{19,3},{4,20},{20... | collective-permute-start | bytes 2064392 | tf_op jit(solution)/shard_map/ppermute | solution.py:51
  (83 other events, 1093.2 us)

commit v2 on v1

v2 whole, which is shorter than its diff:
```python
import functools
import math

import jax
import jax.numpy as jnp
from jax import lax
from jax.experimental import pallas as pl
from jax.experimental.pallas import tpu as pltpu
from jax.sharding import PartitionSpec as P


D = 768
HD = 64
LEN = 4096
HALF = 2048
B = 512
FB = 192
FF = 3072
EPSILON = 1e-06
MASKED = -1e30
SCALE = HD**-0.5
LOG2E = math.log2(math.e)
BF = jnp.bfloat16
F32 = jnp.float32
MIB = 1 << 20


def cost(us):
    return pl.CostEstimate(flops=int(us * 1_150_000_000), bytes_accessed=0, transcendentals=0)


def contract(left, right, dims):
    return lax.dot_general(left, right, (dims, ((), ())), preferred_element_type=F32)


def nn(left, right):
    return contract(left, right, ((1,), (0,)))


def nt(left, right):
    return contract(left, right, ((1,), (1,)))


def cols_swap(value, distance):
    return lax.ppermute(value, "cols", [(i, i ^ distance) for i in range(lax.axis_size("cols"))])


def rows_shift(value, step):
    count = lax.axis_size("rows")
    return lax.ppermute(value, "rows", [(i, (i + step) % count) for i in range(count)])


def dp_swap(value):
    return lax.ppermute(value, "dp", [(i, i ^ 1) for i in range(lax.axis_size("dp"))])


ANY = pl.BlockSpec(memory_space=pl.ANY)


def hold_kernel(tab, source, *refs):
    refs[-1][0] = source[...]


def hold(blocks, source, width, *deps):
    count = blocks.shape[0]
    return pl.pallas_call(
        hold_kernel,
        grid_spec=pltpu.PrefetchScalarGridSpec(
            num_scalar_prefetch=1,
            grid=(count,),
            in_specs=[pl.BlockSpec((FB, width), lambda i, t: (0, t[i]))] + [ANY] * len(deps),
            out_specs=pl.BlockSpec((1, FB, width), lambda i, t: (i // 2, 0, i % 2)),
        ),
        out_shape=jax.ShapeDtypeStruct((count // 2, FB, 2 * width), source.dtype),
        cost_estimate=cost(3),
    )(blocks, source, *deps)


def join_kernel(first, second, *refs):
    refs[-1][:, :D] = first[...]
    refs[-1][:, D:] = second[...]


def join(first, second, *deps):
    vmem = pl.BlockSpec(memory_space=pltpu.VMEM)
    return pl.pallas_call(
        join_kernel,
        in_specs=[vmem, vmem] + [ANY] * len(deps),
        out_specs=vmem,
        out_shape=jax.ShapeDtypeStruct((FB, 2 * D), BF),
        cost_estimate=cost(2),
    )(first, second, *deps)


def tie(value, *deps):
    return pl.pallas_call(
        lambda *refs: None,
        in_specs=[ANY] * (1 + len(deps)),
        out_specs=ANY,
        out_shape=jax.ShapeDtypeStruct(value.shape, value.dtype),
        input_output_aliases={0: 0},
        cost_estimate=cost(0),
    )(value, *deps)


def qkv_kernel(tab, *refs, first, extra):
    x0, x1, x23, gain = refs[:4]
    normed, scale, q_t, k, k_t, v, v_t = refs[4 + extra : 11 + extra]
    i = pl.program_id(0)
    if first:
        w = refs[11 + extra]

        @pl.when(i == 0)
        def _():
            w[0:FB, :] = refs[4][0]
            w[FB : 2 * FB, :] = refs[5][0]
            w[2 * FB : 3 * FB, :] = refs[6][0]
            w[3 * FB :, :] = refs[6][1]
    else:
        w = refs[4]
    x = jnp.concatenate([x0[...], x1[...], x23[0], x23[1]], axis=0).astype(F32)
    r1 = lax.rsqrt(jnp.sum(x * x, axis=0, keepdims=True) * (1.0 / D) + EPSILON)
    n_t = (x * r1 * gain[...]).astype(BF)
    normed[...] = n_t
    scale[...] = r1
    n = n_t.T
    for p in range(3):
        first_col = p * 384
        kv = nn(n, w[:, first_col + 128 : first_col + 384])
        cols = slice(p * 128, (p + 1) * 128)
        k[:, cols] = kv[:, :128].astype(BF)
        v[:, cols] = kv[:, 128:].astype(BF)
        kv_t = kv.T.astype(BF)
        k_t[cols, :] = kv_t[:128]
        v_t[cols, :] = kv_t[128:]

    @pl.when(i < 2)
    def _():
        for p in range(3):
            q = nn(n, w[:, p * 384 : p * 384 + 128]) * (SCALE * LOG2E)
            q_t[p * 128 : (p + 1) * 128, :] = q.T.astype(BF)


def project_half(order, x, gain, weights, half, old, deps):
    base = half * (HALF // B)
    first = half == 0

    def cols_of(rows, offset=0):
        return pl.BlockSpec((rows, B), lambda i, t: (0, offset + t[i]))

    whole = lambda shape: pl.BlockSpec(shape, lambda i, t: (0, 0))
    slots = pl.BlockSpec((1, FB, 1152), lambda i, t: (t[4], 0, 0))
    major = pl.BlockSpec((B, 384), lambda i, t: (base + t[i], 0))
    minor = pl.BlockSpec((384, B), lambda i, t: (0, base + t[i]))
    kv = [jax.ShapeDtypeStruct(s, BF) for s in ((LEN, 384), (384, LEN)) * 2]
    cross = pl.BlockSpec((2, FB, 1152), lambda i, t: (0, 0, 0))
    w_specs = [slots, slots, cross] if first else [whole((D, 1152))]
    extra = len(w_specs) + len(old) + len(deps)
    return pl.pallas_call(
        functools.partial(qkv_kernel, first=first, extra=extra),
        grid_spec=pltpu.PrefetchScalarGridSpec(
            num_scalar_prefetch=1,
            grid=(HALF // B,),
            in_specs=[cols_of(FB, base), cols_of(FB), pl.BlockSpec((2, FB, B), lambda i, t: (0, 0, t[i])), whole((D, 1))]
            + w_specs
            + [ANY] * (len(old) + len(deps)),
            out_specs=[
                cols_of(D),
                cols_of(1),
                pl.BlockSpec((384, B), lambda i, t: (0, jnp.minimum(i, 1))),
                major,
                minor,
                major,
                minor,
            ]
            + [whole((D, 1152))] * first,
        ),
        out_shape=[
            jax.ShapeDtypeStruct((D, HALF), BF),
            jax.ShapeDtypeStruct((1, HALF), F32),
            jax.ShapeDtypeStruct((384, HALF // 2), BF),
        ]
        + kv
        + [jax.ShapeDtypeStruct((D, 1152), BF)] * first,
        input_output_aliases={5 + len(w_specs) + n: 3 + n for n in range(len(old))},
        compiler_params=pltpu.CompilerParams(vmem_limit_bytes=48 * MIB),
        cost_estimate=cost(12),
    )(order, *x, gain, *weights, *old, *deps)


def block_masks(first, last):
    key = lax.broadcasted_iota(jnp.int32, (B, B), 0)
    query = lax.broadcasted_iota(jnp.int32, (B, B), 1)
    piece = (key >= first) & (key < last) & (query >= first) & (query < last)
    return (key > query, (key <= query) | piece)


def masked(scores, masks, step, count):
    if step == count - 1:
        scores = jnp.where(masks[1], scores, MASKED)
    if count == 4 and step == 0:
        scores = jnp.where(masks[0], scores, MASKED)
    return scores


def head_rows(pair_t):
    row = lax.broadcasted_iota(jnp.int32, pair_t.shape, 0)
    zero = jnp.zeros((), pair_t.dtype)
    return [jnp.where((row // HD) == h, pair_t, zero) for h in range(2)]


def head_cols(pair):
    col = lax.broadcasted_iota(jnp.int32, pair.shape, 1)
    zero = jnp.zeros((), pair.dtype)
    return [jnp.where((col // HD) == h, pair, zero) for h in range(2)]


def for_counts(block, counts, body):
    if len(counts) == 1:
        body(counts[0])
        return
    visible = jnp.minimum(block, 3) + 1
    for count in counts:
        pl.when(visible == count)(functools.partial(body, count))


def attend_kernel(tab, q_t, k, v_t, *refs, counts):
    o_own, o_other, log_total = refs[-3:]
    i = pl.program_id(1)
    block, first, last = tab[i], tab[2 + i], tab[4 + i]

    def body(count):
        masks = block_masks(first, last)
        starts = [pl.multiple_of((block - (count - 1) + t) * B, B) for t in range(count)]
        for h, q_head in enumerate(head_rows(q_t[...])):
            scores = [masked(nn(k[pl.ds(s, B), :], q_head), masks, t, count) for t, s in enumerate(starts)]
            peak = functools.reduce(jnp.maximum, [jnp.max(s, axis=0, keepdims=True) for s in scores])
            total, mixed = 0.0, 0.0
            for score, s in zip(scores, starts):
                part = jnp.exp2(score - peak)
                total = total + jnp.sum(part, axis=0, keepdims=True)
                mixed = mixed + nn(v_t[h * HD : (h + 1) * HD, pl.ds(s, B)], part.astype(BF))
            out = (mixed * (1.0 / total)).astype(BF)

            @pl.when(i == 0)
            def _():
                o_own[h * HD : (h + 1) * HD, :] = out

            @pl.when(i == 1)
            def _():
                o_other[h * HD : (h + 1) * HD, :] = out

            log_total[0, h : h + 1, :] = peak + jnp.log2(total)

    for_counts(block, counts, body)


def attend(tab, q_t, k, v_t, half, pairs, *deps):
    base, count = pairs
    span = LEN if half else HALF
    one = pl.BlockSpec((128, B), lambda p, i, t: (p, 0))
    block = jax.ShapeDtypeStruct((count * 128, B), BF)
    return pl.pallas_call(
        functools.partial(attend_kernel, counts=(4,) if half else (1, 2, 3, 4)),
        grid_spec=pltpu.PrefetchScalarGridSpec(
            num_scalar_prefetch=1,
            grid=(count, 2),
            in_specs=[
                pl.BlockSpec((128, B), lambda p, i, t: (base + p, i)),
                pl.BlockSpec((span, 128), lambda p, i, t: (0, base + p)),
                pl.BlockSpec((128, span), lambda p, i, t: (base + p, 0)),
            ]
            + [ANY] * len(deps),
            out_specs=[one, one, pl.BlockSpec((1, 2, B), lambda p, i, t: (p, 0, i))],
        ),
        out_shape=[block, block, jax.ShapeDtypeStruct((count, 2, 2 * B), F32)],
        compiler_params=pltpu.CompilerParams(vmem_limit_bytes=48 * MIB),
        cost_estimate=cost((8 if half else 6) * count),
    )(tab, q_t, k, v_t, *deps)


def attend_back_kernel(tab, q_t, do_own, do_other, o_own, o_other, log_total, k, v, k_t, *refs, counts, half):
    if half:
        dq_t, high, low, dkv = refs[-4:]
    else:
        start = refs[0]
        dq_t, low, dkv = refs[-3:]
    i = pl.program_id(1)
    block, first, last = tab[i], tab[2 + i], tab[4 + i]

    @pl.when(i == 0)
    def _():
        dkv[...] = jnp.zeros_like(dkv) if half else start[0]

    def body(count):
        masks = block_masks(first, last)
        queries, grads = q_t[...], jnp.where(i == 0, do_own[...], do_other[...])
        mixed = jnp.where(i == 0, o_own[...], o_other[...])
        q_rows, g_rows = head_rows(queries), head_rows(grads)
        q_cols, g_cols = head_cols(queries.T), head_cols(grads.T)
        product = grads.astype(F32) * mixed.astype(F32)
        inner = [jnp.sum(product[h * HD : (h + 1) * HD], axis=0, keepdims=True) for h in range(2)]
        dq = [0.0, 0.0]
        for t in range(count):
            rows = pl.ds(pl.multiple_of((block - (count - 1) + t) * B, B), B)
            key_rows, value_rows = k[rows, :], v[rows, :]
            dk_part = dv_part = 0.0
            for h in range(2):
                score = masked(nn(key_rows, q_rows[h]), masks, t, count)
                probs = jnp.exp2(score - log_total[0, h : h + 1, :])
                grad_probs = nn(value_rows, g_rows[h])
                grad_scores = (probs * (grad_probs - inner[h])).astype(BF)
                dv_part = dv_part + nn(probs.astype(BF), g_cols[h])
                dk_part = dk_part + nn(grad_scores, q_cols[h])
                dq[h] = dq[h] + nn(k_t[h * HD : (h + 1) * HD, rows], grad_scores)
            dkv[rows, :128] += dk_part
            dkv[rows, 128:] += dv_part
        for h in range(2):
            dq_t[h * HD : (h + 1) * HD, :] = (dq[h] * SCALE).astype(BF)

    for_counts(block, counts, body)

    @pl.when(i == 1)
    def _():
        target, rows = (high, slice(HALF, LEN)) if half else (low, slice(0, HALF))
        target[0, :, :128] = (dkv[rows, :128] * (1.0 / LOG2E)).astype(BF)
        target[0, :, 128:] = dkv[rows, 128:].astype(BF)
        if half:
            low[0] = dkv[:HALF, :]


def attend_back(tab, q_t, grads, outs, log_total, k, v, k_t, half, pairs, start, *deps):
    base, count = pairs
    one = pl.BlockSpec((128, B), lambda p, i, t: (base + p, 0))
    one_of = pl.BlockSpec((128, B), lambda p, i, t: (base + p, half))
    span = LEN if half else HALF
    query = pl.BlockSpec((128, B), lambda p, i, t: (base + p, i))
    stat = pl.BlockSpec((1, 2, B), lambda p, i, t: (base + p, 0, i))
    major = pl.BlockSpec((span, 128), lambda p, i, t: (0, base + p))
    minor = pl.BlockSpec((128, span), lambda p, i, t: (base + p, 0))
    grad = pl.BlockSpec((1, HALF, 256), lambda p, i, t: (p, 0, 0))
    grad_in = pl.BlockSpec((1, HALF, 256), lambda p, i, t: (base + p, 0, 0))
    return pl.pallas_call(
        functools.partial(attend_back_kernel, counts=(4,) if half else (1, 2, 3, 4), half=half),
        grid_spec=pltpu.PrefetchScalarGridSpec(
            num_scalar_prefetch=1,
            grid=(count, 2),
            in_specs=[query, one_of, one_of, one, one, stat, major, major, minor]
            + [grad_in] * len(start)
            + [ANY] * len(deps),
            out_specs=[pl.BlockSpec((128, B), lambda p, i, t: (p, i)), grad] + [grad] * half,
            scratch_shapes=[pltpu.VMEM((span, 256), F32)],
        ),
        out_shape=[
            jax.ShapeDtypeStruct((count * 128, 2 * B), BF),
            jax.ShapeDtypeStruct((count, HALF, 256), BF),
        ]
        + [jax.ShapeDtypeStruct((count, HALF, 256), F32)] * half,
        compiler_params=pltpu.CompilerParams(vmem_limit_bytes=56 * MIB),
        cost_estimate=cost((16 if half else 12) * count),
    )(tab, q_t, *grads, *outs, log_total, k, v, k_t, *start, *deps)


HEAD_ROWS = ((0, 0, 128), (128, 192, 128), (256, 128, 64), (320, 320, 64))
ROOT = math.sqrt(2.0 / math.pi)


def feed_chunk(up):
    square = up * up
    half = 0.5 + 0.5 * jnp.tanh(up * (ROOT + (ROOT * 0.044715) * square))
    act = (up * half).astype(BF)
    slope = half + (2.0 * up) * (half - half * half) * (ROOT + (3.0 * ROOT * 0.044715) * square)
    return act, slope


def feed_kernel(sel, gain, *refs):
    nears, pairs, crosses = refs[:4], refs[4:8], refs[8:11]
    a_parts, dy_parts, x_parts = refs[11:17], refs[17:20], refs[20:25]
    outs = refs[-26:]
    both_near, both_far, ga_own, ga_other, gain_sum = outs[:5]
    g_near, g_one, g_rest = outs[5:8]
    w_up, w_down, w_out, a_t, dy_t, x_t, n, dy, mid, mlp, gn, stage, stage_out = outs[8:21]
    w_sems, a_sems, in_sems, out_sems, last_sems = outs[21:26]
    core, parity = sel[0], sel[3]

    def start(copies):
        for copy in copies:
            copy.start()

    def wait(copies):
        for copy in copies:
            copy.wait()

    halves = (((0, 768, 0, 0), (768, 896, 1, 0)), ((0, 128, 1, 128), (128, 896, 2, 0)))
    targets = (w_up, w_out, w_down)

    def loads(slot, swapped):
        copies = []

        def add(source, offset, which_half, rel):
            for first, last, which, at in halves[which_half]:
                copies.append(
                    pltpu.make_async_copy(
                        source.at[:, offset + first : offset + last],
                        targets[which].at[slot, rel * FB : (rel + 1) * FB, at : at + last - first],
                        w_sems.at[slot, len(copies)],
                    )
                )

        for half in range(2):
            add(nears[slot], half * 896, half, 0)
            if slot < 2:
                add(pairs[half ^ swapped].at[slot], 0, half, 1)
                add(crosses[0].at[slot], half * 896, half, 2)
                add(crosses[0].at[slot], 1792 + (half ^ swapped) * 896, half, 3)
            else:
                add(pairs[slot], half * 896, half, 1)
                add(crosses[slot - 1].at[0], half * 896, half, 2)
                add(crosses[slot - 1].at[1], half * 896, half, 3)
        return copies

    def a_loads():
        copies = []
        for half in range(2):
            cols = slice(half * B, (half + 1) * B)
            for side in range(2):
                for source, target, size in HEAD_ROWS:
                    if side == 1:
                        part, at = a_parts[4 + half], source
                    elif source < 128:
                        part, at = a_parts[2 * half], source
                    else:
                        part, at = a_parts[2 * half + 1], source - 128
                    copies.append(
                        pltpu.make_async_copy(
                            part.at[at : at + size, :],
                            a_t.at[side * 384 + target : side * 384 + target + size, cols],
                            a_sems.at[len(copies)],
                        )
                    )
        return copies

    def token_loads():
        copies = []

        def add(source, target):
            copies.append(pltpu.make_async_copy(source, target, in_sems.at[len(copies)]))

        for half in range(2):
            cols = slice(half * B, (half + 1) * B)
            place = pl.ds(pl.multiple_of(sel[1 + half] * B, B), B)
            at_whole = pl.ds(pl.multiple_of((sel[1 + half] + 4 * half) * B, B), B)
            add(dy_parts[0].at[:, at_whole], dy_t.at[0:FB, cols])
            add(x_parts[0].at[:, at_whole], x_t.at[0:FB, cols])
            pair, cross = x_parts[1 + 2 * half : 3 + 2 * half]
            add(pair.at[:, place], x_t.at[FB : 2 * FB, cols])
            add(cross.at[0, :, place], x_t.at[2 * FB : 3 * FB, cols])
            add(cross.at[1, :, place], x_t.at[3 * FB :, cols])
        add(dy_parts[1].at[0], dy_t.at[FB : 2 * FB, :])
        add(dy_parts[2].at[0], dy_t.at[2 * FB : 3 * FB, :])
        add(dy_parts[2].at[1], dy_t.at[3 * FB :, :])
        return copies

    def stores(slot):
        far = g_one if slot == 1 else g_rest.at[(0, 0, 1, 2)[slot]]
        copies = []
        for side, target in enumerate((g_near.at[slot], far)):
            for which in range(2):
                copies.append(
                    pltpu.make_async_copy(
                        stage.at[slot % 2, which, pl.ds(side * 384, 384), :],
                        target.at[:, which * 1024 : which * 1024 + D],
                        out_sems.at[slot % 2, side * 2 + which],
                    )
                )
        return copies

    def last_stores(slot):
        far = g_one if slot == 1 else g_rest.at[(0, 0, 1, 2)[slot]]
        return [
            pltpu.make_async_copy(
                stage_out.at[slot, pl.ds(side * 384, 384), :],
                target.at[:, D : D + 256],
                last_sems.at[slot, side],
            )
            for side, target in enumerate((g_near.at[slot], far))
        ]

    start(a_loads())
    start(token_loads())

    @pl.when(parity == 0)
    def _():
        for slot in range(4):
            start(loads(slot, 0))

    @pl.when(parity == 1)
    def _():
        for slot in range(4):
            start(loads(slot, 1))

    a_t[D:, :] = jnp.zeros((64, a_t.shape[1]), BF)

    def a_rows(slot, count):
        place = lax.rem(slot + 2 * core, 4) * FB
        return pl.ds(pl.multiple_of(place, FB), count)

    wait(token_loads())
    dy[...] = dy_t[...].T
    wait(a_loads())
    for slot in range(4):
        wait(loads(slot, 0))
    mixed = nn(w_out[0], a_t[a_rows(0, 256), :])
    for slot in range(1, 4):
        mixed = mixed + nn(w_out[slot], a_t[a_rows(slot, 256), :])
    mid[...] = x_t[...].astype(F32) + mixed
    mlp[...] = mid[...]
    gn[...] = jnp.zeros_like(gn)
    r2 = lax.rsqrt(jnp.sum(mid[...] * mid[...], axis=0, keepdims=True) * (1.0 / D) + EPSILON)
    n_t = x_t
    n_t[...] = (mid[...] * r2 * gain[...]).astype(BF)
    n[...] = n_t[...].T

    def chunk(slot, carry):
        buffer = lax.rem(slot, 2)
        for before in range(2):

            @pl.when(slot == before + 2)
            def _():
                wait(stores(before))

        up = nn(n[...], w_up[slot])
        act, slope = feed_chunk(up)
        stage[buffer, 1] = nn(dy_t[...], act).astype(BF)
        mlp[...] += nt(w_down[slot], act)
        grad_up = (nn(dy[...], w_down[slot]) * slope).astype(BF)
        stage[buffer, 0] = nn(n_t[...], grad_up).astype(BF)
        gn[...] += nt(w_up[slot], grad_up)
        for now in range(4):

            @pl.when(slot == now)
            def _():
                start(stores(now))

        return carry

    lax.fori_loop(0, 4, chunk, 0)
    both_near[0] = mlp[:384].astype(BF)
    both_far[0] = mlp[384:].astype(BF)
    weighted = gn[...] * gain[...]
    inner = jnp.sum(mid[...] * weighted, axis=0, keepdims=True)
    cubed = r2 * r2 * r2 * inner * (1.0 / D)
    gm = (dy_t[...].astype(F32) + r2 * weighted - mid[...] * cubed).astype(BF)
    x_t[...] = gm
    both_near[1] = gm[:384]
    both_far[1] = gm[384:]
    gain_sum[...] = jnp.sum(gn[...] * mid[...] * r2, axis=1, keepdims=True)
    for slot in range(4):
        grad_a = contract(w_out[slot], x_t[...], ((0,), (0,)))[:FB].astype(BF)

        def place(target):
            for to, source, size in HEAD_ROWS:
                if source // FB == slot % 2:
                    target[to : to + size, :] = grad_a[source % FB : source % FB + size]

        pl.when((slot // 2) == core)(functools.partial(place, ga_own))
        pl.when((slot // 2) != core)(functools.partial(place, ga_other))
        part = nt(x_t[...], a_t[a_rows(slot, FB), :])
        stage_out[slot] = jnp.concatenate([part, jnp.zeros((D, 64), F32)], axis=1).astype(BF)
        start(last_stores(slot))
    wait(stores(2))
    wait(stores(3))
    for slot in range(4):
        wait(last_stores(slot))


def feed_forward(sel, gain, nears, pairs, crosses, a_parts, dy_parts, x_parts, *deps):
    count = 2 * B
    vmem = pl.BlockSpec(memory_space=pltpu.VMEM)
    both = jax.ShapeDtypeStruct((2, 384, count), BF)
    heads = jax.ShapeDtypeStruct((384, count), BF)
    inputs = (*nears, *pairs, *crosses, *a_parts, *dy_parts, *x_parts, *deps)
    return pl.pallas_call(
        feed_kernel,
        in_specs=[pl.BlockSpec(memory_space=pltpu.SMEM), vmem] + [ANY] * len(inputs),
        out_specs=[vmem] * 5 + [ANY] * 3,
        out_shape=[both, both, heads, heads, jax.ShapeDtypeStruct((D, 1), F32)]
        + [jax.ShapeDtypeStruct(shape, BF) for shape in ((4, 384, 1792), (384, 1792), (3, 384, 1792))],
        scratch_shapes=[
            pltpu.VMEM((4, D, D), BF),
            pltpu.VMEM((4, D, D), BF),
            pltpu.VMEM((4, D, 256), BF),
            pltpu.VMEM((D + 64, count), BF),
            pltpu.VMEM((D, count), BF),
            pltpu.VMEM((D, count), BF),
            pltpu.VMEM((count, D), BF),
            pltpu.VMEM((count, D), BF),
            pltpu.VMEM((D, count), F32),
            pltpu.VMEM((D, count), F32),
            pltpu.VMEM((D, count), F32),
            pltpu.VMEM((2, 2, D, D), BF),
            pltpu.VMEM((4, D, 256), BF),
            pltpu.SemaphoreType.DMA((4, 16)),
            pltpu.SemaphoreType.DMA((16,)),
            pltpu.SemaphoreType.DMA((13,)),
            pltpu.SemaphoreType.DMA((2, 4)),
            pltpu.SemaphoreType.DMA((4, 2)),
        ],
        compiler_params=pltpu.CompilerParams(vmem_limit_bytes=62 * MIB),
        cost_estimate=cost(50),
    )(sel, gain, *inputs)


def qkv_back_kernel(tab, w, n_t, *refs, half):
    if half:
        dq, dkv, start = refs[:3]
        dq, dkv = [dq[p * 128 : (p + 1) * 128, :] for p in range(3)], [dkv[p] for p in range(3)]
    else:
        first_dq, last_dq, first_dkv, last_dkv, start = refs[:5]
        dq = [first_dq[:128, :], first_dq[128:, :], last_dq[...]]
        dkv = [first_dkv[0], first_dkv[1], last_dkv[0]]
    near, far, inner, gain_out, *grads = refs[-5:] if half else refs[-4:]
    i = pl.program_id(0)
    grad_w = grads[0] if half else None

    @pl.when(i == 0)
    def _():
        gain_out[...] = start[...]
        if half:
            grad_w[...] = jnp.zeros_like(grad_w)

    normed = n_t[...]
    if half:
        for p in range(3):
            grad_w[p, :, 128:] += nn(normed, dkv[p])

    def finish(grad):
        near[...] = grad[:384].astype(BF)
        far[...] = grad[384:].astype(BF)
        product = grad * normed.astype(F32)
        inner[...] = jnp.sum(product, axis=0, keepdims=True)
        gain_out[...] += jnp.sum(product, axis=1, keepdims=True)

    def key_part():
        total = 0.0
        for p in range(3):
            total = total + nt(w[:, p * 384 + 128 : (p + 1) * 384], dkv[p])
        return total

    @pl.when(i < 2)
    def _():
        total = key_part()
        for p in range(3):
            total = total + nn(w[:, p * 384 : p * 384 + 128], dq[p])
            if half:
                grad_w[p, :, :128] += nt(normed, dq[p])
        finish(total)

    @pl.when(i >= 2)
    def _():
        finish(key_part())


def project_back(order, w, n_t, dq, dkv, half, start, *deps):
    whole = lambda shape: pl.BlockSpec(shape, lambda i, t: (0,) * len(shape))

    def cols_of(rows):
        return pl.BlockSpec((rows, B), lambda i, t: (0, t[i]))

    def own(rows):
        return pl.BlockSpec((rows, B), lambda i, t: (0, jnp.minimum(i, 1)))

    low = jax.ShapeDtypeStruct((384, HALF), BF)
    counts = (3,) if half else (2, 1)
    specs = [own(128 * n) for n in counts]
    specs += [pl.BlockSpec((n, B, 256), lambda i, t: (0, t[i], 0)) for n in counts] + [whole((D, 1))]
    return pl.pallas_call(
        functools.partial(qkv_back_kernel, half=half),
        grid_spec=pltpu.PrefetchScalarGridSpec(
            num_scalar_prefetch=1,
            grid=(HALF // B,),
            in_specs=[whole((D, 1152)), cols_of(D)] + specs + [ANY] * len(deps),
            out_specs=[cols_of(384), cols_of(384), cols_of(1), whole((D, 1))] + [whole((3, D, 384))] * half,
        ),
        out_shape=[low, low, jax.ShapeDtypeStruct((1, HALF), F32), jax.ShapeDtypeStruct((D, 1), F32)]
        + [jax.ShapeDtypeStruct((3, D, 384), F32)] * half,
        compiler_params=pltpu.CompilerParams(vmem_limit_bytes=56 * MIB),
        cost_estimate=cost(15 if half else 10),
    )(order, w, n_t, *dq, *dkv, *start, *deps)


def weights_kernel(tab, n_t, dq_t, dkv, start, *refs):
    near, far = refs[-2:]
    kv = start[0, :, 128:] + nn(n_t[...], dkv[0])
    q = start[0, :, :128]
    for i in range(2):
        q = q + nt(n_t[:, pl.ds(pl.multiple_of(tab[i] * B, B), B)], dq_t[:, i * B : (i + 1) * B])
    near[0, :, :128] = q[:384].astype(BF)
    far[0, :, :128] = q[384:].astype(BF)
    near[0, :, 128:] = kv[:384].astype(BF)
    far[0, :, 128:] = kv[384:].astype(BF)


def weights_back(order, n_t, dq_t, dkv, start, pairs, *deps):
    base, count = pairs
    each = lambda shape, base: pl.BlockSpec((1, *shape), lambda i, t: (base + i, 0, 0))
    part = jax.ShapeDtypeStruct((count, 384, 384), BF)
    return pl.pallas_call(
        weights_kernel,
        grid_spec=pltpu.PrefetchScalarGridSpec(
            num_scalar_prefetch=1,
            grid=(count,),
            in_specs=[
                pl.BlockSpec((D, HALF), lambda i, t: (0, 0)),
                pl.BlockSpec((128, 2 * B), lambda i, t: (i, 0)),
                each((HALF, 256), 0),
                each((D, 384), base),
            ]
            + [ANY] * len(deps),
            out_specs=[each((384, 384), 0)] * 2,
        ),
        out_shape=[part, part],
        compiler_params=pltpu.CompilerParams(vmem_limit_bytes=48 * MIB),
        cost_estimate=cost(2 + 2 * count),
    )(order, n_t, dq_t, dkv, start, *deps)


def finish_kernel(sel, *refs):
    here, cross, there = refs[:3]
    near, core_part, pair_part, x, scale, inner, gain = refs[3:10]
    out, grad_x = refs[-2:]
    i = pl.program_id(0)
    pair, device = sel[2 + i], sel[6 + i]
    same, own = pair == sel[0], device == sel[1]
    mine = jnp.where(own, here[...], cross[...])
    theirs = jnp.where(own, there[:, 0], there[:, 1])
    both = jnp.where(same, mine, theirs)
    out[...] = both[0]
    total = near[...].astype(F32) + core_part[...].astype(F32) + pair_part[...].astype(F32)
    r1 = scale[...]
    grad_x[...] = both[1].astype(F32) + r1 * gain[...] * total - x[...].astype(F32) * (r1 * r1 * inner[...] * (1.0 / D))


def finish_half(sel, here, cross, there, near, core_part, pair_part, x, scale, inner, gain, half, old, *deps):
    base = half * (HALF // B)
    piece = pl.BlockSpec((2, FB, B), lambda i, t: (0, 0, half))
    cols = pl.BlockSpec((FB, B), lambda i, t: (0, i))
    into = pl.BlockSpec((FB, B), lambda i, t: (0, base + i))
    row = pl.BlockSpec((1, B), lambda i, t: (0, i))
    return pl.pallas_call(
        finish_kernel,
        grid_spec=pltpu.PrefetchScalarGridSpec(
            num_scalar_prefetch=1,
            grid=(HALF // B,),
            in_specs=[
                piece,
                piece,
                pl.BlockSpec((2, 2, FB, B), lambda i, t: (0, 0, 0, half)),
                cols,
                cols,
                cols,
                into,
                row,
                row,
                pl.BlockSpec((FB, 1), lambda i, t: (0, 0)),
            ]
            + [ANY] * (len(old) + len(deps)),
            out_specs=[into, into],
        ),
        out_shape=[jax.ShapeDtypeStruct((FB, LEN), BF), jax.ShapeDtypeStruct((FB, LEN), F32)],
        input_output_aliases={11 + n: n for n in range(len(old))},
        cost_estimate=cost(6),
    )(sel, here, cross, there, near, core_part, pair_part, x, scale, inner, gain, *old, *deps)


def per_device(
    block_input,
    norm_gain_one,
    w_query,
    w_key,
    w_value,
    w_out,
    norm_gain_two,
    w_up,
    w_down,
    piece_start,
    piece_len,
    grad_y,
):
    c = lax.axis_index("cols")
    r = lax.axis_index("rows")
    y, core = c // 2, c % 2
    parity = lax.axis_index("dp") % 2

    def order_of(table):
        return jnp.array(table, jnp.int32)[c]

    low_order = order_of([[0, 3, 1, 2], [3, 0, 1, 2], [1, 2, 0, 3], [2, 1, 0, 3]])
    high_order = order_of([[0, 1, 2, 3], [1, 0, 2, 3], [2, 3, 0, 1], [3, 2, 0, 1]])
    away = order_of([[3, 5, 1, 6, 2, 7], [0, 4, 2, 7, 1, 6], [2, 7, 0, 4, 3, 5], [1, 6, 3, 5, 0, 4]])

    small = jnp.concatenate(
        [norm_gain_one, norm_gain_two, piece_start[0].astype(F32), piece_len[0].astype(F32)]
    )
    small = jnp.stack([small, cols_swap(small, 2)])
    small = jnp.concatenate([small, cols_swap(small, 1)])
    gain_one = small[:, :FB].reshape(D, 1)
    gain_two = small[:, FB : 2 * FB].reshape(D, 1)
    apart = jnp.bitwise_xor(c, r)
    mine = jnp.where(apart == 0, 0, jnp.where(apart == 2, 1, jnp.where(apart == 1, 2, 3)))
    pieces = lax.dynamic_index_in_dim(small, mine, 0, keepdims=False)[2 * FB :].astype(jnp.int32)
    firsts = pieces[:8] - jnp.arange(8, dtype=jnp.int32) * B
    lasts = firsts + pieces[8:]

    def table(order, half):
        blocks = order[:2] + half * 4
        return jnp.concatenate([blocks, firsts[blocks], lasts[blocks]])

    low_table, high_table = table(low_order, 0), table(high_order, 1)
    low_order = jnp.concatenate([low_order, core[None].astype(jnp.int32)])
    high_order = jnp.concatenate([high_order, core[None].astype(jnp.int32)])

    own_low = block_input[:, :HALF]
    pair_low = cols_swap(own_low, 2)
    w_slots = [
        jnp.concatenate(
            [w[:, :128] for w in (w_query, w_key, w_value)] + [w[:, 128:] for w in (w_query, w_key, w_value)], axis=1
        )
    ]
    w_slots += [rows_shift(w_slots[0], step) for step in (1, 2, 3)]

    def merge(first, second):
        parts = [first[:, :384], second[:, :384]]
        for n in range(3):
            cols = slice(384 + n * HD, 384 + (n + 1) * HD)
            parts += [first[:, cols], second[:, cols]]
        return jnp.concatenate(parts, axis=1)

    w_near = jnp.stack([merge(*w_slots[:2]), merge(*w_slots[2:])])
    cross_low = cols_swap(jnp.stack([own_low, pair_low]), 1)
    x_low = (pair_low, cross_low)
    own_pack = jnp.concatenate([w_up, w_out.T, jnp.zeros((FB, 64), BF), w_down], axis=1)
    ring = [tie(own_pack, w_near)]
    ring.append(rows_shift(ring[0], 1))
    w_pair = tie(cols_swap(w_near, 2), cross_low)
    w_cross = cols_swap(
        jnp.stack([lax.dynamic_index_in_dim(part, 1 - core, 0, keepdims=False) for part in (w_near, w_pair)]), 1
    )

    pair_high = cols_swap(tie(block_input[:, HALF:], w_pair), 2)

    normed_low, scale_low, q_low, *kv, w_qkv = project_half(
        low_order, (block_input, *x_low), gain_one, (w_near, w_pair, w_cross), 0, (), ()
    )
    ring[1] = tie(ring[1], scale_low)
    first_sent = jnp.stack(ring)
    first_sent = jnp.where(parity == 0, first_sent[:, :, :896], first_sent[:, :, 896:])
    outs_low = [attend(low_table, q_low, kv[0], kv[3], 0, (0, 1), first_sent)]
    first_pairs = cols_swap(first_sent, 2)
    ring.append(rows_shift(ring[1], 1))
    pair_high = tie(pair_high, outs_low[0][2])
    cross_sent = jnp.stack([block_input[:, HALF:], pair_high])
    outs_low.append(attend(low_table, q_low, kv[0], kv[3], 0, (1, 2), outs_low[0][2], cross_sent))
    ring[2] = tie(ring[2], outs_low[1][2])
    ring.append(rows_shift(ring[2], 1))
    cross_high = cols_swap(cross_sent, 1)
    x_high = (pair_high, cross_high)
    low_got = cols_swap(jnp.concatenate([out[1] for out in outs_low]), 1)
    dy_core = hold(away[:2], grad_y, B, scale_low)
    dy_away = tie(hold(away[2:], grad_y, B, scale_low), outs_low[1][2])
    normed_high, scale_high, q_high, *kv = project_half(
        high_order, (block_input, *x_high), gain_one, (w_qkv,), 1, tuple(kv), (outs_low[1][2], dy_away, first_pairs)
    )
    k, k_t, v, v_t = kv
    first_crossed = dp_swap(first_pairs)
    dy_pair = cols_swap(dy_away, 2)
    third_pair = cols_swap(ring[2], 2)
    outs_high = [attend(high_table, q_high, k, v_t, 1, (0, 1), low_got)]
    ring[3] = tie(ring[3], outs_high[0][2])
    dy_pair, third_pair = tie(dy_pair, outs_high[0][2]), tie(third_pair, outs_high[0][2])
    dy_cross_sent = jnp.concatenate([dy_core, dy_pair[1:]])
    third_sent = jnp.stack([ring[2], third_pair])
    outs_high.append(
        attend(high_table, q_high, k, v_t, 1, (1, 2), outs_high[0][2], ring[3], dy_cross_sent, third_sent)
    )
    dy_cross = cols_swap(dy_cross_sent, 1)
    third_cross = cols_swap(third_sent, 1)
    first_crossed = tie(first_crossed, outs_high[0][2])
    first_cross = cols_swap(jnp.concatenate([jnp.stack(ring[:2]), first_pairs, first_crossed], axis=2), 1)
    last_pair = cols_swap(ring[3], 2)
    last_pair = tie(last_pair, outs_high[1][2])
    last_cross = cols_swap(jnp.stack([ring[3], last_pair]), 1)
    high_got = cols_swap(jnp.concatenate([out[1] for out in outs_high]), 1)

    sel = jnp.stack([core.astype(jnp.int32), low_order[0], high_order[0], parity.astype(jnp.int32)])
    both_near, both_far, ga_own, ga_other, gain_two_sum, g_near, g_one, g_rest = feed_forward(
        sel,
        gain_two,
        ring,
        (first_pairs, first_crossed, third_pair, last_pair),
        (first_cross, third_cross, last_cross),
        [out[0] for out in outs_low + outs_high] + [low_got, high_got],
        (grad_y, dy_pair, dy_cross),
        (block_input, *x_low, *x_high),
    )

    def three(first, second, third):
        return (first.astype(F32) + second.astype(F32) + third.astype(F32)).astype(BF)

    def two(first, second):
        return (first.astype(F32) + second.astype(F32)).astype(BF)

    ga_got = cols_swap(ga_other, 1)
    total = two(g_near[1], cols_swap(g_one, 1))
    both_cross = cols_swap(both_far, 1)
    there_sent = jnp.stack([both_near[:, FB:], both_cross[:, FB:]], axis=1)
    g_got = cols_swap(g_rest, 1)
    out_low = [jnp.concatenate(parts) for parts in zip(*outs_low)]
    out_high = [jnp.concatenate(parts) for parts in zip(*outs_high)]
    grads = (ga_own, ga_got)
    dq_high, dkv_high, dkv_low = attend_back(
        high_table, q_high, grads, out_high[:2], out_high[2], k, v, k_t, 1, (0, 3), (), total, there_sent
    )
    there = cols_swap(there_sent, 2)
    total = three(tie(rows_shift(total, 1), dq_high), g_near[2], g_got[1])
    near_high, far_high, inner_high, gain_part, w_part = project_back(
        high_order, w_qkv, normed_high, (dq_high,), (dkv_high,), 1, (jnp.zeros((D, 1), F32),), total, there
    )
    low = (low_table, q_low, grads, out_low[:2], out_low[2], k, v, k_t, 0)
    got_high = cols_swap(far_high, 1)
    dq_first, dkv_first = attend_back(*low, (0, 2), (dkv_low,), near_high)
    got_high = tie(got_high, dq_first)
    sent_high = two(near_high[FB:], got_high[FB:])
    total = three(tie(rows_shift(total, 1), dq_first), g_near[3], g_got[2])
    wg_first = weights_back(low_order, normed_low, dq_first, dkv_first, w_part, (0, 2), sent_high, total)
    pair_sent = cols_swap(sent_high, 2)
    dq_last, dkv_last = attend_back(*low, (2, 1), (dkv_low,), wg_first[0])

    def by_core(near, got):
        return jnp.where(core == 0, near, got), jnp.where(core == 0, got, near)

    def half_of(part, which):
        return jnp.concatenate([part[:, n * 128 + which * HD : n * 128 + (which + 1) * HD] for n in range(3)], axis=1)

    got = tie(cols_swap(wg_first[1], 1), dq_last)
    pair_zero, pair_one = by_core(wg_first[0][0], got[0]), by_core(wg_first[0][1], got[1])
    total = three(tie(rows_shift(total, 1), dq_last), g_near[0], g_got[0])
    total_far = total[FB:]
    near_low, far_low, inner_low, gain_part = project_back(
        low_order,
        w_qkv,
        normed_low,
        (dq_first, dq_last),
        (dkv_first, dkv_last),
        0,
        (gain_part,),
        pair_zero[1],
        *pair_one,
        pair_sent,
        total_far,
    )
    firsts = [rows_shift(pair_zero[1], -2), rows_shift(pair_one[0], -1), rows_shift(pair_one[1], -3)]
    feed_got = cols_swap(total_far, 2)
    wg_last = weights_back(low_order, normed_low, dq_last, dkv_last, w_part, (2, 1), near_low, firsts[0])
    got_low = tie(cols_swap(far_low, 1), wg_last[0])
    sent_low = two(near_low[FB:], got_low[FB:])
    got = tie(cols_swap(wg_last[1], 1), sent_low)
    last = by_core(wg_last[0][0], got[0])
    slots = [half_of(last[slot // 2], slot % 2) for slot in range(4)]

    def dp_sum(part, *deps):
        if lax.axis_size("dp") == 2:
            got = dp_swap(part)
            got = tie(got, *deps) if deps else got
            return part.astype(F32) + got.astype(F32)
        return lax.psum(part.astype(F32), "dp")

    feed_sum = two(total[:FB], feed_got)
    pair_got = cols_swap(sent_low, 2)
    gain_one_sum = gain_part / gain_one
    small_near = jnp.concatenate([inner_high[0], inner_low[0], gain_one_sum[:384, 0], gain_two_sum[:384, 0]])
    small_far = jnp.concatenate([inner_high[0], inner_low[0], gain_one_sum[384:, 0], gain_two_sum[384:, 0]])
    small = small_near + cols_swap(small_far, 1)
    inners, gains = small[: 2 * HALF], small[2 * HALF :].reshape(2, 2, FB)
    small = jnp.concatenate([inners, gains[:, 0].reshape(-1)]) + cols_swap(
        jnp.concatenate([inners, gains[:, 1].reshape(-1)]), 2
    )
    inners, gains = small[: 2 * HALF].reshape(2, 1, HALF), small[2 * HALF :]
    where = jnp.stack([y, core]).astype(jnp.int32)
    low_sel = jnp.concatenate([where, jnp.array([0, 1, 1, 0, 0, 0, 1, 1], jnp.int32)])
    high_sel = jnp.concatenate([where, jnp.array([0, 0, 1, 1, 0, 1, 0, 1], jnp.int32)])
    gain_column = norm_gain_one.reshape(FB, 1)
    outputs = finish_half(
        high_sel, both_near, both_cross, there, near_high, got_high, pair_sent, block_input, scale_high,
        inners[0], gain_column, 1, (), sent_low, slots[3],
    )
    output, grad_x = finish_half(
        low_sel, both_near, both_cross, there, near_low, got_low, pair_got, block_input, scale_low,
        inners[1], gain_column, 0, tuple(outputs),
    )

    lasts = [rows_shift(slots[slot], -slot) for slot in (1, 2, 3)]
    lasts[0] = tie(lasts[0], grad_x)

    def total_of(parts):
        return sum(part.astype(F32) for part in parts).astype(BF)

    joined = jnp.concatenate([total_of([pair_zero[0]] + firsts), total_of([slots[0]] + lasts)], axis=1)
    joined_sent = joined
    joined = dp_sum(two(joined[:FB], cols_swap(joined[FB:], 2)))

    feed_total = dp_sum(feed_sum, grad_x)

    def joined_grad(n):
        return jnp.concatenate(
            [joined[:, n * 128 : (n + 1) * 128], joined[:, 384 + n * HD : 384 + (n + 1) * HD]], axis=1
        )

    gains = tie(gains, grad_x)
    slots = jnp.stack([gains] + [rows_shift(gains, step) for step in (1, 2, 3)])
    slots = slots[jnp.mod(r - jnp.arange(4), 4)]
    gains = dp_sum((slots[0] + slots[1]) + (slots[2] + slots[3]))
    return (
        output,
        grad_x,
        gains[:FB],
        joined_grad(0),
        joined_grad(1),
        joined_grad(2),
        feed_total[:, D : D + FB].T,
        gains[FB:],
        feed_total[:, :D],
        feed_total[:, D + 256 :],
    )


def solution(mesh):
    return jax.shard_map(
        per_device,
        mesh=mesh,
        in_specs=(
            P("cols", ("dp", "rows")),
            P("cols"),
            P("cols", "rows"),
            P("cols", "rows"),
            P("cols", "rows"),
            P("rows", "cols"),
            P("cols"),
            P("cols", "rows"),
            P("cols", "rows"),
            P(("dp", "cols"), None),
            P(("dp", "cols"), None),
            P("cols", ("dp", "rows")),
        ),
        out_specs=(
            P("cols", ("dp", "rows")),
            P("cols", ("dp", "rows")),
            P("cols"),
            P("cols", "rows"),
            P("cols", "rows"),
            P("cols", "rows"),
            P("rows", "cols"),
            P("cols"),
            P("cols", "rows"),
            P("cols", "rows"),
        ),
        check_vma=False,
    )
```

time: 615 us -> 475 us (0.77)
  waiting for transfers between devices: 188 us -> 53 us
  Pallas kernels: 206 us -> 243 us
  starting transfers between devices: 30.7 us -> 58 us
  other arithmetic: 73.9 us -> 50.4 us
  local copies, waits for them, and re-layouts: 81.7 us -> 60.9 us
  blocking collectives: 17.3 us -> 0 us
  between operations: 8.78 us -> 2.07 us
    ppermute x12 -> x18, waiting for transfers between devices: 73 us -> 10.5 us  [rows_shift(): lax.ppermute(value, 'rows', [(i, (i + step) % count) for i in range(count)])]
    ppermute x6 -> x4, waiting for transfers between devices: 53.7 us -> 5.43 us  [dp_swap(): lax.ppermute(value, 'dp', [(i, i ^ 1) for i in range(lax.axis_size('dp'))])]
    pallas_call x8 -> x39, Pallas kernels: 161 us -> 191 us  [the longest x3 73.1 us: attend_back(): pl.pallas_call(functools.partial(attend_back_kernel, counts=(4,) if half...]
    ppermute x12 -> x18, starting transfers between devices: 7.63 us -> 35 us  [rows_shift(): lax.ppermute(value, 'rows', [(i, (i + step) % count) for i in range(count)])]
    ppermute x37 -> x33, waiting for transfers between devices: 61 us -> 37.1 us  [cols_swap(): lax.ppermute(value, 'cols', [(i, i ^ distance) for i in range(lax.axis_si...]
    psum x1 -> x0, blocking collectives: 17.3 us -> none  [per_device(): gains = lax.psum(gains, ('dp', 'rows')).reshape(2, 4, FB)]
    unnamed x156 -> x188, local copies, waits for them, and re-layouts: 15.8 us -> 30.8 us
    convert_element_type x9 -> x10, other arithmetic: 7.56 us -> 18.3 us  [the longest x3 7.97 us: three(): (first.astype(F32) + second.astype(F32) + third.astype(F32)).astype(BF)]
  transfers between devices with their start and end apart: 55 -> 55, of which waited for: 23 -> 11; matrix products, arithmetic and copies ran while one was open for 22% -> 16% of each run, Pallas kernels for 26% -> 41%
where the time goes in v2:
time: 475 us; the launch traced here: 467 us
  Pallas kernels  243 us (51%)
  local copies, waits for them, and re-layouts  60.9 us (13%)
  starting transfers between devices  58 us (12%)
  waiting for transfers between devices  53 us (11%)
  other arithmetic  50.4 us (11%)
    pallas_call x3, Pallas kernels, attend_back(): pl.pallas_call(functools.partial(attend_back_kernel, counts=(4,) if half...  73.1 us
    pallas_call x1, Pallas kernels, feed_forward(): pl.pallas_call(feed_kernel, in_specs=[pl.BlockSpec(memory_space=pltpu.SME...  52 us
    pallas_call x4, Pallas kernels, attend(): pl.pallas_call(functools.partial(attend_kernel, counts=(4,) if half else...  41.9 us
    ppermute x33, waiting for transfers between devices, cols_swap(): lax.ppermute(value, 'cols', [(i, i ^ distance) for i in range(lax.axis_si...  37.1 us
    ppermute x18, starting transfers between devices, rows_shift(): lax.ppermute(value, 'rows', [(i, (i + step) % count) for i in range(count)])  35 us
    unnamed x188, local copies, waits for them, and re-layouts  30.8 us
    pallas_call x2, Pallas kernels, project_back(): pl.pallas_call(functools.partial(qkv_back_kernel, half=half), grid_spec=p...  25 us
    pallas_call x2, Pallas kernels, project_half(): pl.pallas_call(functools.partial(qkv_kernel, first=first, extra=extra), g...  23 us
  transfers between devices with their start and end apart: 55, of which 11 were waited for; matrix products, arithmetic and copies ran while one was open for 16% of the time, Pallas kernels for 41%

profile of v2, /device:TPU:24, one launch (start us, length us, event | category | flops | bytes accessed | tf_op | source)
XLA Modules:
  0.0 466.9 jit_solution(7737929770592838575)
XLA Ops:
  6.2 3.6 collective-permute-start.2
  12.8 3.0 slice_bitcast_fusion.9
  20.0 5.0 %collective-permute-done.2 = bf16[192,576]{1,0:T(8,128)(2,1)S(1)} collective-permute-done((bf16[192,576]{1,0:T(8,128)(2,1)S(1)}, bf16[192,576]{1,0:T(8,128)(2,1)S(1)}, u32[]{:S(2)}, u32[]{:S(2)}) %collective-permute-start.2) | collective-permute-done | bytes 221216 | tf_op jit(solution)/shard_map/ppermute | solution.py:50
  25.4 8.7 %collective-permute-done.6.refs_1_.refs_21_ = bf16[192,2048]{1,0:T(8,128)(2,1)S(1)} collective-permute-done((bf16[192,2048]{1,0:T(8,128)(2,1)}, bf16[192,2048]{1,0:T(8,128)(2,1)S(1)}, u32[]{:S(2)}, u32[]{:S(2)}) %collective-permute-start.6) | collective-permute-done | bytes 786464 | tf_op jit(solution)/shard_map/ppermute | solution.py:45
  41.0 17.2 %collective-permute-done.8.refs_0_ = bf16[2,192,1152]{2,1,0:T(8,128)(2,1)S(1)} collective-permute-done((bf16[2,192,1152]{2,1,0:T(8,128)(2,1)S(1)}, bf16[2,192,1152]{2,1,0:T(8,128)(2,1)S(1)}, u32[]{:S(2)}, u32[]{:S(2)}) %collective-permute-start.8) | collective-permute-done | bytes 884768 | tf_op jit(solution)/shard_map/ppermute | solution.py:45
  68.9 11.6 %shard_map.242 = (bf16[768,2048]{1,0:T(8,128)(2,1)}, f32[1,2048]{1,0:T(1,128)S(1)}, bf16[384,1024]{1,0:T(8,128)(2,1)S(1)}, bf16[4096,384]{1,0:T(8,128)(2,1)}, bf...) custom-call(s32[5]{0:T(128)S(1)} %pad_add_fusion.3.tab, ...), custom_call_target="tpu_custom_call" | custom-call | flops 13799999488 | tf_op jit(solution)/shard_map/pallas_call | solution.py:159
  83.2 2.6 collective-permute-start.10
  87.8 1.9 copy-done.45
  89.7 6.5 %shard_map.244 = (bf16[128,512]{1,0:T(8,128)(2,1)S(1)}, bf16[128,512]{1,0:T(8,128)(2,1)S(1)}, f32[1,2,1024]{2,1,0:T(2,128)S(1)}) custom-call(s32[6]{0:T(128)S(1)} %pad_add_fusion.4.tab, bf16[384,1024]{1,0:T(8,128)(2,1)S(1)} %copy-done.49, bf16[4096,384]{1,0:T(8,128)(2,1)S(1)} %copy-done.45, bf16[384,4096]{1,0:T(8,128)(2,1)} %get-tuple-element.72.v_t.refs_8_, ...), custom_call_target="tpu_custom_call" | custom-call | flops 6899999744 | tf_op jit(solution)/shard_map/pallas_call | solution.py:263
  98.4 2.8 pad_maximum_fusion.2.refs_1_
  101.9 11.6 %shard_map.247 = (bf16[256,512]{1,0:T(8,128)(2,1)S(1)}, bf16[256,512]{1,0:T(8,128)(2,1)S(1)}, f32[2,2,1024]{2,1,0:T(2,128)S(1)}) custom-call(s32[6]{0:T(128)S(1)} %pad_add_fusion.4.tab, bf16[384,1024]{1,0:T(8,128)(2,1)S(1)} %copy-done.49, bf16[4096,384]{1,0:T(8,128)(2,1)S(1)} %copy-done.46, bf16[384,4096]{1,0:T(8,128)(2,1)} %get-tuple-element.72.v_t.refs_8_, ...), custom_call_target="tpu_custom_call" | custom-call | flops 13799999488 | tf_op jit(solution)/shard_map/pallas_call | solution.py:263
  115.4 4.0 shard_map.249.refs_0_
  120.9 2.4 shard_map.256
  128.0 11.4 %shard_map.251 = (bf16[768,2048]{1,0:T(8,128)(2,1)}, f32[1,2048]{1,0:T(1,128)S(1)}, bf16[384,1024]{1,0:T(8,128)(2,1)S(1)}, bf16[4096,384]{1,0:T(8,128)(2,1)}, bf...) custom-call(s32[5]{0:T(128)S(1)} %pad_add_fusion.6.tab, ...), custom_call_target="tpu_custom_call", output_to_operand_aliasing={{3}: (6, {}), {4}: (7, {}), {5}: (8, {}), {6}: (9, {})} | custom-call | flops 13799999488 | tf_op jit(solution)/shard_map/pallas_call | solution.py:159
  139.4 2.2 copy-done.47
  141.6 8.5 %shard_map.252 = (bf16[128,512]{1,0:T(8,128)(2,1)S(1)}, bf16[128,512]{1,0:T(8,128)(2,1)S(1)}, f32[1,2,1024]{2,1,0:T(2,128)S(1)}) custom-call(s32[6]{0:T(128)S(1)} %pad_add_fusion.5.tab, bf16[384,1024]{1,0:T(8,128)(2,1)S(1)} %get-tuple-element.78.q_t, bf16[4096,384]{1,0:T(8,128)(2,1)S(1)} %copy-done.47, bf16[384,4096]{1,0:T(8,128)(2,1)} %get-tuple-element.80.v_t, ...), custom_call_target="tpu_custom_call" | custom-call | flops 9200000000 | tf_op jit(solution)/shard_map/pallas_call | solution.py:263
  153.8 1.8 slice.439
  155.6 2.9 pad_maximum_fusion
  161.7 15.2 %shard_map.258 = (bf16[256,512]{1,0:T(8,128)(2,1)S(1)}, bf16[256,512]{1,0:T(8,128)(2,1)S(1)}, f32[2,2,1024]{2,1,0:T(2,128)S(1)}) custom-call(s32[6]{0:T(128)S(1)} %pad_add_fusion.5.tab, bf16[384,1024]{1,0:T(8,128)(2,1)S(1)} %copy-done.51, bf16[4096,384]{1,0:T(8,128)(2,1)} %get-tuple-element.79.k, bf16[384,4096]{1,0:T(8,128)(2,1)} %get-tuple-element.80.v_t, ...), custom_call_target="tpu_custom_call" | custom-call | flops 18400000000 | tf_op jit(solution)/shard_map/pallas_call | solution.py:263
  177.6 2.4 pad_maximum_fusion.5
  185.3 52.0 %shard_map.260 = (bf16[2,384,1024]{2,1,0:T(8,128)(2,1)}, bf16[2,384,1024]{2,1,0:T(8,128)(2,1)}, bf16[384,1024]{1,0:T(8,128)(2,1)}, bf16[384,1024]{1,0:T(8,128)(2...) custom-call(s32[4]{0:T(128)} %pad_add_fusion.2.sel, ...), custom_call_target="tpu_custom_call" | custom-call | flops 57500000256 | tf_op jit(solution)/shard_map/pallas_call | solution.py:583
  241.8 1.8 slice_reduce_fusion.3
  249.9 40.8 %shard_map.261 = (bf16[384,1024]{1,0:T(8,128)(2,1)}, bf16[3,2048,256]{2,1,0:T(8,128)(2,1)}, f32[3,2048,256]{2,1,0:T(8,128)}) custom-call(s32[6]{0:T(128)} %copy-done.38, bf16[384,1024]{1,0:T(8,128)(2,1)} %copy-done.50, bf16[384,1024]{1,0:T(8,128)(2,1)} %get-tuple-element.94.do_own, bf16[384,1024]{1,0:T(8,128)(2,1)} %copy-done.89, ...), custom_call_target="tpu_custom_call" | custom-call | flops 55199997952 | tf_op jit(solution)/shard_map/pallas_call | solution.py:343
  291.8 2.7 fusion.2.refs_3_
  296.3 15.0 %shard_map.263 = (bf16[384,2048]{1,0:T(8,128)(2,1)}, bf16[384,2048]{1,0:T(8,128)(2,1)}, f32[1,2048]{1,0:T(1,128)}, f32[768,1]{1,0:T(8,128)}, f32[3,768,384]{2,1,0:T(8,128)}) custom-call(s32[5]{0:T(128)} %copy-done.42, bf16[768,1152]{1,0:T(8,128)(2,1)} %get-tuple-element.75.refs_4_.w, bf16[768,2048]{1,0:T(8,128)(2,1)} %get-tuple-element.101.n_t, ...), custom_call_target="tpu_custom_call" | custom-call | flops 17250000896 | tf_op jit(solution)/shard_map/pallas_call | solution.py:677
  311.4 19.9 %shard_map.264 = (bf16[256,1024]{1,0:T(8,128)(2,1)}, bf16[2,2048,256]{2,1,0:T(8,128)(2,1)}) custom-call(s32[6]{0:T(128)} %copy-done.37, bf16[384,1024]{1,0:T(8,128)(2,1)} %copy-done.48, bf16[384,1024]{1,0:T(8,128)(2,1)} %get-tuple-element.94.do_own, bf16[384,1024]{1,0:T(8,128)(2,1)} %copy-done.89, bf16[384,512]{1,0:T(8,128)(2,1)} %copy-done.73, ...), custom_call_target="tpu_custom_call" | custom-call | flops 27599998976 | tf_op jit(solution)/shard_map/pallas_call | solution.py:343
  332.4 2.7 fusion.1.refs_1_
  335.1 2.5 collective-permute-start.35
  337.6 2.6 add_convert_fusion.1.refs_0_
  343.3 5.6 %shard_map.267 = (bf16[2,384,384]{2,1,0:T(8,128)(2,1)S(1)}, bf16[2,384,384]{2,1,0:T(8,128)(2,1)S(1)}) custom-call(s32[5]{0:T(128)S(1)} %copy-done.40, bf16[768,2048]{1,0:T(8,128)(2,1)} %get-tuple-element.93.n_t, bf16[256,1024]{1,0:T(8,128)(2,1)S(1)} %copy-done.8, bf16[2,2048,256]{2,1,0:T(8,128)(2,1)S(1)} %copy-done.44, ...), custom_call_target="tpu_custom_call" | custom-call | flops 6899999744 | tf_op jit(solution)/shard_map/pallas_call | solution.py:708
  349.7 12.4 %shard_map.268 = (bf16[128,1024]{1,0:T(8,128)(2,1)}, bf16[1,2048,256]{2,1,0:T(8,128)(2,1)}) custom-call(s32[6]{0:T(128)} %copy-done.37, bf16[384,1024]{1,0:T(8,128)(2,1)} %copy-done.48, bf16[384,1024]{1,0:T(8,128)(2,1)} %get-tuple-element.94.do_own, bf16[384,1024]{1,0:T(8,128)(2,1)} %copy-done.89, bf16[384,512]{1,0:T(8,128)(2,1)} %copy-done.73, ...), custom_call_target="tpu_custom_call" | custom-call | flops 13799999488 | tf_op jit(solution)/shard_map/pallas_call | solution.py:343
  363.5 2.0 select_bitcast_fusion.2
  365.4 1.9 collective-permute-start.47
  368.2 2.7 fusion
  372.9 10.1 %shard_map.271 = (bf16[384,2048]{1,0:T(8,128)(2,1)}, bf16[384,2048]{1,0:T(8,128)(2,1)}, f32[1,2048]{1,0:T(1,128)}, f32[768,1]{1,0:T(8,128)}) custom-call(s32[5]{0:T(128)} %copy-done.39, bf16[768,1152]{1,0:T(8,128)(2,1)} %get-tuple-element.75.refs_4_.w, bf16[768,2048]{1,0:T(8,128)(2,1)} %get-tuple-element.93.n_t, ...), custom_call_target="tpu_custom_call" | custom-call | flops 11500000256 | tf_op jit(solution)/shard_map/pallas_call | solution.py:677
  384.6 3.5 collective-permute-done.46
  393.0 4.2 shard_map.272
  398.1 9.1 %collective-permute-done.40 = f32[4480]{0:T(1024)S(1)} collective-permute-done((f32[4480]{0:T(1024)S(1)}, f32[4480]{0:T(1024)S(1)}, u32[]{:S(2)}, u32[]{:S(2)}) %collective-permute-start.40) | collective-permute-done | bytes 17952 | tf_op jit(solution)/shard_map/ppermute | solution.py:45
  408.5 2.1 add_convert_fusion.2
  415.6 3.6 collective-permute-start.50
  419.4 5.6 %collective-permute-start.49 = (bf16[384,192]{1,0:T(8,128)(2,1)S(1)}, bf16[384,192]{1,0:T(8,128)(2,1)S(1)}, u32[]{:S(2)}, u32[]{:S(2)}) collective-permute-start(bf16[384,192]{1,0:T(8,128)(2,1)S(1)} %pad_maximum_fusion.14), channel_id=1, source_target_pairs={{0,8},{4,12},{8,0},{12,4},{1,9},{5,13},{9,1},{13,5},{2,10},{6,14},... | collective-permute-start | bytes 442376 | tf_op jit(solution)/shard_map/ppermute | solution.py:50
  425.3 2.1 collective-permute-start.48
  427.3 5.7 %shard_map.275 = (bf16[192,4096]{1,0:T(8,128)(2,1)}, f32[192,4096]{1,0:T(8,128)}) custom-call(s32[10]{0:T(128)} %pad_add_fusion.7.sel, bf16[2,384,1024]{2,1,0:T(8,128)(2,1)} %get-tuple-element.91.refs_0_, bf16[2,384,1024]{2,1,0:T(8,128)(2,1)} %copy-done.66, bf16[2,2,192,1024]{3,2,1,0:T(8,128)(2,1)} %collective-permute-done.26.refs_4_.refs_2_, ...), custom_call_target="tpu_custom_call" | custom-call | flops 6899999744 | tf_op jit(solution)/shard_map/pallas_call | solution.py:750
  433.1 5.7 %shard_map.276 = (bf16[192,4096]{1,0:T(8,128)(2,1)}, f32[192,4096]{1,0:T(8,128)}) custom-call(s32[10]{0:T(128)} %pad_add_fusion.sel, bf16[2,384,1024]{2,1,0:T(8,128)(2,1)} %get-tuple-element.91.refs_0_, bf16[2,384,1024]{2,1,0:T(8,128)(2,1)} %copy-done.66, ...), custom_call_target="tpu_custom_call", output_to_operand_aliasing={{0}: (11, {}), {1}: (12, {})} | custom-call | flops 6899999744 | tf_op jit(solution)/shard_map/pallas_call | solution.py:750
  438.7 5.1 %collective-permute-start.44 = (f32[384]{0:T(512)}, f32[384]{0:T(512)S(1)}, u32[]{:S(2)}, u32[]{:S(2)}) collective-permute-start(f32[384]{0:T(512)} %shard_map.277), channel_id=1, source_target_pairs={{0,12},{4,0},{8,4},{12,8},{1,13},{5,1},{9,5},{13,9},{2,14},{6,2},{... | collective-permute-start | bytes 4616 | tf_op jit(solution)/shard_map/ppermute | solution.py:50
  443.9 2.0 collective-permute-start.43
  446.0 2.9 collective-permute-start.42
  460.4 4.1 collective-permute-done.52
  (415 shorter events, 109.2 us)
Async XLA Ops:
  5.6 19.8 %collective-permute-start.3 = (bf16[192,576]{1,0:T(8,128)(2,1)S(1)}, bf16[192,576]{1,0:T(8,128)(2,1)S(1)}, u32[]{:S(2)}, u32[]{:S(2)}) collective-permute-start(bf16[192,576]{1,0:T(8,128)(2,1)S(1)} %concatenate.107), channel_id=1, source_target_pairs={{0,8},{4,12},{8,0},{12,4},{1,9},{5,13},{9,1},{13,5},{2,10},{6,14},... | collective-permute-start | bytes 663560 | tf_op jit(solution)/shard_map/ppermute | solution.py:50
  6.0 19.4 %collective-permute-start.4 = (bf16[192,576]{1,0:T(8,128)(2,1)S(1)}, bf16[192,576]{1,0:T(8,128)(2,1)S(1)}, u32[]{:S(2)}, u32[]{:S(2)}) collective-permute-start(bf16[192,576]{1,0:T(8,128)(2,1)S(1)} %concatenate.107), channel_id=1, source_target_pairs={{0,12},{4,0},{8,4},{12,8},{1,13},{5,1},{9,5},{13,9},{2,14},{6,2},{... | collective-permute-start | bytes 663560 | tf_op jit(solution)/shard_map/ppermute | solution.py:50
  6.2 18.9 %collective-permute-start.2 = (bf16[192,576]{1,0:T(8,128)(2,1)S(1)}, bf16[192,576]{1,0:T(8,128)(2,1)S(1)}, u32[]{:S(2)}, u32[]{:S(2)}) collective-permute-start(bf16[192,576]{1,0:T(8,128)(2,1)S(1)} %concatenate.107), channel_id=1, source_target_pairs={{0,4},{4,8},{8,12},{12,0},{1,5},{5,9},{9,13},{13,1},{2,6},{6,10},{... | collective-permute-start | bytes 663560 | tf_op jit(solution)/shard_map/ppermute | solution.py:50
  11.2 29.3 %collective-permute-start = (f32[400]{0:T(512)S(1)}, f32[400]{0:T(512)S(1)}, u32[]{:S(2)}, u32[]{:S(2)}) collective-permute-start(f32[400]{0:T(512)S(1)} %pad_maximum_fusion.26), channel_id=1, source_target_pairs={{0,2},{1,3},{2,0},{3,1},{4,6},{5,7},{6,4},{7,5},{8,10},{9,11},{10,... | collective-permute-start | bytes 4808 | tf_op jit(solution)/shard_map/ppermute | solution.py:45
  15.7 18.4 %collective-permute-start.6 = (bf16[192,2048]{1,0:T(8,128)(2,1)}, bf16[192,2048]{1,0:T(8,128)(2,1)S(1)}, u32[]{:S(2)}, u32[]{:S(2)}) collective-permute-start(bf16[192,2048]{1,0:T(8,128)(2,1)} %get-tuple-element.157), channel_id=1, source_target_pairs={{0,2},{1,3},{2,0},{3,1},{4,6},{5,7},{6,4},{7,5},{8,10},{9,11},{10,... | collective-permute-start | bytes 2359304 | tf_op jit(solution)/shard_map/ppermute | solution.py:45
  35.5 22.7 %collective-permute-start.7 = (bf16[2,192,2048]{2,1,0:T(8,128)(2,1)}, bf16[2,192,2048]{2,1,0:T(8,128)(2,1)}, u32[]{:S(2)}, u32[]{:S(2)}) collective-permute-start(bf16[2,192,2048]{2,1,0:T(8,128)(2,1)} %pad_maximum_fusion.1), channel_id=1, source_target_pairs={{0,1},{1,0},{2,3},{3,2},{4,5},{5,4},{6,7},{7,6},{8,9},{9,8},{10,11... | collective-permute-start | bytes 4718600 | tf_op jit(solution)/shard_map/ppermute | solution.py:45
  36.1 22.1 %collective-permute-start.8 = (bf16[2,192,1152]{2,1,0:T(8,128)(2,1)S(1)}, bf16[2,192,1152]{2,1,0:T(8,128)(2,1)S(1)}, u32[]{:S(2)}, u32[]{:S(2)}) collective-permute-start(bf16[2,192,1152]{2,1,0:T(8,128)(2,1)S(1)} %pad_maximum_fusion.6.refs_1_.refs_4_), channel_id=1, source_target_pairs={{0,2},{1,3},{2,0},{3,1},{4,6},{5,7},{6,4},{7,5},{8,10},{9,11},{10,... | collective-permute-start | bytes 2654216 | tf_op jit(solution)/shard_map/ppermute | solution.py:45
  40.5 20.7 %collective-permute-start.1 = (f32[2,400]{1,0:T(2,128)S(1)}, f32[2,400]{1,0:T(2,128)S(1)}, u32[]{:S(2)}, u32[]{:S(2)}) collective-permute-start(f32[2,400]{1,0:T(2,128)S(1)} %pad_maximum_fusion.25), channel_id=1, source_target_pairs={{0,1},{1,0},{2,3},{3,2},{4,5},{5,4},{6,7},{7,6},{8,9},{9,8},{10,11... | collective-permute-start | bytes 9608 | tf_op jit(solution)/shard_map/ppermute | solution.py:45
  65.0 18.2 %collective-permute-start.5 = (bf16[192,1792]{1,0:T(8,128)(2,1)}, bf16[192,1792]{1,0:T(8,128)(2,1)}, u32[]{:S(2)}, u32[]{:S(2)}) collective-permute-start(bf16[192,1792]{1,0:T(8,128)(2,1)} %shard_map.240.refs_0_), channel_id=1, source_target_pairs={{0,4},{4,8},{8,12},{12,0},{1,5},{5,9},{9,13},{13,1},{2,6},{6,10},{... | collective-permute-start | bytes 2064392 | tf_op jit(solution)/shard_map/ppermute | solution.py:50
  65.7 31.8 %collective-permute-start.11 = (bf16[192,2048]{1,0:T(8,128)(2,1)}, bf16[192,2048]{1,0:T(8,128)(2,1)S(1)}, u32[]{:S(2)}, u32[]{:S(2)}) collective-permute-start(bf16[192,2048]{1,0:T(8,128)(2,1)} %shard_map.245), channel_id=1, source_target_pairs={{0,2},{1,3},{2,0},{3,1},{4,6},{5,7},{6,4},{7,5},{8,10},{9,11},{10,... | collective-permute-start | bytes 2359304 | tf_op jit(solution)/shard_map/ppermute | solution.py:45
  83.2 40.2 %collective-permute-start.10 = (bf16[192,1792]{1,0:T(8,128)(2,1)}, bf16[192,1792]{1,0:T(8,128)(2,1)}, u32[]{:S(2)}, u32[]{:S(2)}) collective-permute-start(bf16[192,1792]{1,0:T(8,128)(2,1)} %shard_map.243.refs_1_), channel_id=1, source_target_pairs={{0,4},{4,8},{8,12},{12,0},{1,5},{5,9},{9,13},{13,1},{2,6},{6,10},{... | collective-permute-start | bytes 2064392 | tf_op jit(solution)/shard_map/ppermute | solution.py:50
  87.2 36.2 %collective-permute-start.14 = (bf16[2,192,896]{2,1,0:T(8,128)(2,1)S(1)}, bf16[2,192,896]{2,1,0:T(8,128)(2,1)}, u32[]{:S(2)}, u32[]{:S(2)}) collective-permute-start(bf16[2,192,896]{2,1,0:T(8,128)(2,1)S(1)} %fusion.5.refs_0_), channel_id=1, source_target_pairs={{0,2},{1,3},{2,0},{3,1},{4,6},{5,7},{6,4},{7,5},{8,10},{9,11},{10,... | collective-permute-start | bytes 2064392 | tf_op jit(solution)/shard_map/ppermute | solution.py:45
  101.2 22.7 %collective-permute-start.13 = (bf16[2,192,2048]{2,1,0:T(8,128)(2,1)}, bf16[2,192,2048]{2,1,0:T(8,128)(2,1)}, u32[]{:S(2)}, u32[]{:S(2)}) collective-permute-start(bf16[2,192,2048]{2,1,0:T(8,128)(2,1)} %pad_maximum_fusion.2.refs_1_), channel_id=1, source_target_pairs={{0,1},{1,0},{2,3},{3,2},{4,5},{5,4},{6,7},{7,6},{8,9},{9,8},{10,11... | collective-permute-start | bytes 4718600 | tf_op jit(solution)/shard_map/ppermute | solution.py:45
  114.9 24.4 %collective-permute-start.15 = (bf16[384,512]{1,0:T(8,128)(2,1)}, bf16[384,512]{1,0:T(8,128)(2,1)}, u32[]{:S(2)}, u32[]{:S(2)}) collective-permute-start(bf16[384,512]{1,0:T(8,128)(2,1)} %constant_dynamic-update-slice_fusion.o_other), channel_id=1, source_target_pairs={{0,1},{1,0},{2,3},{3,2},{4,5},{5,4},{6,7},{7,6},{8,9},{9,8},{10,11... | collective-permute-start | bytes 1179656 | tf_op jit(solution)/shard_map/ppermute | solution.py:45
  119.4 34.4 %collective-permute-start.19 = (bf16[2,192,1024]{2,1,0:T(8,128)(2,1)}, bf16[2,192,1024]{2,1,0:T(8,128)(2,1)}, u32[]{:S(2)}, u32[]{:S(2)}) collective-permute-start(bf16[2,192,1024]{2,1,0:T(8,128)(2,1)} %shard_map.250.refs_10_), channel_id=1, source_target_pairs={{0,2},{1,3},{2,0},{3,1},{4,6},{5,7},{6,4},{7,5},{8,10},{9,11},{10,... | collective-permute-start | bytes 2359304 | tf_op jit(solution)/shard_map/ppermute | solution.py:45
  123.4 28.0 %collective-permute-start.12 = (bf16[192,1792]{1,0:T(8,128)(2,1)}, bf16[192,1792]{1,0:T(8,128)(2,1)S(1)}, u32[]{:S(2)}, u32[]{:S(2)}) collective-permute-start(bf16[192,1792]{1,0:T(8,128)(2,1)} %shard_map.248.refs_2_), channel_id=1, source_target_pairs={{0,4},{4,8},{8,12},{12,0},{1,5},{5,9},{9,13},{13,1},{2,6},{6,10},{... | collective-permute-start | bytes 2064392 | tf_op jit(solution)/shard_map/ppermute | solution.py:50
  123.4 35.1 %collective-permute-start.17 = (bf16[192,1792]{1,0:T(8,128)(2,1)}, bf16[192,1792]{1,0:T(8,128)(2,1)}, u32[]{:S(2)}, u32[]{:S(2)}) collective-permute-start(bf16[192,1792]{1,0:T(8,128)(2,1)} %shard_map.248.refs_2_), channel_id=1, source_target_pairs={{0,2},{1,3},{2,0},{3,1},{4,6},{5,7},{6,4},{7,5},{8,10},{9,11},{10,... | collective-permute-start | bytes 2064392 | tf_op jit(solution)/shard_map/ppermute | solution.py:45
  123.9 31.7 %collective-permute-start.16 = (bf16[2,192,896]{2,1,0:T(8,128)(2,1)}, bf16[2,192,896]{2,1,0:T(8,128)(2,1)}, u32[]{:S(2)}, u32[]{:S(2)}) collective-permute-start(bf16[2,192,896]{2,1,0:T(8,128)(2,1)} %collective-permute-done.14.refs_11_.refs_4_), channel_id=1, source_target_pairs={{0,16},{16,0},{1,17},{17,1},{2,18},{18,2},{3,19},{19,3},{4,20},{20... | collective-permute-start | bytes 2064392 | tf_op jit(solution)/shard_map/ppermute | solution.py:54
  152.3 25.3 %collective-permute-start.18 = (bf16[192,1792]{1,0:T(8,128)(2,1)}, bf16[192,1792]{1,0:T(8,128)(2,1)}, u32[]{:S(2)}, u32[]{:S(2)}) collective-permute-start(bf16[192,1792]{1,0:T(8,128)(2,1)} %shard_map.253.refs_1_.refs_3_), channel_id=1, source_target_pairs={{0,2},{1,3},{2,0},{3,1},{4,6},{5,7},{6,4},{7,5},{8,10},{9,11},{10,... | collective-permute-start | bytes 2064392 | tf_op jit(solution)/shard_map/ppermute | solution.py:45
  158.5 26.7 %collective-permute-start.20 = (bf16[2,192,3584]{2,1,0:T(8,128)(2,1)}, bf16[2,192,3584]{2,1,0:T(8,128)(2,1)}, u32[]{:S(2)}, u32[]{:S(2)}) collective-permute-start(bf16[2,192,3584]{2,1,0:T(8,128)(2,1)} %pad_maximum_fusion), channel_id=1, source_target_pairs={{0,1},{1,0},{2,3},{3,2},{4,5},{5,4},{6,7},{7,6},{8,9},{9,8},{10,11... | collective-permute-start | bytes 8257544 | tf_op jit(solution)/shard_map/ppermute | solution.py:45
  160.2 25.0 %collective-permute-start.21 = (bf16[2,192,1792]{2,1,0:T(8,128)(2,1)S(1)}, bf16[2,192,1792]{2,1,0:T(8,128)(2,1)}, u32[]{:S(2)}, u32[]{:S(2)}) collective-permute-start(bf16[2,192,1792]{2,1,0:T(8,128)(2,1)S(1)} %pad_maximum_fusion.4.refs_3_), channel_id=1, source_target_pairs={{0,1},{1,0},{2,3},{3,2},{4,5},{5,4},{6,7},{7,6},{8,9},{9,8},{10,11... | collective-permute-start | bytes 4128776 | tf_op jit(solution)/shard_map/ppermute | solution.py:45
  237.3 6.4 %collective-permute-start.28 = (bf16[384,1792]{1,0:T(8,128)(2,1)}, bf16[384,1792]{1,0:T(8,128)(2,1)S(1)}, u32[]{:S(2)}, u32[]{:S(2)}) collective-permute-start(bf16[384,1792]{1,0:T(8,128)(2,1)} %get-tuple-element.99), channel_id=1, source_target_pairs={{0,1},{1,0},{2,3},{3,2},{4,5},{5,4},{6,7},{7,6},{8,9},{9,8},{10,11... | collective-permute-start | bytes 4128776 | tf_op jit(solution)/shard_map/ppermute | solution.py:45
  239.4 6.5 %collective-permute-start.25 = (bf16[2,384,1024]{2,1,0:T(8,128)(2,1)}, bf16[2,384,1024]{2,1,0:T(8,128)(2,1)S(1)}, u32[]{:S(2)}, u32[]{:S(2)}) collective-permute-start(bf16[2,384,1024]{2,1,0:T(8,128)(2,1)} %get-tuple-element.92), channel_id=1, source_target_pairs={{0,1},{1,0},{2,3},{3,2},{4,5},{5,4},{6,7},{7,6},{8,9},{9,8},{10,11... | collective-permute-start | bytes 4718600 | tf_op jit(solution)/shard_map/ppermute | solution.py:45
  241.3 7.7 %collective-permute-start.27 = (bf16[384,1024]{1,0:T(8,128)(2,1)}, bf16[384,1024]{1,0:T(8,128)(2,1)S(1)}, u32[]{:S(2)}, u32[]{:S(2)}) collective-permute-start(bf16[384,1024]{1,0:T(8,128)(2,1)} %get-tuple-element.95), channel_id=1, source_target_pairs={{0,1},{1,0},{2,3},{3,2},{4,5},{5,4},{6,7},{7,6},{8,9},{9,8},{10,11... | collective-permute-start | bytes 2359304 | tf_op jit(solution)/shard_map/ppermute | solution.py:45
  241.5 50.4 %collective-permute-start.30 = (bf16[3,384,1792]{2,1,0:T(8,128)(2,1)}, bf16[3,384,1792]{2,1,0:T(8,128)(2,1)}, u32[]{:S(2)}, u32[]{:S(2)}) collective-permute-start(bf16[3,384,1792]{2,1,0:T(8,128)(2,1)} %get-tuple-element.104), channel_id=1, source_target_pairs={{0,1},{1,0},{2,3},{3,2},{4,5},{5,4},{6,7},{7,6},{8,9},{9,8},{10,11... | collective-permute-start | bytes 12386312 | tf_op jit(solution)/shard_map/ppermute | solution.py:45
  245.4 45.3 %collective-permute-start.29 = (bf16[384,1792]{1,0:T(8,128)(2,1)S(1)}, bf16[384,1792]{1,0:T(8,128)(2,1)S(1)}, u32[]{:S(2)}, u32[]{:S(2)}) collective-permute-start(bf16[384,1792]{1,0:T(8,128)(2,1)S(1)} %fusion.3.refs_0_), channel_id=1, source_target_pairs={{0,4},{4,8},{8,12},{12,0},{1,5},{5,9},{9,13},{13,1},{2,6},{6,10},{... | collective-permute-start | bytes 4128776 | tf_op jit(solution)/shard_map/ppermute | solution.py:50
  247.5 48.0 %collective-permute-start.26 = (bf16[2,2,192,1024]{3,2,1,0:T(8,128)(2,1)}, bf16[2,2,192,1024]{3,2,1,0:T(8,128)(2,1)}, u32[]{:S(2)}, u32[]{:S(2)}) collective-permute-start(bf16[2,2,192,1024]{3,2,1,0:T(8,128)(2,1)} %pad_maximum_fusion.3.refs_1_), channel_id=1, source_target_pairs={{0,2},{1,3},{2,0},{3,1},{4,6},{5,7},{6,4},{7,5},{8,10},{9,11},{10,... | collective-permute-start | bytes 4718600 | tf_op jit(solution)/shard_map/ppermute | solution.py:45
  294.5 36.8 %collective-permute-start.32 = (bf16[384,1792]{1,0:T(8,128)(2,1)S(1)}, bf16[384,1792]{1,0:T(8,128)(2,1)S(1)}, u32[]{:S(2)}, u32[]{:S(2)}) collective-permute-start(bf16[384,1792]{1,0:T(8,128)(2,1)S(1)} %fusion.2.refs_3_), channel_id=1, source_target_pairs={{0,4},{4,8},{8,12},{12,0},{1,5},{5,9},{9,13},{13,1},{2,6},{6,10},{... | collective-permute-start | bytes 4128776 | tf_op jit(solution)/shard_map/ppermute | solution.py:50
  311.3 26.3 %collective-permute-start.31 = (bf16[384,2048]{1,0:T(8,128)(2,1)}, bf16[384,2048]{1,0:T(8,128)(2,1)}, u32[]{:S(2)}, u32[]{:S(2)}) collective-permute-start(bf16[384,2048]{1,0:T(8,128)(2,1)} %get-tuple-element.109), channel_id=1, source_target_pairs={{0,1},{1,0},{2,3},{3,2},{4,5},{5,4},{6,7},{7,6},{8,9},{9,8},{10,11... | collective-permute-start | bytes 4718600 | tf_op jit(solution)/shard_map/ppermute | solution.py:45
  335.1 33.1 %collective-permute-start.35 = (bf16[384,1792]{1,0:T(8,128)(2,1)S(1)}, bf16[384,1792]{1,0:T(8,128)(2,1)}, u32[]{:S(2)}, u32[]{:S(2)}) collective-permute-start(bf16[384,1792]{1,0:T(8,128)(2,1)S(1)} %fusion.1.refs_1_), channel_id=1, source_target_pairs={{0,4},{4,8},{8,12},{12,0},{1,5},{5,9},{9,13},{13,1},{2,6},{6,10},{... | collective-permute-start | bytes 4128776 | tf_op jit(solution)/shard_map/ppermute | solution.py:50
  340.2 32.7 %collective-permute-start.34 = (bf16[192,2048]{1,0:T(8,128)(2,1)}, bf16[192,2048]{1,0:T(8,128)(2,1)}, u32[]{:S(2)}, u32[]{:S(2)}) collective-permute-start(bf16[192,2048]{1,0:T(8,128)(2,1)} %add_convert_fusion.1.refs_0_), channel_id=1, source_target_pairs={{0,2},{1,3},{2,0},{3,1},{4,6},{5,7},{6,4},{7,5},{8,10},{9,11},{10,... | collective-permute-start | bytes 2359304 | tf_op jit(solution)/shard_map/ppermute | solution.py:45
  349.7 12.5 %collective-permute-start.33 = (bf16[2,384,384]{2,1,0:T(8,128)(2,1)S(1)}, bf16[2,384,384]{2,1,0:T(8,128)(2,1)S(1)}, u32[]{:S(2)}, u32[]{:S(2)}) collective-permute-start(bf16[2,384,384]{2,1,0:T(8,128)(2,1)S(1)} %get-tuple-element.114), channel_id=1, source_target_pairs={{0,1},{1,0},{2,3},{3,2},{4,5},{5,4},{6,7},{7,6},{8,9},{9,8},{10,11... | collective-permute-start | bytes 1769480 | tf_op jit(solution)/shard_map/ppermute | solution.py:45
  365.4 19.2 %collective-permute-start.37 = (bf16[384,384]{1,0:T(8,128)(2,1)}, bf16[384,384]{1,0:T(8,128)(2,1)S(1)}, u32[]{:S(2)}, u32[]{:S(2)}) collective-permute-start(bf16[384,384]{1,0:T(8,128)(2,1)} %get-tuple-element.162.refs_5_), channel_id=1, source_target_pairs={{0,8},{4,12},{8,0},{12,4},{1,9},{5,13},{9,1},{13,5},{2,10},{6,14},... | collective-permute-start | bytes 884744 | tf_op jit(solution)/shard_map/ppermute | solution.py:50
  365.4 19.2 %collective-permute-start.47 = (bf16[384,384]{1,0:T(8,128)(2,1)}, bf16[384,384]{1,0:T(8,128)(2,1)}, u32[]{:S(2)}, u32[]{:S(2)}) collective-permute-start(bf16[384,384]{1,0:T(8,128)(2,1)} %get-tuple-element.160.refs_7_), channel_id=1, source_target_pairs={{0,4},{4,8},{8,12},{12,0},{1,5},{5,9},{9,13},{13,1},{2,6},{6,10},{... | collective-permute-start | bytes 884744 | tf_op jit(solution)/shard_map/ppermute | solution.py:50
  367.4 20.8 %collective-permute-start.46 = (bf16[384,384]{1,0:T(8,128)(2,1)S(1)}, bf16[384,384]{1,0:T(8,128)(2,1)}, u32[]{:S(2)}, u32[]{:S(2)}) collective-permute-start(bf16[384,384]{1,0:T(8,128)(2,1)S(1)} %get-tuple-element.161.refs_6_), channel_id=1, source_target_pairs={{0,12},{4,0},{8,4},{12,8},{1,13},{5,1},{9,5},{13,9},{2,14},{6,2},{... | collective-permute-start | bytes 884744 | tf_op jit(solution)/shard_map/ppermute | solution.py:50
  389.4 19.1 %collective-permute-start.53 = (bf16[192,1792]{1,0:T(8,128)(2,1)}, bf16[192,1792]{1,0:T(8,128)(2,1)S(1)}, u32[]{:S(2)}, u32[]{:S(2)}) collective-permute-start(bf16[192,1792]{1,0:T(8,128)(2,1)} %slice.447.refs_9_), channel_id=1, source_target_pairs={{0,2},{1,3},{2,0},{3,1},{4,6},{5,7},{6,4},{7,5},{8,10},{9,11},{10,... | collective-permute-start | bytes 2064392 | tf_op jit(solution)/shard_map/ppermute | solution.py:45
  390.6 20.6 %collective-permute-start.36 = (bf16[384,2048]{1,0:T(8,128)(2,1)}, bf16[384,2048]{1,0:T(8,128)(2,1)}, u32[]{:S(2)}, u32[]{:S(2)}) collective-permute-start(bf16[384,2048]{1,0:T(8,128)(2,1)} %get-tuple-element.116), channel_id=1, source_target_pairs={{0,1},{1,0},{2,3},{3,2},{4,5},{5,4},{6,7},{7,6},{8,9},{9,8},{10,11... | collective-permute-start | bytes 4718600 | tf_op jit(solution)/shard_map/ppermute | solution.py:45
  390.8 16.5 %collective-permute-start.40 = (f32[4480]{0:T(1024)S(1)}, f32[4480]{0:T(1024)S(1)}, u32[]{:S(2)}, u32[]{:S(2)}) collective-permute-start(f32[4480]{0:T(1024)S(1)} %pad_maximum_fusion.19), channel_id=1, source_target_pairs={{0,2},{1,3},{2,0},{3,1},{4,6},{5,7},{6,4},{7,5},{8,10},{9,11},{10,... | collective-permute-start | bytes 53768 | tf_op jit(solution)/shard_map/ppermute | solution.py:45
  397.8 15.7 %collective-permute-start.41 = (bf16[1,384,384]{2,1,0:T(8,128)(2,1)S(1)}, bf16[1,384,384]{2,1,0:T(8,128)(2,1)S(1)}, u32[]{:S(2)}, u32[]{:S(2)}) collective-permute-start(bf16[1,384,384]{2,1,0:T(8,128)(2,1)S(1)} %get-tuple-element.123), channel_id=1, source_target_pairs={{0,1},{1,0},{2,3},{3,2},{4,5},{5,4},{6,7},{7,6},{8,9},{9,8},{10,11... | collective-permute-start | bytes 884744 | tf_op jit(solution)/shard_map/ppermute | solution.py:45
  410.6 40.5 %collective-permute-start.54 = (bf16[192,1792]{1,0:T(8,128)(2,1)}, bf16[192,1792]{1,0:T(8,128)(2,1)}, u32[]{:S(2)}, u32[]{:S(2)}) collective-permute-start(bf16[192,1792]{1,0:T(8,128)(2,1)} %add_convert_fusion.2), channel_id=1, source_target_pairs={{0,16},{16,0},{1,17},{17,1},{2,18},{18,2},{3,19},{19,3},{4,20},{20... | collective-permute-start | bytes 2064392 | tf_op jit(solution)/shard_map/ppermute | solution.py:54
  412.6 20.5 %collective-permute-start.38 = (bf16[192,2048]{1,0:T(8,128)(2,1)S(1)}, bf16[192,2048]{1,0:T(8,128)(2,1)}, u32[]{:S(2)}, u32[]{:S(2)}) collective-permute-start(bf16[192,2048]{1,0:T(8,128)(2,1)S(1)} %add_convert_fusion.refs_1_.refs_10_), channel_id=1, source_target_pairs={{0,2},{1,3},{2,0},{3,1},{4,6},{5,7},{6,4},{7,5},{8,10},{9,11},{10,... | collective-permute-start | bytes 2359304 | tf_op jit(solution)/shard_map/ppermute | solution.py:45
  415.6 30.3 %collective-permute-start.50 = (bf16[384,192]{1,0:T(8,128)(2,1)S(1)}, bf16[384,192]{1,0:T(8,128)(2,1)S(1)}, u32[]{:S(2)}, u32[]{:S(2)}) collective-permute-start(bf16[384,192]{1,0:T(8,128)(2,1)S(1)} %pad_maximum_fusion.12.refs_11_), channel_id=1, source_target_pairs={{0,4},{4,8},{8,12},{12,0},{1,5},{5,9},{9,13},{13,1},{2,6},{6,10},{... | collective-permute-start | bytes 442376 | tf_op jit(solution)/shard_map/ppermute | solution.py:50
  419.4 29.4 %collective-permute-start.49 = (bf16[384,192]{1,0:T(8,128)(2,1)S(1)}, bf16[384,192]{1,0:T(8,128)(2,1)S(1)}, u32[]{:S(2)}, u32[]{:S(2)}) collective-permute-start(bf16[384,192]{1,0:T(8,128)(2,1)S(1)} %pad_maximum_fusion.14), channel_id=1, source_target_pairs={{0,8},{4,12},{8,0},{12,4},{1,9},{5,13},{9,1},{13,5},{2,10},{6,14},... | collective-permute-start | bytes 442376 | tf_op jit(solution)/shard_map/ppermute | solution.py:50
  425.3 18.6 %collective-permute-start.48 = (bf16[384,192]{1,0:T(8,128)(2,1)S(1)}, bf16[384,192]{1,0:T(8,128)(2,1)S(1)}, u32[]{:S(2)}, u32[]{:S(2)}) collective-permute-start(bf16[384,192]{1,0:T(8,128)(2,1)S(1)} %pad_maximum_fusion.13), channel_id=1, source_target_pairs={{0,12},{4,0},{8,4},{12,8},{1,13},{5,1},{9,5},{13,9},{2,14},{6,2},{... | collective-permute-start | bytes 442376 | tf_op jit(solution)/shard_map/ppermute | solution.py:50
  438.7 14.9 %collective-permute-start.44 = (f32[384]{0:T(512)}, f32[384]{0:T(512)S(1)}, u32[]{:S(2)}, u32[]{:S(2)}) collective-permute-start(f32[384]{0:T(512)} %shard_map.277), channel_id=1, source_target_pairs={{0,12},{4,0},{8,4},{12,8},{1,13},{5,1},{9,5},{13,9},{2,14},{6,2},{... | collective-permute-start | bytes 4616 | tf_op jit(solution)/shard_map/ppermute | solution.py:50
  443.9 9.8 %collective-permute-start.43 = (f32[384]{0:T(512)}, f32[384]{0:T(512)S(1)}, u32[]{:S(2)}, u32[]{:S(2)}) collective-permute-start(f32[384]{0:T(512)} %shard_map.277), channel_id=1, source_target_pairs={{0,8},{4,12},{8,0},{12,4},{1,9},{5,13},{9,1},{13,5},{2,10},{6,14},... | collective-permute-start | bytes 4616 | tf_op jit(solution)/shard_map/ppermute | solution.py:50
  446.0 7.7 %collective-permute-start.42 = (f32[384]{0:T(512)S(1)}, f32[384]{0:T(512)S(1)}, u32[]{:S(2)}, u32[]{:S(2)}) collective-permute-start(f32[384]{0:T(512)S(1)} %copy-done.76), channel_id=1, source_target_pairs={{0,4},{4,8},{8,12},{12,0},{1,5},{5,9},{9,13},{13,1},{2,6},{6,10},{... | collective-permute-start | bytes 4616 | tf_op jit(solution)/shard_map/ppermute | solution.py:50
  450.0 8.1 %collective-permute-start.51 = (bf16[192,576]{1,0:T(8,128)(2,1)S(1)}, bf16[192,576]{1,0:T(8,128)(2,1)S(1)}, u32[]{:S(2)}, u32[]{:S(2)}) collective-permute-start(bf16[192,576]{1,0:T(8,128)(2,1)S(1)} %pad_maximum_fusion.11), channel_id=1, source_target_pairs={{0,2},{1,3},{2,0},{3,1},{4,6},{5,7},{6,4},{7,5},{8,10},{9,11},{10,... | collective-permute-start | bytes 663560 | tf_op jit(solution)/shard_map/ppermute | solution.py:45
  (98 other events, 993.9 us)

commit v3 on v2

--- a/solution.py
+++ b/solution.py
@@ -92,6 +92,44 @@
     )(first, second, *deps)
 
 
+def pack_kernel(q, k, v, out):
+    for n, w in enumerate((q, k, v)):
+        out[:, n * 128 : (n + 1) * 128] = w[:, :128]
+        out[:, 384 + n * HD : 384 + (n + 1) * HD] = w[:, 128:]
+
+
+def pack(*weights):
+    vmem = pl.BlockSpec(memory_space=pltpu.VMEM)
+    return pl.pallas_call(
+        pack_kernel,
+        in_specs=[vmem] * 3,
+        out_specs=vmem,
+        out_shape=jax.ShapeDtypeStruct((FB, 576), BF),
+        cost_estimate=cost(1),
+    )(*weights)
+
+
+def pick_kernel(tab, first, second, out):
+    out[0] = first[0]
+    out[1] = second[0]
+
+
+def pick(index, first, second):
+    part = pl.BlockSpec((1, *first.shape[1:]), lambda i, t: (t[0], 0, 0))
+    shape = (2, *first.shape[1:])
+    return pl.pallas_call(
+        pick_kernel,
+        grid_spec=pltpu.PrefetchScalarGridSpec(
+            num_scalar_prefetch=1,
+            grid=(1,),
+            in_specs=[part, part],
+            out_specs=pl.BlockSpec(shape, lambda i, t: (0, 0, 0)),
+        ),
+        out_shape=jax.ShapeDtypeStruct(shape, first.dtype),
+        cost_estimate=cost(1),
+    )(index[None].astype(jnp.int32), first, second)
+
+
 def tie(value, *deps):
     return pl.pallas_call(
         lambda *refs: None,
@@ -104,21 +142,21 @@
 
 
 def qkv_kernel(tab, *refs, first, extra):
-    x0, x1, x23, gain = refs[:4]
-    normed, scale, q_t, k, k_t, v, v_t = refs[4 + extra : 11 + extra]
+    x0, x1, x2, x3, gain = refs[:5]
+    normed, scale, q_t, k, k_t, v, v_t = refs[5 + extra : 12 + extra]
     i = pl.program_id(0)
     if first:
-        w = refs[11 + extra]
+        w = refs[12 + extra]
 
         @pl.when(i == 0)
         def _():
-            w[0:FB, :] = refs[4][0]
-            w[FB : 2 * FB, :] = refs[5][0]
-            w[2 * FB : 3 * FB, :] = refs[6][0]
-            w[3 * FB :, :] = refs[6][1]
+            w[0:FB, :] = refs[5][0]
+            w[FB : 2 * FB, :] = refs[6][0]
+            w[2 * FB : 3 * FB, :] = refs[7][0]
+            w[3 * FB :, :] = refs[7][1]
     else:
-        w = refs[4]
-    x = jnp.concatenate([x0[...], x1[...], x23[0], x23[1]], axis=0).astype(F32)
+        w = refs[5]
+    x = jnp.concatenate([x0[...], x1[...], x2[...], x3[...]], axis=0).astype(F32)
     r1 = lax.rsqrt(jnp.sum(x * x, axis=0, keepdims=True) * (1.0 / D) + EPSILON)
     n_t = (x * r1 * gain[...]).astype(BF)
     normed[...] = n_t
@@ -161,7 +199,7 @@
         grid_spec=pltpu.PrefetchScalarGridSpec(
             num_scalar_prefetch=1,
             grid=(HALF // B,),
-            in_specs=[cols_of(FB, base), cols_of(FB), pl.BlockSpec((2, FB, B), lambda i, t: (0, 0, t[i])), whole((D, 1))]
+            in_specs=[cols_of(FB, base)] + [cols_of(FB)] * 3 + [whole((D, 1))]
             + w_specs
             + [ANY] * (len(old) + len(deps)),
             out_specs=[
@@ -182,8 +220,8 @@
         ]
         + kv
         + [jax.ShapeDtypeStruct((D, 1152), BF)] * first,
-        input_output_aliases={5 + len(w_specs) + n: 3 + n for n in range(len(old))},
-        compiler_params=pltpu.CompilerParams(vmem_limit_bytes=48 * MIB),
+        input_output_aliases={6 + len(w_specs) + n: 3 + n for n in range(len(old))},
+        compiler_params=pltpu.CompilerParams(vmem_limit_bytes=62 * MIB),
         cost_estimate=cost(12),
     )(order, *x, gain, *weights, *old, *deps)
 
@@ -227,7 +265,8 @@
 def attend_kernel(tab, q_t, k, v_t, *refs, counts):
     o_own, o_other, log_total = refs[-3:]
     i = pl.program_id(1)
-    block, first, last = tab[i], tab[2 + i], tab[4 + i]
+    block = tab[i]
+    first, last = tab[2 + block], tab[10 + block]
 
     def body(count):
         masks = block_masks(first, last)
@@ -255,11 +294,11 @@
     for_counts(block, counts, body)
 
 
-def attend(tab, q_t, k, v_t, half, pairs, *deps):
+def attend(tab, q_t, k, v_t, half, pairs, old, *deps):
     base, count = pairs
     span = LEN if half else HALF
-    one = pl.BlockSpec((128, B), lambda p, i, t: (p, 0))
-    block = jax.ShapeDtypeStruct((count * 128, B), BF)
+    one = pl.BlockSpec((128, B), lambda p, i, t: (base + p, 0))
+    block = jax.ShapeDtypeStruct((384, B), BF)
     return pl.pallas_call(
         functools.partial(attend_kernel, counts=(4,) if half else (1, 2, 3, 4)),
         grid_spec=pltpu.PrefetchScalarGridSpec(
@@ -270,13 +309,14 @@
                 pl.BlockSpec((span, 128), lambda p, i, t: (0, base + p)),
                 pl.BlockSpec((128, span), lambda p, i, t: (base + p, 0)),
             ]
-            + [ANY] * len(deps),
+            + [ANY] * (len(old) + len(deps)),
             out_specs=[one, one, pl.BlockSpec((1, 2, B), lambda p, i, t: (p, 0, i))],
         ),
         out_shape=[block, block, jax.ShapeDtypeStruct((count, 2, 2 * B), F32)],
-        compiler_params=pltpu.CompilerParams(vmem_limit_bytes=48 * MIB),
+        input_output_aliases={4 + n: n for n in range(len(old))},
+        compiler_params=pltpu.CompilerParams(vmem_limit_bytes=62 * MIB),
         cost_estimate=cost((8 if half else 6) * count),
-    )(tab, q_t, k, v_t, *deps)
+    )(tab, q_t, k, v_t, *old, *deps)
 
 
 def attend_back_kernel(tab, q_t, do_own, do_other, o_own, o_other, log_total, k, v, k_t, *refs, counts, half):
@@ -286,7 +326,8 @@
         start = refs[0]
         dq_t, low, dkv = refs[-3:]
     i = pl.program_id(1)
-    block, first, last = tab[i], tab[2 + i], tab[4 + i]
+    block = tab[i]
+    first, last = tab[2 + block], tab[10 + block]
 
     @pl.when(i == 0)
     def _():
@@ -356,7 +397,7 @@
             jax.ShapeDtypeStruct((count, HALF, 256), BF),
         ]
         + [jax.ShapeDtypeStruct((count, HALF, 256), F32)] * half,
-        compiler_params=pltpu.CompilerParams(vmem_limit_bytes=56 * MIB),
+        compiler_params=pltpu.CompilerParams(vmem_limit_bytes=62 * MIB),
         cost_estimate=cost((16 if half else 12) * count),
     )(tab, q_t, *grads, *outs, log_total, k, v, k_t, *start, *deps)
 
@@ -375,10 +416,11 @@
 
 def feed_kernel(sel, gain, *refs):
     nears, pairs, crosses = refs[:4], refs[4:8], refs[8:11]
-    a_parts, dy_parts, x_parts = refs[11:17], refs[17:20], refs[20:25]
-    outs = refs[-26:]
-    both_near, both_far, ga_own, ga_other, gain_sum = outs[:5]
-    g_near, g_one, g_rest = outs[5:8]
+    a_parts, dy_parts, x_parts = refs[11:15], refs[15:18], refs[18:25]
+    outs = refs[-28:]
+    boths, (ga_own, ga_other, gain_sum) = outs[:4], outs[4:7]
+    g_near, g_one, g_rest = outs[7:10]
+    outs = outs[2:]
     w_up, w_down, w_out, a_t, dy_t, x_t, n, dy, mid, mlp, gn, stage, stage_out = outs[8:21]
     w_sems, a_sems, in_sems, out_sems, last_sems = outs[21:26]
     core, parity = sel[0], sel[3]
@@ -394,18 +436,22 @@
     halves = (((0, 768, 0, 0), (768, 896, 1, 0)), ((0, 128, 1, 128), (128, 896, 2, 0)))
     targets = (w_up, w_out, w_down)
 
-    def loads(slot, swapped):
+    def loads(slot, swapped, kinds):
+        count = 0
         copies = []
 
         def add(source, offset, which_half, rel):
+            nonlocal count
             for first, last, which, at in halves[which_half]:
-                copies.append(
-                    pltpu.make_async_copy(
-                        source.at[:, offset + first : offset + last],
-                        targets[which].at[slot, rel * FB : (rel + 1) * FB, at : at + last - first],
-                        w_sems.at[slot, len(copies)],
+                if which in kinds:
+                    copies.append(
+                        pltpu.make_async_copy(
+                            source.at[:, offset + first : offset + last],
+                            targets[which].at[slot, rel * FB : (rel + 1) * FB, at : at + last - first],
+                            w_sems.at[slot, count],
+                        )
                     )
-                )
+                count += 1
 
         for half in range(2):
             add(nears[slot], half * 896, half, 0)
@@ -425,15 +471,10 @@
             cols = slice(half * B, (half + 1) * B)
             for side in range(2):
                 for source, target, size in HEAD_ROWS:
-                    if side == 1:
-                        part, at = a_parts[4 + half], source
-                    elif source < 128:
-                        part, at = a_parts[2 * half], source
-                    else:
-                        part, at = a_parts[2 * half + 1], source - 128
+                    part = a_parts[2 * side + half]
                     copies.append(
                         pltpu.make_async_copy(
-                            part.at[at : at + size, :],
+                            part.at[source : source + size, :],
                             a_t.at[side * 384 + target : side * 384 + target + size, cols],
                             a_sems.at[len(copies)],
                         )
@@ -452,10 +493,8 @@
             at_whole = pl.ds(pl.multiple_of((sel[1 + half] + 4 * half) * B, B), B)
             add(dy_parts[0].at[:, at_whole], dy_t.at[0:FB, cols])
             add(x_parts[0].at[:, at_whole], x_t.at[0:FB, cols])
-            pair, cross = x_parts[1 + 2 * half : 3 + 2 * half]
-            add(pair.at[:, place], x_t.at[FB : 2 * FB, cols])
-            add(cross.at[0, :, place], x_t.at[2 * FB : 3 * FB, cols])
-            add(cross.at[1, :, place], x_t.at[3 * FB :, cols])
+            for rel in range(1, 4):
+                add(x_parts[half * 3 + rel].at[:, place], x_t.at[rel * FB : (rel + 1) * FB, cols])
         add(dy_parts[1].at[0], dy_t.at[FB : 2 * FB, :])
         add(dy_parts[2].at[0], dy_t.at[2 * FB : 3 * FB, :])
         add(dy_parts[2].at[1], dy_t.at[3 * FB :, :])
@@ -487,17 +526,18 @@
         ]
 
     start(a_loads())
+
+    def start_weights(kinds):
+        for swapped in range(2):
+
+            @pl.when(parity == swapped)
+            def _():
+                for slot in range(4):
+                    start(loads(slot, swapped, kinds))
+
+    start_weights((1,))
     start(token_loads())
-
-    @pl.when(parity == 0)
-    def _():
-        for slot in range(4):
-            start(loads(slot, 0))
-
-    @pl.when(parity == 1)
-    def _():
-        for slot in range(4):
-            start(loads(slot, 1))
+    start_weights((0, 2))
 
     a_t[D:, :] = jnp.zeros((64, a_t.shape[1]), BF)
 
@@ -509,7 +549,7 @@
     dy[...] = dy_t[...].T
     wait(a_loads())
     for slot in range(4):
-        wait(loads(slot, 0))
+        wait(loads(slot, 0, (1,)))
     mixed = nn(w_out[0], a_t[a_rows(0, 256), :])
     for slot in range(1, 4):
         mixed = mixed + nn(w_out[slot], a_t[a_rows(slot, 256), :])
@@ -529,6 +569,12 @@
             def _():
                 wait(stores(before))
 
+        for now in range(4):
+
+            @pl.when(slot == now)
+            def _():
+                wait(loads(now, 0, (0, 2)))
+
         up = nn(n[...], w_up[slot])
         act, slope = feed_chunk(up)
         stage[buffer, 1] = nn(dy_t[...], act).astype(BF)
@@ -545,15 +591,15 @@
         return carry
 
     lax.fori_loop(0, 4, chunk, 0)
-    both_near[0] = mlp[:384].astype(BF)
-    both_far[0] = mlp[384:].astype(BF)
+    for rel, both in enumerate(boths):
+        both[0] = mlp[rel * FB : (rel + 1) * FB].astype(BF)
     weighted = gn[...] * gain[...]
     inner = jnp.sum(mid[...] * weighted, axis=0, keepdims=True)
     cubed = r2 * r2 * r2 * inner * (1.0 / D)
     gm = (dy_t[...].astype(F32) + r2 * weighted - mid[...] * cubed).astype(BF)
     x_t[...] = gm
-    both_near[1] = gm[:384]
-    both_far[1] = gm[384:]
+    for rel, both in enumerate(boths):
+        both[1] = gm[rel * FB : (rel + 1) * FB]
     gain_sum[...] = jnp.sum(gn[...] * mid[...] * r2, axis=1, keepdims=True)
     for slot in range(4):
         grad_a = contract(w_out[slot], x_t[...], ((0,), (0,)))[:FB].astype(BF)
@@ -577,14 +623,14 @@
 def feed_forward(sel, gain, nears, pairs, crosses, a_parts, dy_parts, x_parts, *deps):
     count = 2 * B
     vmem = pl.BlockSpec(memory_space=pltpu.VMEM)
-    both = jax.ShapeDtypeStruct((2, 384, count), BF)
+    both = jax.ShapeDtypeStruct((2, FB, count), BF)
     heads = jax.ShapeDtypeStruct((384, count), BF)
     inputs = (*nears, *pairs, *crosses, *a_parts, *dy_parts, *x_parts, *deps)
     return pl.pallas_call(
         feed_kernel,
         in_specs=[pl.BlockSpec(memory_space=pltpu.SMEM), vmem] + [ANY] * len(inputs),
-        out_specs=[vmem] * 5 + [ANY] * 3,
-        out_shape=[both, both, heads, heads, jax.ShapeDtypeStruct((D, 1), F32)]
+        out_specs=[vmem] * 7 + [ANY] * 3,
+        out_shape=[both, both, both, both, heads, heads, jax.ShapeDtypeStruct((D, 1), F32)]
         + [jax.ShapeDtypeStruct(shape, BF) for shape in ((4, 384, 1792), (384, 1792), (3, 384, 1792))],
         scratch_shapes=[
             pltpu.VMEM((4, D, D), BF),
@@ -612,14 +658,9 @@
 
 
 def qkv_back_kernel(tab, w, n_t, *refs, half):
-    if half:
-        dq, dkv, start = refs[:3]
-        dq, dkv = [dq[p * 128 : (p + 1) * 128, :] for p in range(3)], [dkv[p] for p in range(3)]
-    else:
-        first_dq, last_dq, first_dkv, last_dkv, start = refs[:5]
-        dq = [first_dq[:128, :], first_dq[128:, :], last_dq[...]]
-        dkv = [first_dkv[0], first_dkv[1], last_dkv[0]]
-    near, far, inner, gain_out, *grads = refs[-5:] if half else refs[-4:]
+    dq, dkv, start = refs[:3]
+    dq, dkv = [dq[p * 128 : (p + 1) * 128, :] for p in range(3)], [dkv[p] for p in range(3)]
+    near, far, gain_out, *grads = refs[-4:] if half else refs[-3:]
     i = pl.program_id(0)
     grad_w = grads[0] if half else None
 
@@ -635,10 +676,12 @@
             grad_w[p, :, 128:] += nn(normed, dkv[p])
 
     def finish(grad):
-        near[...] = grad[:384].astype(BF)
-        far[...] = grad[384:].astype(BF)
+        near[:384, :] = grad[:384].astype(BF)
+        far[:384, :] = grad[384:].astype(BF)
         product = grad * normed.astype(F32)
-        inner[...] = jnp.sum(product, axis=0, keepdims=True)
+        inner = jnp.broadcast_to(jnp.sum(product, axis=0, keepdims=True), (16, B)).astype(BF)
+        near[384:, :] = inner
+        far[384:, :] = inner
         gain_out[...] += jnp.sum(product, axis=1, keepdims=True)
 
     def key_part():
@@ -670,23 +713,21 @@
     def own(rows):
         return pl.BlockSpec((rows, B), lambda i, t: (0, jnp.minimum(i, 1)))
 
-    low = jax.ShapeDtypeStruct((384, HALF), BF)
-    counts = (3,) if half else (2, 1)
-    specs = [own(128 * n) for n in counts]
-    specs += [pl.BlockSpec((n, B, 256), lambda i, t: (0, t[i], 0)) for n in counts] + [whole((D, 1))]
+    low = jax.ShapeDtypeStruct((400, HALF), BF)
+    specs = [own(384), pl.BlockSpec((3, B, 256), lambda i, t: (0, t[i], 0)), whole((D, 1))]
     return pl.pallas_call(
         functools.partial(qkv_back_kernel, half=half),
         grid_spec=pltpu.PrefetchScalarGridSpec(
             num_scalar_prefetch=1,
             grid=(HALF // B,),
             in_specs=[whole((D, 1152)), cols_of(D)] + specs + [ANY] * len(deps),
-            out_specs=[cols_of(384), cols_of(384), cols_of(1), whole((D, 1))] + [whole((3, D, 384))] * half,
+            out_specs=[cols_of(400), cols_of(400), whole((D, 1))] + [whole((3, D, 384))] * half,
         ),
-        out_shape=[low, low, jax.ShapeDtypeStruct((1, HALF), F32), jax.ShapeDtypeStruct((D, 1), F32)]
+        out_shape=[low, low, jax.ShapeDtypeStruct((D, 1), F32)]
         + [jax.ShapeDtypeStruct((3, D, 384), F32)] * half,
-        compiler_params=pltpu.CompilerParams(vmem_limit_bytes=56 * MIB),
+        compiler_params=pltpu.CompilerParams(vmem_limit_bytes=62 * MIB),
         cost_estimate=cost(15 if half else 10),
-    )(order, w, n_t, *dq, *dkv, *start, *deps)
+    )(order, w, n_t, dq, dkv, start, *deps)
 
 
 def weights_kernel(tab, n_t, dq_t, dkv, start, *refs):
@@ -720,33 +761,35 @@
             out_specs=[each((384, 384), 0)] * 2,
         ),
         out_shape=[part, part],
-        compiler_params=pltpu.CompilerParams(vmem_limit_bytes=48 * MIB),
+        compiler_params=pltpu.CompilerParams(vmem_limit_bytes=62 * MIB),
         cost_estimate=cost(2 + 2 * count),
     )(order, n_t, dq_t, dkv, start, *deps)
 
 
 def finish_kernel(sel, *refs):
-    here, cross, there = refs[:3]
-    near, core_part, pair_part, x, scale, inner, gain = refs[3:10]
+    here, cross, there, there_cross = refs[:4]
+    near, core_part, pair_part, near_inner, core_inner, pair_inner, x, scale, gain = refs[4:13]
     out, grad_x = refs[-2:]
     i = pl.program_id(0)
     pair, device = sel[2 + i], sel[6 + i]
     same, own = pair == sel[0], device == sel[1]
     mine = jnp.where(own, here[...], cross[...])
-    theirs = jnp.where(own, there[:, 0], there[:, 1])
+    theirs = jnp.where(own, there[...], there_cross[...])
     both = jnp.where(same, mine, theirs)
     out[...] = both[0]
     total = near[...].astype(F32) + core_part[...].astype(F32) + pair_part[...].astype(F32)
+    inner = near_inner[:1].astype(F32) + core_inner[:1].astype(F32) + pair_inner[:1].astype(F32)
     r1 = scale[...]
-    grad_x[...] = both[1].astype(F32) + r1 * gain[...] * total - x[...].astype(F32) * (r1 * r1 * inner[...] * (1.0 / D))
-
-
-def finish_half(sel, here, cross, there, near, core_part, pair_part, x, scale, inner, gain, half, old, *deps):
+    grad_x[...] = both[1].astype(F32) + r1 * gain[...] * total - x[...].astype(F32) * (r1 * r1 * inner * (1.0 / D))
+
+
+def finish_half(sel, here, cross, there, there_cross, near, core_part, pair_part, x, scale, gain, half, old, *deps):
     base = half * (HALF // B)
     piece = pl.BlockSpec((2, FB, B), lambda i, t: (0, 0, half))
     cols = pl.BlockSpec((FB, B), lambda i, t: (0, i))
     into = pl.BlockSpec((FB, B), lambda i, t: (0, base + i))
     row = pl.BlockSpec((1, B), lambda i, t: (0, i))
+    inner = lambda first: pl.BlockSpec((16, B), lambda i, t: (first // 16, i))
     return pl.pallas_call(
         finish_kernel,
         grid_spec=pltpu.PrefetchScalarGridSpec(
@@ -755,12 +798,15 @@
             in_specs=[
                 piece,
                 piece,
-                pl.BlockSpec((2, 2, FB, B), lambda i, t: (0, 0, 0, half)),
+                piece,
+                piece,
                 cols,
                 cols,
                 cols,
+                inner(384),
+                inner(384),
+                inner(FB),
                 into,
-                row,
                 row,
                 pl.BlockSpec((FB, 1), lambda i, t: (0, 0)),
             ]
@@ -768,9 +814,9 @@
             out_specs=[into, into],
         ),
         out_shape=[jax.ShapeDtypeStruct((FB, LEN), BF), jax.ShapeDtypeStruct((FB, LEN), F32)],
-        input_output_aliases={11 + n: n for n in range(len(old))},
+        input_output_aliases={14 + n: n for n in range(len(old))},
         cost_estimate=cost(6),
-    )(sel, here, cross, there, near, core_part, pair_part, x, scale, inner, gain, *old, *deps)
+    )(sel, here, cross, there, there_cross, near, core_part, pair_part, near, core_part, pair_part, x, scale, gain, *old, *deps)
 
 
 def per_device(
@@ -814,19 +860,14 @@
 
     def table(order, half):
         blocks = order[:2] + half * 4
-        return jnp.concatenate([blocks, firsts[blocks], lasts[blocks]])
+        return jnp.concatenate([blocks, firsts, lasts])
 
     low_table, high_table = table(low_order, 0), table(high_order, 1)
     low_order = jnp.concatenate([low_order, core[None].astype(jnp.int32)])
     high_order = jnp.concatenate([high_order, core[None].astype(jnp.int32)])
 
-    own_low = block_input[:, :HALF]
-    pair_low = cols_swap(own_low, 2)
-    w_slots = [
-        jnp.concatenate(
-            [w[:, :128] for w in (w_query, w_key, w_value)] + [w[:, 128:] for w in (w_query, w_key, w_value)], axis=1
-        )
-    ]
+    own_low, own_high = block_input[:, :HALF], block_input[:, HALF:]
+    w_slots = [pack(w_query, w_key, w_value)]
     w_slots += [rows_shift(w_slots[0], step) for step in (1, 2, 3)]
 
     def merge(first, second):
@@ -837,69 +878,66 @@
         return jnp.concatenate(parts, axis=1)
 
     w_near = jnp.stack([merge(*w_slots[:2]), merge(*w_slots[2:])])
-    cross_low = cols_swap(jnp.stack([own_low, pair_low]), 1)
-    x_low = (pair_low, cross_low)
+    pair_low = tie(cols_swap(own_low, 2), w_near)
+    x_low = (pair_low, cols_swap(own_low, 1), cols_swap(pair_low, 1))
     own_pack = jnp.concatenate([w_up, w_out.T, jnp.zeros((FB, 64), BF), w_down], axis=1)
+    dy_core = hold(away[:2], grad_y, B)
+    dy_away = hold(away[2:], grad_y, B)
     ring = [tie(own_pack, w_near)]
     ring.append(rows_shift(ring[0], 1))
-    w_pair = tie(cols_swap(w_near, 2), cross_low)
-    w_cross = cols_swap(
-        jnp.stack([lax.dynamic_index_in_dim(part, 1 - core, 0, keepdims=False) for part in (w_near, w_pair)]), 1
-    )
-
-    pair_high = cols_swap(tie(block_input[:, HALF:], w_pair), 2)
+    cross_high = cols_swap(own_high, 1)
+    w_pair = tie(cols_swap(w_near, 2), x_low[1], x_low[2], dy_core, dy_away, ring[1])
+    w_cross = cols_swap(pick(1 - core, w_near, w_pair), 1)
+    pair_high = cols_swap(tie(own_high, w_pair), 2)
 
     normed_low, scale_low, q_low, *kv, w_qkv = project_half(
         low_order, (block_input, *x_low), gain_one, (w_near, w_pair, w_cross), 0, (), ()
     )
-    ring[1] = tie(ring[1], scale_low)
-    first_sent = jnp.stack(ring)
-    first_sent = jnp.where(parity == 0, first_sent[:, :, :896], first_sent[:, :, 896:])
-    outs_low = [attend(low_table, q_low, kv[0], kv[3], 0, (0, 1), first_sent)]
+    ring.append(rows_shift(ring[1], 1))
+    first_sent = jnp.stack(ring[:2])
+    first_sent = tie(jnp.where(parity == 0, first_sent[:, :, :896], first_sent[:, :, 896:]), scale_low)
+    *out_low, log_first = attend(low_table, q_low, kv[0], kv[3], 0, (0, 1), (), first_sent)
     first_pairs = cols_swap(first_sent, 2)
-    ring.append(rows_shift(ring[1], 1))
-    pair_high = tie(pair_high, outs_low[0][2])
-    cross_sent = jnp.stack([block_input[:, HALF:], pair_high])
-    outs_low.append(attend(low_table, q_low, kv[0], kv[3], 0, (1, 2), outs_low[0][2], cross_sent))
-    ring[2] = tie(ring[2], outs_low[1][2])
+    ring[2] = tie(ring[2], log_first)
     ring.append(rows_shift(ring[2], 1))
-    cross_high = cols_swap(cross_sent, 1)
-    x_high = (pair_high, cross_high)
-    low_got = cols_swap(jnp.concatenate([out[1] for out in outs_low]), 1)
-    dy_core = hold(away[:2], grad_y, B, scale_low)
-    dy_away = tie(hold(away[2:], grad_y, B, scale_low), outs_low[1][2])
+    pair_high = tie(pair_high, log_first)
+    *out_low, log_low = attend(low_table, q_low, kv[0], kv[3], 0, (1, 2), out_low, log_first, pair_high, ring[2])
+    x_high = (pair_high, cross_high, cols_swap(pair_high, 1))
+    low_got = cols_swap(out_low[1], 1)
+    dy_sent, third_sent = tie(dy_away, log_low), tie(ring[2], log_low)
+    ring[2] = third_sent
     normed_high, scale_high, q_high, *kv = project_half(
-        high_order, (block_input, *x_high), gain_one, (w_qkv,), 1, tuple(kv), (outs_low[1][2], dy_away, first_pairs)
+        high_order, (block_input, *x_high), gain_one, (w_qkv,), 1, tuple(kv), (log_low, first_pairs)
     )
     k, k_t, v, v_t = kv
     first_crossed = dp_swap(first_pairs)
-    dy_pair = cols_swap(dy_away, 2)
-    third_pair = cols_swap(ring[2], 2)
-    outs_high = [attend(high_table, q_high, k, v_t, 1, (0, 1), low_got)]
-    ring[3] = tie(ring[3], outs_high[0][2])
-    dy_pair, third_pair = tie(dy_pair, outs_high[0][2]), tie(third_pair, outs_high[0][2])
+    dy_pair = cols_swap(dy_sent, 2)
+    third_pair = cols_swap(third_sent, 2)
+    *out_high, log_other = attend(high_table, q_high, k, v_t, 1, (0, 1), (), low_got)
+    ring[3] = tie(ring[3], log_other)
+    dy_pair, third_pair = tie(dy_pair, log_other), tie(third_pair, log_other)
+    first_crossed = tie(first_crossed, log_other)
     dy_cross_sent = jnp.concatenate([dy_core, dy_pair[1:]])
-    third_sent = jnp.stack([ring[2], third_pair])
-    outs_high.append(
-        attend(high_table, q_high, k, v_t, 1, (1, 2), outs_high[0][2], ring[3], dy_cross_sent, third_sent)
+    third_cross_sent = jnp.stack([ring[2], third_pair])
+    *out_high, log_high = attend(
+        high_table, q_high, k, v_t, 1, (1, 2), out_high, log_other, ring[3], dy_cross_sent, third_cross_sent
     )
     dy_cross = cols_swap(dy_cross_sent, 1)
-    third_cross = cols_swap(third_sent, 1)
-    first_crossed = tie(first_crossed, outs_high[0][2])
+    third_cross = cols_swap(third_cross_sent, 1)
     first_cross = cols_swap(jnp.concatenate([jnp.stack(ring[:2]), first_pairs, first_crossed], axis=2), 1)
-    last_pair = cols_swap(ring[3], 2)
-    last_pair = tie(last_pair, outs_high[1][2])
+    last_pair = tie(cols_swap(ring[3], 2), log_high)
     last_cross = cols_swap(jnp.stack([ring[3], last_pair]), 1)
-    high_got = cols_swap(jnp.concatenate([out[1] for out in outs_high]), 1)
+    high_got = cols_swap(out_high[1], 1)
+    log_low, log_high = jnp.concatenate([log_first, log_low]), jnp.concatenate([log_other, log_high])
 
     sel = jnp.stack([core.astype(jnp.int32), low_order[0], high_order[0], parity.astype(jnp.int32)])
-    both_near, both_far, ga_own, ga_other, gain_two_sum, g_near, g_one, g_rest = feed_forward(
+    *boths, ga_own, ga_other, gain_two_sum, g_near, g_one, g_rest = feed_forward(
         sel,
         gain_two,
         ring,
         (first_pairs, first_crossed, third_pair, last_pair),
         (first_cross, third_cross, last_cross),
-        [out[0] for out in outs_low + outs_high] + [low_got, high_got],
+        (out_low[0], out_high[0], low_got, high_got),
         (grad_y, dy_pair, dy_cross),
         (block_input, *x_low, *x_high),
     )
@@ -912,61 +950,56 @@
 
     ga_got = cols_swap(ga_other, 1)
     total = two(g_near[1], cols_swap(g_one, 1))
-    both_cross = cols_swap(both_far, 1)
-    there_sent = jnp.stack([both_near[:, FB:], both_cross[:, FB:]], axis=1)
+    crosses = [cols_swap(both, 1) for both in boths[2:]]
     g_got = cols_swap(g_rest, 1)
-    out_low = [jnp.concatenate(parts) for parts in zip(*outs_low)]
-    out_high = [jnp.concatenate(parts) for parts in zip(*outs_high)]
     grads = (ga_own, ga_got)
     dq_high, dkv_high, dkv_low = attend_back(
-        high_table, q_high, grads, out_high[:2], out_high[2], k, v, k_t, 1, (0, 3), (), total, there_sent
-    )
-    there = cols_swap(there_sent, 2)
+        high_table, q_high, grads, out_high, log_high, k, v, k_t, 1, (0, 3), (), total, *crosses
+    )
+    theres = [cols_swap(boths[1], 2), cols_swap(crosses[1], 2)]
     total = three(tie(rows_shift(total, 1), dq_high), g_near[2], g_got[1])
-    near_high, far_high, inner_high, gain_part, w_part = project_back(
-        high_order, w_qkv, normed_high, (dq_high,), (dkv_high,), 1, (jnp.zeros((D, 1), F32),), total, there
-    )
-    low = (low_table, q_low, grads, out_low[:2], out_low[2], k, v, k_t, 0)
+    near_high, far_high, gain_part, w_part = project_back(
+        high_order, w_qkv, normed_high, dq_high, dkv_high, 1, jnp.zeros((D, 1), F32), total, *theres
+    )
     got_high = cols_swap(far_high, 1)
-    dq_first, dkv_first = attend_back(*low, (0, 2), (dkv_low,), near_high)
-    got_high = tie(got_high, dq_first)
+    dq_low, dkv_low = attend_back(
+        low_table, q_low, grads, out_low, log_low, k, v, k_t, 0, (0, 3), (dkv_low,), near_high
+    )
+    got_high = tie(got_high, dq_low)
     sent_high = two(near_high[FB:], got_high[FB:])
-    total = three(tie(rows_shift(total, 1), dq_first), g_near[3], g_got[2])
-    wg_first = weights_back(low_order, normed_low, dq_first, dkv_first, w_part, (0, 2), sent_high, total)
+    total = three(tie(rows_shift(total, 1), sent_high), g_near[3], g_got[2])
     pair_sent = cols_swap(sent_high, 2)
-    dq_last, dkv_last = attend_back(*low, (2, 1), (dkv_low,), wg_first[0])
-
-    def by_core(near, got):
-        return jnp.where(core == 0, near, got), jnp.where(core == 0, got, near)
-
-    def half_of(part, which):
-        return jnp.concatenate([part[:, n * 128 + which * HD : n * 128 + (which + 1) * HD] for n in range(3)], axis=1)
-
-    got = tie(cols_swap(wg_first[1], 1), dq_last)
-    pair_zero, pair_one = by_core(wg_first[0][0], got[0]), by_core(wg_first[0][1], got[1])
-    total = three(tie(rows_shift(total, 1), dq_last), g_near[0], g_got[0])
-    total_far = total[FB:]
-    near_low, far_low, inner_low, gain_part = project_back(
-        low_order,
-        w_qkv,
-        normed_low,
-        (dq_first, dq_last),
-        (dkv_first, dkv_last),
-        0,
-        (gain_part,),
-        pair_zero[1],
-        *pair_one,
-        pair_sent,
-        total_far,
-    )
-    firsts = [rows_shift(pair_zero[1], -2), rows_shift(pair_one[0], -1), rows_shift(pair_one[1], -3)]
-    feed_got = cols_swap(total_far, 2)
-    wg_last = weights_back(low_order, normed_low, dq_last, dkv_last, w_part, (2, 1), near_low, firsts[0])
-    got_low = tie(cols_swap(far_low, 1), wg_last[0])
+    wg_near, wg_far = weights_back(low_order, normed_low, dq_low, dkv_low, w_part, (0, 3), sent_high, total)
+    near_low, far_low, gain_part = project_back(
+        low_order, w_qkv, normed_low, dq_low, dkv_low, 0, gain_part, wg_near, pair_sent
+    )
+
+    wg_got = tie(cols_swap(wg_far, 1), near_low)
+    by_core = jnp.where(core == 0, wg_near, wg_got), jnp.where(core == 0, wg_got, wg_near)
+
+    def split(values):
+        high = lax.reduce_precision(values, 8, 7)
+        middle = lax.reduce_precision(values - high, 8, 7)
+        parts = [high, middle, values - high - middle, jnp.zeros((values.shape[0], 58), F32)]
+        return jnp.concatenate(parts, axis=1).astype(BF)
+
+    def unsplit(columns):
+        columns = columns.astype(F32)
+        return columns[:, 576:578] + columns[:, 578:580] + columns[:, 580:582]
+
+    gains = jnp.concatenate([gain_part / gain_one, gain_two_sum], axis=1).T
+    gains = split((gains[:, :384] + cols_swap(gains[:, 384:], 1)).T)
+
+    def slot_of(slot):
+        part = by_core[slot // 2]
+        which = slot % 2
+        last = [part[2, :, n * 128 + which * HD : n * 128 + (which + 1) * HD] for n in range(3)]
+        return jnp.concatenate([part[which]] + last + [gains], axis=1)
+
+    slots = [slot_of(slot) for slot in range(4)]
+    got_low = tie(cols_swap(far_low, 1), wg_near)
     sent_low = two(near_low[FB:], got_low[FB:])
-    got = tie(cols_swap(wg_last[1], 1), sent_low)
-    last = by_core(wg_last[0][0], got[0])
-    slots = [half_of(last[slot // 2], slot % 2) for slot in range(4)]
+    total = three(tie(rows_shift(total, 1), near_low), g_near[0], g_got[0])
 
     def dp_sum(part, *deps):
         if lax.axis_size("dp") == 2:
@@ -975,40 +1008,41 @@
             return part.astype(F32) + got.astype(F32)
         return lax.psum(part.astype(F32), "dp")
 
-    feed_sum = two(total[:FB], feed_got)
     pair_got = cols_swap(sent_low, 2)
-    gain_one_sum = gain_part / gain_one
-    small_near = jnp.concatenate([inner_high[0], inner_low[0], gain_one_sum[:384, 0], gain_two_sum[:384, 0]])
-    small_far = jnp.concatenate([inner_high[0], inner_low[0], gain_one_sum[384:, 0], gain_two_sum[384:, 0]])
-    small = small_near + cols_swap(small_far, 1)
-    inners, gains = small[: 2 * HALF], small[2 * HALF :].reshape(2, 2, FB)
-    small = jnp.concatenate([inners, gains[:, 0].reshape(-1)]) + cols_swap(
-        jnp.concatenate([inners, gains[:, 1].reshape(-1)]), 2
-    )
-    inners, gains = small[: 2 * HALF].reshape(2, 1, HALF), small[2 * HALF :]
+    feed_sum = two(total[:FB], cols_swap(total[FB:], 2))
+    parts = [slots[0]] + [rows_shift(slots[slot], -slot) for slot in (1, 2, 3)]
+    parts[1] = tie(parts[1], pair_got, total)
+    joined = sum(part[:, :576].astype(F32) for part in parts).astype(BF)
+    shares = [unsplit(part) for part in parts]
+
+    def share_of(row):
+        slot = jnp.mod(r - row, 4)
+        last = jnp.where(slot == 2, shares[2], shares[3])
+        return jnp.where(slot == 0, shares[0], jnp.where(slot == 1, shares[1], last))
+
+    shares = [share_of(row) for row in range(4)]
+    gains = (shares[0] + shares[1]) + (shares[2] + shares[3])
+    joined_sent = jnp.concatenate([joined[FB:], split(gains[FB:])], axis=1)
+    joined_got = cols_swap(joined_sent, 2)
+    joined_pair = jnp.concatenate(
+        [two(joined[:FB], joined_got[:, :576]), split(gains[:FB] + unsplit(joined_got))], axis=1
+    )
+
     where = jnp.stack([y, core]).astype(jnp.int32)
     low_sel = jnp.concatenate([where, jnp.array([0, 1, 1, 0, 0, 0, 1, 1], jnp.int32)])
     high_sel = jnp.concatenate([where, jnp.array([0, 0, 1, 1, 0, 1, 0, 1], jnp.int32)])
     gain_column = norm_gain_one.reshape(FB, 1)
     outputs = finish_half(
-        high_sel, both_near, both_cross, there, near_high, got_high, pair_sent, block_input, scale_high,
-        inners[0], gain_column, 1, (), sent_low, slots[3],
+        high_sel, boths[0], crosses[0], *theres, near_high, got_high, pair_sent, block_input, scale_high,
+        gain_column, 1, (), joined_sent,
     )
     output, grad_x = finish_half(
-        low_sel, both_near, both_cross, there, near_low, got_low, pair_got, block_input, scale_low,
-        inners[1], gain_column, 0, tuple(outputs),
-    )
-
-    lasts = [rows_shift(slots[slot], -slot) for slot in (1, 2, 3)]
-    lasts[0] = tie(lasts[0], grad_x)
-
-    def total_of(parts):
-        return sum(part.astype(F32) for part in parts).astype(BF)
-
-    joined = jnp.concatenate([total_of([pair_zero[0]] + firsts), total_of([slots[0]] + lasts)], axis=1)
-    joined_sent = joined
-    joined = dp_sum(two(joined[:FB], cols_swap(joined[FB:], 2)))
-
+        low_sel, boths[0], crosses[0], *theres, near_low, got_low, pair_got, block_input, scale_low,
+        gain_column, 0, tuple(outputs), joined_pair, feed_sum,
+    )
+
+    joined = dp_sum(joined_pair)
+    gains = unsplit(joined)
     feed_total = dp_sum(feed_sum, grad_x)
 
     def joined_grad(n):
@@ -1016,19 +1050,15 @@
             [joined[:, n * 128 : (n + 1) * 128], joined[:, 384 + n * HD : 384 + (n + 1) * HD]], axis=1
         )
 
-    gains = tie(gains, grad_x)
-    slots = jnp.stack([gains] + [rows_shift(gains, step) for step in (1, 2, 3)])
-    slots = slots[jnp.mod(r - jnp.arange(4), 4)]
-    gains = dp_sum((slots[0] + slots[1]) + (slots[2] + slots[3]))
     return (
         output,
         grad_x,
-        gains[:FB],
+        gains[:, 0],
         joined_grad(0),
         joined_grad(1),
         joined_grad(2),
         feed_total[:, D : D + FB].T,
-        gains[FB:],
+        gains[:, 1],
         feed_total[:, :D],
         feed_total[:, D + 256 :],
     )

time: 475 us -> 440 us (0.926)
  local copies, waits for them, and re-layouts: 60.9 us -> 33.2 us
  starting transfers between devices: 58 us -> 40.8 us
  waiting for transfers between devices: 53 us -> 60.3 us
  Pallas kernels: 243 us -> 249 us
    ppermute x18 -> x12, waiting for transfers between devices: 10.5 us -> 51.7 us  [rows_shift(): lax.ppermute(value, 'rows', [(i, (i + step) % count) for i in range(count)])]
    ppermute x33 -> x35, waiting for transfers between devices: 37.1 us -> 8.62 us  [cols_swap(): lax.ppermute(value, 'cols', [(i, i ^ distance) for i in range(lax.axis_si...]
    unnamed x188 -> x108, local copies, waits for them, and re-layouts: 30.8 us -> 13 us
    ppermute x18 -> x12, starting transfers between devices: 35 us -> 17.6 us  [rows_shift(): lax.ppermute(value, 'rows', [(i, (i + step) % count) for i in range(count)])]
    slice x19 -> x7, local copies, waits for them, and re-layouts: 10.9 us -> 4.14 us  [the longest x1 1.24 us: per_device(): own_low, own_high = (block_input[:, :HALF], block_input[:, HALF:])]
    another operation x6 -> x5, other arithmetic: 8.24 us -> 1.7 us  [the longest x1 1.44 us: per_device(): third_cross_sent = jnp.stack([ring[2], third_pair])]
    convert_element_type x2 -> x6, other arithmetic: 2.39 us -> 7.97 us  [the longest x5 6.32 us: unsplit(): columns = columns.astype(F32)]
    ppermute x4 -> x3, waiting for transfers between devices: 5.43 us -> 0.01 us  [dp_swap(): lax.ppermute(value, 'dp', [(i, i ^ 1) for i in range(lax.axis_size('dp'))])]
  transfers between devices with their start and end apart: 55 -> 50, of which waited for: 11 -> 8; matrix products, arithmetic and copies ran while one was open for 16% -> 15% of each run, Pallas kernels for 41% -> 45%
where the time goes in v3:
time: 440 us; the launch traced here: 435 us
  Pallas kernels  249 us (57%)
  waiting for transfers between devices  60.3 us (14%)
  other arithmetic  50.2 us (11%)
  starting transfers between devices  40.8 us (9%)
  local copies, waits for them, and re-layouts  33.2 us (8%)
    pallas_call x2, Pallas kernels, attend_back(): pl.pallas_call(functools.partial(attend_back_kernel, counts=(4,) if half...  68.8 us
    pallas_call x1, Pallas kernels, feed_forward(): pl.pallas_call(feed_kernel, in_specs=[pl.BlockSpec(memory_space=pltpu.SME...  52.8 us
    ppermute x12, waiting for transfers between devices, rows_shift(): lax.ppermute(value, 'rows', [(i, (i + step) % count) for i in range(count)])  51.7 us
    pallas_call x4, Pallas kernels, attend(): pl.pallas_call(functools.partial(attend_kernel, counts=(4,) if half else...  45.8 us
    pallas_call x2, Pallas kernels, project_half(): pl.pallas_call(functools.partial(qkv_kernel, first=first, extra=extra), g...  25.2 us
    pallas_call x2, Pallas kernels, project_back(): pl.pallas_call(functools.partial(qkv_back_kernel, half=half), grid_spec=p...  25.1 us
    ppermute x35, starting transfers between devices, cols_swap(): lax.ppermute(value, 'cols', [(i, i ^ distance) for i in range(lax.axis_si...  19.6 us
    ppermute x12, starting transfers between devices, rows_shift(): lax.ppermute(value, 'rows', [(i, (i + step) % count) for i in range(count)])  17.6 us
  transfers between devices with their start and end apart: 50, of which 8 were waited for; matrix products, arithmetic and copies ran while one was open for 15% of the time, Pallas kernels for 45%

profile of v3, /device:TPU:24, one launch (start us, length us, event | category | flops | bytes accessed | tf_op | source)
XLA Modules:
  0.0 435.2 jit_solution(368810728107886089)
XLA Ops:
  0.7 1.9 shard_map.240
  3.1 3.6 collective-permute-start.2
  8.0 1.5 collective-permute-start.7
  12.1 2.5 shard_map.243.refs_3_
  14.8 7.3 %collective-permute-done.3 = bf16[192,576]{1,0:T(8,128)(2,1)} collective-permute-done((bf16[192,576]{1,0:T(8,128)(2,1)}, bf16[192,576]{1,0:T(8,128)(2,1)}, u32[]{:S(2)}, u32[]{:S(2)}) %collective-permute-start.3) | collective-permute-done | bytes 221216 | tf_op jit(solution)/shard_map/ppermute | solution.py:50
  28.8 2.2 collective-permute-start.5
  31.7 4.0 shard_map.244.refs_4_.refs_0_
  36.3 11.5 %collective-permute-done.5.refs_5_.refs_1_ = bf16[192,1792]{1,0:T(8,128)(2,1)S(1)} collective-permute-done((bf16[192,1792]{1,0:T(8,128)(2,1)}, bf16[192,1792]{1,0:T(8,128)(2,1)S(1)}, u32[]{:S(2)}, u32[]{:S(2)}) %collective-permute-start.5) | collective-permute-done | bytes 688160 | tf_op jit(solution)/shard_map/ppermute | solution.py:50
  48.9 2.2 shard_map.246
  53.0 3.3 collective-permute-start.6
  57.3 1.5 collective-permute-start.12
  58.9 13.0 %shard_map.247 = (bf16[768,2048]{1,0:T(8,128)(2,1)}, f32[1,2048]{1,0:T(1,128)}, bf16[384,1024]{1,0:T(8,128)(2,1)}, bf16[4096,384]{1,0:T(8,128)(2,1)}, bf16[384,4...) custom-call(s32[5]{0:T(128)} %pad_add_fusion.3.tab, ...), custom_call_target="tpu_custom_call" | custom-call | flops 13799999488 | tf_op jit(solution)/shard_map/pallas_call | solution.py:197
  72.5 7.4 %shard_map.249 = (bf16[384,512]{1,0:T(8,128)(2,1)}, bf16[384,512]{1,0:T(8,128)(2,1)}, f32[1,2,1024]{2,1,0:T(2,128)}) custom-call(s32[18]{0:T(128)} %get-tuple-element.229.tab, bf16[384,1024]{1,0:T(8,128)(2,1)} %get-tuple-element.65.q_t, bf16[4096,384]{1,0:T(8,128)(2,1)} %get-tuple-element.66.k.refs_6_, bf16[384,4096]{1,0:T(8,128)(2,1)} %get-tuple-element.67.v_t.refs_9_, ...), custom_call_target="tpu_custom_call" | custom-call | flops 6899999744 | tf_op jit(solution)/shard_map/pallas_call | solution.py:302
  80.3 12.3 %shard_map.253 = (bf16[384,512]{1,0:T(8,128)(2,1)}, bf16[384,512]{1,0:T(8,128)(2,1)}, f32[2,2,1024]{2,1,0:T(2,128)}) custom-call(s32[18]{0:T(128)} %get-tuple-element.229.tab, bf16[384,1024]{1,0:T(8,128)(2,1)} %get-tuple-element.65.q_t, bf16[4096,384]{1,0:T(8,128)(2,1)} %get-tuple-element.66.k.refs_6_, ...), custom_call_target="tpu_custom_call", output_to_operand_aliasing={{0}: (4, {}), {1}: (5, {})} | custom-call | flops 13799999488 | tf_op jit(solution)/shard_map/pallas_call | solution.py:302
  93.1 1.6 collective-permute-start.21
  94.6 2.8 collective-permute-done.13.refs_0_
  97.5 1.5 collective-permute-start.19
  100.5 12.2 %shard_map.255 = (bf16[768,2048]{1,0:T(8,128)(2,1)}, f32[1,2048]{1,0:T(1,128)}, bf16[384,1024]{1,0:T(8,128)(2,1)}, bf16[4096,384]{1,0:T(8,128)(2,1)}, bf16[384,4...) custom-call(s32[5]{0:T(128)} %pad_add_fusion.4.tab, ...), custom_call_target="tpu_custom_call", output_to_operand_aliasing={{3}: (7, {}), {4}: (8, {}), {5}: (9, {}), {6}: (10, {})} | custom-call | flops 13799999488 | tf_op jit(solution)/shard_map/pallas_call | solution.py:197
  113.5 9.9 %shard_map.256 = (bf16[384,512]{1,0:T(8,128)(2,1)}, bf16[384,512]{1,0:T(8,128)(2,1)}, f32[1,2,1024]{2,1,0:T(2,128)}) custom-call(s32[18]{0:T(128)} %get-tuple-element.228.tab, bf16[384,1024]{1,0:T(8,128)(2,1)} %get-tuple-element.76.q_t, bf16[4096,384]{1,0:T(8,128)(2,1)} %get-tuple-element.77.k, bf16[384,4096]{1,0:T(8,128)(2,1)} %get-tuple-element.78.v_t, ...), custom_call_target="tpu_custom_call" | custom-call | flops 9200000000 | tf_op jit(solution)/shard_map/pallas_call | solution.py:302
  125.9 3.1 pad_maximum_fusion
  131.6 16.1 %shard_map.262 = (bf16[384,512]{1,0:T(8,128)(2,1)}, bf16[384,512]{1,0:T(8,128)(2,1)}, f32[2,2,1024]{2,1,0:T(2,128)}) custom-call(s32[18]{0:T(128)} %get-tuple-element.228.tab, bf16[384,1024]{1,0:T(8,128)(2,1)} %get-tuple-element.76.q_t, bf16[4096,384]{1,0:T(8,128)(2,1)} %get-tuple-element.77.k, ...), custom_call_target="tpu_custom_call", output_to_operand_aliasing={{0}: (4, {}), {1}: (5, {})} | custom-call | flops 18400000000 | tf_op jit(solution)/shard_map/pallas_call | solution.py:302
  151.9 2.5 collective-permute-done.26.refs_17_
  155.2 52.8 %shard_map.264 = (bf16[2,192,1024]{2,1,0:T(8,128)(2,1)}, bf16[2,192,1024]{2,1,0:T(8,128)(2,1)}, bf16[2,192,1024]{2,1,0:T(8,128)(2,1)}, bf16[2,192,1024]{2,1,0:T(...) custom-call(s32[4]{0:T(128)} %pad_add_fusion.2.sel, ...), custom_call_target="tpu_custom_call" | custom-call | flops 57500000256 | tf_op jit(solution)/shard_map/pallas_call | solution.py:629
  211.5 1.6 collective-permute-start.28
  214.6 2.7 fusion.3.refs_0_
  217.3 2.1 collective-permute-start.33
  219.5 40.8 %shard_map.265 = (bf16[384,1024]{1,0:T(8,128)(2,1)}, bf16[3,2048,256]{2,1,0:T(8,128)(2,1)}, f32[3,2048,256]{2,1,0:T(8,128)}) custom-call(s32[18]{0:T(128)} %get-tuple-element.228.tab, bf16[384,1024]{1,0:T(8,128)(2,1)} %get-tuple-element.76.q_t, bf16[384,1024]{1,0:T(8,128)(2,1)} %get-tuple-element.92.do_own, ...), custom_call_target="tpu_custom_call" | custom-call | flops 55199997952 | tf_op jit(solution)/shard_map/pallas_call | solution.py:384
  261.4 3.7 fusion.2.refs_3_
  265.9 14.9 %shard_map.267 = (bf16[400,2048]{1,0:T(8,128)(2,1)}, bf16[400,2048]{1,0:T(8,128)(2,1)}, f32[768,1]{1,0:T(8,128)}, f32[3,768,384]{2,1,0:T(8,128)}) custom-call(s32[5]{0:T(128)} %pad_add_fusion.4.tab, bf16[768,1152]{1,0:T(8,128)(2,1)} %get-tuple-element.73.refs_5_.w, bf16[768,2048]{1,0:T(8,128)(2,1)} %get-tuple-element.99.n_t, ...), custom_call_target="tpu_custom_call" | custom-call | flops 17250000896 | tf_op jit(solution)/shard_map/pallas_call | solution.py:718
  280.9 28.0 %shard_map.268 = (bf16[384,1024]{1,0:T(8,128)(2,1)}, bf16[3,2048,256]{2,1,0:T(8,128)(2,1)}) custom-call(s32[18]{0:T(128)} %get-tuple-element.229.tab, bf16[384,1024]{1,0:T(8,128)(2,1)} %get-tuple-element.65.q_t, bf16[384,1024]{1,0:T(8,128)(2,1)} %get-tuple-element.92.do_own, bf16[384,1024]{1,0:T(8,128)(2,1)} %collective-permute-done.31.do_other, ...), custom_call_target="tpu_custom_call" | custom-call | flops 41400000512 | tf_op jit(solution)/shard_map/pallas_call | solution.py:384
  308.9 2.6 add_convert_fusion.1.refs_1_.refs_0_
  313.0 3.7 fusion.1.refs_1_
  316.8 2.0 collective-permute-start.43
  318.8 9.0 %shard_map.271 = (bf16[3,384,384]{2,1,0:T(8,128)(2,1)}, bf16[3,384,384]{2,1,0:T(8,128)(2,1)}) custom-call(s32[5]{0:T(128)} %pad_add_fusion.3.tab, bf16[768,2048]{1,0:T(8,128)(2,1)} %get-tuple-element.91.n_t, bf16[384,1024]{1,0:T(8,128)(2,1)} %get-tuple-element.104.refs_1_.dq_t.refs_0_, bf16[3,2048,256]{2,1,0:T(8,128)(2,1)} %get-tuple-element.105.dkv.refs_1_, ...), custom_call_target="tpu_custom_call" | custom-call | flops 9200000000 | tf_op jit(solution)/shard_map/pallas_call | solution.py:749
  328.1 5.3 %collective-permute-done.37.refs_4_.refs_6_.refs_9_ = bf16[208,2048]{1,0:T(8,128)(2,1)} collective-permute-done((bf16[208,2048]{1,0:T(8,128)(2,1)}, bf16[208,2048]{1,0:T(8,128)(2,1)}, u32[]{:S(2)}, u32[]{:S(2)}) %collective-permute-start.37) | collective-permute-done | bytes 852000 | tf_op jit(solution)/shard_map/ppermute | solution.py:45
  333.3 10.2 %shard_map.272 = (bf16[400,2048]{1,0:T(8,128)(2,1)}, bf16[400,2048]{1,0:T(8,128)(2,1)}, f32[768,1]{1,0:T(8,128)}) custom-call(s32[5]{0:T(128)} %pad_add_fusion.3.tab, bf16[768,1152]{1,0:T(8,128)(2,1)} %get-tuple-element.73.refs_5_.w, bf16[768,2048]{1,0:T(8,128)(2,1)} %get-tuple-element.91.n_t, bf16[384,1024]{1,0:T(8,128)(2,1)} %get-tuple-element.104.refs_1_.dq_t.refs_0_, ...), custom_call_target="tpu_custom_call" | custom-call | flops 11500000256 | tf_op jit(solution)/shard_map/pallas_call | solution.py:718
  348.6 2.2 broadcast_select_fusion.1
  352.2 1.8 collective-permute-start.45
  355.2 1.6 collective-permute-start.44
  357.9 2.7 fusion.refs_2_
  363.0 2.4 add_convert_fusion
  369.0 30.1 %collective-permute-done.44 = bf16[384,640]{1,0:T(8,128)(2,1)} collective-permute-done((bf16[384,640]{1,0:T(8,128)(2,1)}, bf16[384,640]{1,0:T(8,128)(2,1)}, u32[]{:S(2)}, u32[]{:S(2)}) %collective-permute-start.44) | collective-permute-done | bytes 491552 | tf_op jit(solution)/shard_map/ppermute | solution.py:50
  399.0 2.1 convert_element_type.203
  401.1 2.0 convert_element_type.204
  407.0 1.7 add_convert_fusion.3
  410.7 5.8 %shard_map.277 = (bf16[192,4096]{1,0:T(8,128)(2,1)}, f32[192,4096]{1,0:T(8,128)}) custom-call(s32[10]{0:T(128)} %pad_add_fusion.5.sel, bf16[2,192,1024]{2,1,0:T(8,128)(2,1)} %get-tuple-element.87.refs_0_, bf16[2,192,1024]{2,1,0:T(8,128)(2,1)} %collective-permute-done.27.refs_1_, bf16[2,192,1024]{2,1,0:T(8,128)(2,1)} %collective-permute-done.28.refs_4_.refs_2_, ...), custom_call_target="tpu_custom_call" | custom-call | flops 6899999744 | tf_op jit(solution)/shard_map/pallas_call | solution.py:793
  418.3 1.6 collective-permute-start.48
  419.8 5.8 %shard_map.278 = (bf16[192,4096]{1,0:T(8,128)(2,1)}, f32[192,4096]{1,0:T(8,128)}) custom-call(s32[10]{0:T(128)} %pad_add_fusion.sel, bf16[2,192,1024]{2,1,0:T(8,128)(2,1)} %get-tuple-element.87.refs_0_, bf16[2,192,1024]{2,1,0:T(8,128)(2,1)} %collective-permute-done.27.refs_1_, ...), custom_call_target="tpu_custom_call", output_to_operand_aliasing={{0}: (14, {}), {1}: (15, {})} | custom-call | flops 6899999744 | tf_op jit(solution)/shard_map/pallas_call | solution.py:793
  (293 shorter events, 69.9 us)
Async XLA Ops:
  2.6 19.5 %collective-permute-start.3 = (bf16[192,576]{1,0:T(8,128)(2,1)}, bf16[192,576]{1,0:T(8,128)(2,1)}, u32[]{:S(2)}, u32[]{:S(2)}) collective-permute-start(bf16[192,576]{1,0:T(8,128)(2,1)} %shard_map.240), channel_id=1, source_target_pairs={{0,8},{4,12},{8,0},{12,4},{1,9},{5,13},{9,1},{13,5},{2,10},{6,14},... | collective-permute-start | bytes 663560 | tf_op jit(solution)/shard_map/ppermute | solution.py:50
  2.9 22.5 %collective-permute-start.4 = (bf16[192,576]{1,0:T(8,128)(2,1)}, bf16[192,576]{1,0:T(8,128)(2,1)S(1)}, u32[]{:S(2)}, u32[]{:S(2)}) collective-permute-start(bf16[192,576]{1,0:T(8,128)(2,1)} %shard_map.240), channel_id=1, source_target_pairs={{0,12},{4,0},{8,4},{12,8},{1,13},{5,1},{9,5},{13,9},{2,14},{6,2},{... | collective-permute-start | bytes 663560 | tf_op jit(solution)/shard_map/ppermute | solution.py:50
  3.1 22.7 %collective-permute-start.2 = (bf16[192,576]{1,0:T(8,128)(2,1)}, bf16[192,576]{1,0:T(8,128)(2,1)S(1)}, u32[]{:S(2)}, u32[]{:S(2)}) collective-permute-start(bf16[192,576]{1,0:T(8,128)(2,1)} %shard_map.240), channel_id=1, source_target_pairs={{0,4},{4,8},{8,12},{12,0},{1,5},{5,9},{9,13},{13,1},{2,6},{6,10},{... | collective-permute-start | bytes 663560 | tf_op jit(solution)/shard_map/ppermute | solution.py:50
  8.0 18.8 %collective-permute-start.7 = (bf16[192,2048]{1,0:T(8,128)(2,1)}, bf16[192,2048]{1,0:T(8,128)(2,1)}, u32[]{:S(2)}, u32[]{:S(2)}) collective-permute-start(bf16[192,2048]{1,0:T(8,128)(2,1)} %get-tuple-element.177), channel_id=1, source_target_pairs={{0,2},{1,3},{2,0},{3,1},{4,6},{5,7},{6,4},{7,5},{8,10},{9,11},{10,... | collective-permute-start | bytes 2359304 | tf_op jit(solution)/shard_map/ppermute | solution.py:45
  9.5 26.4 %collective-permute-start.8 = (bf16[192,2048]{1,0:T(8,128)(2,1)}, bf16[192,2048]{1,0:T(8,128)(2,1)S(1)}, u32[]{:S(2)}, u32[]{:S(2)}) collective-permute-start(bf16[192,2048]{1,0:T(8,128)(2,1)} %get-tuple-element.177), channel_id=1, source_target_pairs={{0,1},{1,0},{2,3},{3,2},{4,5},{5,4},{6,7},{7,6},{8,9},{9,8},{10,11... | collective-permute-start | bytes 2359304 | tf_op jit(solution)/shard_map/ppermute | solution.py:45
  22.0 13.6 %collective-permute-start = (f32[400]{0:T(512)S(1)}, f32[400]{0:T(512)S(1)}, u32[]{:S(2)}, u32[]{:S(2)}) collective-permute-start(f32[400]{0:T(512)S(1)} %pad_maximum_fusion.13), channel_id=1, source_target_pairs={{0,2},{1,3},{2,0},{3,1},{4,6},{5,7},{6,4},{7,5},{8,10},{9,11},{10,... | collective-permute-start | bytes 4808 | tf_op jit(solution)/shard_map/ppermute | solution.py:45
  26.2 21.6 %collective-permute-start.10 = (bf16[2,192,1152]{2,1,0:T(8,128)(2,1)S(1)}, bf16[2,192,1152]{2,1,0:T(8,128)(2,1)S(1)}, u32[]{:S(2)}, u32[]{:S(2)}) collective-permute-start(bf16[2,192,1152]{2,1,0:T(8,128)(2,1)S(1)} %pad_maximum_fusion.3.refs_1_.first.refs_5_), channel_id=1, source_target_pairs={{0,2},{1,3},{2,0},{3,1},{4,6},{5,7},{6,4},{7,5},{8,10},{9,11},{10,... | collective-permute-start | bytes 2654216 | tf_op jit(solution)/shard_map/ppermute | solution.py:45
  27.1 20.7 %collective-permute-start.9 = (bf16[192,2048]{1,0:T(8,128)(2,1)}, bf16[192,2048]{1,0:T(8,128)(2,1)}, u32[]{:S(2)}, u32[]{:S(2)}) collective-permute-start(bf16[192,2048]{1,0:T(8,128)(2,1)} %shard_map.242.refs_1_.refs_19_), channel_id=1, source_target_pairs={{0,1},{1,0},{2,3},{3,2},{4,5},{5,4},{6,7},{7,6},{8,9},{9,8},{10,11... | collective-permute-start | bytes 2359304 | tf_op jit(solution)/shard_map/ppermute | solution.py:45
  28.8 18.9 %collective-permute-start.5 = (bf16[192,1792]{1,0:T(8,128)(2,1)}, bf16[192,1792]{1,0:T(8,128)(2,1)S(1)}, u32[]{:S(2)}, u32[]{:S(2)}) collective-permute-start(bf16[192,1792]{1,0:T(8,128)(2,1)} %shard_map.241.refs_0_), channel_id=1, source_target_pairs={{0,4},{4,8},{8,12},{12,0},{1,5},{5,9},{9,13},{13,1},{2,6},{6,10},{... | collective-permute-start | bytes 2064392 | tf_op jit(solution)/shard_map/ppermute | solution.py:50
  35.7 21.7 %collective-permute-start.14 = (bf16[192,2048]{1,0:T(8,128)(2,1)}, bf16[192,2048]{1,0:T(8,128)(2,1)}, u32[]{:S(2)}, u32[]{:S(2)}) collective-permute-start(bf16[192,2048]{1,0:T(8,128)(2,1)} %get-tuple-element.176.refs_0_), channel_id=1, source_target_pairs={{0,1},{1,0},{2,3},{3,2},{4,5},{5,4},{6,7},{7,6},{8,9},{9,8},{10,11... | collective-permute-start | bytes 2359304 | tf_op jit(solution)/shard_map/ppermute | solution.py:45
  35.9 15.2 %collective-permute-start.1 = (f32[2,400]{1,0:T(2,128)S(1)}, f32[2,400]{1,0:T(2,128)S(1)}, u32[]{:S(2)}, u32[]{:S(2)}) collective-permute-start(f32[2,400]{1,0:T(2,128)S(1)} %pad_maximum_fusion.12), channel_id=1, source_target_pairs={{0,1},{1,0},{2,3},{3,2},{4,5},{5,4},{6,7},{7,6},{8,9},{9,8},{10,11... | collective-permute-start | bytes 9608 | tf_op jit(solution)/shard_map/ppermute | solution.py:45
  51.1 7.7 %collective-permute-start.11 = (bf16[2,192,1152]{2,1,0:T(8,128)(2,1)}, bf16[2,192,1152]{2,1,0:T(8,128)(2,1)}, u32[]{:S(2)}, u32[]{:S(2)}) collective-permute-start(bf16[2,192,1152]{2,1,0:T(8,128)(2,1)} %shard_map.246), channel_id=1, source_target_pairs={{0,1},{1,0},{2,3},{3,2},{4,5},{5,4},{6,7},{7,6},{8,9},{9,8},{10,11... | collective-permute-start | bytes 2654216 | tf_op jit(solution)/shard_map/ppermute | solution.py:45
  53.0 26.9 %collective-permute-start.6 = (bf16[192,1792]{1,0:T(8,128)(2,1)S(1)}, bf16[192,1792]{1,0:T(8,128)(2,1)}, u32[]{:S(2)}, u32[]{:S(2)}) collective-permute-start(bf16[192,1792]{1,0:T(8,128)(2,1)S(1)} %copy-done.5), channel_id=1, source_target_pairs={{0,4},{4,8},{8,12},{12,0},{1,5},{5,9},{9,13},{13,1},{2,6},{6,10},{... | collective-permute-start | bytes 2064392 | tf_op jit(solution)/shard_map/ppermute | solution.py:50
  57.3 22.9 %collective-permute-start.12 = (bf16[192,2048]{1,0:T(8,128)(2,1)}, bf16[192,2048]{1,0:T(8,128)(2,1)}, u32[]{:S(2)}, u32[]{:S(2)}) collective-permute-start(bf16[192,2048]{1,0:T(8,128)(2,1)} %shard_map.251), channel_id=1, source_target_pairs={{0,2},{1,3},{2,0},{3,1},{4,6},{5,7},{6,4},{7,5},{8,10},{9,11},{10,... | collective-permute-start | bytes 2359304 | tf_op jit(solution)/shard_map/ppermute | solution.py:45
  71.9 27.1 %collective-permute-start.16 = (bf16[2,192,896]{2,1,0:T(8,128)(2,1)}, bf16[2,192,896]{2,1,0:T(8,128)(2,1)}, u32[]{:S(2)}, u32[]{:S(2)}) collective-permute-start(bf16[2,192,896]{2,1,0:T(8,128)(2,1)} %shard_map.248.refs_0_), channel_id=1, source_target_pairs={{0,2},{1,3},{2,0},{3,1},{4,6},{5,7},{6,4},{7,5},{8,10},{9,11},{10,... | collective-permute-start | bytes 2064392 | tf_op jit(solution)/shard_map/ppermute | solution.py:45
  79.9 17.6 %collective-permute-start.13 = (bf16[192,1792]{1,0:T(8,128)(2,1)}, bf16[192,1792]{1,0:T(8,128)(2,1)}, u32[]{:S(2)}, u32[]{:S(2)}) collective-permute-start(bf16[192,1792]{1,0:T(8,128)(2,1)} %shard_map.250.refs_4_.refs_0_), channel_id=1, source_target_pairs={{0,4},{4,8},{8,12},{12,0},{1,5},{5,9},{9,13},{13,1},{2,6},{6,10},{... | collective-permute-start | bytes 2064392 | tf_op jit(solution)/shard_map/ppermute | solution.py:50
  80.2 20.3 %collective-permute-start.15 = (bf16[192,2048]{1,0:T(8,128)(2,1)}, bf16[192,2048]{1,0:T(8,128)(2,1)}, u32[]{:S(2)}, u32[]{:S(2)}) collective-permute-start(bf16[192,2048]{1,0:T(8,128)(2,1)} %shard_map.252.refs_3_.refs_1_.refs_22_), channel_id=1, source_target_pairs={{0,1},{1,0},{2,3},{3,2},{4,5},{5,4},{6,7},{7,6},{8,9},{9,8},{10,11... | collective-permute-start | bytes 2359304 | tf_op jit(solution)/shard_map/ppermute | solution.py:45
  92.6 20.1 %collective-permute-start.17 = (bf16[384,512]{1,0:T(8,128)(2,1)}, bf16[384,512]{1,0:T(8,128)(2,1)S(1)}, u32[]{:S(2)}, u32[]{:S(2)}) collective-permute-start(bf16[384,512]{1,0:T(8,128)(2,1)} %get-tuple-element.79.o_other), channel_id=1, source_target_pairs={{0,1},{1,0},{2,3},{3,2},{4,5},{5,4},{6,7},{7,6},{8,9},{9,8},{10,11... | collective-permute-start | bytes 1179656 | tf_op jit(solution)/shard_map/ppermute | solution.py:45
  93.1 30.9 %collective-permute-start.21 = (bf16[2,192,1024]{2,1,0:T(8,128)(2,1)}, bf16[2,192,1024]{2,1,0:T(8,128)(2,1)}, u32[]{:S(2)}, u32[]{:S(2)}) collective-permute-start(bf16[2,192,1024]{2,1,0:T(8,128)(2,1)} %shard_map.260), channel_id=1, source_target_pairs={{0,2},{1,3},{2,0},{3,1},{4,6},{5,7},{6,4},{7,5},{8,10},{9,11},{10,... | collective-permute-start | bytes 2359304 | tf_op jit(solution)/shard_map/ppermute | solution.py:45
  97.5 31.6 %collective-permute-start.19 = (bf16[192,1792]{1,0:T(8,128)(2,1)}, bf16[192,1792]{1,0:T(8,128)(2,1)}, u32[]{:S(2)}, u32[]{:S(2)}) collective-permute-start(bf16[192,1792]{1,0:T(8,128)(2,1)} %shard_map.254.refs_2_), channel_id=1, source_target_pairs={{0,2},{1,3},{2,0},{3,1},{4,6},{5,7},{6,4},{7,5},{8,10},{9,11},{10,... | collective-permute-start | bytes 2064392 | tf_op jit(solution)/shard_map/ppermute | solution.py:45
  99.0 26.9 %collective-permute-start.18 = (bf16[2,192,896]{2,1,0:T(8,128)(2,1)}, bf16[2,192,896]{2,1,0:T(8,128)(2,1)}, u32[]{:S(2)}, u32[]{:S(2)}) collective-permute-start(bf16[2,192,896]{2,1,0:T(8,128)(2,1)} %collective-permute-done.16.refs_11_.refs_4_), channel_id=1, source_target_pairs={{0,16},{16,0},{1,17},{17,1},{2,18},{18,2},{3,19},{19,3},{4,20},{20... | collective-permute-start | bytes 2064392 | tf_op jit(solution)/shard_map/ppermute | solution.py:54
  123.4 24.3 %collective-permute-start.20 = (bf16[192,1792]{1,0:T(8,128)(2,1)}, bf16[192,1792]{1,0:T(8,128)(2,1)}, u32[]{:S(2)}, u32[]{:S(2)}) collective-permute-start(bf16[192,1792]{1,0:T(8,128)(2,1)} %shard_map.257.refs_3_), channel_id=1, source_target_pairs={{0,2},{1,3},{2,0},{3,1},{4,6},{5,7},{6,4},{7,5},{8,10},{9,11},{10,... | collective-permute-start | bytes 2064392 | tf_op jit(solution)/shard_map/ppermute | solution.py:45
  129.0 25.4 %collective-permute-start.22 = (bf16[2,192,3584]{2,1,0:T(8,128)(2,1)}, bf16[2,192,3584]{2,1,0:T(8,128)(2,1)}, u32[]{:S(2)}, u32[]{:S(2)}) collective-permute-start(bf16[2,192,3584]{2,1,0:T(8,128)(2,1)} %pad_maximum_fusion), channel_id=1, source_target_pairs={{0,1},{1,0},{2,3},{3,2},{4,5},{5,4},{6,7},{7,6},{8,9},{9,8},{10,11... | collective-permute-start | bytes 8257544 | tf_op jit(solution)/shard_map/ppermute | solution.py:45
  130.5 23.9 %collective-permute-start.23 = (bf16[2,192,1792]{2,1,0:T(8,128)(2,1)S(1)}, bf16[2,192,1792]{2,1,0:T(8,128)(2,1)}, u32[]{:S(2)}, u32[]{:S(2)}) collective-permute-start(bf16[2,192,1792]{2,1,0:T(8,128)(2,1)S(1)} %pad_maximum_fusion.1.refs_5_), channel_id=1, source_target_pairs={{0,1},{1,0},{2,3},{3,2},{4,5},{5,4},{6,7},{7,6},{8,9},{9,8},{10,11... | collective-permute-start | bytes 4128776 | tf_op jit(solution)/shard_map/ppermute | solution.py:45
  149.2 5.2 %collective-permute-start.24 = (bf16[2,192,1792]{2,1,0:T(8,128)(2,1)S(1)}, bf16[2,192,1792]{2,1,0:T(8,128)(2,1)}, u32[]{:S(2)}, u32[]{:S(2)}) collective-permute-start(bf16[2,192,1792]{2,1,0:T(8,128)(2,1)S(1)} %pad_maximum_fusion.2), channel_id=1, source_target_pairs={{0,1},{1,0},{2,3},{3,2},{4,5},{5,4},{6,7},{7,6},{8,9},{9,8},{10,11... | collective-permute-start | bytes 4128776 | tf_op jit(solution)/shard_map/ppermute | solution.py:45
  149.7 4.7 %collective-permute-start.26 = (bf16[2,192,1024]{2,1,0:T(8,128)(2,1)}, bf16[2,192,1024]{2,1,0:T(8,128)(2,1)}, u32[]{:S(2)}, u32[]{:S(2)}) collective-permute-start(bf16[2,192,1024]{2,1,0:T(8,128)(2,1)} %pad_maximum_fusion.4.refs_4_), channel_id=1, source_target_pairs={{0,1},{1,0},{2,3},{3,2},{4,5},{5,4},{6,7},{7,6},{8,9},{9,8},{10,11... | collective-permute-start | bytes 2359304 | tf_op jit(solution)/shard_map/ppermute | solution.py:45
  208.0 5.1 %collective-permute-start.32 = (bf16[384,1792]{1,0:T(8,128)(2,1)}, bf16[384,1792]{1,0:T(8,128)(2,1)S(1)}, u32[]{:S(2)}, u32[]{:S(2)}) collective-permute-start(bf16[384,1792]{1,0:T(8,128)(2,1)} %get-tuple-element.97), channel_id=1, source_target_pairs={{0,1},{1,0},{2,3},{3,2},{4,5},{5,4},{6,7},{7,6},{8,9},{9,8},{10,11... | collective-permute-start | bytes 4128776 | tf_op jit(solution)/shard_map/ppermute | solution.py:45
  208.4 4.6 %collective-permute-start.29 = (bf16[2,192,1024]{2,1,0:T(8,128)(2,1)}, bf16[2,192,1024]{2,1,0:T(8,128)(2,1)}, u32[]{:S(2)}, u32[]{:S(2)}) collective-permute-start(bf16[2,192,1024]{2,1,0:T(8,128)(2,1)} %get-tuple-element.90), channel_id=1, source_target_pairs={{0,1},{1,0},{2,3},{3,2},{4,5},{5,4},{6,7},{7,6},{8,9},{9,8},{10,11... | collective-permute-start | bytes 2359304 | tf_op jit(solution)/shard_map/ppermute | solution.py:45
  209.7 7.6 %collective-permute-start.27 = (bf16[2,192,1024]{2,1,0:T(8,128)(2,1)}, bf16[2,192,1024]{2,1,0:T(8,128)(2,1)}, u32[]{:S(2)}, u32[]{:S(2)}) collective-permute-start(bf16[2,192,1024]{2,1,0:T(8,128)(2,1)} %get-tuple-element.88), channel_id=1, source_target_pairs={{0,1},{1,0},{2,3},{3,2},{4,5},{5,4},{6,7},{7,6},{8,9},{9,8},{10,11... | collective-permute-start | bytes 2359304 | tf_op jit(solution)/shard_map/ppermute | solution.py:45
  210.1 9.4 %collective-permute-start.31 = (bf16[384,1024]{1,0:T(8,128)(2,1)}, bf16[384,1024]{1,0:T(8,128)(2,1)}, u32[]{:S(2)}, u32[]{:S(2)}) collective-permute-start(bf16[384,1024]{1,0:T(8,128)(2,1)} %get-tuple-element.93), channel_id=1, source_target_pairs={{0,1},{1,0},{2,3},{3,2},{4,5},{5,4},{6,7},{7,6},{8,9},{9,8},{10,11... | collective-permute-start | bytes 2359304 | tf_op jit(solution)/shard_map/ppermute | solution.py:45
  211.5 53.6 %collective-permute-start.28 = (bf16[2,192,1024]{2,1,0:T(8,128)(2,1)}, bf16[2,192,1024]{2,1,0:T(8,128)(2,1)}, u32[]{:S(2)}, u32[]{:S(2)}) collective-permute-start(bf16[2,192,1024]{2,1,0:T(8,128)(2,1)} %get-tuple-element.89), channel_id=1, source_target_pairs={{0,2},{1,3},{2,0},{3,1},{4,6},{5,7},{6,4},{7,5},{8,10},{9,11},{10,... | collective-permute-start | bytes 2359304 | tf_op jit(solution)/shard_map/ppermute | solution.py:45
  213.0 48.3 %collective-permute-start.34 = (bf16[3,384,1792]{2,1,0:T(8,128)(2,1)}, bf16[3,384,1792]{2,1,0:T(8,128)(2,1)}, u32[]{:S(2)}, u32[]{:S(2)}) collective-permute-start(bf16[3,384,1792]{2,1,0:T(8,128)(2,1)} %get-tuple-element.102), channel_id=1, source_target_pairs={{0,1},{1,0},{2,3},{3,2},{4,5},{5,4},{6,7},{7,6},{8,9},{9,8},{10,11... | collective-permute-start | bytes 12386312 | tf_op jit(solution)/shard_map/ppermute | solution.py:45
  213.1 52.0 %collective-permute-start.30 = (bf16[2,192,1024]{2,1,0:T(8,128)(2,1)}, bf16[2,192,1024]{2,1,0:T(8,128)(2,1)}, u32[]{:S(2)}, u32[]{:S(2)}) collective-permute-start(bf16[2,192,1024]{2,1,0:T(8,128)(2,1)} %collective-permute-done.29.refs_2_), channel_id=1, source_target_pairs={{0,2},{1,3},{2,0},{3,1},{4,6},{5,7},{6,4},{7,5},{8,10},{9,11},{10,... | collective-permute-start | bytes 2359304 | tf_op jit(solution)/shard_map/ppermute | solution.py:45
  217.3 42.9 %collective-permute-start.33 = (bf16[384,1792]{1,0:T(8,128)(2,1)}, bf16[384,1792]{1,0:T(8,128)(2,1)S(1)}, u32[]{:S(2)}, u32[]{:S(2)}) collective-permute-start(bf16[384,1792]{1,0:T(8,128)(2,1)} %fusion.3.refs_0_), channel_id=1, source_target_pairs={{0,4},{4,8},{8,12},{12,0},{1,5},{5,9},{9,13},{13,1},{2,6},{6,10},{... | collective-permute-start | bytes 4128776 | tf_op jit(solution)/shard_map/ppermute | solution.py:50
  265.1 46.9 %collective-permute-start.36 = (bf16[384,1792]{1,0:T(8,128)(2,1)}, bf16[384,1792]{1,0:T(8,128)(2,1)S(1)}, u32[]{:S(2)}, u32[]{:S(2)}) collective-permute-start(bf16[384,1792]{1,0:T(8,128)(2,1)} %fusion.2.refs_3_), channel_id=1, source_target_pairs={{0,4},{4,8},{8,12},{12,0},{1,5},{5,9},{9,13},{13,1},{2,6},{6,10},{... | collective-permute-start | bytes 4128776 | tf_op jit(solution)/shard_map/ppermute | solution.py:50
  280.8 28.0 %collective-permute-start.35 = (bf16[400,2048]{1,0:T(8,128)(2,1)}, bf16[400,2048]{1,0:T(8,128)(2,1)}, u32[]{:S(2)}, u32[]{:S(2)}) collective-permute-start(bf16[400,2048]{1,0:T(8,128)(2,1)} %get-tuple-element.108), channel_id=1, source_target_pairs={{0,1},{1,0},{2,3},{3,2},{4,5},{5,4},{6,7},{7,6},{8,9},{9,8},{10,11... | collective-permute-start | bytes 4915208 | tf_op jit(solution)/shard_map/ppermute | solution.py:45
  311.5 21.8 %collective-permute-start.37 = (bf16[208,2048]{1,0:T(8,128)(2,1)}, bf16[208,2048]{1,0:T(8,128)(2,1)}, u32[]{:S(2)}, u32[]{:S(2)}) collective-permute-start(bf16[208,2048]{1,0:T(8,128)(2,1)} %add_convert_fusion.1.refs_1_.refs_0_), channel_id=1, source_target_pairs={{0,2},{1,3},{2,0},{3,1},{4,6},{5,7},{6,4},{7,5},{8,10},{9,11},{10,... | collective-permute-start | bytes 2555912 | tf_op jit(solution)/shard_map/ppermute | solution.py:45
  316.8 40.0 %collective-permute-start.43 = (bf16[384,1792]{1,0:T(8,128)(2,1)}, bf16[384,1792]{1,0:T(8,128)(2,1)S(1)}, u32[]{:S(2)}, u32[]{:S(2)}) collective-permute-start(bf16[384,1792]{1,0:T(8,128)(2,1)} %fusion.1.refs_1_), channel_id=1, source_target_pairs={{0,4},{4,8},{8,12},{12,0},{1,5},{5,9},{9,13},{13,1},{2,6},{6,10},{... | collective-permute-start | bytes 4128776 | tf_op jit(solution)/shard_map/ppermute | solution.py:50
  327.8 19.6 %collective-permute-start.40 = (bf16[3,384,384]{2,1,0:T(8,128)(2,1)}, bf16[3,384,384]{2,1,0:T(8,128)(2,1)}, u32[]{:S(2)}, u32[]{:S(2)}) collective-permute-start(bf16[3,384,384]{2,1,0:T(8,128)(2,1)} %get-tuple-element.113), channel_id=1, source_target_pairs={{0,1},{1,0},{2,3},{3,2},{4,5},{5,4},{6,7},{7,6},{8,9},{9,8},{10,11... | collective-permute-start | bytes 2654216 | tf_op jit(solution)/shard_map/ppermute | solution.py:45
  346.9 15.3 %collective-permute-start.38 = (bf16[400,2048]{1,0:T(8,128)(2,1)}, bf16[400,2048]{1,0:T(8,128)(2,1)}, u32[]{:S(2)}, u32[]{:S(2)}) collective-permute-start(bf16[400,2048]{1,0:T(8,128)(2,1)} %get-tuple-element.111), channel_id=1, source_target_pairs={{0,1},{1,0},{2,3},{3,2},{4,5},{5,4},{6,7},{7,6},{8,9},{9,8},{10,11... | collective-permute-start | bytes 4915208 | tf_op jit(solution)/shard_map/ppermute | solution.py:45
  352.2 48.9 %collective-permute-start.45 = (bf16[384,640]{1,0:T(8,128)(2,1)}, bf16[384,640]{1,0:T(8,128)(2,1)}, u32[]{:S(2)}, u32[]{:S(2)}) collective-permute-start(bf16[384,640]{1,0:T(8,128)(2,1)} %concatenate.112), channel_id=1, source_target_pairs={{0,4},{4,8},{8,12},{12,0},{1,5},{5,9},{9,13},{13,1},{2,6},{6,10},{... | collective-permute-start | bytes 1474568 | tf_op jit(solution)/shard_map/ppermute | solution.py:50
  355.2 43.8 %collective-permute-start.44 = (bf16[384,640]{1,0:T(8,128)(2,1)}, bf16[384,640]{1,0:T(8,128)(2,1)}, u32[]{:S(2)}, u32[]{:S(2)}) collective-permute-start(bf16[384,640]{1,0:T(8,128)(2,1)} %concatenate.111), channel_id=1, source_target_pairs={{0,8},{4,12},{8,0},{12,4},{1,9},{5,13},{9,1},{13,5},{2,10},{6,14},... | collective-permute-start | bytes 1474568 | tf_op jit(solution)/shard_map/ppermute | solution.py:50
  361.6 41.6 %collective-permute-start.47 = (bf16[192,1792]{1,0:T(8,128)(2,1)}, bf16[192,1792]{1,0:T(8,128)(2,1)}, u32[]{:S(2)}, u32[]{:S(2)}) collective-permute-start(bf16[192,1792]{1,0:T(8,128)(2,1)} %slice.500), channel_id=1, source_target_pairs={{0,2},{1,3},{2,0},{3,1},{4,6},{5,7},{6,4},{7,5},{8,10},{9,11},{10,... | collective-permute-start | bytes 2064392 | tf_op jit(solution)/shard_map/ppermute | solution.py:45
  365.4 39.5 %collective-permute-start.39 = (bf16[208,2048]{1,0:T(8,128)(2,1)}, bf16[208,2048]{1,0:T(8,128)(2,1)}, u32[]{:S(2)}, u32[]{:S(2)}) collective-permute-start(bf16[208,2048]{1,0:T(8,128)(2,1)} %add_convert_fusion), channel_id=1, source_target_pairs={{0,2},{1,3},{2,0},{3,1},{4,6},{5,7},{6,4},{7,5},{8,10},{9,11},{10,... | collective-permute-start | bytes 2555912 | tf_op jit(solution)/shard_map/ppermute | solution.py:45
  367.5 37.5 %collective-permute-start.42 = (bf16[384,640]{1,0:T(8,128)(2,1)}, bf16[384,640]{1,0:T(8,128)(2,1)S(1)}, u32[]{:S(2)}, u32[]{:S(2)}) collective-permute-start(bf16[384,640]{1,0:T(8,128)(2,1)} %concatenate.110), channel_id=1, source_target_pairs={{0,12},{4,0},{8,4},{12,8},{1,13},{5,1},{9,5},{13,9},{2,14},{6,2},{... | collective-permute-start | bytes 1474568 | tf_op jit(solution)/shard_map/ppermute | solution.py:50
  404.4 21.2 %collective-permute-start.49 = (bf16[192,1792]{1,0:T(8,128)(2,1)S(1)}, bf16[192,1792]{1,0:T(8,128)(2,1)S(1)}, u32[]{:S(2)}, u32[]{:S(2)}) collective-permute-start(bf16[192,1792]{1,0:T(8,128)(2,1)S(1)} %add_convert_fusion.2.refs_16_), channel_id=1, source_target_pairs={{0,16},{16,0},{1,17},{17,1},{2,18},{18,2},{3,19},{19,3},{4,20},{20... | collective-permute-start | bytes 2064392 | tf_op jit(solution)/shard_map/ppermute | solution.py:54
  410.0 7.1 %collective-permute-start.46 = (bf16[192,640]{1,0:T(8,128)(2,1)S(1)}, bf16[192,640]{1,0:T(8,128)(2,1)S(1)}, u32[]{:S(2)}, u32[]{:S(2)}) collective-permute-start(bf16[192,640]{1,0:T(8,128)(2,1)S(1)} %concatenate.114.refs_13_), channel_id=1, source_target_pairs={{0,2},{1,3},{2,0},{3,1},{4,6},{5,7},{6,4},{7,5},{8,10},{9,11},{10,... | collective-permute-start | bytes 737288 | tf_op jit(solution)/shard_map/ppermute | solution.py:45
  418.3 12.6 %collective-permute-start.48 = (bf16[192,640]{1,0:T(8,128)(2,1)}, bf16[192,640]{1,0:T(8,128)(2,1)S(1)}, u32[]{:S(2)}, u32[]{:S(2)}) collective-permute-start(bf16[192,640]{1,0:T(8,128)(2,1)} %concatenate.115.refs_15_), channel_id=1, source_target_pairs={{0,16},{16,0},{1,17},{17,1},{2,18},{18,2},{3,19},{19,3},{4,20},{20... | collective-permute-start | bytes 737288 | tf_op jit(solution)/shard_map/ppermute | solution.py:54
  (55 other events, 515.3 us)

commit v4 on v3

--- a/solution.py
+++ b/solution.py
@@ -415,8 +415,8 @@
 
 
 def feed_kernel(sel, gain, *refs):
-    nears, pairs, crosses = refs[:4], refs[4:8], refs[8:11]
-    a_parts, dy_parts, x_parts = refs[11:15], refs[15:18], refs[18:25]
+    nears, pairs, crosses = refs[:4], refs[4:8], refs[8:12]
+    a_parts, dy_parts, x_parts = refs[12:16], refs[16:19], refs[19:26]
     outs = refs[-28:]
     boths, (ga_own, ga_other, gain_sum) = outs[:4], outs[4:7]
     g_near, g_one, g_rest = outs[7:10]
@@ -444,12 +444,13 @@
             nonlocal count
             for first, last, which, at in halves[which_half]:
                 if which in kinds:
+                    rows = slice(rel * FB, (rel + 1) * FB)
+                    if which == 1:
+                        target = w_out.at[rows, slot * 256 + at : slot * 256 + at + last - first]
+                    else:
+                        target = targets[which].at[slot, rows, at : at + last - first]
                     copies.append(
-                        pltpu.make_async_copy(
-                            source.at[:, offset + first : offset + last],
-                            targets[which].at[slot, rel * FB : (rel + 1) * FB, at : at + last - first],
-                            w_sems.at[slot, count],
-                        )
+                        pltpu.make_async_copy(source.at[:, offset + first : offset + last], target, w_sems.at[slot, count])
                     )
                 count += 1
 
@@ -461,8 +462,9 @@
                 add(crosses[0].at[slot], 1792 + (half ^ swapped) * 896, half, 3)
             else:
                 add(pairs[slot], half * 896, half, 1)
-                add(crosses[slot - 1].at[0], half * 896, half, 2)
-                add(crosses[slot - 1].at[1], half * 896, half, 3)
+                near, pair = (crosses[1].at[0], crosses[1].at[1]) if slot == 2 else crosses[2:]
+                add(near, half * 896, half, 2)
+                add(pair, half * 896, half, 3)
         return copies
 
     def a_loads():
@@ -470,34 +472,38 @@
         for half in range(2):
             cols = slice(half * B, (half + 1) * B)
             for side in range(2):
+                first_row = 512 * (core if side == 0 else 1 - core)
                 for source, target, size in HEAD_ROWS:
-                    part = a_parts[2 * side + half]
+                    at = pl.multiple_of(first_row + target // FB * 256 + target % FB, 64)
                     copies.append(
                         pltpu.make_async_copy(
-                            part.at[source : source + size, :],
-                            a_t.at[side * 384 + target : side * 384 + target + size, cols],
+                            a_parts[2 * side + half].at[source : source + size, :],
+                            a_t.at[pl.ds(at, size), cols],
                             a_sems.at[len(copies)],
                         )
                     )
         return copies
 
-    def token_loads():
+    def token_loads(group):
         copies = []
 
         def add(source, target):
-            copies.append(pltpu.make_async_copy(source, target, in_sems.at[len(copies)]))
+            copies.append(pltpu.make_async_copy(source, target, in_sems.at[group, len(copies)]))
 
         for half in range(2):
             cols = slice(half * B, (half + 1) * B)
             place = pl.ds(pl.multiple_of(sel[1 + half] * B, B), B)
             at_whole = pl.ds(pl.multiple_of((sel[1 + half] + 4 * half) * B, B), B)
-            add(dy_parts[0].at[:, at_whole], dy_t.at[0:FB, cols])
+            if group:
+                add(dy_parts[0].at[:, at_whole], dy_t.at[0:FB, cols])
+                continue
             add(x_parts[0].at[:, at_whole], x_t.at[0:FB, cols])
             for rel in range(1, 4):
                 add(x_parts[half * 3 + rel].at[:, place], x_t.at[rel * FB : (rel + 1) * FB, cols])
-        add(dy_parts[1].at[0], dy_t.at[FB : 2 * FB, :])
-        add(dy_parts[2].at[0], dy_t.at[2 * FB : 3 * FB, :])
-        add(dy_parts[2].at[1], dy_t.at[3 * FB :, :])
+        if group:
+            add(dy_parts[1].at[0], dy_t.at[FB : 2 * FB, :])
+            add(dy_parts[2].at[0], dy_t.at[2 * FB : 3 * FB, :])
+            add(dy_parts[2].at[1], dy_t.at[3 * FB :, :])
         return copies
 
     def stores(slot):
@@ -518,7 +524,7 @@
         far = g_one if slot == 1 else g_rest.at[(0, 0, 1, 2)[slot]]
         return [
             pltpu.make_async_copy(
-                stage_out.at[slot, pl.ds(side * 384, 384), :],
+                stage_out.at[pl.ds(side * 384, 384), slot * 256 : (slot + 1) * 256],
                 target.at[:, D : D + 256],
                 last_sems.at[slot, side],
             )
@@ -536,30 +542,24 @@
                     start(loads(slot, swapped, kinds))
 
     start_weights((1,))
-    start(token_loads())
-    start_weights((0, 2))
-
-    a_t[D:, :] = jnp.zeros((64, a_t.shape[1]), BF)
-
-    def a_rows(slot, count):
-        place = lax.rem(slot + 2 * core, 4) * FB
-        return pl.ds(pl.multiple_of(place, FB), count)
-
-    wait(token_loads())
-    dy[...] = dy_t[...].T
+    start(token_loads(0))
+    for slot in range(4):
+        a_t[slot * 256 + FB : (slot + 1) * 256, :] = jnp.zeros((64, a_t.shape[1]), BF)
     wait(a_loads())
     for slot in range(4):
         wait(loads(slot, 0, (1,)))
-    mixed = nn(w_out[0], a_t[a_rows(0, 256), :])
-    for slot in range(1, 4):
-        mixed = mixed + nn(w_out[slot], a_t[a_rows(slot, 256), :])
-    mid[...] = x_t[...].astype(F32) + mixed
+    wait(token_loads(0))
+    start(token_loads(1))
+    start_weights((0, 2))
+    mid[...] = x_t[...].astype(F32) + nn(w_out[...], a_t[...])
     mlp[...] = mid[...]
     gn[...] = jnp.zeros_like(gn)
     r2 = lax.rsqrt(jnp.sum(mid[...] * mid[...], axis=0, keepdims=True) * (1.0 / D) + EPSILON)
     n_t = x_t
     n_t[...] = (mid[...] * r2 * gain[...]).astype(BF)
     n[...] = n_t[...].T
+    wait(token_loads(1))
+    dy[...] = dy_t[...].T
 
     def chunk(slot, carry):
         buffer = lax.rem(slot, 2)
@@ -601,19 +601,20 @@
     for rel, both in enumerate(boths):
         both[1] = gm[rel * FB : (rel + 1) * FB]
     gain_sum[...] = jnp.sum(gn[...] * mid[...] * r2, axis=1, keepdims=True)
+    stage_out[...] = nt(x_t[...], a_t[...]).astype(BF)
     for slot in range(4):
-        grad_a = contract(w_out[slot], x_t[...], ((0,), (0,)))[:FB].astype(BF)
+        start(last_stores(slot))
+    grad_a = contract(w_out[...], x_t[...], ((0,), (0,))).astype(BF)
+    for slot in range(4):
 
         def place(target):
             for to, source, size in HEAD_ROWS:
                 if source // FB == slot % 2:
-                    target[to : to + size, :] = grad_a[source % FB : source % FB + size]
+                    row = slot * 256 + source % FB
+                    target[to : to + size, :] = grad_a[row : row + size]
 
         pl.when((slot // 2) == core)(functools.partial(place, ga_own))
         pl.when((slot // 2) != core)(functools.partial(place, ga_other))
-        part = nt(x_t[...], a_t[a_rows(slot, FB), :])
-        stage_out[slot] = jnp.concatenate([part, jnp.zeros((D, 64), F32)], axis=1).astype(BF)
-        start(last_stores(slot))
     wait(stores(2))
     wait(stores(3))
     for slot in range(4):
@@ -635,8 +636,8 @@
         scratch_shapes=[
             pltpu.VMEM((4, D, D), BF),
             pltpu.VMEM((4, D, D), BF),
-            pltpu.VMEM((4, D, 256), BF),
-            pltpu.VMEM((D + 64, count), BF),
+            pltpu.VMEM((D, 1024), BF),
+            pltpu.VMEM((1024, count), BF),
             pltpu.VMEM((D, count), BF),
             pltpu.VMEM((D, count), BF),
             pltpu.VMEM((count, D), BF),
@@ -645,10 +646,10 @@
             pltpu.VMEM((D, count), F32),
             pltpu.VMEM((D, count), F32),
             pltpu.VMEM((2, 2, D, D), BF),
-            pltpu.VMEM((4, D, 256), BF),
+            pltpu.VMEM((D, 1024), BF),
             pltpu.SemaphoreType.DMA((4, 16)),
             pltpu.SemaphoreType.DMA((16,)),
-            pltpu.SemaphoreType.DMA((13,)),
+            pltpu.SemaphoreType.DMA((2, 8)),
             pltpu.SemaphoreType.DMA((2, 4)),
             pltpu.SemaphoreType.DMA((4, 2)),
         ],
@@ -879,7 +880,7 @@
 
     w_near = jnp.stack([merge(*w_slots[:2]), merge(*w_slots[2:])])
     pair_low = tie(cols_swap(own_low, 2), w_near)
-    x_low = (pair_low, cols_swap(own_low, 1), cols_swap(pair_low, 1))
+    x_low = (pair_low, cols_swap(tie(own_low, w_near), 1), cols_swap(pair_low, 1))
     own_pack = jnp.concatenate([w_up, w_out.T, jnp.zeros((FB, 64), BF), w_down], axis=1)
     dy_core = hold(away[:2], grad_y, B)
     dy_away = hold(away[2:], grad_y, B)
@@ -925,8 +926,9 @@
     dy_cross = cols_swap(dy_cross_sent, 1)
     third_cross = cols_swap(third_cross_sent, 1)
     first_cross = cols_swap(jnp.concatenate([jnp.stack(ring[:2]), first_pairs, first_crossed], axis=2), 1)
+    last_cross = cols_swap(ring[3], 1)
     last_pair = tie(cols_swap(ring[3], 2), log_high)
-    last_cross = cols_swap(jnp.stack([ring[3], last_pair]), 1)
+    last_cross = (last_cross, cols_swap(last_pair, 1))
     high_got = cols_swap(out_high[1], 1)
     log_low, log_high = jnp.concatenate([log_first, log_low]), jnp.concatenate([log_other, log_high])
 
@@ -936,7 +938,7 @@
         gain_two,
         ring,
         (first_pairs, first_crossed, third_pair, last_pair),
-        (first_cross, third_cross, last_cross),
+        (first_cross, third_cross, *last_cross),
         (out_low[0], out_high[0], low_got, high_got),
         (grad_y, dy_pair, dy_cross),
         (block_input, *x_low, *x_high),
@@ -974,7 +976,8 @@
         low_order, w_qkv, normed_low, dq_low, dkv_low, 0, gain_part, wg_near, pair_sent
     )
 
-    wg_got = tie(cols_swap(wg_far, 1), near_low)
+    ring_got = tie(rows_shift(total, 1), near_low)
+    wg_got = tie(cols_swap(wg_far, 1), near_low, ring_got)
     by_core = jnp.where(core == 0, wg_near, wg_got), jnp.where(core == 0, wg_got, wg_near)
 
     def split(values):
@@ -984,8 +987,8 @@
         return jnp.concatenate(parts, axis=1).astype(BF)
 
     def unsplit(columns):
-        columns = columns.astype(F32)
-        return columns[:, 576:578] + columns[:, 578:580] + columns[:, 580:582]
+        columns = columns[:, 576:582].astype(F32)
+        return columns[:, :2] + columns[:, 2:4] + columns[:, 4:]
 
     gains = jnp.concatenate([gain_part / gain_one, gain_two_sum], axis=1).T
     gains = split((gains[:, :384] + cols_swap(gains[:, 384:], 1)).T)
@@ -999,7 +1002,7 @@
     slots = [slot_of(slot) for slot in range(4)]
     got_low = tie(cols_swap(far_low, 1), wg_near)
     sent_low = two(near_low[FB:], got_low[FB:])
-    total = three(tie(rows_shift(total, 1), near_low), g_near[0], g_got[0])
+    total = three(ring_got, g_near[0], g_got[0])
 
     def dp_sum(part, *deps):
         if lax.axis_size("dp") == 2:

time: 440 us -> 432 us (0.982)
  other arithmetic: 50.2 us -> 44.4 us
  waiting for transfers between devices: 60.3 us -> 65.4 us
  Pallas kernels: 249 us -> 244 us
    pallas_call x1, Pallas kernels: 52.8 us -> 47.5 us  [feed_forward(): pl.pallas_call(feed_kernel, in_specs=[pl.BlockSpec(memory_space=pltpu.SME...]
    unnamed x108 -> x84, local copies, waits for them, and re-layouts: 13 us -> 9.98 us
    ppermute x35 -> x36, starting transfers between devices: 19.6 us -> 21.7 us  [cols_swap(): lax.ppermute(value, 'cols', [(i, i ^ distance) for i in range(lax.axis_si...]
    ppermute x35 -> x36, waiting for transfers between devices: 8.62 us -> 9.94 us  [cols_swap(): lax.ppermute(value, 'cols', [(i, i ^ distance) for i in range(lax.axis_si...]
  transfers between devices with their start and end apart: 50 -> 51, of which waited for: 8 -> 11; matrix products, arithmetic and copies ran while one was open for 15% -> 15% of each run, Pallas kernels for 45% -> 46%
where the time goes in v4:
time: 432 us; the launch traced here: 427 us
  Pallas kernels  244 us (56%)
  waiting for transfers between devices  65.4 us (15%)
  other arithmetic  44.4 us (10%)
  starting transfers between devices  40.3 us (9%)
  local copies, waits for them, and re-layouts  31.6 us (7%)
    pallas_call x2, Pallas kernels, attend_back(): pl.pallas_call(functools.partial(attend_back_kernel, counts=(4,) if half...  69.1 us
    ppermute x12, waiting for transfers between devices, rows_shift(): lax.ppermute(value, 'rows', [(i, (i + step) % count) for i in range(count)])  55.4 us
    pallas_call x1, Pallas kernels, feed_forward(): pl.pallas_call(feed_kernel, in_specs=[pl.BlockSpec(memory_space=pltpu.SME...  47.5 us
    pallas_call x4, Pallas kernels, attend(): pl.pallas_call(functools.partial(attend_kernel, counts=(4,) if half else...  45.7 us
    pallas_call x2, Pallas kernels, project_half(): pl.pallas_call(functools.partial(qkv_kernel, first=first, extra=extra), g...  25.2 us
    pallas_call x2, Pallas kernels, project_back(): pl.pallas_call(functools.partial(qkv_back_kernel, half=half), grid_spec=p...  25.1 us
    ppermute x36, starting transfers between devices, cols_swap(): lax.ppermute(value, 'cols', [(i, i ^ distance) for i in range(lax.axis_si...  21.7 us
    ppermute x12, starting transfers between devices, rows_shift(): lax.ppermute(value, 'rows', [(i, (i + step) % count) for i in range(count)])  15.3 us
  transfers between devices with their start and end apart: 51, of which 11 were waited for; matrix products, arithmetic and copies ran while one was open for 15% of the time, Pallas kernels for 46%

profile of v4, /device:TPU:24, one launch (start us, length us, event | category | flops | bytes accessed | tf_op | source)
XLA Modules:
  0.0 427.3 jit_solution(12707058389423408698)
XLA Ops:
  0.7 1.9 shard_map.240
  3.0 3.7 collective-permute-start.2
  6.9 1.5 collective-permute-start
  12.5 2.4 shard_map.244.refs_3_
  15.0 7.0 %collective-permute-done.3 = bf16[192,576]{1,0:T(8,128)(2,1)S(1)} collective-permute-done((bf16[192,576]{1,0:T(8,128)(2,1)}, bf16[192,576]{1,0:T(8,128)(2,1)S(1)}, u32[]{:S(2)}, u32[]{:S(2)}) %collective-permute-start.3) | collective-permute-done | bytes 221216 | tf_op jit(solution)/shard_map/ppermute | solution.py:50
  24.6 1.6 collective-permute-start.10
  26.2 1.9 collective-permute-done.7.refs_0_
  32.4 4.1 shard_map.245.refs_4_.refs_0_
  36.4 13.5 %collective-permute-done.5.refs_5_.refs_1_ = bf16[192,1792]{1,0:T(8,128)(2,1)S(1)} collective-permute-done((bf16[192,1792]{1,0:T(8,128)(2,1)}, bf16[192,1792]{1,0:T(8,128)(2,1)S(1)}, u32[]{:S(2)}, u32[]{:S(2)}) %collective-permute-start.5) | collective-permute-done | bytes 688160 | tf_op jit(solution)/shard_map/ppermute | solution.py:50
  51.3 2.2 shard_map.247
  58.2 13.0 %shard_map.248 = (bf16[768,2048]{1,0:T(8,128)(2,1)}, f32[1,2048]{1,0:T(1,128)}, bf16[384,1024]{1,0:T(8,128)(2,1)}, bf16[4096,384]{1,0:T(8,128)(2,1)}, bf16[384,4...) custom-call(s32[5]{0:T(128)} %pad_add_fusion.3.tab, ...), custom_call_target="tpu_custom_call" | custom-call | flops 13799999488 | tf_op jit(solution)/shard_map/pallas_call | solution.py:197
  71.2 2.1 collective-permute-start.16
  73.3 7.4 %shard_map.250 = (bf16[384,512]{1,0:T(8,128)(2,1)}, bf16[384,512]{1,0:T(8,128)(2,1)}, f32[1,2,1024]{2,1,0:T(2,128)}) custom-call(s32[18]{0:T(128)} %get-tuple-element.229.tab, bf16[384,1024]{1,0:T(8,128)(2,1)} %get-tuple-element.65.q_t, bf16[4096,384]{1,0:T(8,128)(2,1)} %get-tuple-element.66.k.refs_6_, bf16[384,4096]{1,0:T(8,128)(2,1)} %get-tuple-element.67.v_t.refs_9_, ...), custom_call_target="tpu_custom_call" | custom-call | flops 6899999744 | tf_op jit(solution)/shard_map/pallas_call | solution.py:302
  82.0 12.3 %shard_map.254 = (bf16[384,512]{1,0:T(8,128)(2,1)}, bf16[384,512]{1,0:T(8,128)(2,1)}, f32[2,2,1024]{2,1,0:T(2,128)}) custom-call(s32[18]{0:T(128)} %get-tuple-element.229.tab, bf16[384,1024]{1,0:T(8,128)(2,1)} %get-tuple-element.65.q_t, bf16[4096,384]{1,0:T(8,128)(2,1)} %get-tuple-element.66.k.refs_6_, ...), custom_call_target="tpu_custom_call", output_to_operand_aliasing={{0}: (4, {}), {1}: (5, {})} | custom-call | flops 13799999488 | tf_op jit(solution)/shard_map/pallas_call | solution.py:302
  95.7 2.2 collective-permute-done.13.refs_0_
  98.3 1.5 collective-permute-start.18
  99.8 12.2 %shard_map.256 = (bf16[768,2048]{1,0:T(8,128)(2,1)}, f32[1,2048]{1,0:T(1,128)}, bf16[384,1024]{1,0:T(8,128)(2,1)}, bf16[4096,384]{1,0:T(8,128)(2,1)}, bf16[384,4...) custom-call(s32[5]{0:T(128)} %pad_add_fusion.4.tab, ...), custom_call_target="tpu_custom_call", output_to_operand_aliasing={{3}: (7, {}), {4}: (8, {}), {5}: (9, {}), {6}: (10, {})} | custom-call | flops 13799999488 | tf_op jit(solution)/shard_map/pallas_call | solution.py:197
  112.8 9.9 %shard_map.257 = (bf16[384,512]{1,0:T(8,128)(2,1)}, bf16[384,512]{1,0:T(8,128)(2,1)}, f32[1,2,1024]{2,1,0:T(2,128)}) custom-call(s32[18]{0:T(128)} %get-tuple-element.228.tab, bf16[384,1024]{1,0:T(8,128)(2,1)} %get-tuple-element.76.q_t, bf16[4096,384]{1,0:T(8,128)(2,1)} %get-tuple-element.77.k, bf16[384,4096]{1,0:T(8,128)(2,1)} %get-tuple-element.78.v_t, ...), custom_call_target="tpu_custom_call" | custom-call | flops 9200000000 | tf_op jit(solution)/shard_map/pallas_call | solution.py:302
  122.7 1.7 collective-permute-start.20
  125.5 3.1 pad_maximum_fusion
  130.3 1.4 pad_maximum_fusion.1.refs_5_
  132.8 16.1 %shard_map.263 = (bf16[384,512]{1,0:T(8,128)(2,1)}, bf16[384,512]{1,0:T(8,128)(2,1)}, f32[2,2,1024]{2,1,0:T(2,128)}) custom-call(s32[18]{0:T(128)} %get-tuple-element.228.tab, bf16[384,1024]{1,0:T(8,128)(2,1)} %get-tuple-element.76.q_t, bf16[4096,384]{1,0:T(8,128)(2,1)} %get-tuple-element.77.k, ...), custom_call_target="tpu_custom_call", output_to_operand_aliasing={{0}: (4, {}), {1}: (5, {})} | custom-call | flops 18400000000 | tf_op jit(solution)/shard_map/pallas_call | solution.py:302
  152.9 47.5 %shard_map.265 = (bf16[2,192,1024]{2,1,0:T(8,128)(2,1)}, bf16[2,192,1024]{2,1,0:T(8,128)(2,1)}, bf16[2,192,1024]{2,1,0:T(8,128)(2,1)}, bf16[2,192,1024]{2,1,0:T(...) custom-call(s32[4]{0:T(128)} %pad_add_fusion.2.sel, ...), custom_call_target="tpu_custom_call" | custom-call | flops 57500000256 | tf_op jit(solution)/shard_map/pallas_call | solution.py:630
  206.2 2.7 fusion.3.refs_0_
  208.9 3.3 collective-permute-start.34
  212.2 41.0 %shard_map.266 = (bf16[384,1024]{1,0:T(8,128)(2,1)}, bf16[3,2048,256]{2,1,0:T(8,128)(2,1)}, f32[3,2048,256]{2,1,0:T(8,128)}) custom-call(s32[18]{0:T(128)} %get-tuple-element.228.tab, bf16[384,1024]{1,0:T(8,128)(2,1)} %get-tuple-element.76.q_t, bf16[384,1024]{1,0:T(8,128)(2,1)} %get-tuple-element.92.do_own, ...), custom_call_target="tpu_custom_call" | custom-call | flops 55199997952 | tf_op jit(solution)/shard_map/pallas_call | solution.py:384
  254.3 3.7 fusion.2.refs_3_
  259.5 14.9 %shard_map.268 = (bf16[400,2048]{1,0:T(8,128)(2,1)}, bf16[400,2048]{1,0:T(8,128)(2,1)}, f32[768,1]{1,0:T(8,128)}, f32[3,768,384]{2,1,0:T(8,128)}) custom-call(s32[5]{0:T(128)} %pad_add_fusion.4.tab, bf16[768,1152]{1,0:T(8,128)(2,1)} %get-tuple-element.73.refs_5_.w, bf16[768,2048]{1,0:T(8,128)(2,1)} %get-tuple-element.99.n_t, ...), custom_call_target="tpu_custom_call" | custom-call | flops 17250000896 | tf_op jit(solution)/shard_map/pallas_call | solution.py:719
  274.5 28.1 %shard_map.269 = (bf16[384,1024]{1,0:T(8,128)(2,1)}, bf16[3,2048,256]{2,1,0:T(8,128)(2,1)}) custom-call(s32[18]{0:T(128)} %get-tuple-element.229.tab, bf16[384,1024]{1,0:T(8,128)(2,1)} %get-tuple-element.65.q_t, bf16[384,1024]{1,0:T(8,128)(2,1)} %get-tuple-element.92.do_own, bf16[384,1024]{1,0:T(8,128)(2,1)} %collective-permute-done.32.do_other, ...), custom_call_target="tpu_custom_call" | custom-call | flops 41400000512 | tf_op jit(solution)/shard_map/pallas_call | solution.py:384
  302.6 2.6 add_convert_fusion.1.refs_1_.refs_0_
  306.9 3.7 fusion.1.refs_1_
  311.0 9.0 %shard_map.272 = (bf16[3,384,384]{2,1,0:T(8,128)(2,1)}, bf16[3,384,384]{2,1,0:T(8,128)(2,1)}) custom-call(s32[5]{0:T(128)} %pad_add_fusion.3.tab, bf16[768,2048]{1,0:T(8,128)(2,1)} %get-tuple-element.91.n_t, bf16[384,1024]{1,0:T(8,128)(2,1)} %get-tuple-element.104.refs_1_.dq_t.refs_0_, bf16[3,2048,256]{2,1,0:T(8,128)(2,1)} %get-tuple-element.105.dkv.refs_1_, ...), custom_call_target="tpu_custom_call" | custom-call | flops 9200000000 | tf_op jit(solution)/shard_map/pallas_call | solution.py:750
  320.3 6.8 %collective-permute-done.38.refs_4_.refs_6_.refs_9_ = bf16[208,2048]{1,0:T(8,128)(2,1)} collective-permute-done((bf16[208,2048]{1,0:T(8,128)(2,1)}, bf16[208,2048]{1,0:T(8,128)(2,1)}, u32[]{:S(2)}, u32[]{:S(2)}) %collective-permute-start.38) | collective-permute-done | bytes 852000 | tf_op jit(solution)/shard_map/ppermute | solution.py:45
  327.1 10.2 %shard_map.273 = (bf16[400,2048]{1,0:T(8,128)(2,1)}, bf16[400,2048]{1,0:T(8,128)(2,1)}, f32[768,1]{1,0:T(8,128)}) custom-call(s32[5]{0:T(128)} %pad_add_fusion.3.tab, bf16[768,1152]{1,0:T(8,128)(2,1)} %get-tuple-element.73.refs_5_.w, bf16[768,2048]{1,0:T(8,128)(2,1)} %get-tuple-element.91.n_t, bf16[384,1024]{1,0:T(8,128)(2,1)} %get-tuple-element.104.refs_1_.dq_t.refs_0_, ...), custom_call_target="tpu_custom_call" | custom-call | flops 11500000256 | tf_op jit(solution)/shard_map/pallas_call | solution.py:719
  341.3 2.3 collective-permute-done.42.refs_0_
  348.6 2.1 collective-permute-start.46
  354.1 1.8 concatenate.109
  355.9 2.2 fusion.refs_2_
  359.2 1.7 collective-permute-start.48
  360.9 1.4 add_convert_fusion
  362.4 1.5 collective-permute-start.40
  363.9 30.4 %collective-permute-done.45 = bf16[384,640]{1,0:T(8,128)(2,1)} collective-permute-done((bf16[384,640]{1,0:T(8,128)(2,1)}, bf16[384,640]{1,0:T(8,128)(2,1)}, u32[]{:S(2)}, u32[]{:S(2)}) %collective-permute-start.45) | collective-permute-done | bytes 491552 | tf_op jit(solution)/shard_map/ppermute | solution.py:50
  396.3 2.1 add_convert_fusion.2.refs_16_
  400.0 1.7 add_convert_fusion.3
  402.4 2.2 collective-permute-start.47
  404.6 5.8 %shard_map.278 = (bf16[192,4096]{1,0:T(8,128)(2,1)}, f32[192,4096]{1,0:T(8,128)}) custom-call(s32[10]{0:T(128)} %pad_add_fusion.5.sel, bf16[2,192,1024]{2,1,0:T(8,128)(2,1)} %get-tuple-element.87.refs_0_, bf16[2,192,1024]{2,1,0:T(8,128)(2,1)} %collective-permute-done.28.refs_1_, bf16[2,192,1024]{2,1,0:T(8,128)(2,1)} %collective-permute-done.29.refs_4_.refs_2_, ...), custom_call_target="tpu_custom_call" | custom-call | flops 6899999744 | tf_op jit(solution)/shard_map/pallas_call | solution.py:794
  412.9 5.8 %shard_map.279 = (bf16[192,4096]{1,0:T(8,128)(2,1)}, f32[192,4096]{1,0:T(8,128)}) custom-call(s32[10]{0:T(128)} %pad_add_fusion.sel, bf16[2,192,1024]{2,1,0:T(8,128)(2,1)} %get-tuple-element.87.refs_0_, bf16[2,192,1024]{2,1,0:T(8,128)(2,1)} %collective-permute-done.28.refs_1_, ...), custom_call_target="tpu_custom_call", output_to_operand_aliasing={{0}: (14, {}), {1}: (15, {})} | custom-call | flops 6899999744 | tf_op jit(solution)/shard_map/pallas_call | solution.py:794
  419.6 1.4 convert_add_fusion.7
  (270 shorter events, 66.5 us)
Async XLA Ops:
  2.6 19.4 %collective-permute-start.3 = (bf16[192,576]{1,0:T(8,128)(2,1)}, bf16[192,576]{1,0:T(8,128)(2,1)S(1)}, u32[]{:S(2)}, u32[]{:S(2)}) collective-permute-start(bf16[192,576]{1,0:T(8,128)(2,1)} %shard_map.240), channel_id=1, source_target_pairs={{0,8},{4,12},{8,0},{12,4},{1,9},{5,13},{9,1},{13,5},{2,10},{6,14},... | collective-permute-start | bytes 663560 | tf_op jit(solution)/shard_map/ppermute | solution.py:50
  2.9 19.1 %collective-permute-start.4 = (bf16[192,576]{1,0:T(8,128)(2,1)}, bf16[192,576]{1,0:T(8,128)(2,1)S(1)}, u32[]{:S(2)}, u32[]{:S(2)}) collective-permute-start(bf16[192,576]{1,0:T(8,128)(2,1)} %shard_map.240), channel_id=1, source_target_pairs={{0,12},{4,0},{8,4},{12,8},{1,13},{5,1},{9,5},{13,9},{2,14},{6,2},{... | collective-permute-start | bytes 663560 | tf_op jit(solution)/shard_map/ppermute | solution.py:50
  3.0 19.3 %collective-permute-start.2 = (bf16[192,576]{1,0:T(8,128)(2,1)}, bf16[192,576]{1,0:T(8,128)(2,1)}, u32[]{:S(2)}, u32[]{:S(2)}) collective-permute-start(bf16[192,576]{1,0:T(8,128)(2,1)} %shard_map.240), channel_id=1, source_target_pairs={{0,4},{4,8},{8,12},{12,0},{1,5},{5,9},{9,13},{13,1},{2,6},{6,10},{... | collective-permute-start | bytes 663560 | tf_op jit(solution)/shard_map/ppermute | solution.py:50
  6.9 29.6 %collective-permute-start = (f32[400]{0:T(512)S(1)}, f32[400]{0:T(512)S(1)}, u32[]{:S(2)}, u32[]{:S(2)}) collective-permute-start(f32[400]{0:T(512)S(1)} %pad_maximum_fusion.12), channel_id=1, source_target_pairs={{0,2},{1,3},{2,0},{3,1},{4,6},{5,7},{6,4},{7,5},{8,10},{9,11},{10,... | collective-permute-start | bytes 4808 | tf_op jit(solution)/shard_map/ppermute | solution.py:45
  9.4 18.6 %collective-permute-start.7 = (bf16[192,2048]{1,0:T(8,128)(2,1)S(1)}, bf16[192,2048]{1,0:T(8,128)(2,1)}, u32[]{:S(2)}, u32[]{:S(2)}) collective-permute-start(bf16[192,2048]{1,0:T(8,128)(2,1)S(1)} %get-tuple-element.177.refs_0_), channel_id=1, source_target_pairs={{0,2},{1,3},{2,0},{3,1},{4,6},{5,7},{6,4},{7,5},{8,10},{9,11},{10,... | collective-permute-start | bytes 2359304 | tf_op jit(solution)/shard_map/ppermute | solution.py:45
  24.6 25.3 %collective-permute-start.10 = (bf16[2,192,1152]{2,1,0:T(8,128)(2,1)S(1)}, bf16[2,192,1152]{2,1,0:T(8,128)(2,1)S(1)}, u32[]{:S(2)}, u32[]{:S(2)}) collective-permute-start(bf16[2,192,1152]{2,1,0:T(8,128)(2,1)S(1)} %pad_maximum_fusion.2.refs_1_.first.refs_5_), channel_id=1, source_target_pairs={{0,2},{1,3},{2,0},{3,1},{4,6},{5,7},{6,4},{7,5},{8,10},{9,11},{10,... | collective-permute-start | bytes 2654216 | tf_op jit(solution)/shard_map/ppermute | solution.py:45
  28.1 21.8 %collective-permute-start.8 = (bf16[192,2048]{1,0:T(8,128)(2,1)}, bf16[192,2048]{1,0:T(8,128)(2,1)S(1)}, u32[]{:S(2)}, u32[]{:S(2)}) collective-permute-start(bf16[192,2048]{1,0:T(8,128)(2,1)} %shard_map.243), channel_id=1, source_target_pairs={{0,1},{1,0},{2,3},{3,2},{4,5},{5,4},{6,7},{7,6},{8,9},{9,8},{10,11... | collective-permute-start | bytes 2359304 | tf_op jit(solution)/shard_map/ppermute | solution.py:45
  28.2 21.8 %collective-permute-start.9 = (bf16[192,2048]{1,0:T(8,128)(2,1)}, bf16[192,2048]{1,0:T(8,128)(2,1)}, u32[]{:S(2)}, u32[]{:S(2)}) collective-permute-start(bf16[192,2048]{1,0:T(8,128)(2,1)} %shard_map.242.refs_1_.refs_20_), channel_id=1, source_target_pairs={{0,1},{1,0},{2,3},{3,2},{4,5},{5,4},{6,7},{7,6},{8,9},{9,8},{10,11... | collective-permute-start | bytes 2359304 | tf_op jit(solution)/shard_map/ppermute | solution.py:45
  30.5 19.4 %collective-permute-start.5 = (bf16[192,1792]{1,0:T(8,128)(2,1)}, bf16[192,1792]{1,0:T(8,128)(2,1)S(1)}, u32[]{:S(2)}, u32[]{:S(2)}) collective-permute-start(bf16[192,1792]{1,0:T(8,128)(2,1)} %shard_map.241.refs_0_), channel_id=1, source_target_pairs={{0,4},{4,8},{8,12},{12,0},{1,5},{5,9},{9,13},{13,1},{2,6},{6,10},{... | collective-permute-start | bytes 2064392 | tf_op jit(solution)/shard_map/ppermute | solution.py:50
  36.4 21.7 %collective-permute-start.14 = (bf16[192,2048]{1,0:T(8,128)(2,1)}, bf16[192,2048]{1,0:T(8,128)(2,1)}, u32[]{:S(2)}, u32[]{:S(2)}) collective-permute-start(bf16[192,2048]{1,0:T(8,128)(2,1)} %get-tuple-element.176.refs_0_), channel_id=1, source_target_pairs={{0,1},{1,0},{2,3},{3,2},{4,5},{5,4},{6,7},{7,6},{8,9},{9,8},{10,11... | collective-permute-start | bytes 2359304 | tf_op jit(solution)/shard_map/ppermute | solution.py:45
  49.9 3.9 collective-permute-start.1
  53.5 4.6 %collective-permute-start.11 = (bf16[2,192,1152]{2,1,0:T(8,128)(2,1)}, bf16[2,192,1152]{2,1,0:T(8,128)(2,1)}, u32[]{:S(2)}, u32[]{:S(2)}) collective-permute-start(bf16[2,192,1152]{2,1,0:T(8,128)(2,1)} %shard_map.247), channel_id=1, source_target_pairs={{0,1},{1,0},{2,3},{3,2},{4,5},{5,4},{6,7},{7,6},{8,9},{9,8},{10,11... | collective-permute-start | bytes 2654216 | tf_op jit(solution)/shard_map/ppermute | solution.py:45
  55.7 25.0 %collective-permute-start.6 = (bf16[192,1792]{1,0:T(8,128)(2,1)S(1)}, bf16[192,1792]{1,0:T(8,128)(2,1)}, u32[]{:S(2)}, u32[]{:S(2)}) collective-permute-start(bf16[192,1792]{1,0:T(8,128)(2,1)S(1)} %copy-done.7), channel_id=1, source_target_pairs={{0,4},{4,8},{8,12},{12,0},{1,5},{5,9},{9,13},{13,1},{2,6},{6,10},{... | collective-permute-start | bytes 2064392 | tf_op jit(solution)/shard_map/ppermute | solution.py:50
  58.2 23.8 %collective-permute-start.12 = (bf16[192,2048]{1,0:T(8,128)(2,1)}, bf16[192,2048]{1,0:T(8,128)(2,1)}, u32[]{:S(2)}, u32[]{:S(2)}) collective-permute-start(bf16[192,2048]{1,0:T(8,128)(2,1)} %shard_map.252), channel_id=1, source_target_pairs={{0,2},{1,3},{2,0},{3,1},{4,6},{5,7},{6,4},{7,5},{8,10},{9,11},{10,... | collective-permute-start | bytes 2359304 | tf_op jit(solution)/shard_map/ppermute | solution.py:45
  71.2 27.1 %collective-permute-start.16 = (bf16[2,192,896]{2,1,0:T(8,128)(2,1)}, bf16[2,192,896]{2,1,0:T(8,128)(2,1)}, u32[]{:S(2)}, u32[]{:S(2)}) collective-permute-start(bf16[2,192,896]{2,1,0:T(8,128)(2,1)} %shard_map.249.refs_0_), channel_id=1, source_target_pairs={{0,2},{1,3},{2,0},{3,1},{4,6},{5,7},{6,4},{7,5},{8,10},{9,11},{10,... | collective-permute-start | bytes 2064392 | tf_op jit(solution)/shard_map/ppermute | solution.py:45
  80.7 17.3 %collective-permute-start.13 = (bf16[192,1792]{1,0:T(8,128)(2,1)}, bf16[192,1792]{1,0:T(8,128)(2,1)}, u32[]{:S(2)}, u32[]{:S(2)}) collective-permute-start(bf16[192,1792]{1,0:T(8,128)(2,1)} %shard_map.251.refs_4_.refs_0_), channel_id=1, source_target_pairs={{0,4},{4,8},{8,12},{12,0},{1,5},{5,9},{9,13},{13,1},{2,6},{6,10},{... | collective-permute-start | bytes 2064392 | tf_op jit(solution)/shard_map/ppermute | solution.py:50
  82.0 17.8 %collective-permute-start.15 = (bf16[192,2048]{1,0:T(8,128)(2,1)}, bf16[192,2048]{1,0:T(8,128)(2,1)}, u32[]{:S(2)}, u32[]{:S(2)}) collective-permute-start(bf16[192,2048]{1,0:T(8,128)(2,1)} %shard_map.253.refs_3_.refs_1_.refs_23_), channel_id=1, source_target_pairs={{0,1},{1,0},{2,3},{3,2},{4,5},{5,4},{6,7},{7,6},{8,9},{9,8},{10,11... | collective-permute-start | bytes 2359304 | tf_op jit(solution)/shard_map/ppermute | solution.py:45
  94.3 17.7 %collective-permute-start.17 = (bf16[384,512]{1,0:T(8,128)(2,1)}, bf16[384,512]{1,0:T(8,128)(2,1)S(1)}, u32[]{:S(2)}, u32[]{:S(2)}) collective-permute-start(bf16[384,512]{1,0:T(8,128)(2,1)} %get-tuple-element.79.o_other), channel_id=1, source_target_pairs={{0,1},{1,0},{2,3},{3,2},{4,5},{5,4},{6,7},{7,6},{8,9},{9,8},{10,11... | collective-permute-start | bytes 1179656 | tf_op jit(solution)/shard_map/ppermute | solution.py:45
  94.8 29.6 %collective-permute-start.21 = (bf16[2,192,1024]{2,1,0:T(8,128)(2,1)}, bf16[2,192,1024]{2,1,0:T(8,128)(2,1)}, u32[]{:S(2)}, u32[]{:S(2)}) collective-permute-start(bf16[2,192,1024]{2,1,0:T(8,128)(2,1)} %shard_map.261), channel_id=1, source_target_pairs={{0,2},{1,3},{2,0},{3,1},{4,6},{5,7},{6,4},{7,5},{8,10},{9,11},{10,... | collective-permute-start | bytes 2359304 | tf_op jit(solution)/shard_map/ppermute | solution.py:45
  98.0 32.3 %collective-permute-start.19 = (bf16[192,1792]{1,0:T(8,128)(2,1)}, bf16[192,1792]{1,0:T(8,128)(2,1)}, u32[]{:S(2)}, u32[]{:S(2)}) collective-permute-start(bf16[192,1792]{1,0:T(8,128)(2,1)} %shard_map.255.refs_2_), channel_id=1, source_target_pairs={{0,2},{1,3},{2,0},{3,1},{4,6},{5,7},{6,4},{7,5},{8,10},{9,11},{10,... | collective-permute-start | bytes 2064392 | tf_op jit(solution)/shard_map/ppermute | solution.py:45
  98.3 27.1 %collective-permute-start.18 = (bf16[2,192,896]{2,1,0:T(8,128)(2,1)}, bf16[2,192,896]{2,1,0:T(8,128)(2,1)}, u32[]{:S(2)}, u32[]{:S(2)}) collective-permute-start(bf16[2,192,896]{2,1,0:T(8,128)(2,1)} %collective-permute-done.16.refs_11_.refs_4_), channel_id=1, source_target_pairs={{0,16},{16,0},{1,17},{17,1},{2,18},{18,2},{3,19},{19,3},{4,20},{20... | collective-permute-start | bytes 2064392 | tf_op jit(solution)/shard_map/ppermute | solution.py:54
  122.7 26.2 %collective-permute-start.20 = (bf16[192,1792]{1,0:T(8,128)(2,1)}, bf16[192,1792]{1,0:T(8,128)(2,1)}, u32[]{:S(2)}, u32[]{:S(2)}) collective-permute-start(bf16[192,1792]{1,0:T(8,128)(2,1)} %shard_map.258.refs_3_), channel_id=1, source_target_pairs={{0,2},{1,3},{2,0},{3,1},{4,6},{5,7},{6,4},{7,5},{8,10},{9,11},{10,... | collective-permute-start | bytes 2064392 | tf_op jit(solution)/shard_map/ppermute | solution.py:45
  124.4 24.9 %collective-permute-start.24 = (bf16[192,1792]{1,0:T(8,128)(2,1)}, bf16[192,1792]{1,0:T(8,128)(2,1)}, u32[]{:S(2)}, u32[]{:S(2)}) collective-permute-start(bf16[192,1792]{1,0:T(8,128)(2,1)} %shard_map.258.refs_3_), channel_id=1, source_target_pairs={{0,1},{1,0},{2,3},{3,2},{4,5},{5,4},{6,7},{7,6},{8,9},{9,8},{10,11... | collective-permute-start | bytes 2064392 | tf_op jit(solution)/shard_map/ppermute | solution.py:45
  128.6 23.3 %collective-permute-start.22 = (bf16[2,192,3584]{2,1,0:T(8,128)(2,1)}, bf16[2,192,3584]{2,1,0:T(8,128)(2,1)}, u32[]{:S(2)}, u32[]{:S(2)}) collective-permute-start(bf16[2,192,3584]{2,1,0:T(8,128)(2,1)} %pad_maximum_fusion), channel_id=1, source_target_pairs={{0,1},{1,0},{2,3},{3,2},{4,5},{5,4},{6,7},{7,6},{8,9},{9,8},{10,11... | collective-permute-start | bytes 8257544 | tf_op jit(solution)/shard_map/ppermute | solution.py:45
  130.1 21.1 %collective-permute-start.27 = (bf16[2,192,1024]{2,1,0:T(8,128)(2,1)}, bf16[2,192,1024]{2,1,0:T(8,128)(2,1)}, u32[]{:S(2)}, u32[]{:S(2)}) collective-permute-start(bf16[2,192,1024]{2,1,0:T(8,128)(2,1)} %pad_maximum_fusion.3.refs_4_), channel_id=1, source_target_pairs={{0,1},{1,0},{2,3},{3,2},{4,5},{5,4},{6,7},{7,6},{8,9},{9,8},{10,11... | collective-permute-start | bytes 2359304 | tf_op jit(solution)/shard_map/ppermute | solution.py:45
  131.7 20.2 %collective-permute-start.23 = (bf16[2,192,1792]{2,1,0:T(8,128)(2,1)S(1)}, bf16[2,192,1792]{2,1,0:T(8,128)(2,1)}, u32[]{:S(2)}, u32[]{:S(2)}) collective-permute-start(bf16[2,192,1792]{2,1,0:T(8,128)(2,1)S(1)} %pad_maximum_fusion.1.refs_5_), channel_id=1, source_target_pairs={{0,1},{1,0},{2,3},{3,2},{4,5},{5,4},{6,7},{7,6},{8,9},{9,8},{10,11... | collective-permute-start | bytes 4128776 | tf_op jit(solution)/shard_map/ppermute | solution.py:45
  200.4 5.0 %collective-permute-start.33 = (bf16[384,1792]{1,0:T(8,128)(2,1)}, bf16[384,1792]{1,0:T(8,128)(2,1)S(1)}, u32[]{:S(2)}, u32[]{:S(2)}) collective-permute-start(bf16[384,1792]{1,0:T(8,128)(2,1)} %get-tuple-element.97), channel_id=1, source_target_pairs={{0,1},{1,0},{2,3},{3,2},{4,5},{5,4},{6,7},{7,6},{8,9},{9,8},{10,11... | collective-permute-start | bytes 4128776 | tf_op jit(solution)/shard_map/ppermute | solution.py:45
  200.8 4.2 collective-permute-start.30
  202.3 6.6 %collective-permute-start.28 = (bf16[2,192,1024]{2,1,0:T(8,128)(2,1)}, bf16[2,192,1024]{2,1,0:T(8,128)(2,1)}, u32[]{:S(2)}, u32[]{:S(2)}) collective-permute-start(bf16[2,192,1024]{2,1,0:T(8,128)(2,1)} %get-tuple-element.88), channel_id=1, source_target_pairs={{0,1},{1,0},{2,3},{3,2},{4,5},{5,4},{6,7},{7,6},{8,9},{9,8},{10,11... | collective-permute-start | bytes 2359304 | tf_op jit(solution)/shard_map/ppermute | solution.py:45
  202.6 9.6 %collective-permute-start.32 = (bf16[384,1024]{1,0:T(8,128)(2,1)}, bf16[384,1024]{1,0:T(8,128)(2,1)}, u32[]{:S(2)}, u32[]{:S(2)}) collective-permute-start(bf16[384,1024]{1,0:T(8,128)(2,1)} %get-tuple-element.93), channel_id=1, source_target_pairs={{0,1},{1,0},{2,3},{3,2},{4,5},{5,4},{6,7},{7,6},{8,9},{9,8},{10,11... | collective-permute-start | bytes 2359304 | tf_op jit(solution)/shard_map/ppermute | solution.py:45
  204.0 54.7 %collective-permute-start.29 = (bf16[2,192,1024]{2,1,0:T(8,128)(2,1)}, bf16[2,192,1024]{2,1,0:T(8,128)(2,1)}, u32[]{:S(2)}, u32[]{:S(2)}) collective-permute-start(bf16[2,192,1024]{2,1,0:T(8,128)(2,1)} %get-tuple-element.89), channel_id=1, source_target_pairs={{0,2},{1,3},{2,0},{3,1},{4,6},{5,7},{6,4},{7,5},{8,10},{9,11},{10,... | collective-permute-start | bytes 2359304 | tf_op jit(solution)/shard_map/ppermute | solution.py:45
  205.1 49.2 %collective-permute-start.35 = (bf16[3,384,1792]{2,1,0:T(8,128)(2,1)}, bf16[3,384,1792]{2,1,0:T(8,128)(2,1)}, u32[]{:S(2)}, u32[]{:S(2)}) collective-permute-start(bf16[3,384,1792]{2,1,0:T(8,128)(2,1)} %get-tuple-element.102), channel_id=1, source_target_pairs={{0,1},{1,0},{2,3},{3,2},{4,5},{5,4},{6,7},{7,6},{8,9},{9,8},{10,11... | collective-permute-start | bytes 12386312 | tf_op jit(solution)/shard_map/ppermute | solution.py:45
  205.4 53.2 %collective-permute-start.31 = (bf16[2,192,1024]{2,1,0:T(8,128)(2,1)}, bf16[2,192,1024]{2,1,0:T(8,128)(2,1)}, u32[]{:S(2)}, u32[]{:S(2)}) collective-permute-start(bf16[2,192,1024]{2,1,0:T(8,128)(2,1)} %collective-permute-done.30.refs_2_), channel_id=1, source_target_pairs={{0,2},{1,3},{2,0},{3,1},{4,6},{5,7},{6,4},{7,5},{8,10},{9,11},{10,... | collective-permute-start | bytes 2359304 | tf_op jit(solution)/shard_map/ppermute | solution.py:45
  208.9 44.3 %collective-permute-start.34 = (bf16[384,1792]{1,0:T(8,128)(2,1)}, bf16[384,1792]{1,0:T(8,128)(2,1)S(1)}, u32[]{:S(2)}, u32[]{:S(2)}) collective-permute-start(bf16[384,1792]{1,0:T(8,128)(2,1)} %fusion.3.refs_0_), channel_id=1, source_target_pairs={{0,4},{4,8},{8,12},{12,0},{1,5},{5,9},{9,13},{13,1},{2,6},{6,10},{... | collective-permute-start | bytes 4128776 | tf_op jit(solution)/shard_map/ppermute | solution.py:50
  258.0 47.8 %collective-permute-start.37 = (bf16[384,1792]{1,0:T(8,128)(2,1)}, bf16[384,1792]{1,0:T(8,128)(2,1)S(1)}, u32[]{:S(2)}, u32[]{:S(2)}) collective-permute-start(bf16[384,1792]{1,0:T(8,128)(2,1)} %fusion.2.refs_3_), channel_id=1, source_target_pairs={{0,4},{4,8},{8,12},{12,0},{1,5},{5,9},{9,13},{13,1},{2,6},{6,10},{... | collective-permute-start | bytes 4128776 | tf_op jit(solution)/shard_map/ppermute | solution.py:50
  274.4 28.2 %collective-permute-start.36 = (bf16[400,2048]{1,0:T(8,128)(2,1)}, bf16[400,2048]{1,0:T(8,128)(2,1)}, u32[]{:S(2)}, u32[]{:S(2)}) collective-permute-start(bf16[400,2048]{1,0:T(8,128)(2,1)} %get-tuple-element.108), channel_id=1, source_target_pairs={{0,1},{1,0},{2,3},{3,2},{4,5},{5,4},{6,7},{7,6},{8,9},{9,8},{10,11... | collective-permute-start | bytes 4915208 | tf_op jit(solution)/shard_map/ppermute | solution.py:45
  305.3 21.9 %collective-permute-start.38 = (bf16[208,2048]{1,0:T(8,128)(2,1)}, bf16[208,2048]{1,0:T(8,128)(2,1)}, u32[]{:S(2)}, u32[]{:S(2)}) collective-permute-start(bf16[208,2048]{1,0:T(8,128)(2,1)} %add_convert_fusion.1.refs_1_.refs_0_), channel_id=1, source_target_pairs={{0,2},{1,3},{2,0},{3,1},{4,6},{5,7},{6,4},{7,5},{8,10},{9,11},{10,... | collective-permute-start | bytes 2555912 | tf_op jit(solution)/shard_map/ppermute | solution.py:45
  310.7 33.0 %collective-permute-start.42 = (bf16[384,1792]{1,0:T(8,128)(2,1)}, bf16[384,1792]{1,0:T(8,128)(2,1)S(1)}, u32[]{:S(2)}, u32[]{:S(2)}) collective-permute-start(bf16[384,1792]{1,0:T(8,128)(2,1)} %fusion.1.refs_1_), channel_id=1, source_target_pairs={{0,4},{4,8},{8,12},{12,0},{1,5},{5,9},{9,13},{13,1},{2,6},{6,10},{... | collective-permute-start | bytes 4128776 | tf_op jit(solution)/shard_map/ppermute | solution.py:50
  320.0 24.7 %collective-permute-start.41 = (bf16[3,384,384]{2,1,0:T(8,128)(2,1)}, bf16[3,384,384]{2,1,0:T(8,128)(2,1)}, u32[]{:S(2)}, u32[]{:S(2)}) collective-permute-start(bf16[3,384,384]{2,1,0:T(8,128)(2,1)} %get-tuple-element.113), channel_id=1, source_target_pairs={{0,1},{1,0},{2,3},{3,2},{4,5},{5,4},{6,7},{7,6},{8,9},{9,8},{10,11... | collective-permute-start | bytes 2654216 | tf_op jit(solution)/shard_map/ppermute | solution.py:45
  340.7 20.2 %collective-permute-start.39 = (bf16[400,2048]{1,0:T(8,128)(2,1)}, bf16[400,2048]{1,0:T(8,128)(2,1)}, u32[]{:S(2)}, u32[]{:S(2)}) collective-permute-start(bf16[400,2048]{1,0:T(8,128)(2,1)} %get-tuple-element.111), channel_id=1, source_target_pairs={{0,1},{1,0},{2,3},{3,2},{4,5},{5,4},{6,7},{7,6},{8,9},{9,8},{10,11... | collective-permute-start | bytes 4915208 | tf_op jit(solution)/shard_map/ppermute | solution.py:45
  348.6 46.7 %collective-permute-start.46 = (bf16[384,640]{1,0:T(8,128)(2,1)}, bf16[384,640]{1,0:T(8,128)(2,1)}, u32[]{:S(2)}, u32[]{:S(2)}) collective-permute-start(bf16[384,640]{1,0:T(8,128)(2,1)} %concatenate.111), channel_id=1, source_target_pairs={{0,4},{4,8},{8,12},{12,0},{1,5},{5,9},{9,13},{13,1},{2,6},{6,10},{... | collective-permute-start | bytes 1474568 | tf_op jit(solution)/shard_map/ppermute | solution.py:50
  351.8 42.5 %collective-permute-start.45 = (bf16[384,640]{1,0:T(8,128)(2,1)}, bf16[384,640]{1,0:T(8,128)(2,1)}, u32[]{:S(2)}, u32[]{:S(2)}) collective-permute-start(bf16[384,640]{1,0:T(8,128)(2,1)} %concatenate.110), channel_id=1, source_target_pairs={{0,8},{4,12},{8,0},{12,4},{1,9},{5,13},{9,1},{13,5},{2,10},{6,14},... | collective-permute-start | bytes 1474568 | tf_op jit(solution)/shard_map/ppermute | solution.py:50
  355.9 43.0 %collective-permute-start.44 = (bf16[384,640]{1,0:T(8,128)(2,1)}, bf16[384,640]{1,0:T(8,128)(2,1)}, u32[]{:S(2)}, u32[]{:S(2)}) collective-permute-start(bf16[384,640]{1,0:T(8,128)(2,1)} %concatenate.109), channel_id=1, source_target_pairs={{0,12},{4,0},{8,4},{12,8},{1,13},{5,1},{9,5},{13,9},{2,14},{6,2},{... | collective-permute-start | bytes 1474568 | tf_op jit(solution)/shard_map/ppermute | solution.py:50
  359.2 37.1 %collective-permute-start.48 = (bf16[192,1792]{1,0:T(8,128)(2,1)}, bf16[192,1792]{1,0:T(8,128)(2,1)}, u32[]{:S(2)}, u32[]{:S(2)}) collective-permute-start(bf16[192,1792]{1,0:T(8,128)(2,1)} %slice.524), channel_id=1, source_target_pairs={{0,2},{1,3},{2,0},{3,1},{4,6},{5,7},{6,4},{7,5},{8,10},{9,11},{10,... | collective-permute-start | bytes 2064392 | tf_op jit(solution)/shard_map/ppermute | solution.py:45
  362.4 36.6 %collective-permute-start.40 = (bf16[208,2048]{1,0:T(8,128)(2,1)S(1)}, bf16[208,2048]{1,0:T(8,128)(2,1)}, u32[]{:S(2)}, u32[]{:S(2)}) collective-permute-start(bf16[208,2048]{1,0:T(8,128)(2,1)S(1)} %add_convert_fusion), channel_id=1, source_target_pairs={{0,2},{1,3},{2,0},{3,1},{4,6},{5,7},{6,4},{7,5},{8,10},{9,11},{10,... | collective-permute-start | bytes 2555912 | tf_op jit(solution)/shard_map/ppermute | solution.py:45
  398.4 20.4 %collective-permute-start.50 = (bf16[192,1792]{1,0:T(8,128)(2,1)}, bf16[192,1792]{1,0:T(8,128)(2,1)S(1)}, u32[]{:S(2)}, u32[]{:S(2)}) collective-permute-start(bf16[192,1792]{1,0:T(8,128)(2,1)} %add_convert_fusion.2.refs_16_), channel_id=1, source_target_pairs={{0,16},{16,0},{1,17},{17,1},{2,18},{18,2},{3,19},{19,3},{4,20},{20... | collective-permute-start | bytes 2064392 | tf_op jit(solution)/shard_map/ppermute | solution.py:54
  402.4 8.0 %collective-permute-start.47 = (bf16[192,640]{1,0:T(8,128)(2,1)S(1)}, bf16[192,640]{1,0:T(8,128)(2,1)S(1)}, u32[]{:S(2)}, u32[]{:S(2)}) collective-permute-start(bf16[192,640]{1,0:T(8,128)(2,1)S(1)} %concatenate.113.refs_13_), channel_id=1, source_target_pairs={{0,2},{1,3},{2,0},{3,1},{4,6},{5,7},{6,4},{7,5},{8,10},{9,11},{10,... | collective-permute-start | bytes 737288 | tf_op jit(solution)/shard_map/ppermute | solution.py:45
  411.5 11.4 %collective-permute-start.49 = (bf16[192,640]{1,0:T(8,128)(2,1)}, bf16[192,640]{1,0:T(8,128)(2,1)S(1)}, u32[]{:S(2)}, u32[]{:S(2)}) collective-permute-start(bf16[192,640]{1,0:T(8,128)(2,1)} %concatenate.114.refs_15_), channel_id=1, source_target_pairs={{0,16},{16,0},{1,17},{17,1},{2,18},{18,2},{3,19},{19,3},{4,20},{20... | collective-permute-start | bytes 737288 | tf_op jit(solution)/shard_map/ppermute | solution.py:54
  (44 other events, 446.4 us)

commit v5 on v4

--- a/solution.py
+++ b/solution.py
@@ -967,17 +967,17 @@
     dq_low, dkv_low = attend_back(
         low_table, q_low, grads, out_low, log_low, k, v, k_t, 0, (0, 3), (dkv_low,), near_high
     )
-    got_high = tie(got_high, dq_low)
+    total = three(tie(rows_shift(total, 1), dq_low), g_near[3], g_got[2])
+    got_high = tie(got_high, dq_low, total)
     sent_high = two(near_high[FB:], got_high[FB:])
-    total = three(tie(rows_shift(total, 1), sent_high), g_near[3], g_got[2])
     pair_sent = cols_swap(sent_high, 2)
     wg_near, wg_far = weights_back(low_order, normed_low, dq_low, dkv_low, w_part, (0, 3), sent_high, total)
     near_low, far_low, gain_part = project_back(
-        low_order, w_qkv, normed_low, dq_low, dkv_low, 0, gain_part, wg_near, pair_sent
+        low_order, w_qkv, normed_low, dq_low, dkv_low, 0, gain_part, wg_near
     )
 
     ring_got = tie(rows_shift(total, 1), near_low)
-    wg_got = tie(cols_swap(wg_far, 1), near_low, ring_got)
+    wg_got = tie(cols_swap(wg_far, 1), near_low, ring_got, pair_sent)
     by_core = jnp.where(core == 0, wg_near, wg_got), jnp.where(core == 0, wg_got, wg_near)
 
     def split(values):

time: 432 us -> 428 us (level)
    ppermute x36, waiting for transfers between devices: 9.94 us -> 3.54 us  [cols_swap(): lax.ppermute(value, 'cols', [(i, i ^ distance) for i in range(lax.axis_si...]
    ppermute x12, waiting for transfers between devices: 55.4 us -> 60.5 us  [rows_shift(): lax.ppermute(value, 'rows', [(i, (i + step) % count) for i in range(count)])]
where the time goes in v5:
time: 428 us; the launch traced here: 423 us
  Pallas kernels  244 us (57%)
  waiting for transfers between devices  64.1 us (15%)
  other arithmetic  44.4 us (10%)
  starting transfers between devices  36.5 us (9%)
  local copies, waits for them, and re-layouts  33 us (8%)
    pallas_call x2, Pallas kernels, attend_back(): pl.pallas_call(functools.partial(attend_back_kernel, counts=(4,) if half...  69.1 us
    ppermute x12, waiting for transfers between devices, rows_shift(): lax.ppermute(value, 'rows', [(i, (i + step) % count) for i in range(count)])  60.5 us
    pallas_call x1, Pallas kernels, feed_forward(): pl.pallas_call(feed_kernel, in_specs=[pl.BlockSpec(memory_space=pltpu.SME...  47.5 us
    pallas_call x4, Pallas kernels, attend(): pl.pallas_call(functools.partial(attend_kernel, counts=(4,) if half else...  45.7 us
    pallas_call x2, Pallas kernels, project_half(): pl.pallas_call(functools.partial(qkv_kernel, first=first, extra=extra), g...  25.2 us
    pallas_call x2, Pallas kernels, project_back(): pl.pallas_call(functools.partial(qkv_back_kernel, half=half), grid_spec=p...  25.1 us
    ppermute x36, starting transfers between devices, cols_swap(): lax.ppermute(value, 'cols', [(i, i ^ distance) for i in range(lax.axis_si...  17.7 us
    ppermute x12, starting transfers between devices, rows_shift(): lax.ppermute(value, 'rows', [(i, (i + step) % count) for i in range(count)])  15.3 us
  transfers between devices with their start and end apart: 51, of which 11 were waited for; matrix products, arithmetic and copies ran while one was open for 15% of the time, Pallas kernels for 46%

profile of v5, /device:TPU:24, one launch (start us, length us, event | category | flops | bytes accessed | tf_op | source)
XLA Modules:
  0.0 423.4 jit_solution(9686114741728307262)
XLA Ops:
  0.7 1.9 shard_map.240
  3.0 3.7 collective-permute-start.2
  6.9 1.5 collective-permute-start
  12.5 2.4 shard_map.244.refs_3_
  15.0 7.0 %collective-permute-done.3 = bf16[192,576]{1,0:T(8,128)(2,1)S(1)} collective-permute-done((bf16[192,576]{1,0:T(8,128)(2,1)}, bf16[192,576]{1,0:T(8,128)(2,1)S(1)}, u32[]{:S(2)}, u32[]{:S(2)}) %collective-permute-start.3) | collective-permute-done | bytes 221216 | tf_op jit(solution)/shard_map/ppermute | solution.py:50
  24.6 1.6 collective-permute-start.10
  26.2 1.9 collective-permute-done.7.refs_0_
  32.4 4.1 shard_map.245.refs_4_.refs_0_
  36.4 13.5 %collective-permute-done.5.refs_5_.refs_1_ = bf16[192,1792]{1,0:T(8,128)(2,1)S(1)} collective-permute-done((bf16[192,1792]{1,0:T(8,128)(2,1)}, bf16[192,1792]{1,0:T(8,128)(2,1)S(1)}, u32[]{:S(2)}, u32[]{:S(2)}) %collective-permute-start.5) | collective-permute-done | bytes 688160 | tf_op jit(solution)/shard_map/ppermute | solution.py:50
  51.3 2.2 shard_map.247
  55.7 1.4 collective-permute-start.6
  58.2 13.0 %shard_map.248 = (bf16[768,2048]{1,0:T(8,128)(2,1)}, f32[1,2048]{1,0:T(1,128)}, bf16[384,1024]{1,0:T(8,128)(2,1)}, bf16[4096,384]{1,0:T(8,128)(2,1)}, bf16[384,4...) custom-call(s32[5]{0:T(128)} %pad_add_fusion.3.tab, ...), custom_call_target="tpu_custom_call" | custom-call | flops 13799999488 | tf_op jit(solution)/shard_map/pallas_call | solution.py:197
  71.2 2.1 collective-permute-start.16
  73.3 7.4 %shard_map.250 = (bf16[384,512]{1,0:T(8,128)(2,1)}, bf16[384,512]{1,0:T(8,128)(2,1)}, f32[1,2,1024]{2,1,0:T(2,128)}) custom-call(s32[18]{0:T(128)} %get-tuple-element.229.tab, bf16[384,1024]{1,0:T(8,128)(2,1)} %get-tuple-element.65.q_t, bf16[4096,384]{1,0:T(8,128)(2,1)} %get-tuple-element.66.k.refs_6_, bf16[384,4096]{1,0:T(8,128)(2,1)} %get-tuple-element.67.v_t.refs_9_, ...), custom_call_target="tpu_custom_call" | custom-call | flops 6899999744 | tf_op jit(solution)/shard_map/pallas_call | solution.py:302
  80.7 1.3 collective-permute-start.13
  82.0 12.3 %shard_map.254 = (bf16[384,512]{1,0:T(8,128)(2,1)}, bf16[384,512]{1,0:T(8,128)(2,1)}, f32[2,2,1024]{2,1,0:T(2,128)}) custom-call(s32[18]{0:T(128)} %get-tuple-element.229.tab, bf16[384,1024]{1,0:T(8,128)(2,1)} %get-tuple-element.65.q_t, bf16[4096,384]{1,0:T(8,128)(2,1)} %get-tuple-element.66.k.refs_6_, ...), custom_call_target="tpu_custom_call", output_to_operand_aliasing={{0}: (4, {}), {1}: (5, {})} | custom-call | flops 13799999488 | tf_op jit(solution)/shard_map/pallas_call | solution.py:302
  95.7 2.2 collective-permute-done.13.refs_0_
  98.3 1.5 collective-permute-start.18
  99.8 12.2 %shard_map.256 = (bf16[768,2048]{1,0:T(8,128)(2,1)}, f32[1,2048]{1,0:T(1,128)}, bf16[384,1024]{1,0:T(8,128)(2,1)}, bf16[4096,384]{1,0:T(8,128)(2,1)}, bf16[384,4...) custom-call(s32[5]{0:T(128)} %pad_add_fusion.4.tab, ...), custom_call_target="tpu_custom_call", output_to_operand_aliasing={{3}: (7, {}), {4}: (8, {}), {5}: (9, {}), {6}: (10, {})} | custom-call | flops 13799999488 | tf_op jit(solution)/shard_map/pallas_call | solution.py:197
  112.8 9.9 %shard_map.257 = (bf16[384,512]{1,0:T(8,128)(2,1)}, bf16[384,512]{1,0:T(8,128)(2,1)}, f32[1,2,1024]{2,1,0:T(2,128)}) custom-call(s32[18]{0:T(128)} %get-tuple-element.228.tab, bf16[384,1024]{1,0:T(8,128)(2,1)} %get-tuple-element.76.q_t, bf16[4096,384]{1,0:T(8,128)(2,1)} %get-tuple-element.77.k, bf16[384,4096]{1,0:T(8,128)(2,1)} %get-tuple-element.78.v_t, ...), custom_call_target="tpu_custom_call" | custom-call | flops 9200000000 | tf_op jit(solution)/shard_map/pallas_call | solution.py:302
  122.7 1.7 collective-permute-start.20
  125.5 3.1 pad_maximum_fusion
  130.3 1.4 pad_maximum_fusion.1.refs_5_
  132.8 16.1 %shard_map.263 = (bf16[384,512]{1,0:T(8,128)(2,1)}, bf16[384,512]{1,0:T(8,128)(2,1)}, f32[2,2,1024]{2,1,0:T(2,128)}) custom-call(s32[18]{0:T(128)} %get-tuple-element.228.tab, bf16[384,1024]{1,0:T(8,128)(2,1)} %get-tuple-element.76.q_t, bf16[4096,384]{1,0:T(8,128)(2,1)} %get-tuple-element.77.k, ...), custom_call_target="tpu_custom_call", output_to_operand_aliasing={{0}: (4, {}), {1}: (5, {})} | custom-call | flops 18400000000 | tf_op jit(solution)/shard_map/pallas_call | solution.py:302
  152.9 47.5 %shard_map.265 = (bf16[2,192,1024]{2,1,0:T(8,128)(2,1)}, bf16[2,192,1024]{2,1,0:T(8,128)(2,1)}, bf16[2,192,1024]{2,1,0:T(8,128)(2,1)}, bf16[2,192,1024]{2,1,0:T(...) custom-call(s32[4]{0:T(128)} %pad_add_fusion.2.sel, ...), custom_call_target="tpu_custom_call" | custom-call | flops 57500000256 | tf_op jit(solution)/shard_map/pallas_call | solution.py:630
  206.2 2.7 fusion.3.refs_0_
  208.9 3.3 collective-permute-start.34
  212.2 41.0 %shard_map.266 = (bf16[384,1024]{1,0:T(8,128)(2,1)}, bf16[3,2048,256]{2,1,0:T(8,128)(2,1)}, f32[3,2048,256]{2,1,0:T(8,128)}) custom-call(s32[18]{0:T(128)} %get-tuple-element.228.tab, bf16[384,1024]{1,0:T(8,128)(2,1)} %get-tuple-element.76.q_t, bf16[384,1024]{1,0:T(8,128)(2,1)} %get-tuple-element.92.do_own, ...), custom_call_target="tpu_custom_call" | custom-call | flops 55199997952 | tf_op jit(solution)/shard_map/pallas_call | solution.py:384
  254.3 3.7 fusion.2.refs_3_
  259.5 14.9 %shard_map.268 = (bf16[400,2048]{1,0:T(8,128)(2,1)}, bf16[400,2048]{1,0:T(8,128)(2,1)}, f32[768,1]{1,0:T(8,128)}, f32[3,768,384]{2,1,0:T(8,128)}) custom-call(s32[5]{0:T(128)} %pad_add_fusion.4.tab, bf16[768,1152]{1,0:T(8,128)(2,1)} %get-tuple-element.73.refs_5_.w, bf16[768,2048]{1,0:T(8,128)(2,1)} %get-tuple-element.99.n_t, ...), custom_call_target="tpu_custom_call" | custom-call | flops 17250000896 | tf_op jit(solution)/shard_map/pallas_call | solution.py:719
  274.5 28.1 %shard_map.269 = (bf16[384,1024]{1,0:T(8,128)(2,1)}, bf16[3,2048,256]{2,1,0:T(8,128)(2,1)}) custom-call(s32[18]{0:T(128)} %get-tuple-element.229.tab, bf16[384,1024]{1,0:T(8,128)(2,1)} %get-tuple-element.65.q_t, bf16[384,1024]{1,0:T(8,128)(2,1)} %get-tuple-element.92.do_own, bf16[384,1024]{1,0:T(8,128)(2,1)} %collective-permute-done.32.do_other, ...), custom_call_target="tpu_custom_call" | custom-call | flops 41400000512 | tf_op jit(solution)/shard_map/pallas_call | solution.py:384
  303.7 3.7 fusion.1.refs_2_.refs_1_
  307.8 2.6 add_convert_fusion.1.refs_0_
  310.9 9.0 %shard_map.272 = (bf16[3,384,384]{2,1,0:T(8,128)(2,1)}, bf16[3,384,384]{2,1,0:T(8,128)(2,1)}) custom-call(s32[5]{0:T(128)} %pad_add_fusion.3.tab, bf16[768,2048]{1,0:T(8,128)(2,1)} %get-tuple-element.91.n_t, bf16[384,1024]{1,0:T(8,128)(2,1)} %get-tuple-element.104.refs_1_.dq_t.refs_0_, bf16[3,2048,256]{2,1,0:T(8,128)(2,1)} %get-tuple-element.105.dkv.refs_1_, ...), custom_call_target="tpu_custom_call" | custom-call | flops 9200000000 | tf_op jit(solution)/shard_map/pallas_call | solution.py:750
  320.3 10.2 %shard_map.273 = (bf16[400,2048]{1,0:T(8,128)(2,1)}, bf16[400,2048]{1,0:T(8,128)(2,1)}, f32[768,1]{1,0:T(8,128)}) custom-call(s32[5]{0:T(128)} %pad_add_fusion.3.tab, bf16[768,1152]{1,0:T(8,128)(2,1)} %get-tuple-element.73.refs_5_.w, bf16[768,2048]{1,0:T(8,128)(2,1)} %get-tuple-element.91.n_t, bf16[384,1024]{1,0:T(8,128)(2,1)} %get-tuple-element.104.refs_1_.dq_t.refs_0_, ...), custom_call_target="tpu_custom_call" | custom-call | flops 11500000256 | tf_op jit(solution)/shard_map/pallas_call | solution.py:719
  334.5 6.0 %collective-permute-done.42.refs_0_ = bf16[384,1792]{1,0:T(8,128)(2,1)S(1)} collective-permute-done((bf16[384,1792]{1,0:T(8,128)(2,1)}, bf16[384,1792]{1,0:T(8,128)(2,1)S(1)}, u32[]{:S(2)}, u32[]{:S(2)}) %collective-permute-start.42) | collective-permute-done | bytes 1376288 | tf_op jit(solution)/shard_map/ppermute | solution.py:50
  342.7 1.3 broadcast_select_fusion.1
  345.4 2.1 collective-permute-start.46
  350.9 1.8 concatenate.109
  352.7 2.2 fusion.refs_2_
  357.4 1.4 add_convert_fusion
  359.5 31.8 %collective-permute-done.45 = bf16[384,640]{1,0:T(8,128)(2,1)} collective-permute-done((bf16[384,640]{1,0:T(8,128)(2,1)}, bf16[384,640]{1,0:T(8,128)(2,1)}, u32[]{:S(2)}, u32[]{:S(2)}) %collective-permute-start.45) | collective-permute-done | bytes 491552 | tf_op jit(solution)/shard_map/ppermute | solution.py:50
  393.4 2.1 add_convert_fusion.2.refs_16_
  397.2 1.7 add_convert_fusion.3
  400.3 5.8 %shard_map.278 = (bf16[192,4096]{1,0:T(8,128)(2,1)}, f32[192,4096]{1,0:T(8,128)}) custom-call(s32[10]{0:T(128)} %pad_add_fusion.5.sel, bf16[2,192,1024]{2,1,0:T(8,128)(2,1)} %get-tuple-element.87.refs_0_, bf16[2,192,1024]{2,1,0:T(8,128)(2,1)} %collective-permute-done.28.refs_1_, bf16[2,192,1024]{2,1,0:T(8,128)(2,1)} %collective-permute-done.29.refs_4_.refs_2_, ...), custom_call_target="tpu_custom_call" | custom-call | flops 6899999744 | tf_op jit(solution)/shard_map/pallas_call | solution.py:794
  407.7 1.4 collective-permute-start.49
  409.0 5.8 %shard_map.279 = (bf16[192,4096]{1,0:T(8,128)(2,1)}, f32[192,4096]{1,0:T(8,128)}) custom-call(s32[10]{0:T(128)} %pad_add_fusion.sel, bf16[2,192,1024]{2,1,0:T(8,128)(2,1)} %get-tuple-element.87.refs_0_, bf16[2,192,1024]{2,1,0:T(8,128)(2,1)} %collective-permute-done.28.refs_1_, ...), custom_call_target="tpu_custom_call", output_to_operand_aliasing={{0}: (14, {}), {1}: (15, {})} | custom-call | flops 6899999744 | tf_op jit(solution)/shard_map/pallas_call | solution.py:794
  415.7 1.4 convert_add_fusion.7
  (270 shorter events, 64.4 us)
Async XLA Ops:
  2.6 19.4 %collective-permute-start.3 = (bf16[192,576]{1,0:T(8,128)(2,1)}, bf16[192,576]{1,0:T(8,128)(2,1)S(1)}, u32[]{:S(2)}, u32[]{:S(2)}) collective-permute-start(bf16[192,576]{1,0:T(8,128)(2,1)} %shard_map.240), channel_id=1, source_target_pairs={{0,8},{4,12},{8,0},{12,4},{1,9},{5,13},{9,1},{13,5},{2,10},{6,14},... | collective-permute-start | bytes 663560 | tf_op jit(solution)/shard_map/ppermute | solution.py:50
  2.9 19.1 %collective-permute-start.4 = (bf16[192,576]{1,0:T(8,128)(2,1)}, bf16[192,576]{1,0:T(8,128)(2,1)S(1)}, u32[]{:S(2)}, u32[]{:S(2)}) collective-permute-start(bf16[192,576]{1,0:T(8,128)(2,1)} %shard_map.240), channel_id=1, source_target_pairs={{0,12},{4,0},{8,4},{12,8},{1,13},{5,1},{9,5},{13,9},{2,14},{6,2},{... | collective-permute-start | bytes 663560 | tf_op jit(solution)/shard_map/ppermute | solution.py:50
  3.0 19.3 %collective-permute-start.2 = (bf16[192,576]{1,0:T(8,128)(2,1)}, bf16[192,576]{1,0:T(8,128)(2,1)}, u32[]{:S(2)}, u32[]{:S(2)}) collective-permute-start(bf16[192,576]{1,0:T(8,128)(2,1)} %shard_map.240), channel_id=1, source_target_pairs={{0,4},{4,8},{8,12},{12,0},{1,5},{5,9},{9,13},{13,1},{2,6},{6,10},{... | collective-permute-start | bytes 663560 | tf_op jit(solution)/shard_map/ppermute | solution.py:50
  6.9 29.6 %collective-permute-start = (f32[400]{0:T(512)S(1)}, f32[400]{0:T(512)S(1)}, u32[]{:S(2)}, u32[]{:S(2)}) collective-permute-start(f32[400]{0:T(512)S(1)} %pad_maximum_fusion.12), channel_id=1, source_target_pairs={{0,2},{1,3},{2,0},{3,1},{4,6},{5,7},{6,4},{7,5},{8,10},{9,11},{10,... | collective-permute-start | bytes 4808 | tf_op jit(solution)/shard_map/ppermute | solution.py:45
  9.4 18.6 %collective-permute-start.7 = (bf16[192,2048]{1,0:T(8,128)(2,1)S(1)}, bf16[192,2048]{1,0:T(8,128)(2,1)}, u32[]{:S(2)}, u32[]{:S(2)}) collective-permute-start(bf16[192,2048]{1,0:T(8,128)(2,1)S(1)} %get-tuple-element.177.refs_0_), channel_id=1, source_target_pairs={{0,2},{1,3},{2,0},{3,1},{4,6},{5,7},{6,4},{7,5},{8,10},{9,11},{10,... | collective-permute-start | bytes 2359304 | tf_op jit(solution)/shard_map/ppermute | solution.py:45
  24.6 25.3 %collective-permute-start.10 = (bf16[2,192,1152]{2,1,0:T(8,128)(2,1)S(1)}, bf16[2,192,1152]{2,1,0:T(8,128)(2,1)S(1)}, u32[]{:S(2)}, u32[]{:S(2)}) collective-permute-start(bf16[2,192,1152]{2,1,0:T(8,128)(2,1)S(1)} %pad_maximum_fusion.2.refs_1_.first.refs_5_), channel_id=1, source_target_pairs={{0,2},{1,3},{2,0},{3,1},{4,6},{5,7},{6,4},{7,5},{8,10},{9,11},{10,... | collective-permute-start | bytes 2654216 | tf_op jit(solution)/shard_map/ppermute | solution.py:45
  28.1 21.8 %collective-permute-start.8 = (bf16[192,2048]{1,0:T(8,128)(2,1)}, bf16[192,2048]{1,0:T(8,128)(2,1)S(1)}, u32[]{:S(2)}, u32[]{:S(2)}) collective-permute-start(bf16[192,2048]{1,0:T(8,128)(2,1)} %shard_map.243), channel_id=1, source_target_pairs={{0,1},{1,0},{2,3},{3,2},{4,5},{5,4},{6,7},{7,6},{8,9},{9,8},{10,11... | collective-permute-start | bytes 2359304 | tf_op jit(solution)/shard_map/ppermute | solution.py:45
  28.2 21.8 %collective-permute-start.9 = (bf16[192,2048]{1,0:T(8,128)(2,1)}, bf16[192,2048]{1,0:T(8,128)(2,1)}, u32[]{:S(2)}, u32[]{:S(2)}) collective-permute-start(bf16[192,2048]{1,0:T(8,128)(2,1)} %shard_map.242.refs_1_.refs_20_), channel_id=1, source_target_pairs={{0,1},{1,0},{2,3},{3,2},{4,5},{5,4},{6,7},{7,6},{8,9},{9,8},{10,11... | collective-permute-start | bytes 2359304 | tf_op jit(solution)/shard_map/ppermute | solution.py:45
  30.5 19.4 %collective-permute-start.5 = (bf16[192,1792]{1,0:T(8,128)(2,1)}, bf16[192,1792]{1,0:T(8,128)(2,1)S(1)}, u32[]{:S(2)}, u32[]{:S(2)}) collective-permute-start(bf16[192,1792]{1,0:T(8,128)(2,1)} %shard_map.241.refs_0_), channel_id=1, source_target_pairs={{0,4},{4,8},{8,12},{12,0},{1,5},{5,9},{9,13},{13,1},{2,6},{6,10},{... | collective-permute-start | bytes 2064392 | tf_op jit(solution)/shard_map/ppermute | solution.py:50
  36.4 21.7 %collective-permute-start.14 = (bf16[192,2048]{1,0:T(8,128)(2,1)}, bf16[192,2048]{1,0:T(8,128)(2,1)}, u32[]{:S(2)}, u32[]{:S(2)}) collective-permute-start(bf16[192,2048]{1,0:T(8,128)(2,1)} %get-tuple-element.176.refs_0_), channel_id=1, source_target_pairs={{0,1},{1,0},{2,3},{3,2},{4,5},{5,4},{6,7},{7,6},{8,9},{9,8},{10,11... | collective-permute-start | bytes 2359304 | tf_op jit(solution)/shard_map/ppermute | solution.py:45
  49.9 3.9 collective-permute-start.1
  53.5 4.6 %collective-permute-start.11 = (bf16[2,192,1152]{2,1,0:T(8,128)(2,1)}, bf16[2,192,1152]{2,1,0:T(8,128)(2,1)}, u32[]{:S(2)}, u32[]{:S(2)}) collective-permute-start(bf16[2,192,1152]{2,1,0:T(8,128)(2,1)} %shard_map.247), channel_id=1, source_target_pairs={{0,1},{1,0},{2,3},{3,2},{4,5},{5,4},{6,7},{7,6},{8,9},{9,8},{10,11... | collective-permute-start | bytes 2654216 | tf_op jit(solution)/shard_map/ppermute | solution.py:45
  55.7 25.0 %collective-permute-start.6 = (bf16[192,1792]{1,0:T(8,128)(2,1)S(1)}, bf16[192,1792]{1,0:T(8,128)(2,1)}, u32[]{:S(2)}, u32[]{:S(2)}) collective-permute-start(bf16[192,1792]{1,0:T(8,128)(2,1)S(1)} %copy-done.7), channel_id=1, source_target_pairs={{0,4},{4,8},{8,12},{12,0},{1,5},{5,9},{9,13},{13,1},{2,6},{6,10},{... | collective-permute-start | bytes 2064392 | tf_op jit(solution)/shard_map/ppermute | solution.py:50
  58.2 23.8 %collective-permute-start.12 = (bf16[192,2048]{1,0:T(8,128)(2,1)}, bf16[192,2048]{1,0:T(8,128)(2,1)}, u32[]{:S(2)}, u32[]{:S(2)}) collective-permute-start(bf16[192,2048]{1,0:T(8,128)(2,1)} %shard_map.252), channel_id=1, source_target_pairs={{0,2},{1,3},{2,0},{3,1},{4,6},{5,7},{6,4},{7,5},{8,10},{9,11},{10,... | collective-permute-start | bytes 2359304 | tf_op jit(solution)/shard_map/ppermute | solution.py:45
  71.2 27.1 %collective-permute-start.16 = (bf16[2,192,896]{2,1,0:T(8,128)(2,1)}, bf16[2,192,896]{2,1,0:T(8,128)(2,1)}, u32[]{:S(2)}, u32[]{:S(2)}) collective-permute-start(bf16[2,192,896]{2,1,0:T(8,128)(2,1)} %shard_map.249.refs_0_), channel_id=1, source_target_pairs={{0,2},{1,3},{2,0},{3,1},{4,6},{5,7},{6,4},{7,5},{8,10},{9,11},{10,... | collective-permute-start | bytes 2064392 | tf_op jit(solution)/shard_map/ppermute | solution.py:45
  80.7 17.3 %collective-permute-start.13 = (bf16[192,1792]{1,0:T(8,128)(2,1)}, bf16[192,1792]{1,0:T(8,128)(2,1)}, u32[]{:S(2)}, u32[]{:S(2)}) collective-permute-start(bf16[192,1792]{1,0:T(8,128)(2,1)} %shard_map.251.refs_4_.refs_0_), channel_id=1, source_target_pairs={{0,4},{4,8},{8,12},{12,0},{1,5},{5,9},{9,13},{13,1},{2,6},{6,10},{... | collective-permute-start | bytes 2064392 | tf_op jit(solution)/shard_map/ppermute | solution.py:50
  82.0 17.8 %collective-permute-start.15 = (bf16[192,2048]{1,0:T(8,128)(2,1)}, bf16[192,2048]{1,0:T(8,128)(2,1)}, u32[]{:S(2)}, u32[]{:S(2)}) collective-permute-start(bf16[192,2048]{1,0:T(8,128)(2,1)} %shard_map.253.refs_3_.refs_1_.refs_23_), channel_id=1, source_target_pairs={{0,1},{1,0},{2,3},{3,2},{4,5},{5,4},{6,7},{7,6},{8,9},{9,8},{10,11... | collective-permute-start | bytes 2359304 | tf_op jit(solution)/shard_map/ppermute | solution.py:45
  94.3 17.7 %collective-permute-start.17 = (bf16[384,512]{1,0:T(8,128)(2,1)}, bf16[384,512]{1,0:T(8,128)(2,1)S(1)}, u32[]{:S(2)}, u32[]{:S(2)}) collective-permute-start(bf16[384,512]{1,0:T(8,128)(2,1)} %get-tuple-element.79.o_other), channel_id=1, source_target_pairs={{0,1},{1,0},{2,3},{3,2},{4,5},{5,4},{6,7},{7,6},{8,9},{9,8},{10,11... | collective-permute-start | bytes 1179656 | tf_op jit(solution)/shard_map/ppermute | solution.py:45
  94.8 29.6 %collective-permute-start.21 = (bf16[2,192,1024]{2,1,0:T(8,128)(2,1)}, bf16[2,192,1024]{2,1,0:T(8,128)(2,1)}, u32[]{:S(2)}, u32[]{:S(2)}) collective-permute-start(bf16[2,192,1024]{2,1,0:T(8,128)(2,1)} %shard_map.261), channel_id=1, source_target_pairs={{0,2},{1,3},{2,0},{3,1},{4,6},{5,7},{6,4},{7,5},{8,10},{9,11},{10,... | collective-permute-start | bytes 2359304 | tf_op jit(solution)/shard_map/ppermute | solution.py:45
  98.0 32.3 %collective-permute-start.19 = (bf16[192,1792]{1,0:T(8,128)(2,1)}, bf16[192,1792]{1,0:T(8,128)(2,1)}, u32[]{:S(2)}, u32[]{:S(2)}) collective-permute-start(bf16[192,1792]{1,0:T(8,128)(2,1)} %shard_map.255.refs_2_), channel_id=1, source_target_pairs={{0,2},{1,3},{2,0},{3,1},{4,6},{5,7},{6,4},{7,5},{8,10},{9,11},{10,... | collective-permute-start | bytes 2064392 | tf_op jit(solution)/shard_map/ppermute | solution.py:45
  98.3 27.1 %collective-permute-start.18 = (bf16[2,192,896]{2,1,0:T(8,128)(2,1)}, bf16[2,192,896]{2,1,0:T(8,128)(2,1)}, u32[]{:S(2)}, u32[]{:S(2)}) collective-permute-start(bf16[2,192,896]{2,1,0:T(8,128)(2,1)} %collective-permute-done.16.refs_11_.refs_4_), channel_id=1, source_target_pairs={{0,16},{16,0},{1,17},{17,1},{2,18},{18,2},{3,19},{19,3},{4,20},{20... | collective-permute-start | bytes 2064392 | tf_op jit(solution)/shard_map/ppermute | solution.py:54
  122.7 26.2 %collective-permute-start.20 = (bf16[192,1792]{1,0:T(8,128)(2,1)}, bf16[192,1792]{1,0:T(8,128)(2,1)}, u32[]{:S(2)}, u32[]{:S(2)}) collective-permute-start(bf16[192,1792]{1,0:T(8,128)(2,1)} %shard_map.258.refs_3_), channel_id=1, source_target_pairs={{0,2},{1,3},{2,0},{3,1},{4,6},{5,7},{6,4},{7,5},{8,10},{9,11},{10,... | collective-permute-start | bytes 2064392 | tf_op jit(solution)/shard_map/ppermute | solution.py:45
  124.4 24.9 %collective-permute-start.24 = (bf16[192,1792]{1,0:T(8,128)(2,1)}, bf16[192,1792]{1,0:T(8,128)(2,1)}, u32[]{:S(2)}, u32[]{:S(2)}) collective-permute-start(bf16[192,1792]{1,0:T(8,128)(2,1)} %shard_map.258.refs_3_), channel_id=1, source_target_pairs={{0,1},{1,0},{2,3},{3,2},{4,5},{5,4},{6,7},{7,6},{8,9},{9,8},{10,11... | collective-permute-start | bytes 2064392 | tf_op jit(solution)/shard_map/ppermute | solution.py:45
  128.6 23.3 %collective-permute-start.22 = (bf16[2,192,3584]{2,1,0:T(8,128)(2,1)}, bf16[2,192,3584]{2,1,0:T(8,128)(2,1)}, u32[]{:S(2)}, u32[]{:S(2)}) collective-permute-start(bf16[2,192,3584]{2,1,0:T(8,128)(2,1)} %pad_maximum_fusion), channel_id=1, source_target_pairs={{0,1},{1,0},{2,3},{3,2},{4,5},{5,4},{6,7},{7,6},{8,9},{9,8},{10,11... | collective-permute-start | bytes 8257544 | tf_op jit(solution)/shard_map/ppermute | solution.py:45
  130.1 21.1 %collective-permute-start.27 = (bf16[2,192,1024]{2,1,0:T(8,128)(2,1)}, bf16[2,192,1024]{2,1,0:T(8,128)(2,1)}, u32[]{:S(2)}, u32[]{:S(2)}) collective-permute-start(bf16[2,192,1024]{2,1,0:T(8,128)(2,1)} %pad_maximum_fusion.3.refs_4_), channel_id=1, source_target_pairs={{0,1},{1,0},{2,3},{3,2},{4,5},{5,4},{6,7},{7,6},{8,9},{9,8},{10,11... | collective-permute-start | bytes 2359304 | tf_op jit(solution)/shard_map/ppermute | solution.py:45
  131.7 20.2 %collective-permute-start.23 = (bf16[2,192,1792]{2,1,0:T(8,128)(2,1)S(1)}, bf16[2,192,1792]{2,1,0:T(8,128)(2,1)}, u32[]{:S(2)}, u32[]{:S(2)}) collective-permute-start(bf16[2,192,1792]{2,1,0:T(8,128)(2,1)S(1)} %pad_maximum_fusion.1.refs_5_), channel_id=1, source_target_pairs={{0,1},{1,0},{2,3},{3,2},{4,5},{5,4},{6,7},{7,6},{8,9},{9,8},{10,11... | collective-permute-start | bytes 4128776 | tf_op jit(solution)/shard_map/ppermute | solution.py:45
  200.4 5.0 %collective-permute-start.33 = (bf16[384,1792]{1,0:T(8,128)(2,1)}, bf16[384,1792]{1,0:T(8,128)(2,1)S(1)}, u32[]{:S(2)}, u32[]{:S(2)}) collective-permute-start(bf16[384,1792]{1,0:T(8,128)(2,1)} %get-tuple-element.97), channel_id=1, source_target_pairs={{0,1},{1,0},{2,3},{3,2},{4,5},{5,4},{6,7},{7,6},{8,9},{9,8},{10,11... | collective-permute-start | bytes 4128776 | tf_op jit(solution)/shard_map/ppermute | solution.py:45
  200.8 4.2 collective-permute-start.30
  202.3 6.6 %collective-permute-start.28 = (bf16[2,192,1024]{2,1,0:T(8,128)(2,1)}, bf16[2,192,1024]{2,1,0:T(8,128)(2,1)}, u32[]{:S(2)}, u32[]{:S(2)}) collective-permute-start(bf16[2,192,1024]{2,1,0:T(8,128)(2,1)} %get-tuple-element.88), channel_id=1, source_target_pairs={{0,1},{1,0},{2,3},{3,2},{4,5},{5,4},{6,7},{7,6},{8,9},{9,8},{10,11... | collective-permute-start | bytes 2359304 | tf_op jit(solution)/shard_map/ppermute | solution.py:45
  202.6 9.6 %collective-permute-start.32 = (bf16[384,1024]{1,0:T(8,128)(2,1)}, bf16[384,1024]{1,0:T(8,128)(2,1)}, u32[]{:S(2)}, u32[]{:S(2)}) collective-permute-start(bf16[384,1024]{1,0:T(8,128)(2,1)} %get-tuple-element.93), channel_id=1, source_target_pairs={{0,1},{1,0},{2,3},{3,2},{4,5},{5,4},{6,7},{7,6},{8,9},{9,8},{10,11... | collective-permute-start | bytes 2359304 | tf_op jit(solution)/shard_map/ppermute | solution.py:45
  204.0 54.7 %collective-permute-start.29 = (bf16[2,192,1024]{2,1,0:T(8,128)(2,1)}, bf16[2,192,1024]{2,1,0:T(8,128)(2,1)}, u32[]{:S(2)}, u32[]{:S(2)}) collective-permute-start(bf16[2,192,1024]{2,1,0:T(8,128)(2,1)} %get-tuple-element.89), channel_id=1, source_target_pairs={{0,2},{1,3},{2,0},{3,1},{4,6},{5,7},{6,4},{7,5},{8,10},{9,11},{10,... | collective-permute-start | bytes 2359304 | tf_op jit(solution)/shard_map/ppermute | solution.py:45
  205.1 49.2 %collective-permute-start.35 = (bf16[3,384,1792]{2,1,0:T(8,128)(2,1)}, bf16[3,384,1792]{2,1,0:T(8,128)(2,1)}, u32[]{:S(2)}, u32[]{:S(2)}) collective-permute-start(bf16[3,384,1792]{2,1,0:T(8,128)(2,1)} %get-tuple-element.102), channel_id=1, source_target_pairs={{0,1},{1,0},{2,3},{3,2},{4,5},{5,4},{6,7},{7,6},{8,9},{9,8},{10,11... | collective-permute-start | bytes 12386312 | tf_op jit(solution)/shard_map/ppermute | solution.py:45
  205.4 53.2 %collective-permute-start.31 = (bf16[2,192,1024]{2,1,0:T(8,128)(2,1)}, bf16[2,192,1024]{2,1,0:T(8,128)(2,1)}, u32[]{:S(2)}, u32[]{:S(2)}) collective-permute-start(bf16[2,192,1024]{2,1,0:T(8,128)(2,1)} %collective-permute-done.30.refs_2_), channel_id=1, source_target_pairs={{0,2},{1,3},{2,0},{3,1},{4,6},{5,7},{6,4},{7,5},{8,10},{9,11},{10,... | collective-permute-start | bytes 2359304 | tf_op jit(solution)/shard_map/ppermute | solution.py:45
  208.9 44.3 %collective-permute-start.34 = (bf16[384,1792]{1,0:T(8,128)(2,1)}, bf16[384,1792]{1,0:T(8,128)(2,1)S(1)}, u32[]{:S(2)}, u32[]{:S(2)}) collective-permute-start(bf16[384,1792]{1,0:T(8,128)(2,1)} %fusion.3.refs_0_), channel_id=1, source_target_pairs={{0,4},{4,8},{8,12},{12,0},{1,5},{5,9},{9,13},{13,1},{2,6},{6,10},{... | collective-permute-start | bytes 4128776 | tf_op jit(solution)/shard_map/ppermute | solution.py:50
  258.0 44.6 %collective-permute-start.37 = (bf16[384,1792]{1,0:T(8,128)(2,1)}, bf16[384,1792]{1,0:T(8,128)(2,1)S(1)}, u32[]{:S(2)}, u32[]{:S(2)}) collective-permute-start(bf16[384,1792]{1,0:T(8,128)(2,1)} %fusion.2.refs_3_), channel_id=1, source_target_pairs={{0,4},{4,8},{8,12},{12,0},{1,5},{5,9},{9,13},{13,1},{2,6},{6,10},{... | collective-permute-start | bytes 4128776 | tf_op jit(solution)/shard_map/ppermute | solution.py:50
  274.4 33.4 %collective-permute-start.36 = (bf16[400,2048]{1,0:T(8,128)(2,1)}, bf16[400,2048]{1,0:T(8,128)(2,1)}, u32[]{:S(2)}, u32[]{:S(2)}) collective-permute-start(bf16[400,2048]{1,0:T(8,128)(2,1)} %get-tuple-element.108), channel_id=1, source_target_pairs={{0,1},{1,0},{2,3},{3,2},{4,5},{5,4},{6,7},{7,6},{8,9},{9,8},{10,11... | collective-permute-start | bytes 4915208 | tf_op jit(solution)/shard_map/ppermute | solution.py:45
  307.4 33.0 %collective-permute-start.42 = (bf16[384,1792]{1,0:T(8,128)(2,1)}, bf16[384,1792]{1,0:T(8,128)(2,1)S(1)}, u32[]{:S(2)}, u32[]{:S(2)}) collective-permute-start(bf16[384,1792]{1,0:T(8,128)(2,1)} %fusion.1.refs_2_.refs_1_), channel_id=1, source_target_pairs={{0,4},{4,8},{8,12},{12,0},{1,5},{5,9},{9,13},{13,1},{2,6},{6,10},{... | collective-permute-start | bytes 4128776 | tf_op jit(solution)/shard_map/ppermute | solution.py:50
  310.4 31.2 %collective-permute-start.40 = (bf16[208,2048]{1,0:T(8,128)(2,1)}, bf16[208,2048]{1,0:T(8,128)(2,1)}, u32[]{:S(2)}, u32[]{:S(2)}) collective-permute-start(bf16[208,2048]{1,0:T(8,128)(2,1)} %add_convert_fusion.1.refs_0_), channel_id=1, source_target_pairs={{0,2},{1,3},{2,0},{3,1},{4,6},{5,7},{6,4},{7,5},{8,10},{9,11},{10,... | collective-permute-start | bytes 2555912 | tf_op jit(solution)/shard_map/ppermute | solution.py:45
  319.9 21.6 %collective-permute-start.41 = (bf16[3,384,384]{2,1,0:T(8,128)(2,1)}, bf16[3,384,384]{2,1,0:T(8,128)(2,1)}, u32[]{:S(2)}, u32[]{:S(2)}) collective-permute-start(bf16[3,384,384]{2,1,0:T(8,128)(2,1)} %get-tuple-element.113), channel_id=1, source_target_pairs={{0,1},{1,0},{2,3},{3,2},{4,5},{5,4},{6,7},{7,6},{8,9},{9,8},{10,11... | collective-permute-start | bytes 2654216 | tf_op jit(solution)/shard_map/ppermute | solution.py:45
  333.7 22.7 %collective-permute-start.38 = (bf16[400,2048]{1,0:T(8,128)(2,1)}, bf16[400,2048]{1,0:T(8,128)(2,1)}, u32[]{:S(2)}, u32[]{:S(2)}) collective-permute-start(bf16[400,2048]{1,0:T(8,128)(2,1)} %get-tuple-element.111), channel_id=1, source_target_pairs={{0,1},{1,0},{2,3},{3,2},{4,5},{5,4},{6,7},{7,6},{8,9},{9,8},{10,11... | collective-permute-start | bytes 4915208 | tf_op jit(solution)/shard_map/ppermute | solution.py:45
  345.4 47.0 %collective-permute-start.46 = (bf16[384,640]{1,0:T(8,128)(2,1)}, bf16[384,640]{1,0:T(8,128)(2,1)}, u32[]{:S(2)}, u32[]{:S(2)}) collective-permute-start(bf16[384,640]{1,0:T(8,128)(2,1)} %concatenate.111), channel_id=1, source_target_pairs={{0,4},{4,8},{8,12},{12,0},{1,5},{5,9},{9,13},{13,1},{2,6},{6,10},{... | collective-permute-start | bytes 1474568 | tf_op jit(solution)/shard_map/ppermute | solution.py:50
  348.6 42.8 %collective-permute-start.45 = (bf16[384,640]{1,0:T(8,128)(2,1)}, bf16[384,640]{1,0:T(8,128)(2,1)}, u32[]{:S(2)}, u32[]{:S(2)}) collective-permute-start(bf16[384,640]{1,0:T(8,128)(2,1)} %concatenate.110), channel_id=1, source_target_pairs={{0,8},{4,12},{8,0},{12,4},{1,9},{5,13},{9,1},{13,5},{2,10},{6,14},... | collective-permute-start | bytes 1474568 | tf_op jit(solution)/shard_map/ppermute | solution.py:50
  352.7 43.4 %collective-permute-start.44 = (bf16[384,640]{1,0:T(8,128)(2,1)}, bf16[384,640]{1,0:T(8,128)(2,1)}, u32[]{:S(2)}, u32[]{:S(2)}) collective-permute-start(bf16[384,640]{1,0:T(8,128)(2,1)} %concatenate.109), channel_id=1, source_target_pairs={{0,12},{4,0},{8,4},{12,8},{1,13},{5,1},{9,5},{13,9},{2,14},{6,2},{... | collective-permute-start | bytes 1474568 | tf_op jit(solution)/shard_map/ppermute | solution.py:50
  356.0 37.4 %collective-permute-start.48 = (bf16[192,1792]{1,0:T(8,128)(2,1)}, bf16[192,1792]{1,0:T(8,128)(2,1)}, u32[]{:S(2)}, u32[]{:S(2)}) collective-permute-start(bf16[192,1792]{1,0:T(8,128)(2,1)} %slice.524), channel_id=1, source_target_pairs={{0,2},{1,3},{2,0},{3,1},{4,6},{5,7},{6,4},{7,5},{8,10},{9,11},{10,... | collective-permute-start | bytes 2064392 | tf_op jit(solution)/shard_map/ppermute | solution.py:45
  358.9 37.3 %collective-permute-start.39 = (bf16[208,2048]{1,0:T(8,128)(2,1)S(1)}, bf16[208,2048]{1,0:T(8,128)(2,1)}, u32[]{:S(2)}, u32[]{:S(2)}) collective-permute-start(bf16[208,2048]{1,0:T(8,128)(2,1)S(1)} %add_convert_fusion), channel_id=1, source_target_pairs={{0,2},{1,3},{2,0},{3,1},{4,6},{5,7},{6,4},{7,5},{8,10},{9,11},{10,... | collective-permute-start | bytes 2555912 | tf_op jit(solution)/shard_map/ppermute | solution.py:45
  395.5 19.4 %collective-permute-start.50 = (bf16[192,1792]{1,0:T(8,128)(2,1)}, bf16[192,1792]{1,0:T(8,128)(2,1)S(1)}, u32[]{:S(2)}, u32[]{:S(2)}) collective-permute-start(bf16[192,1792]{1,0:T(8,128)(2,1)} %add_convert_fusion.2.refs_16_), channel_id=1, source_target_pairs={{0,16},{16,0},{1,17},{17,1},{2,18},{18,2},{3,19},{19,3},{4,20},{20... | collective-permute-start | bytes 2064392 | tf_op jit(solution)/shard_map/ppermute | solution.py:54
  399.6 6.9 %collective-permute-start.47 = (bf16[192,640]{1,0:T(8,128)(2,1)S(1)}, bf16[192,640]{1,0:T(8,128)(2,1)S(1)}, u32[]{:S(2)}, u32[]{:S(2)}) collective-permute-start(bf16[192,640]{1,0:T(8,128)(2,1)S(1)} %concatenate.113.refs_13_), channel_id=1, source_target_pairs={{0,2},{1,3},{2,0},{3,1},{4,6},{5,7},{6,4},{7,5},{8,10},{9,11},{10,... | collective-permute-start | bytes 737288 | tf_op jit(solution)/shard_map/ppermute | solution.py:45
  407.7 11.4 %collective-permute-start.49 = (bf16[192,640]{1,0:T(8,128)(2,1)}, bf16[192,640]{1,0:T(8,128)(2,1)S(1)}, u32[]{:S(2)}, u32[]{:S(2)}) collective-permute-start(bf16[192,640]{1,0:T(8,128)(2,1)} %concatenate.114.refs_15_), channel_id=1, source_target_pairs={{0,16},{16,0},{1,17},{17,1},{2,18},{18,2},{3,19},{19,3},{4,20},{20... | collective-permute-start | bytes 737288 | tf_op jit(solution)/shard_map/ppermute | solution.py:54
  (44 other events, 445.2 us)
